TPU v7x, 32 devices: a whole 2x2x4 slice. The times are simulated.
32 devices in a mesh: paths: 32 (over z, y, x, core).
Axes of the slice: x: 2, y: 2, z: 4, core: 2. Of those that a mesh axis runs over, the one named last changes fastest.
Arguments:
- params: float32 [256, 4], replicated, may hold values from -0.9 to 2, as said below
- increments: bfloat16 [2, 64, 4096], P(None, None, 'paths'), may hold values from -5 to 5
- w_in: bfloat16 [6, 1024], replicated, may hold values from -2.5 to 2.5
- b_in: float32 [1024], replicated, may hold values from -3 to 3
- w_mid: bfloat16 [1024, 1024], replicated, may hold values from -0.1875 to 0.1875
- b_mid: float32 [1024], replicated, may hold values from -3 to 3
- w_out: bfloat16 [1024], replicated, may hold values from -0.1875 to 0.1875
- b_out: float32 [1], replicated, may hold values from -3 to 3
Outputs:
- prices: float32 [256, 88], P('paths')
- direction_w_in: float32 [6, 1024], replicated
- direction_b_in: float32 [1024], replicated
- direction_w_mid: float32 [1024, 1024], replicated
- direction_b_mid: float32 [1024], replicated
- direction_w_out: float32 [1024], replicated
- direction_b_out: float32 [1], replicated
Inputs may be any that keep to these rules, and one draw needn't show every extreme that they name: `params`: each row holds a Hurst index in [0.05, 0.45], a vol-of-vol in [0.8, 2.0], a correlation in [-0.9, -0.3] and an initial forward variance in [0.01, 0.15].
All inputs are finite; a program needn't handle non-finite values.
Results may differ from a plain program's by a relative error of at most 0.0003.
The roundings to bfloat16 on the way count: a program that leaves them out, or rounds other values in their place, can miss the bound.
Values sent between devices are 32-bit elements; how exact they have to be, the bound alone decides.
No kernel may reach another device: no remote copies, remote signals or barrier semaphores. Data moves between devices by JAX's collectives and lax.ppermute only.
A program may use at most 64 MiB of HBM per device.

v0:
```python
import math

import jax
import jax.numpy as jnp
from jax import lax
from jax.sharding import PartitionSpec as P

STEPS = 64
MATS = 8
STRIKES = 11
PAIRS = 88


EPSILON = 1e-06


def strike_grid():
    tenors = (jnp.arange(MATS, dtype=jnp.float32) + 1.0) / MATS
    offsets = jnp.arange(STRIKES, dtype=jnp.float32) - (STRIKES - 1) / 2.0
    log_strike = 0.05 * offsets[None, :] * jnp.sqrt(tenors)[:, None]
    return (tenors, log_strike)


def payoff_sums(block_params, increments):
    count = block_params.shape[0]
    paths_here = increments.shape[2]
    hurst = block_params[:, 0]
    vol_of_vol = block_params[:, 1]
    correl = block_params[:, 2]
    forward_var = block_params[:, 3]
    delta_t = 1.0 / STEPS
    position = jnp.arange(STEPS, dtype=jnp.float32)
    lag = position[:, None] - position[None, :]
    lag_high = jnp.maximum(lag, 1.0)
    exponent = (hurst + 0.5)[:, None, None]
    powers = jnp.power(lag_high[None], exponent) - jnp.power(lag_high[None] - 1.0, exponent)
    front = jnp.sqrt(2.0 * hurst) * jnp.power(delta_t, hurst) / (hurst + 0.5)
    kernel = jnp.where((lag >= 1.0)[None], powers * front[:, None, None], 0.0).astype(jnp.bfloat16)
    drive = jnp.dot(
        kernel.reshape(count * STEPS, STEPS), increments[0], preferred_element_type=jnp.float32
    )
    drive = drive.reshape(count, STEPS, paths_here)
    times = position * delta_t
    compensator = (
        0.5
        * vol_of_vol[:, None]
        * vol_of_vol[:, None]
        * jnp.power(times[None, :], 2.0 * hurst[:, None])
    )
    variance = forward_var[:, None, None] * jnp.exp(
        vol_of_vol[:, None, None] * drive - compensator[:, :, None]
    )
    first_noise = increments[0].astype(jnp.float32)
    second_noise = increments[1].astype(jnp.float32)
    shock = (
        correl[:, None, None] * first_noise[None]
        + jnp.sqrt(1.0 - correl * correl)[:, None, None] * second_noise[None]
    )
    moves = jnp.sqrt(variance * delta_t) * shock - 0.5 * delta_t * variance
    log_spot = jnp.cumsum(moves.reshape(count, MATS, STEPS // MATS, paths_here).sum(axis=2), axis=1)
    tenors, log_strike = strike_grid()
    spot = jnp.exp(log_spot)
    gains = jnp.maximum(spot[:, :, None, :] - jnp.exp(log_strike)[None, :, :, None], 0.0)
    return jnp.sum(gains, axis=3).reshape(count, PAIRS)


def evolve(set_rows, increments, total_paths):
    count = set_rows.shape[0]
    block = math.gcd(count, 128)
    groups = set_rows.reshape(count // block, block, 4)
    sums = lax.map(lambda group: payoff_sums(group, increments), groups)
    return sums.reshape(count, PAIRS) / total_paths


def features(set_rows):
    count = set_rows.shape[0]
    tenors, log_strike = strike_grid()
    scaled = set_rows * jnp.array([4.0, 1.0, 1.0, 20.0], dtype=jnp.float32)
    per_pair = jnp.stack([4.0 * log_strike.reshape(PAIRS), jnp.repeat(tenors, STRIKES)], axis=1)
    left = jnp.broadcast_to(scaled[:, None, :], (count, PAIRS, 4))
    right = jnp.broadcast_to(per_pair[None], (count, PAIRS, 2))
    return jnp.concatenate([left, right], axis=2).reshape(count * PAIRS, 6).astype(jnp.bfloat16)


def silu_slope(value):
    logistic = jax.nn.sigmoid(value)
    return logistic * (1.0 + value * (1.0 - logistic))


def contract_rows(left, right):
    return lax.dot_general(
        left, right, (((0,), (0,)), ((), ())), preferred_element_type=jnp.float32
    )


def local_terms(inputs, target, w_in, b_in, w_mid, b_mid, w_out, b_out, inv_sets):
    raw_in = jnp.dot(inputs, w_in, preferred_element_type=jnp.float32) + b_in
    hidden_in = jax.nn.silu(raw_in).astype(jnp.bfloat16)
    raw_mid = jnp.dot(hidden_in, w_mid, preferred_element_type=jnp.float32) + b_mid
    hidden_mid = jax.nn.silu(raw_mid).astype(jnp.bfloat16)
    predicted = jnp.dot(hidden_mid, w_out, preferred_element_type=jnp.float32) + b_out[0]
    slope = (predicted - target) * inv_sets
    grad_out = jnp.sum(hidden_mid.astype(jnp.float32) * slope[:, None], axis=0)
    grad_bout = jnp.sum(slope, keepdims=True)
    delta_mid = (slope[:, None] * w_out.astype(jnp.float32)[None, :] * silu_slope(raw_mid)).astype(
        jnp.bfloat16
    )
    grad_bmid = jnp.sum(delta_mid.astype(jnp.float32), axis=0)
    backward = lax.dot_general(
        delta_mid, w_mid, (((1,), (1,)), ((), ())), preferred_element_type=jnp.float32
    )
    delta_in = (backward * silu_slope(raw_in)).astype(jnp.bfloat16)
    grad_in = contract_rows(inputs, delta_in)
    grad_bin = jnp.sum(delta_in.astype(jnp.float32), axis=0)
    return ((grad_in, grad_bin, grad_bmid, grad_out, grad_bout), hidden_in, delta_mid)


def directions(grad_w, grad_b):
    entries = grad_w.size + grad_b.size
    mean_square = (jnp.sum(grad_w * grad_w) + jnp.sum(grad_b * grad_b)) / entries
    factor = lax.rsqrt(mean_square + EPSILON)
    return (grad_w * factor, grad_b * factor)


def on_device(params, increments, w_in, b_in, w_mid, b_mid, w_out, b_out):
    devices = lax.axis_size("paths")
    total_paths = increments.shape[2] * devices
    set_count = params.shape[0]
    set_dev = set_count // devices
    owner = lax.axis_index("paths")
    every_set = evolve(params, increments, total_paths)
    summed = lax.psum(every_set, "paths")
    prices = lax.dynamic_slice_in_dim(summed, owner * set_dev, set_dev, 0)
    own_params = lax.dynamic_slice_in_dim(params, owner * set_dev, set_dev, 0)
    small, hidden_in, delta_mid = local_terms(
        features(own_params),
        prices.reshape(-1),
        w_in,
        b_in,
        w_mid,
        b_mid,
        w_out,
        b_out,
        1.0 / set_count,
    )
    grad_mid = contract_rows(hidden_in, delta_mid)
    grad_in, grad_bin, grad_bmid, grad_out, grad_bout, grad_mid = lax.psum(
        (small[0], small[1], small[2], small[3], small[4], grad_mid), "paths"
    )
    direction_w_mid, direction_b_mid = directions(grad_mid, grad_bmid)
    direction_w_in, direction_b_in = directions(grad_in, grad_bin)
    direction_w_out, direction_b_out = directions(grad_out, grad_bout)
    return (
        prices,
        direction_w_in,
        direction_b_in,
        direction_w_mid,
        direction_b_mid,
        direction_w_out,
        direction_b_out,
    )


def solution(mesh):
    in_specs = (P(), P(None, None, "paths"), P(), P(), P(), P(), P(), P())
    out_specs = (P("paths", None), P(), P(), P(), P(), P(), P())
    return jax.shard_map(
        on_device, mesh=mesh, in_specs=in_specs, out_specs=out_specs, check_vma=False
    )
```

profile of v0, /device:TPU:0, one launch (start us, length us, event | category | flops | bytes accessed | tf_op | source)
XLA Modules:
  0.0 334.6 jit_solution(1939465560943707398)
XLA Ops:
  7.3 28.0 %while.12 = (s32[]{:T(128)}, f32[2,128,88]{1,2,0:T(8,128)S(1)}, f32[2,128,4]{1,2,0:T(4,128)}, bf16[2,64,128]{2,1,0:T(8,128)(2,1)}, s32[]{:T(128)}) while((s32[]{:T(128)}, f32[2,128,88]{1,2,0:T(8,128)S(1)}, f32[2,128,4]{1,2,0:T(4,128)}, bf16[2,64,128]{2,1,0:T(8,128)(2,1)}, s32[]{:T(128)}) %tuple.59), condition=%wide.region_4.5_spmd, body=%wide.region_0.4_spmd.sunk | while | flops 152996288 | bytes 3797413 | solution.py:71
  7.4 0.9 bitcast_convert_fusion.3
  8.2 0.7 dynamic-slice_bitcast_fusion.2
  9.0 0.1 power_multiply_fusion.2
  9.1 9.3 %bitcast_reduce_fusion.2 = f32[128,8,128]{2,0,1:T(8,128)S(1)} fusion(f32[64,128]{1,0:T(8,128)S(1)} %get-tuple-element.135, f32[128]{0:T(128)S(1)} %get-tuple-element.136, f32[64,128]{1,0:T(8,128)S(1)} %get-tuple-element.137, f32[128]{0:T(128)S(1)} %get-tuple-element.138, f32[128,64]{0,1:T(8,128)S(1)} %power_multiply_fusion.2, ...), kind=kOutput, calls=%fused_computation.1.clone.1 | convolution fusion | flops 147718144 | bytes 678912 | tf_op jit(solution)/shard_map/while/body/eval_jaxpr/dot_general | solution.py:39
  18.4 0.5 reduce-window_exponential_fusion.2
  18.9 0.3 copy.28
  19.2 1.6 maximum_reduce_fusion.2
  20.9 0.4 copy.29
  21.5 0.7 bitcast_convert_fusion.3
  22.2 0.7 dynamic-slice_bitcast_fusion.2
  22.9 0.1 power_multiply_fusion.2
  23.1 9.3 %bitcast_reduce_fusion.2 = f32[128,8,128]{2,0,1:T(8,128)S(1)} fusion(f32[64,128]{1,0:T(8,128)S(1)} %get-tuple-element.135, f32[128]{0:T(128)S(1)} %get-tuple-element.136, f32[64,128]{1,0:T(8,128)S(1)} %get-tuple-element.137, f32[128]{0:T(128)S(1)} %get-tuple-element.138, f32[128,64]{0,1:T(8,128)S(1)} %power_multiply_fusion.2, ...), kind=kOutput, calls=%fused_computation.1.clone.1 | convolution fusion | flops 147718144 | bytes 678912 | tf_op jit(solution)/shard_map/while/body/eval_jaxpr/dot_general | solution.py:39
  32.4 0.5 reduce-window_exponential_fusion.2
  32.9 0.3 copy.28
  33.2 1.6 maximum_reduce_fusion.2
  34.8 0.4 copy.29
  35.3 0.8 copy.25
  36.1 0.2 all-reduce.6.cloned.1.call-start
  36.5 0.1 stack_reshape.3
  36.6 0.1 mul.419
  36.8 0.8 multiply_convert_fusion.4
  37.6 0.1 convert_element_type.50
  37.7 0.6 fusion.16
  38.4 4.3 %multiply_convert_fusion.2 = (bf16[704,1024]{1,0:T(8,128)(2,1)S(1)}, f32[704,1024]{1,0:T(8,128)}) fusion(f32[1024]{0:T(1024)S(1)} %copy-done.8, bf16[1024,1024]{1,0:T(8,128)(2,1)S(1)} %copy-done, f32[704,1024]{1,0:T(8,128)S(1)} %fusion.16, f32[1024]{0:T(1024)} %param.14), kind=kOutput, calls=%fused_computation.42 | convolution fusion | flops 1485045760 | bytes 9314304 | tf_op jit(solution)/shard_map/dot_general | solution.py:99
  42.7 0.5 convolution_reduce_fusion
  43.2 0.6 convert_element_type.53
  44.5 117.0 %all-reduce.4.cloned.1.call-done = f32[256,88]{1,0:T(8,128)} async-done(((f32[256,88]{1,0:T(8,128)}), f32[256,88]{1,0:T(8,128)}) %all-reduce.4.cloned.1.call-update) | async-done | bytes 90128 | tf_op jit(solution)/shard_map/psum | solution.py:132
  161.4 1.3 constant_dynamic-slice_fusion
  162.7 1.4 reshape.304
  164.1 1.3 fusion.15
  165.4 4.1 %convert_reduce_fusion = (f32[1024]{0:T(1024)S(1)}, bf16[704,1024]{1,0:T(8,128)(2,1)S(1)}, f32[1024]{0:T(1024)}) fusion(f32[704,1024]{1,0:T(8,128)} %get-tuple-element.93, f32[1024]{0:T(1024)} %param.16, f32[1024]{0:T(1024)} %convert_element_type.53, f32[704]{0:T(1024)S(1)} %get-tuple-element.76, bf16[704,1024]{1,0:T(8,128)(2,1)S(1)} %get-tuple-element.92), kind=kLoop, calls=%fused_computation.38 | loop fusion | flops 11532288 | bytes 5786368 | tf_op jit(solution)/shard_map/reduce_sum | solution.py:108
  169.4 1.1 copy-done.3
  170.6 3.9 %fusion.13 = f32[1024,1024]{1,0:T(8,128)} fusion(bf16[704,1024]{1,0:T(8,128)(2,1)S(1)} %get-tuple-element.78, f32[704,1024]{1,0:T(8,128)S(1)} %copy-done.2, f32[1024]{0:T(1024)S(1)} %copy-done.10), kind=kOutput, calls=%fused_computation.66 | convolution fusion | flops 1480720384 | bytes 8523776 | tf_op jit(solution)/shard_map/dot_general | solution.py:91
  174.5 1.3 copy-done.4
  175.8 4.7 %convert_reduce_fusion.1 = (f32[1024]{0:T(1024)}, bf16[704,1024]{1,0:T(8,128)(2,1)S(1)}) fusion(f32[704,1024]{1,0:T(8,128)} %copy-done.1, f32[1024]{0:T(1024)} %param.14, bf16[704,1024]{1,0:T(8,128)(2,1)S(1)} %copy-done.4, bf16[1024,1024]{1,0:T(8,128)(2,1)S(1)} %copy-done), kind=kOutput, calls=%fused_computation.39 | convolution fusion | flops 1485044736 | bytes 7872512 | tf_op jit(solution)/shard_map/dot_general | solution.py:109
  180.6 0.3 fusion.17
  180.9 40.6 %all-reduce = (f32[6,1024]{1,0:T(8,128)S(1)}, f32[1024]{0:T(1024)S(1)}, f32[1024]{0:T(1024)S(1)}, f32[1024]{0:T(1024)S(1)}, f32[1]{0:T(128)}) all-reduce(f32[6,1024]{1,0:T(8,128)S(1)} %fusion.17, f32[1024]{0:T(1024)} %get-tuple-element.94, f32[1024]{0:T(1024)S(1)} %get-tuple-element.77, ...), channel_id=1, replica_groups=mesh['paths'=32] {'paths'}, use_global_device_ids=true, to_apply=%region_6.7 | all-reduce | flops 9217 | bytes 73736 | tf_op jit(solution)/shard_map/psum | solution.py:147
  221.4 0.6 multiply_reduce_fusion.3
  222.0 0.6 multiply_reduce_fusion.2
  226.6 0.6 multiply_reduce_fusion.4
  227.2 0.6 broadcast_multiply_fusion.3
  227.8 0.6 broadcast_multiply_fusion.5
  228.4 0.6 broadcast_multiply_fusion.2
  229.0 86.8 %all-reduce.6.cloned.1.call-done = f32[1024,1024]{1,0:T(8,128)} async-done(((f32[1024,1024]{1,0:T(8,128)}), f32[1024,1024]{1,0:T(8,128)}) %all-reduce.6.cloned.1.call-update) | async-done | bytes 4194320 | tf_op jit(solution)/shard_map/psum | solution.py:147
  315.8 3.9 %multiply_reduce_fusion = f32[]{:T(128)} fusion(f32[1024,1024]{1,0:T(8,128)} %all-reduce.6.cloned.1.call-done), kind=kLoop, calls=%fused_computation.36 | loop fusion | flops 2097151 | bytes 4194308 | tf_op jit(solution)/shard_map/reduce_sum | solution.py:120
  321.0 0.6 broadcast_multiply_fusion.4
  321.6 5.0 %broadcast_multiply_fusion = f32[1024,1024]{1,0:T(8,128)} fusion(f32[1024,1024]{1,0:T(8,128)} %all-reduce.6.cloned.1.call-done, f32[]{:T(128)S(6)} %rsqrt.10), kind=kLoop, calls=%fused_computation.46 | loop fusion | flops 1048576 | bytes 8388612 | tf_op jit(solution)/shard_map/mul | solution.py:122
  (55 shorter events, 0.8 us)
Async XLA Ops:
  7.2 31.2 %copy-start = (bf16[1024,1024]{1,0:T(8,128)(2,1)S(1)}, bf16[1024,1024]{1,0:T(8,128)(2,1)}, u32[]{:S(2)}) copy-start(bf16[1024,1024]{1,0:T(8,128)(2,1)} %param.15) | copy-start | bytes 6291460
  7.2 154.3 %all-reduce.4.cloned.1.call-start = ((), (), s32[]{:S(2)}) async-start(), calls=%async_computation | async-start | bytes 262144 | tf_op jit(solution)/shard_map/psum | solution.py:132
  7.2 29.5 %copy-start.9 = (f32[4]{0:T(128)S(1)}, f32[4]{0:T(128)}, u32[]{:S(2)}) copy-start(f32[4]{0:T(128)} %constant.125.clone) | copy-start | bytes 52
  7.2 30.5 %copy-start.6 = (bf16[1024]{0:T(1024)(128)(2,1)S(1)}, bf16[1024]{0:T(1024)(128)(2,1)}, u32[]{:S(2)}) copy-start(bf16[1024]{0:T(1024)(128)(2,1)} %param.17) | copy-start | bytes 6148
  7.3 30.5 %copy-start.5 = (bf16[6,1024]{1,0:T(8,128)(2,1)S(1)}, bf16[6,1024]{1,0:T(8,128)(2,1)}, u32[]{:S(2)}) copy-start(bf16[6,1024]{1,0:T(8,128)(2,1)} %param.13) | copy-start | bytes 36868
  35.3 3.0 copy-start.8
  36.1 279.7 %all-reduce.6.cloned.1.call-start = ((), (), s32[]{:S(2)}) async-start(), calls=%async_computation.1 | async-start | bytes 8388608 | tf_op jit(solution)/shard_map/psum | solution.py:147
  38.3 4.3 %copy-start.1 = (f32[704,1024]{1,0:T(8,128)}, f32[704,1024]{1,0:T(8,128)S(1)}, u32[]{:S(2)}) copy-start(f32[704,1024]{1,0:T(8,128)S(1)} %fusion.16) | copy-start | bytes 8650756
  38.4 4.8 %copy-start.7 = (bf16[1024]{0:T(1024)(128)(2,1)S(1)}, bf16[1024]{0:T(1024)(128)(2,1)}, u32[]{:S(2)}) copy-start(bf16[1024]{0:T(1024)(128)(2,1)} %param.17) | copy-start | bytes 6148
  165.4 5.2 %copy-start.2 = (f32[704,1024]{1,0:T(8,128)S(1)}, f32[704,1024]{1,0:T(8,128)}, u32[]{:S(2)}) copy-start(f32[704,1024]{1,0:T(8,128)} %copy-done.1) | copy-start | bytes 8650756
  165.4 5.2 %copy-start.10 = (f32[1024]{0:T(1024)S(1)}, f32[1024]{0:T(1024)}, u32[]{:S(2)}) copy-start(f32[1024]{0:T(1024)} %param.14) | copy-start | bytes 12292
  169.4 1.1 copy-start.3
  174.5 1.4 copy-start.4
Sparse Core Ops, SparseCore 0:
  36.2 125.1 all-reduce.3
  174.6 141.1 all-reduce.5
where the time goes:
time: 336 us; the launch traced here: 335 us
  waiting for transfers between devices  204 us (61%)
  blocking collectives  40.6 us (12%)
  matrix products  32.9 us (10%)
  other arithmetic  26.4 us (8%)
  between operations  21.3 us (6%)
  local copies, waits for them, and re-layouts  9.2 us (3%)
    psum x1, waiting for transfers between devices, on_device(): summed = lax.psum(every_set, 'paths')  117 us
    psum x1, waiting for transfers between devices, on_device(): lax.psum((small[0], small[1], small[2], small[3], small[4], grad_mid), 'p...  86.8 us
    psum x1, blocking collectives, on_device(): lax.psum((small[0], small[1], small[2], small[3], small[4], grad_mid), 'p...  40.6 us
    dot_general x2, matrix products, payoff_sums(): jnp.dot(kernel.reshape(count * STEPS, STEPS), increments[0], preferred_el...  18.5 us
    mul x5, other arithmetic, directions(): return (grad_w * factor, grad_b * factor)  7.43 us
  transfers between devices with their start and end apart: 2, of which 2 were waited for; matrix products, arithmetic and copies ran while one was open for 5% of the time, Pallas kernels for 0%

commit v1 on v0

v1 whole, which is shorter than its diff:
```python
import math

import jax
import jax.numpy as jnp
import numpy as np
from jax import lax
from jax.experimental import pallas as pl
from jax.experimental.pallas import tpu as pltpu
from jax.sharding import PartitionSpec as P

STEPS = 64
MATS = 8
STRIKES = 11
PAIRS = 88
WIDTH = 1024
LANES = 128
SMALL_ROWS = 10
EPSILON = 1e-06


TENORS = (np.arange(MATS, dtype=np.float32) + np.float32(1.0)) / np.float32(MATS)
OFFSETS = np.arange(STRIKES, dtype=np.float32) - np.float32((STRIKES - 1) / 2.0)
LOG_STRIKE = np.float32(0.05) * OFFSETS[None, :] * np.sqrt(TENORS)[:, None]
STRIKE = np.exp(LOG_STRIKE).astype(np.float32)
SET_BLOCK = 256
LOG2E = 1.4426950408889634


def strike_grid():
    return (jnp.asarray(TENORS), jnp.asarray(LOG_STRIKE))


def bf16_pieces(value):
    high = value.astype(jnp.bfloat16)
    rest = value - high.astype(jnp.float32)
    mid = rest.astype(jnp.bfloat16)
    low = (rest - mid.astype(jnp.float32)).astype(jnp.bfloat16)
    return high, mid, low


def pricing_kernel(strike_ref, params_ref, inc_ref, out_ref, lags_ref, noise_ref, comp_ref, pay_ref):
    sets = params_ref.shape[1]
    paths = inc_ref.shape[2]
    hurst = params_ref[0:1, :]
    vol_of_vol = params_ref[1:2, :]
    correl = params_ref[2:3, :]
    forward_var = params_ref[3:4, :]
    delta_t = 1.0 / STEPS

    lag = (LANES - lax.broadcasted_iota(jnp.int32, (LANES, 1), 0)).astype(jnp.float32)
    exponent = hurst + 0.5
    here = jnp.exp2(exponent * jnp.log2(lag))
    before = jnp.exp2(exponent * jnp.log2(jnp.maximum(lag - 1.0, 1.0)))
    before = jnp.where(lag > 1.5, before, 0.0)
    front = jnp.sqrt(2.0 * hurst) * jnp.exp2(hurst * math.log2(delta_t)) / exponent
    weights = jnp.where(lag < STEPS - 0.5, (here - before) * front, 0.0).astype(jnp.bfloat16)

    half_scale = vol_of_vol * (0.5 * LOG2E)
    step = lax.broadcasted_iota(jnp.int32, (STEPS, 1), 0).astype(jnp.float32)
    powers = jnp.exp2(2.0 * hurst * jnp.log2(jnp.maximum(step, 1.0) * delta_t))
    comp_ref[...] = jnp.where(step > 0.5, powers * (0.25 * LOG2E * vol_of_vol * vol_of_vol), 0.0)

    root = jnp.sqrt(forward_var * delta_t)
    back = 2.0 / root
    growth = (0.5 * LOG2E) * forward_var * delta_t
    noise_weights = jnp.concatenate(
        [
            jnp.broadcast_to(piece.astype(jnp.float32), (8, sets))
            for value in (correl * back, jnp.sqrt(1.0 - correl * correl) * back)
            for piece in bf16_pieces(value)
        ]
        + [jnp.zeros((LANES - 48, sets), jnp.float32)],
        axis=0,
    ).astype(jnp.bfloat16)

    first = inc_ref[0].astype(jnp.float32)
    second = inc_ref[1].astype(jnp.float32)
    lags_ref[...] = jnp.concatenate([first, jnp.zeros((LANES - STEPS, paths), jnp.float32)], 0).T
    for m in range(MATS):
        rows = slice(8 * m, 8 * m + 8)
        block = jnp.concatenate(
            [first[rows]] * 3 + [second[rows]] * 3 + [jnp.zeros((LANES - 48, paths), jnp.float32)], 0
        )
        noise_ref[m] = block.T.astype(jnp.bfloat16)
    lane = lax.broadcasted_iota(jnp.int32, (paths, LANES), 1)

    def maturity(m, total):
        noise = noise_ref[m]
        for k in range(8):
            i = 8 * m + k
            window = lags_ref[...] if k == 0 else pltpu.roll(lags_ref[...], LANES - k, 1)
            drive = jnp.dot(
                window.astype(jnp.bfloat16), weights, preferred_element_type=jnp.float32
            )
            picked = jnp.where(lane % 8 == k, noise.astype(jnp.float32), 0.0).astype(jnp.bfloat16)
            shock = jnp.dot(picked, noise_weights, preferred_element_type=jnp.float32)
            root_variance = jnp.exp2(drive * half_scale - comp_ref[pl.ds(i, 1), :])
            total = total + root_variance * (shock - root_variance)
        lags_ref[...] = pltpu.roll(lags_ref[...], LANES - 8, 1)
        spot = jnp.exp2(total * growth)
        for j in range(STRIKES):
            strike = strike_ref[m, j]
            gains = jnp.maximum(spot, strike).reshape(paths // 8, 8, sets).sum(axis=0)
            gains = gains - strike * (paths // 8)
            pay_ref[pl.ds(m * STRIKES + j, 1), :] = jnp.sum(gains, axis=0, keepdims=True)
        return total

    lax.fori_loop(0, MATS, maturity, jnp.zeros((paths, sets), jnp.float32))
    out_ref[...] = pay_ref[...].T[:, :PAIRS]


def payoff_sums(params, increments):
    count = params.shape[0]
    paths = increments.shape[2]
    sets = math.gcd(count, SET_BLOCK)
    return pl.pallas_call(
        pricing_kernel,
        grid=(count // sets,),
        in_specs=[
            pl.BlockSpec(memory_space=pltpu.SMEM),
            pl.BlockSpec((4, sets), lambda b: (0, b)),
            pl.BlockSpec((2, STEPS, paths), lambda b: (0, 0, 0)),
        ],
        out_specs=pl.BlockSpec((sets, PAIRS), lambda b: (b, 0)),
        out_shape=jax.ShapeDtypeStruct((count, PAIRS), jnp.float32),
        scratch_shapes=[
            pltpu.VMEM((paths, LANES), jnp.float32),
            pltpu.VMEM((MATS, paths, LANES), jnp.bfloat16),
            pltpu.VMEM((STEPS, sets), jnp.float32),
            pltpu.VMEM((LANES, sets), jnp.float32),
        ],
        compiler_params=pltpu.CompilerParams(vmem_limit_bytes=32 * 1024 * 1024),
        name="pricing",
    )(jnp.asarray(STRIKE), params.T, increments)


def features(set_rows):
    count = set_rows.shape[0]
    tenors, log_strike = strike_grid()
    scaled = set_rows * jnp.array([4.0, 1.0, 1.0, 20.0], dtype=jnp.float32)
    per_pair = jnp.stack([4.0 * log_strike.reshape(PAIRS), jnp.repeat(tenors, STRIKES)], axis=1)
    left = jnp.broadcast_to(scaled[:, None, :], (count, PAIRS, 4))
    right = jnp.broadcast_to(per_pair[None], (count, PAIRS, 2))
    return jnp.concatenate([left, right], axis=2).reshape(count * PAIRS, 6).astype(jnp.bfloat16)


def silu_slope(value):
    logistic = jax.nn.sigmoid(value)
    return logistic * (1.0 + value * (1.0 - logistic))


def contract_rows(left, right):
    return lax.dot_general(
        left, right, (((0,), (0,)), ((), ())), preferred_element_type=jnp.float32
    )


def block_gradients(inputs, target, w_in, b_in, w_mid, b_mid, w_out, b_out, inv_sets, block, cols):
    def own(array, axis):
        return lax.dynamic_slice_in_dim(array, block * cols, cols, axis)

    raw_in = jnp.dot(inputs, w_in, preferred_element_type=jnp.float32) + b_in
    hidden_in = jax.nn.silu(raw_in).astype(jnp.bfloat16)
    raw_mid = jnp.dot(hidden_in, w_mid, preferred_element_type=jnp.float32) + b_mid
    hidden_mid = jax.nn.silu(raw_mid).astype(jnp.bfloat16)
    predicted = jnp.dot(hidden_mid, w_out, preferred_element_type=jnp.float32) + b_out[0]
    slope = (predicted - target) * inv_sets
    grad_out = jnp.sum(own(hidden_mid, 1).astype(jnp.float32) * slope[:, None], axis=0)
    grad_bout = jnp.broadcast_to(jnp.sum(slope), (cols,))
    delta_mid = (slope[:, None] * w_out.astype(jnp.float32)[None, :] * silu_slope(raw_mid)).astype(
        jnp.bfloat16
    )
    own_mid = own(delta_mid, 1)
    grad_bmid = jnp.sum(own_mid.astype(jnp.float32), axis=0)
    backward = lax.dot_general(
        delta_mid, own(w_mid, 0), (((1,), (1,)), ((), ())), preferred_element_type=jnp.float32
    )
    delta_in = (backward * silu_slope(own(raw_in, 1))).astype(jnp.bfloat16)
    grad_in = contract_rows(inputs, delta_in)
    grad_bin = jnp.sum(delta_in.astype(jnp.float32), axis=0)
    small = jnp.concatenate(
        [grad_in, grad_bin[None], grad_bmid[None], grad_out[None], grad_bout[None]], axis=0
    )
    return contract_rows(hidden_in, own_mid), small


def swap(array, bit, devices):
    return lax.ppermute(array, "paths", [(i, i ^ bit) for i in range(devices)])


def pick(array, index):
    return lax.dynamic_index_in_dim(array, index, 0, keepdims=False)


def on_device(params, increments, w_in, b_in, w_mid, b_mid, w_out, b_out):
    devices = lax.axis_size("paths")
    top = devices // 2
    groups = devices // 4
    total_paths = increments.shape[2] * devices
    set_count = params.shape[0]
    set_dev = set_count // devices
    owner = lax.axis_index("paths")
    core = owner % 2
    high = owner // top
    group = (owner // 2) % groups

    sums = payoff_sums(params, increments).reshape(devices, set_dev, PAIRS)
    parts = lax.all_to_all(sums, "paths", 0, 0, tiled=True)
    prices = jnp.sum(parts, axis=0) / total_paths
    other = swap(prices, 1, devices)
    pair = jnp.stack([jnp.where(core == 0, prices, other), jnp.where(core == 0, other, prices)])
    far = swap(pair, top, devices)
    quad = jnp.stack([jnp.where(high == 0, pair, far), jnp.where(high == 0, far, pair)])

    rows = pick(params.reshape(2, groups, 2 * set_dev, 4).swapaxes(0, 1), group).reshape(-1, 4)
    cols = WIDTH // 4
    block = 2 * high + core
    big, small = block_gradients(
        features(rows), quad.reshape(-1), w_in, b_in, w_mid, b_mid, w_out, b_out,
        1.0 / set_count, block, cols,
    )
    piece_rows = WIDTH // groups
    big = big.reshape(groups, piece_rows, 2, LANES).swapaxes(1, 2)
    small = small.reshape(2 * SMALL_ROWS, LANES)
    small = jnp.pad(small, ((0, 8 * groups - 2 * SMALL_ROWS), (0, 0))).reshape(groups, 8, LANES)
    held = jnp.concatenate([big.reshape(groups, 2 * piece_rows, LANES), small], axis=1)

    bit = groups // 2
    while bit:
        mine = (group // bit) % 2
        halves = held.reshape((2, held.shape[0] // 2) + held.shape[1:])
        held = pick(halves, mine) + swap(pick(halves, 1 - mine), 2 * bit, devices)
        bit //= 2

    gathered = held.reshape((1,) + held.shape[1:])
    bit = top
    while bit:
        came = swap(gathered, bit, devices)
        first = (owner // bit) % 2 == 0
        pair = jnp.stack([jnp.where(first, gathered, came), jnp.where(first, came, gathered)])
        if bit == top:
            gathered = pair.reshape((-1,) + pair.shape[2:])
        else:
            gathered = jnp.swapaxes(pair, 0, 1).reshape((-1,) + pair.shape[2:])
        bit //= 2
    whole = gathered.reshape(2, groups, 2, 2 * piece_rows + 8, LANES)
    big = whole[:, :, :, : 2 * piece_rows].reshape(2, groups, 2, 2, piece_rows, LANES)
    grad_mid = big.transpose(1, 4, 0, 2, 3, 5).reshape(WIDTH, WIDTH)
    small = whole[:, :, :, 2 * piece_rows :].transpose(1, 3, 0, 2, 4)
    small = small.reshape(groups * 8, 2, 2, LANES)[: 2 * SMALL_ROWS]
    small = small.reshape(SMALL_ROWS, 2, 2, 2, LANES).transpose(0, 2, 3, 1, 4)
    small = small.reshape(SMALL_ROWS, WIDTH)

    def directions(grad_w, grad_b):
        entries = grad_w.size + grad_b.size
        mean_square = (jnp.sum(grad_w * grad_w) + jnp.sum(grad_b * grad_b)) / entries
        factor = lax.rsqrt(mean_square + EPSILON)
        return (grad_w * factor, grad_b * factor)

    direction_w_mid, direction_b_mid = directions(grad_mid, small[7])
    direction_w_in, direction_b_in = directions(small[:6], small[6])
    direction_w_out, direction_b_out = directions(small[8], small[9, :1])
    return (
        prices.reshape(set_dev, PAIRS),
        direction_w_in,
        direction_b_in,
        direction_w_mid,
        direction_b_mid,
        direction_w_out,
        direction_b_out,
    )


def solution(mesh):
    in_specs = (P(), P(None, None, "paths"), P(), P(), P(), P(), P(), P())
    out_specs = (P("paths", None), P(), P(), P(), P(), P(), P())
    return jax.shard_map(
        on_device, mesh=mesh, in_specs=in_specs, out_specs=out_specs, check_vma=False
    )
```

time: 336 us -> 186 us (0.55)
  waiting for transfers between devices: 204 us -> 65.9 us
  blocking collectives: 40.6 us -> 0 us
  starting transfers between devices: 0.26 us -> 20.4 us
  local copies, waits for them, and re-layouts: 9.2 us -> 23.9 us
  between operations: 21.3 us -> 8.19 us
  Pallas kernels: 0 us -> 6.21 us
  matrix products: 32.9 us -> 38.2 us
  other arithmetic: 26.4 us -> 22.7 us
    psum x2 -> x0, waiting for transfers between devices: 204 us -> none  [the longest x1 117 us: on_device(): summed = lax.psum(every_set, 'paths')]
    ppermute x0 -> x10, waiting for transfers between devices: none -> 65.9 us  [swap(): return lax.ppermute(array, 'paths', [(i, i ^ bit) for i in range(devices)])]
    psum x1 -> x0, blocking collectives: 40.6 us -> none  [on_device(): lax.psum((small[0], small[1], small[2], small[3], small[4], grad_mid), 'p...]
    ppermute x0 -> x10, starting transfers between devices: none -> 13.1 us  [swap(): return lax.ppermute(array, 'paths', [(i, i ^ bit) for i in range(devices)])]
    unnamed x23 -> x21, local copies, waits for them, and re-layouts: 2.53 us -> 14.7 us
    all_to_all x0 -> x1, starting transfers between devices: none -> 7.3 us  [on_device(): parts = lax.all_to_all(sums, 'paths', 0, 0, tiled=True)]
    convert_element_type x1 -> x2, other arithmetic: 0.6 us -> 7.56 us  [the longest x1 7.56 us: block_gradients(): (slope[:, None] * w_out.astype(jnp.float32)[None, :] * silu_slope(raw_mid...]
    reduce_sum x5 -> x3, other arithmetic: 9.25 us -> 2.69 us  [the longest x1 2.05 us: block_gradients(): jnp.sum(own(hidden_mid, 1).astype(jnp.float32) * slope[:, None], axis=0)]
  transfers between devices with their start and end apart: 2 -> 11, of which waited for: 2 -> 8; matrix products, arithmetic and copies ran while one was open for 5% -> 16% of each run, Pallas kernels for 0% -> 0%
where the time goes in v1:
time: 186 us; the launch traced here: 185 us
  waiting for transfers between devices  65.9 us (35%)
  matrix products  38.2 us (21%)
  local copies, waits for them, and re-layouts  23.9 us (13%)
  other arithmetic  22.7 us (12%)
  starting transfers between devices  20.4 us (11%)
  between operations  8.19 us (4%)
  Pallas kernels  6.21 us (3%)
    ppermute x10, waiting for transfers between devices, swap(): return lax.ppermute(array, 'paths', [(i, i ^ bit) for i in range(devices)])  65.9 us
    unnamed x21, local copies, waits for them, and re-layouts  14.7 us
    dot_general x1, matrix products, block_gradients(): jnp.dot(hidden_in, w_mid, preferred_element_type=jnp.float32) + b_mid  14.2 us
    ppermute x10, starting transfers between devices, swap(): return lax.ppermute(array, 'paths', [(i, i ^ bit) for i in range(devices)])  13.1 us
    dot_general x1, matrix products, block_gradients(): raw_in = jnp.dot(inputs, w_in, preferred_element_type=jnp.float32) + b_in  8.56 us
    convert_element_type x1, other arithmetic, block_gradients(): (slope[:, None] * w_out.astype(jnp.float32)[None, :] * silu_slope(raw_mid...  7.56 us
    all_to_all x1, starting transfers between devices, on_device(): parts = lax.all_to_all(sums, 'paths', 0, 0, tiled=True)  7.3 us
    pallas_call x1, Pallas kernels, payoff_sums(): pl.pallas_call(pricing_kernel, grid=(count // sets,), in_specs=[pl.BlockS...  6.21 us
  transfers between devices with their start and end apart: 11, of which 8 were waited for; matrix products, arithmetic and copies ran while one was open for 16% of the time, Pallas kernels for 0%

profile of v1, /device:TPU:0, one launch (start us, length us, event | category | flops | bytes accessed | tf_op | source)
XLA Modules:
  0.0 185.4 jit_solution(17454368230456462789)
XLA Ops:
  0.7 0.9 copy-done.1
  1.6 0.7 copy-done.2
  2.2 0.7 copy-done.3
  2.9 6.2 %pricing.1 = f32[256,88]{1,0:T(8,128)} custom-call(f32[8,11]{1,0:T(8,128)S(1)} %copy-done.3, f32[4,256]{1,0:T(4,128)S(1)} %bitcast.114, bf16[2,64,128]{2,1,0:T(8,128)(2,1)S(1)} %copy-done.1), custom_call_target="tpu_custom_call" | custom-call | tf_op jit(solution)/shard_map/pricing/pallas_call | solution.py:116
  9.1 7.3 %all-to-all-start = ((f32[32,8,88]{2,1,0:T(8,128)}), f32[32,8,88]{2,1,0:T(8,128)S(1)}, u32[]{:S(2)}, u32[]{:S(2)}) async-start(f32[32,8,88]{2,1,0:T(8,128)} %bitcast.1), calls=%async_computation | async-start | bytes 262144 | tf_op jit(solution)/shard_map/all_to_all | solution.py:208
  16.5 0.8 reshape.131
  17.2 0.7 broadcast_in_dim.13
  18.2 0.7 maximum_convert_fusion
  18.8 0.7 multiply_convert_fusion.3
  19.8 8.6 %multiply_convert_fusion.2 = (bf16[2816,1024]{1,0:T(8,128)(2,1)}, f32[2816,1024]{1,0:T(8,128)}) fusion(f32[1024]{0:T(1024)} %param.15, bf16[2816,6]{0,1:T(8,128)(2,1)S(1)} %convert_element_type.30, bf16[6,1024]{1,0:T(8,128)(2,1)} %param.14), kind=kOutput, calls=%fused_computation.3 | convolution fusion | flops 51904512 | bytes 17351680 | tf_op jit(solution)/shard_map/dot_general | solution.py:162
  28.8 14.2 %multiply_convert_fusion.1 = (bf16[2816,1024]{1,0:T(8,128)(2,1)}, f32[2816,1024]{1,0:T(8,128)}) fusion(f32[1024]{0:T(1024)S(1)} %copy-done.8, bf16[2816,1024]{1,0:T(8,128)(2,1)} %get-tuple-element.57, bf16[1024,1024]{1,0:T(8,128)(2,1)S(1)} %copy-done), kind=kOutput, calls=%fused_computation.1 | convolution fusion | flops 5922881536 | bytes 25169920 | tf_op jit(solution)/shard_map/dot_general | solution.py:164
  43.0 2.6 %collective-permute-start.1 = (f32[2,8,88]{2,1,0:T(8,128)S(1)}, f32[2,8,88]{2,1,0:T(8,128)S(1)}, u32[]{:S(2)}, u32[]{:S(2)}) collective-permute-start(f32[2,8,88]{2,1,0:T(8,128)S(1)} %pad_maximum_fusion.3), channel_id=1, source_target_pairs={{0,16},{1,17},{2,18},{3,19},{4,20},{5,21},{6,22},{7,23},{8,24},{9,... | collective-permute-start | bytes 16904 | tf_op jit(solution)/shard_map/ppermute | solution.py:188
  45.7 4.2 %convolution_reduce_fusion = f32[2816]{0:T(1024)S(1)} fusion(bf16[2816,1024]{1,0:T(8,128)(2,1)} %get-tuple-element.59, bf16[1024,1]{0,1:T(2,128)(2,1)S(1)} %reshape.144), kind=kOutput, calls=%fused_computation.20 | convolution fusion | flops 5767168 | bytes 5780480 | tf_op jit(solution)/shard_map/dot_general | solution.py:166
  50.8 0.6 fusion.11
  51.4 7.6 %multiply_convert_fusion = bf16[2816,1024]{1,0:T(8,128)(2,1)S(1)} fusion(f32[2816,1024]{1,0:T(8,128)} %get-tuple-element.60, f32[1024]{0:T(1024)S(1)} %convert_element_type.33, f32[2816]{0:T(1024)S(1)} %get-tuple-element.39, f32[1024]{0:T(1024)S(1)} %copy-done.8), kind=kLoop, calls=%fused_computation | loop fusion | flops 31719424 | bytes 17320960 | tf_op jit(solution)/shard_map/convert_element_type | solution.py:170
  59.0 2.1 %multiply_reduce_fusion.1 = (f32[256]{0:T(256)S(1)}, f32[256]{0:T(256)S(1)}) fusion(f32[2816]{0:T(1024)S(1)} %get-tuple-element.39, bf16[2816,1024]{1,0:T(8,128)(2,1)} %get-tuple-element.59, s32[]{:T(128)S(6)} %select_n.201, bf16[2816,1024]{1,0:T(8,128)(2,1)S(1)} %multiply_convert_fusion), kind=kLoop, calls=%fused_computation.10 | loop fusion | flops 3603968 | bytes 2896900 | tf_op jit(solution)/shard_map/reduce_sum | solution.py:168
  61.0 4.3 %fusion.1 = f32[1024,256]{1,0:T(8,128)S(1)} fusion(bf16[2816,1024]{1,0:T(8,128)(2,1)} %get-tuple-element.57, bf16[2816,1024]{1,0:T(8,128)(2,1)S(1)} %multiply_convert_fusion, s32[]{:T(128)S(6)} %select_n.201), kind=kOutput, calls=%fused_computation.18 | convolution fusion | flops 1476395008 | bytes 8257540 | tf_op jit(solution)/shard_map/dot_general | solution.py:153
  65.4 5.2 %convert_reduce_fusion.1 = (f32[256]{0:T(256)S(1)}, bf16[2816,256]{1,0:T(8,128)(2,1)}) fusion(f32[2816,1024]{1,0:T(8,128)} %get-tuple-element.58, s32[]{:T(128)S(6)} %select_n.201, bf16[2816,1024]{1,0:T(8,128)(2,1)S(1)} %multiply_convert_fusion, bf16[1024,1024]{1,0:T(8,128)(2,1)S(1)} %copy-done), kind=kOutput, calls=%fused_computation.12 | convolution fusion | flops 1484324608 | bytes 10618880 | tf_op jit(solution)/shard_map/dot_general | solution.py:175
  70.6 1.5 reshape.134
  72.1 1.3 copy.85
  73.4 1.6 fusion.12
  75.0 0.7 broadcast_in_dim_broadcast_in_dim.3
  75.8 0.8 fusion.4
  76.6 1.5 collective-permute-start.2
  78.1 13.1 %collective-permute-done.2 = f32[4,264,128]{2,1,0:T(8,128)} collective-permute-done((f32[4,264,128]{2,1,0:T(8,128)}, f32[4,264,128]{2,1,0:T(8,128)}, u32[]{:S(2)}, u32[]{:S(2)}) %collective-permute-start.2) | collective-permute-done | bytes 540704 | tf_op jit(solution)/shard_map/ppermute | solution.py:188
  91.3 1.1 fusion.7
  92.4 0.8 copy-done.5
  93.2 1.5 collective-permute-start.3
  94.7 6.2 %collective-permute-done.3 = f32[2,264,128]{2,1,0:T(8,128)S(1)} collective-permute-done((f32[2,264,128]{2,1,0:T(8,128)S(1)}, f32[2,264,128]{2,1,0:T(8,128)S(1)}, u32[]{:S(2)}, u32[]{:S(2)}) %collective-permute-start.3) | collective-permute-done | bytes 270368 | tf_op jit(solution)/shard_map/ppermute | solution.py:188
  101.0 1.0 bitcast_add_fusion
  102.0 1.5 collective-permute-start.4
  103.5 3.5 %collective-permute-done.4 = f32[1,264,128]{2,1,0:T(8,128)S(1)} collective-permute-done((f32[1,264,128]{2,1,0:T(8,128)S(1)}, f32[1,264,128]{2,1,0:T(8,128)S(1)}, u32[]{:S(2)}, u32[]{:S(2)}) %collective-permute-start.4) | collective-permute-done | bytes 135200 | tf_op jit(solution)/shard_map/ppermute | solution.py:188
  107.3 6.4 %collective-permute-done.5 = f32[1,264,128]{2,1,0:T(8,128)S(1)} collective-permute-done((f32[1,264,128]{2,1,0:T(8,128)S(1)}, f32[1,264,128]{2,1,0:T(8,128)S(1)}, u32[]{:S(2)}, u32[]{:S(2)}) %collective-permute-start.5) | collective-permute-done | bytes 135200 | tf_op jit(solution)/shard_map/ppermute | solution.py:188
  113.8 2.1 %collective-permute-start.6 = (f32[2,264,128]{2,1,0:T(8,128)S(1)}, f32[2,264,128]{2,1,0:T(8,128)S(1)}, u32[]{:S(2)}, u32[]{:S(2)}) collective-permute-start(f32[2,264,128]{2,1,0:T(8,128)S(1)} %maximum_bitcast_fusion.3), channel_id=1, source_target_pairs={{0,8},{1,9},{2,10},{3,11},{4,12},{5,13},{6,14},{7,15},{8,0},{9,1},... | collective-permute-start | bytes 811016 | tf_op jit(solution)/shard_map/ppermute | solution.py:188
  115.9 4.4 %collective-permute-done.6 = f32[2,264,128]{2,1,0:T(8,128)S(1)} collective-permute-done((f32[2,264,128]{2,1,0:T(8,128)S(1)}, f32[2,264,128]{2,1,0:T(8,128)S(1)}, u32[]{:S(2)}, u32[]{:S(2)}) %collective-permute-start.6) | collective-permute-done | bytes 270368 | tf_op jit(solution)/shard_map/ppermute | solution.py:188
  120.5 1.6 collective-permute-start.7
  122.0 8.6 %collective-permute-done.7 = f32[4,264,128]{2,1,0:T(8,128)S(1)} collective-permute-done((f32[4,264,128]{2,1,0:T(8,128)S(1)}, f32[4,264,128]{2,1,0:T(8,128)S(1)}, u32[]{:S(2)}, u32[]{:S(2)}) %collective-permute-start.7) | collective-permute-done | bytes 540704 | tf_op jit(solution)/shard_map/ppermute | solution.py:188
  130.8 1.6 collective-permute-start.8
  132.4 19.3 %collective-permute-done.8 = f32[8,264,128]{2,1,0:T(8,128)} collective-permute-done((f32[8,264,128]{2,1,0:T(8,128)S(1)}, f32[8,264,128]{2,1,0:T(8,128)}, u32[]{:S(2)}, u32[]{:S(2)}) %collective-permute-start.8) | collective-permute-done | bytes 1081376 | tf_op jit(solution)/shard_map/ppermute | solution.py:188
  151.7 1.4 select_bitcast_fusion.3
  153.5 4.2 %collective-permute-done.9 = f32[16,264,128]{2,1,0:T(8,128)S(1)} collective-permute-done((f32[16,264,128]{2,1,0:T(8,128)S(1)}, f32[16,264,128]{2,1,0:T(8,128)S(1)}, u32[]{:S(2)}, u32[]{:S(2)}) %collective-permute-start.9) | collective-permute-done | bytes 2162720 | tf_op jit(solution)/shard_map/ppermute | solution.py:188
  158.6 1.9 %multiply_reduce_fusion = f32[]{:T(128)} fusion(f32[2,8,2,264,128]{4,3,2,1,0:T(8,128)S(1)} %bitcast.115), kind=kLoop, calls=%fused_computation.6 | loop fusion | flops 2097151 | bytes 4194308 | tf_op jit(solution)/shard_map/reduce_sum | solution.py:256
  160.6 0.6 multiply_reduce_fusion.2
  161.3 0.6 multiply_reduce_fusion.3
  164.6 2.5 %slice_multiply_fusion = f32[2,8,2,256,128]{4,3,2,1,0:T(8,128)S(1)} fusion(f32[2,8,2,264,128]{4,3,2,1,0:T(8,128)} %bitcast.117, f32[]{:T(128)S(6)} %rsqrt.10), kind=kLoop, calls=%fused_computation.8 | loop fusion | flops 1048576 | bytes 8388612 | tf_op jit(solution)/shard_map/mul | solution.py:258
  167.1 5.2 %copy.100 = f32[8,128,2,2,2,128]{5,4,3,2,1,0:T(2,128)} copy(f32[8,128,2,2,2,128]{5,1,4,3,0,2:T(8,128)S(1)} %bitcast.118) | data formatting | bytes 8388608
  172.2 6.4 %reshape.146 = f32[1024,1024]{1,0:T(8,128)} reshape(f32[8,128,2,2,2,128]{5,4,3,2,1,0:T(2,128)} %copy.100) | data formatting | bytes 8388608
  178.7 0.6 mul.197
  (66 shorter events, 5.4 us)
Async XLA Ops:
  0.6 28.1 %copy-start = (bf16[1024,1024]{1,0:T(8,128)(2,1)S(1)}, bf16[1024,1024]{1,0:T(8,128)(2,1)}, u32[]{:S(2)}) copy-start(bf16[1024,1024]{1,0:T(8,128)(2,1)} %param.16) | copy-start | bytes 6291460
  0.6 0.9 copy-start.1
  1.6 0.7 copy-start.2
  2.2 0.7 copy-start.3
  9.1 19.2 %all-to-all-start = ((f32[32,8,88]{2,1,0:T(8,128)}), f32[32,8,88]{2,1,0:T(8,128)S(1)}, u32[]{:S(2)}, u32[]{:S(2)}) async-start(f32[32,8,88]{2,1,0:T(8,128)} %bitcast.1), calls=%async_computation | async-start | bytes 262144 | tf_op jit(solution)/shard_map/all_to_all | solution.py:208
  19.8 8.9 %copy-start.8 = (f32[1024]{0:T(1024)S(1)}, f32[1024]{0:T(1024)}, u32[]{:S(2)}) copy-start(f32[1024]{0:T(1024)} %param.17) | copy-start | bytes 12292
  28.4 14.6 %copy-start.7 = (f32[8,88]{1,0:T(8,128)}, f32[8,88]{1,0:T(8,128)S(1)}, u32[]{:S(2)}) copy-start(f32[8,88]{1,0:T(8,128)S(1)} %broadcast_multiply_fusion) | copy-start | bytes 8452
  28.4 14.6 %collective-permute-start = (f32[8,88]{1,0:T(8,128)S(1)}, f32[8,88]{1,0:T(8,128)S(1)}, u32[]{:S(2)}, u32[]{:S(2)}) collective-permute-start(f32[8,88]{1,0:T(8,128)S(1)} %broadcast_multiply_fusion), channel_id=1, source_target_pairs={{0,1},{1,0},{2,3},{3,2},{4,5},{5,4},{6,7},{7,6},{8,9},{9,8},{10,11... | collective-permute-start | bytes 8456 | tf_op jit(solution)/shard_map/ppermute | solution.py:188
  28.8 14.2 %copy-start.6 = (bf16[1024]{0:T(1024)(128)(2,1)S(1)}, bf16[1024]{0:T(1024)(128)(2,1)}, u32[]{:S(2)}) copy-start(bf16[1024]{0:T(1024)(128)(2,1)} %param.18) | copy-start | bytes 6148
  43.0 7.6 %collective-permute-start.1 = (f32[2,8,88]{2,1,0:T(8,128)S(1)}, f32[2,8,88]{2,1,0:T(8,128)S(1)}, u32[]{:S(2)}, u32[]{:S(2)}) collective-permute-start(f32[2,8,88]{2,1,0:T(8,128)S(1)} %pad_maximum_fusion.3), channel_id=1, source_target_pairs={{0,16},{1,17},{2,18},{3,19},{4,20},{5,21},{6,22},{7,23},{8,24},{9,... | collective-permute-start | bytes 16904 | tf_op jit(solution)/shard_map/ppermute | solution.py:188
  76.6 14.6 %collective-permute-start.2 = (f32[4,264,128]{2,1,0:T(8,128)}, f32[4,264,128]{2,1,0:T(8,128)}, u32[]{:S(2)}, u32[]{:S(2)}) collective-permute-start(f32[4,264,128]{2,1,0:T(8,128)} %fusion.4), channel_id=1, source_target_pairs={{0,8},{1,9},{2,10},{3,11},{4,12},{5,13},{6,14},{7,15},{8,0},{9,1},... | collective-permute-start | bytes 1622024 | tf_op jit(solution)/shard_map/ppermute | solution.py:188
  92.4 0.8 copy-start.5
  93.2 7.8 %collective-permute-start.3 = (f32[2,264,128]{2,1,0:T(8,128)S(1)}, f32[2,264,128]{2,1,0:T(8,128)S(1)}, u32[]{:S(2)}, u32[]{:S(2)}) collective-permute-start(f32[2,264,128]{2,1,0:T(8,128)S(1)} %dynamic-slice_bitcast_fusion), channel_id=1, source_target_pairs={{0,4},{1,5},{2,6},{3,7},{4,0},{5,1},{6,2},{7,3},{8,12},{9,13},{10,... | collective-permute-start | bytes 811016 | tf_op jit(solution)/shard_map/ppermute | solution.py:188
  102.0 5.1 %collective-permute-start.4 = (f32[1,264,128]{2,1,0:T(8,128)S(1)}, f32[1,264,128]{2,1,0:T(8,128)S(1)}, u32[]{:S(2)}, u32[]{:S(2)}) collective-permute-start(f32[1,264,128]{2,1,0:T(8,128)S(1)} %constant_dynamic-slice_fusion), channel_id=1, source_target_pairs={{0,2},{1,3},{2,0},{3,1},{4,6},{5,7},{6,4},{7,5},{8,10},{9,11},{10,... | collective-permute-start | bytes 405512 | tf_op jit(solution)/shard_map/ppermute | solution.py:188
  107.1 6.7 %collective-permute-start.5 = (f32[1,264,128]{2,1,0:T(8,128)S(1)}, f32[1,264,128]{2,1,0:T(8,128)S(1)}, u32[]{:S(2)}, u32[]{:S(2)}) collective-permute-start(f32[1,264,128]{2,1,0:T(8,128)S(1)} %dynamic-slice_add_fusion), channel_id=1, source_target_pairs={{0,16},{1,17},{2,18},{3,19},{4,20},{5,21},{6,22},{7,23},{8,24},{9,... | collective-permute-start | bytes 405512 | tf_op jit(solution)/shard_map/ppermute | solution.py:188
  113.8 6.5 %collective-permute-start.6 = (f32[2,264,128]{2,1,0:T(8,128)S(1)}, f32[2,264,128]{2,1,0:T(8,128)S(1)}, u32[]{:S(2)}, u32[]{:S(2)}) collective-permute-start(f32[2,264,128]{2,1,0:T(8,128)S(1)} %maximum_bitcast_fusion.3), channel_id=1, source_target_pairs={{0,8},{1,9},{2,10},{3,11},{4,12},{5,13},{6,14},{7,15},{8,0},{9,1},... | collective-permute-start | bytes 811016 | tf_op jit(solution)/shard_map/ppermute | solution.py:188
  120.5 10.1 %collective-permute-start.7 = (f32[4,264,128]{2,1,0:T(8,128)S(1)}, f32[4,264,128]{2,1,0:T(8,128)S(1)}, u32[]{:S(2)}, u32[]{:S(2)}) collective-permute-start(f32[4,264,128]{2,1,0:T(8,128)S(1)} %bitcast.123), channel_id=1, source_target_pairs={{0,4},{1,5},{2,6},{3,7},{4,0},{5,1},{6,2},{7,3},{8,12},{9,13},{10,... | collective-permute-start | bytes 1622024 | tf_op jit(solution)/shard_map/ppermute | solution.py:188
  130.8 20.9 %collective-permute-start.8 = (f32[8,264,128]{2,1,0:T(8,128)S(1)}, f32[8,264,128]{2,1,0:T(8,128)}, u32[]{:S(2)}, u32[]{:S(2)}) collective-permute-start(f32[8,264,128]{2,1,0:T(8,128)S(1)} %bitcast.122), channel_id=1, source_target_pairs={{0,2},{1,3},{2,0},{3,1},{4,6},{5,7},{6,4},{7,5},{8,10},{9,11},{10,... | collective-permute-start | bytes 3244040 | tf_op jit(solution)/shard_map/ppermute | solution.py:188
  153.4 4.3 %collective-permute-start.9 = (f32[16,264,128]{2,1,0:T(8,128)S(1)}, f32[16,264,128]{2,1,0:T(8,128)S(1)}, u32[]{:S(2)}, u32[]{:S(2)}) collective-permute-start(f32[16,264,128]{2,1,0:T(8,128)S(1)} %bitcast.121), channel_id=1, source_target_pairs={{0,1},{1,0},{2,3},{3,2},{4,5},{5,4},{6,7},{7,6},{8,9},{9,8},{10,11... | collective-permute-start | bytes 6488072 | tf_op jit(solution)/shard_map/ppermute | solution.py:188
  158.6 2.0 %copy-start.4 = (f32[16,2,264,128]{3,2,1,0:T(8,128)}, f32[16,2,264,128]{3,2,1,0:T(8,128)S(1)}, u32[]{:S(2)}) copy-start(f32[16,2,264,128]{3,2,1,0:T(8,128)S(1)} %copy.90) | copy-start | bytes 12976132

commit v2 on v1

--- a/solution.py
+++ b/solution.py
@@ -1,3 +1,4 @@
+import functools
 import math
 
 import jax
@@ -14,7 +15,8 @@
 PAIRS = 88
 WIDTH = 1024
 LANES = 128
-SMALL_ROWS = 10
+FEATURE_ROWS = 16
+ROW_TILE = 256
 EPSILON = 1e-06
 
 
@@ -24,10 +26,6 @@
 STRIKE = np.exp(LOG_STRIKE).astype(np.float32)
 SET_BLOCK = 256
 LOG2E = 1.4426950408889634
-
-
-def strike_grid():
-    return (jnp.asarray(TENORS), jnp.asarray(LOG_STRIKE))
 
 
 def bf16_pieces(value):
@@ -110,7 +108,7 @@
 
 
 def payoff_sums(params, increments):
-    count = params.shape[0]
+    count = params.shape[1]
     paths = increments.shape[2]
     sets = math.gcd(count, SET_BLOCK)
     return pl.pallas_call(
@@ -131,57 +129,230 @@
         ],
         compiler_params=pltpu.CompilerParams(vmem_limit_bytes=32 * 1024 * 1024),
         name="pricing",
-    )(jnp.asarray(STRIKE), params.T, increments)
-
-
-def features(set_rows):
-    count = set_rows.shape[0]
-    tenors, log_strike = strike_grid()
-    scaled = set_rows * jnp.array([4.0, 1.0, 1.0, 20.0], dtype=jnp.float32)
-    per_pair = jnp.stack([4.0 * log_strike.reshape(PAIRS), jnp.repeat(tenors, STRIKES)], axis=1)
-    left = jnp.broadcast_to(scaled[:, None, :], (count, PAIRS, 4))
-    right = jnp.broadcast_to(per_pair[None], (count, PAIRS, 2))
-    return jnp.concatenate([left, right], axis=2).reshape(count * PAIRS, 6).astype(jnp.bfloat16)
-
-
-def silu_slope(value):
-    logistic = jax.nn.sigmoid(value)
-    return logistic * (1.0 + value * (1.0 - logistic))
-
-
-def contract_rows(left, right):
+    )(jnp.asarray(STRIKE), params, increments)
+
+
+def row_maps(sets):
+    row = np.arange(sets * PAIRS, dtype=np.int32)
+    return np.stack([row % PAIRS, PAIRS + row // PAIRS])
+
+
+def feature_base(sets):
+    base = np.zeros((FEATURE_ROWS, LANES), np.float32)
+    base[4, :PAIRS] = (np.float32(4.0) * LOG_STRIKE).reshape(PAIRS)
+    base[5, :PAIRS] = np.repeat(TENORS, STRIKES)
+    base[6:9, PAIRS : PAIRS + sets] = 1.0
+    return base
+
+
+def dot(left, right):
+    return jnp.dot(left, right, preferred_element_type=jnp.float32)
+
+
+def dot_rows(left, right):
     return lax.dot_general(
-        left, right, (((0,), (0,)), ((), ())), preferred_element_type=jnp.float32
+        left, right, (((1,), (1,)), ((), ())), preferred_element_type=jnp.float32
     )
 
 
-def block_gradients(inputs, target, w_in, b_in, w_mid, b_mid, w_out, b_out, inv_sets, block, cols):
-    def own(array, axis):
-        return lax.dynamic_slice_in_dim(array, block * cols, cols, axis)
-
-    raw_in = jnp.dot(inputs, w_in, preferred_element_type=jnp.float32) + b_in
-    hidden_in = jax.nn.silu(raw_in).astype(jnp.bfloat16)
-    raw_mid = jnp.dot(hidden_in, w_mid, preferred_element_type=jnp.float32) + b_mid
-    hidden_mid = jax.nn.silu(raw_mid).astype(jnp.bfloat16)
-    predicted = jnp.dot(hidden_mid, w_out, preferred_element_type=jnp.float32) + b_out[0]
-    slope = (predicted - target) * inv_sets
-    grad_out = jnp.sum(own(hidden_mid, 1).astype(jnp.float32) * slope[:, None], axis=0)
-    grad_bout = jnp.broadcast_to(jnp.sum(slope), (cols,))
-    delta_mid = (slope[:, None] * w_out.astype(jnp.float32)[None, :] * silu_slope(raw_mid)).astype(
-        jnp.bfloat16
+def network_kernel(
+    inv_sets, place_ref, maps_ref, feat_ref, sums_ref, w_in_ref, b_in_ref, w_mid_ref, b_mid_ref,
+    w_out_ref, b_out_ref, out_ref, left_ref, win_ref, turned_ref, bias_ref, read_ref, grad_ref,
+    small_ref, slope_ref, hidden_ref,
+):
+    block = place_ref[0]
+    sets = sums_ref.shape[0]
+    rows = maps_ref.shape[1]
+    cols = WIDTH // 4
+    own = pl.ds(pl.multiple_of(block * cols, cols), cols)
+    groups = out_ref.shape[0]
+    piece_rows = WIDTH // groups
+    bf16 = jnp.bfloat16
+
+    left_ref[...] = jnp.zeros_like(left_ref)
+    left_ref[0:FEATURE_ROWS, :] = feat_ref[...]
+    for p, piece in enumerate(bf16_pieces(sums_ref[...])):
+        first = FEATURE_ROWS + p * sets
+        left_ref[first : first + sets, :PAIRS] = piece.astype(jnp.float32)
+    left = left_ref[...].astype(bf16)
+
+    weights_in = w_in_ref[...].astype(jnp.float32)
+    bias_in = [piece.astype(jnp.float32) for piece in bf16_pieces(b_in_ref[...])]
+    pad = jnp.zeros((FEATURE_ROWS - weights_in.shape[0] - 3, WIDTH), jnp.float32)
+    win_ref[...] = (0.5 * jnp.concatenate([weights_in] + bias_in + [pad], 0)).T.astype(bf16)
+    turned_ref[...] = (0.5 * w_mid_ref[...].astype(jnp.float32)).T.astype(bf16)
+    bias_ref[...] = jnp.broadcast_to((0.5 * b_mid_ref[...]).T, bias_ref.shape)
+    read_ref[...] = jnp.broadcast_to((0.5 * w_out_ref[...].astype(jnp.float32)).T, read_ref.shape)
+    grad_ref[...] = jnp.zeros_like(grad_ref)
+    small_ref[...] = jnp.zeros_like(small_ref)
+    slope_ref[...] = jnp.zeros_like(slope_ref)
+    readout = jnp.broadcast_to(w_out_ref[...].astype(jnp.float32), (16, WIDTH)).astype(bf16)
+
+    def tile(t, carry):
+        here = pl.ds(pl.multiple_of(t * ROW_TILE, ROW_TILE), ROW_TILE)
+        pair, group_set = maps_ref[0:1, here], maps_ref[1:2, here]
+        code = lax.broadcasted_iota(jnp.int32, (LANES, ROW_TILE), 0)
+        hot = jnp.where((code == pair) | (code == group_set), 1.0, 0.0).astype(bf16)
+        looked = dot(left, hot)
+        feat = looked[:FEATURE_ROWS].astype(bf16)
+        target = looked[FEATURE_ROWS : FEATURE_ROWS + sets]
+        for p in (1, 2):
+            first = FEATURE_ROWS + p * sets
+            target = target + looked[first : first + sets]
+        member = lax.broadcasted_iota(jnp.int32, (sets, ROW_TILE), 0) + PAIRS
+        target = jnp.sum(jnp.where(member == group_set, target, 0.0), axis=0, keepdims=True)
+
+        half_in = dot(win_ref[...], feat)
+        hidden_in = (half_in + half_in * jnp.tanh(half_in)).astype(bf16)
+        half_mid = dot(turned_ref[...], hidden_in) + bias_ref[...]
+        wave = jnp.tanh(half_mid)
+        rise = 1.0 + wave
+        hidden_mid = (half_mid * rise).astype(bf16)
+        hidden_ref[...] = hidden_mid
+        predicted = dot(readout, hidden_mid)[0:1] + b_out_ref[0]
+        slope = (predicted - target) * inv_sets
+        slope_ref[...] += slope
+        curve = read_ref[...] * (rise * (1.0 + half_mid * (1.0 - wave)))
+        delta_mid = (slope * curve).astype(bf16)
+        backward = dot(w_mid_ref[own, :], delta_mid)
+        own_half = dot(win_ref[own, :], feat)
+        own_wave = jnp.tanh(own_half)
+        own_curve = (0.5 * (1.0 + own_wave)) * (1.0 + own_half * (1.0 - own_wave))
+        delta_in = (backward * own_curve).astype(bf16)
+        own_curve_mid = slope * own_rows(curve, block, cols)
+        own_delta = own_curve_mid.astype(bf16)
+        grad_ref[...] += dot_rows(hidden_in, own_delta)
+        pieces = [piece.astype(jnp.float32) for piece in bf16_pieces(slope)]
+        lines = jnp.concatenate(
+            [feat.astype(jnp.float32)] + pieces + [jnp.zeros((13, ROW_TILE), jnp.float32)], 0
+        ).astype(bf16)
+        small_ref[:, 0:cols] += dot_rows(lines, delta_in)
+        small_ref[:, cols : 2 * cols] += dot_rows(lines, own_delta)
+        small_ref[:, 2 * cols :] += dot_rows(lines, hidden_ref[own, :])
+        return carry
+
+    lax.fori_loop(0, rows // ROW_TILE, tile, 0)
+
+    extra = [small_ref[0:7, 0:cols], small_ref[6:7, cols : 2 * cols]]
+    extra.append(jnp.sum(small_ref[16:19, 2 * cols :], axis=0, keepdims=True))
+    total = jnp.sum(slope_ref[...], axis=1, keepdims=True)
+    extra.append(jnp.broadcast_to(total, (1, cols)))
+    extra.append(jnp.zeros((6, cols), jnp.float32))
+    extra = jnp.concatenate(extra, 0)
+    for j in range(groups):
+        for h in range(2):
+            lanes = slice(h * LANES, (h + 1) * LANES)
+            out_ref[j, h * piece_rows : (h + 1) * piece_rows, :] = grad_ref[
+                j * piece_rows : (j + 1) * piece_rows, lanes
+            ]
+        if j < 4:
+            lanes = slice((j % 2) * LANES, (j % 2 + 1) * LANES)
+            out_ref[j, 2 * piece_rows :, :] = extra[8 * (j // 2) : 8 * (j // 2) + 8, lanes]
+        else:
+            out_ref[j, 2 * piece_rows :, :] = jnp.zeros((8, LANES), jnp.float32)
+
+
+def own_rows(value, block, cols):
+    part = value[0:cols]
+    for b in range(1, 4):
+        part = jnp.where(block == b, value[b * cols : (b + 1) * cols], part)
+    return part
+
+
+def block_gradients(rows, sums, w_in, b_in, w_mid, b_mid, w_out, b_out, inv_sets, block, groups):
+    sets = rows.shape[1]
+    cols = WIDTH // 4
+    scale = jnp.array([[4.0], [1.0], [1.0], [20.0]], jnp.float32)
+    feat = jnp.pad(rows * scale, ((0, FEATURE_ROWS - 4), (PAIRS, LANES - PAIRS - sets)))
+    vmem = pl.BlockSpec(memory_space=pltpu.VMEM)
+    smem = pl.BlockSpec(memory_space=pltpu.SMEM)
+    return pl.pallas_call(
+        functools.partial(network_kernel, inv_sets),
+        in_specs=[smem] + [vmem] * 8 + [smem],
+        out_specs=vmem,
+        out_shape=jax.ShapeDtypeStruct((groups, 2 * (WIDTH // groups) + 8, LANES), jnp.float32),
+        scratch_shapes=[
+            pltpu.VMEM((FEATURE_ROWS + 3 * sets, LANES), jnp.float32),
+            pltpu.VMEM((WIDTH, FEATURE_ROWS), jnp.bfloat16),
+            pltpu.VMEM((WIDTH, WIDTH), jnp.bfloat16),
+            pltpu.VMEM((WIDTH, ROW_TILE), jnp.float32),
+            pltpu.VMEM((WIDTH, ROW_TILE), jnp.float32),
+            pltpu.VMEM((WIDTH, cols), jnp.float32),
+            pltpu.VMEM((32, 3 * cols), jnp.float32),
+            pltpu.VMEM((1, ROW_TILE), jnp.float32),
+            pltpu.VMEM((WIDTH, ROW_TILE), jnp.bfloat16),
+        ],
+        compiler_params=pltpu.CompilerParams(vmem_limit_bytes=48 * 1024 * 1024),
+        name="network",
+    )(
+        block.reshape(1), jnp.asarray(row_maps(sets)), feat + feature_base(sets), sums, w_in,
+        b_in.reshape(1, -1), w_mid, b_mid.reshape(1, -1), w_out.reshape(1, -1), b_out,
     )
-    own_mid = own(delta_mid, 1)
-    grad_bmid = jnp.sum(own_mid.astype(jnp.float32), axis=0)
-    backward = lax.dot_general(
-        delta_mid, own(w_mid, 0), (((1,), (1,)), ((), ())), preferred_element_type=jnp.float32
-    )
-    delta_in = (backward * silu_slope(own(raw_in, 1))).astype(jnp.bfloat16)
-    grad_in = contract_rows(inputs, delta_in)
-    grad_bin = jnp.sum(delta_in.astype(jnp.float32), axis=0)
-    small = jnp.concatenate(
-        [grad_in, grad_bin[None], grad_bmid[None], grad_out[None], grad_bout[None]], axis=0
-    )
-    return contract_rows(hidden_in, own_mid), small
+
+
+def scaling_kernel(
+    pieces_ref, w_in_ref, b_in_ref, w_mid_ref, b_mid_ref, w_out_ref, b_out_ref, small_ref
+):
+    groups = pieces_ref.shape[1]
+    piece_rows = WIDTH // groups
+    for high in range(2):
+        for core in range(2):
+            for j in range(4):
+                start = (2 * high + core) * (WIDTH // 4) + (j % 2) * LANES
+                small_ref[8 * (j // 2) : 8 * (j // 2) + 8, start : start + LANES] = pieces_ref[
+                    high, j, core, 2 * piece_rows :, :
+                ]
+    small = small_ref[...]
+    squares = jnp.sum(small * small, axis=1, keepdims=True)
+    bias_out = small_ref[9:10, 0:1]
+    last = bias_out * bias_out
+
+    def factor(total, entries):
+        return lax.rsqrt(total / entries + EPSILON)
+
+    def add(j, total):
+        for high in range(2):
+            for core in range(2):
+                part = pieces_ref[high, j, core, 0 : 2 * piece_rows, :]
+                total = total + jnp.sum((part * part).reshape(-1, 8, LANES), axis=0)
+        return total
+
+    total = lax.fori_loop(0, groups, add, jnp.zeros((8, LANES), jnp.float32))
+    total = jnp.sum(jnp.sum(total, axis=1, keepdims=True), axis=0, keepdims=True)
+    scale_mid = factor(total + squares[7:8], WIDTH * WIDTH + WIDTH)
+    scale_in = factor(jnp.sum(squares[0:7], axis=0, keepdims=True), 7 * WIDTH)
+    scale_out = factor(squares[8:9] + last, WIDTH + 1)
+    w_in_ref[...] = small[0:6] * scale_in
+    b_in_ref[...] = small[6:7] * scale_in
+    b_mid_ref[...] = small[7:8] * scale_mid
+    w_out_ref[...] = small[8:9] * scale_out
+    b_out_ref[...] = bias_out * scale_out
+
+    def place(j, carry):
+        rows = pl.ds(pl.multiple_of(j * piece_rows, 8), piece_rows)
+        for high in range(2):
+            for core in range(2):
+                for h in range(2):
+                    start = (2 * high + core) * (WIDTH // 4) + h * LANES
+                    part = pieces_ref[high, j, core, h * piece_rows : (h + 1) * piece_rows, :]
+                    w_mid_ref[rows, start : start + LANES] = part * scale_mid
+        return carry
+
+    lax.fori_loop(0, groups, place, 0)
+
+
+def scaled(pieces):
+    vmem = pl.BlockSpec(memory_space=pltpu.VMEM)
+    shapes = [(6, WIDTH), (1, WIDTH), (WIDTH, WIDTH), (1, WIDTH), (1, WIDTH), (1, 1)]
+    return pl.pallas_call(
+        scaling_kernel,
+        in_specs=[vmem],
+        out_specs=[vmem] * 6,
+        out_shape=[jax.ShapeDtypeStruct(shape, jnp.float32) for shape in shapes],
+        scratch_shapes=[pltpu.VMEM((16, WIDTH), jnp.float32)],
+        compiler_params=pltpu.CompilerParams(vmem_limit_bytes=32 * 1024 * 1024),
+        name="scaling",
+    )(pieces)
 
 
 def swap(array, bit, devices):
@@ -203,27 +374,23 @@
     core = owner % 2
     high = owner // top
     group = (owner // 2) % groups
-
-    sums = payoff_sums(params, increments).reshape(devices, set_dev, PAIRS)
-    parts = lax.all_to_all(sums, "paths", 0, 0, tiled=True)
-    prices = jnp.sum(parts, axis=0) / total_paths
-    other = swap(prices, 1, devices)
-    pair = jnp.stack([jnp.where(core == 0, prices, other), jnp.where(core == 0, other, prices)])
-    far = swap(pair, top, devices)
-    quad = jnp.stack([jnp.where(high == 0, pair, far), jnp.where(high == 0, far, pair)])
-
-    rows = pick(params.reshape(2, groups, 2 * set_dev, 4).swapaxes(0, 1), group).reshape(-1, 4)
-    cols = WIDTH // 4
     block = 2 * high + core
-    big, small = block_gradients(
-        features(rows), quad.reshape(-1), w_in, b_in, w_mid, b_mid, w_out, b_out,
-        1.0 / set_count, block, cols,
+    turned = params.T
+
+    sums = payoff_sums(turned, increments)
+    sums = sums + swap(sums, 1, devices)
+    sums = sums.reshape(2, groups, 2 * set_dev, PAIRS).swapaxes(0, 1)
+    sums = jnp.broadcast_to(sums[None], (2,) + sums.shape).reshape(top, 4 * set_dev, PAIRS)
+    lanes = [[2 * chip + c for chip in range(top)] for c in range(2)]
+    parts = lax.all_to_all(sums, "paths", 0, 0, axis_index_groups=lanes, tiled=True)
+    sums = jnp.sum(parts, axis=0) / total_paths
+    prices = pick(sums.reshape(4, set_dev, PAIRS), block)
+
+    rows = pick(turned.reshape(4, 2, groups, 2 * set_dev).transpose(2, 0, 1, 3), group)
+    held = block_gradients(
+        rows.reshape(4, 4 * set_dev), sums, w_in, b_in, w_mid, b_mid, w_out, b_out,
+        1.0 / set_count, block, groups,
     )
-    piece_rows = WIDTH // groups
-    big = big.reshape(groups, piece_rows, 2, LANES).swapaxes(1, 2)
-    small = small.reshape(2 * SMALL_ROWS, LANES)
-    small = jnp.pad(small, ((0, 8 * groups - 2 * SMALL_ROWS), (0, 0))).reshape(groups, 8, LANES)
-    held = jnp.concatenate([big.reshape(groups, 2 * piece_rows, LANES), small], axis=1)
 
     bit = groups // 2
     while bit:
@@ -243,31 +410,16 @@
         else:
             gathered = jnp.swapaxes(pair, 0, 1).reshape((-1,) + pair.shape[2:])
         bit //= 2
-    whole = gathered.reshape(2, groups, 2, 2 * piece_rows + 8, LANES)
-    big = whole[:, :, :, : 2 * piece_rows].reshape(2, groups, 2, 2, piece_rows, LANES)
-    grad_mid = big.transpose(1, 4, 0, 2, 3, 5).reshape(WIDTH, WIDTH)
-    small = whole[:, :, :, 2 * piece_rows :].transpose(1, 3, 0, 2, 4)
-    small = small.reshape(groups * 8, 2, 2, LANES)[: 2 * SMALL_ROWS]
-    small = small.reshape(SMALL_ROWS, 2, 2, 2, LANES).transpose(0, 2, 3, 1, 4)
-    small = small.reshape(SMALL_ROWS, WIDTH)
-
-    def directions(grad_w, grad_b):
-        entries = grad_w.size + grad_b.size
-        mean_square = (jnp.sum(grad_w * grad_w) + jnp.sum(grad_b * grad_b)) / entries
-        factor = lax.rsqrt(mean_square + EPSILON)
-        return (grad_w * factor, grad_b * factor)
-
-    direction_w_mid, direction_b_mid = directions(grad_mid, small[7])
-    direction_w_in, direction_b_in = directions(small[:6], small[6])
-    direction_w_out, direction_b_out = directions(small[8], small[9, :1])
+    result = scaled(gathered.reshape((2, groups, 2) + gathered.shape[1:]))
+    direction_w_in, direction_b_in, direction_w_mid, direction_b_mid, direction_w_out, direction_b_out = result
     return (
-        prices.reshape(set_dev, PAIRS),
+        prices,
         direction_w_in,
-        direction_b_in,
+        direction_b_in.reshape(WIDTH),
         direction_w_mid,
-        direction_b_mid,
-        direction_w_out,
-        direction_b_out,
+        direction_b_mid.reshape(WIDTH),
+        direction_w_out.reshape(WIDTH),
+        direction_b_out.reshape(1),
     )
 
 

time: 186 us -> 138 us (0.74)
  matrix products: 38.2 us -> 0 us
  Pallas kernels: 6.21 us -> 38.7 us
  local copies, waits for them, and re-layouts: 23.9 us -> 4.58 us
  other arithmetic: 22.7 us -> 4.42 us
  waiting for transfers between devices: 65.9 us -> 73.1 us
  between operations: 8.19 us -> 1.55 us
  starting transfers between devices: 20.4 us -> 15.5 us
    dot_general x6 -> x0, matrix products: 38.2 us -> none  [the longest x1 14.2 us: block_gradients(): jnp.dot(hidden_in, w_mid, preferred_element_type=jnp.float32) + b_mid]
    pallas_call x0 -> x2, Pallas kernels: none -> 33.1 us  [the longest x1 30.1 us: block_gradients(): pl.pallas_call(functools.partial(network_kernel, inv_sets), in_specs=[sme...]
    unnamed x21 -> x16, local copies, waits for them, and re-layouts: 14.7 us -> 2.29 us
    all_to_all x1, waiting for transfers between devices: 0.01 us -> 8.97 us  [on_device(): lax.all_to_all(sums, 'paths', 0, 0, axis_index_groups=lanes, tiled=True)]
    convert_element_type x2 -> x0, other arithmetic: 7.56 us -> none  [the longest x1 7.56 us: block_gradients(): (slope[:, None] * w_out.astype(jnp.float32)[None, :] * silu_slope(raw_mid...]
    reduce_sum x6 -> x1, other arithmetic: 5.85 us -> 0.03 us  [on_device(): sums = jnp.sum(parts, axis=0) / total_paths]
    ppermute x10 -> x9, starting transfers between devices: 13.1 us -> 7.6 us  [swap(): return lax.ppermute(array, 'paths', [(i, i ^ bit) for i in range(devices)])]
    reshape x8 -> x3, local copies, waits for them, and re-layouts: 3.8 us -> 0.85 us  [the longest x1 0.69 us: block_gradients(): w_out.reshape(1, -1)]
  transfers between devices with their start and end apart: 11 -> 10, of which waited for: 8 -> 9; matrix products, arithmetic and copies ran while one was open for 16% -> 2% of each run, Pallas kernels for 0% -> 0%
where the time goes in v2:
time: 138 us
  waiting for transfers between devices  73.1 us (53%)
  Pallas kernels  38.7 us (28%)
  starting transfers between devices  15.5 us (11%)
  local copies, waits for them, and re-layouts  4.58 us (3%)
  other arithmetic  4.42 us (3%)
  between operations  1.55 us (1%)
    ppermute x9, waiting for transfers between devices, swap(): return lax.ppermute(array, 'paths', [(i, i ^ bit) for i in range(devices)])  64.2 us
    pallas_call x1, Pallas kernels, block_gradients(): pl.pallas_call(functools.partial(network_kernel, inv_sets), in_specs=[sme...  30.1 us
    all_to_all x1, waiting for transfers between devices, on_device(): lax.all_to_all(sums, 'paths', 0, 0, axis_index_groups=lanes, tiled=True)  8.97 us
    all_to_all x1, starting transfers between devices, on_device(): lax.all_to_all(sums, 'paths', 0, 0, axis_index_groups=lanes, tiled=True)  7.95 us
    ppermute x9, starting transfers between devices, swap(): return lax.ppermute(array, 'paths', [(i, i ^ bit) for i in range(devices)])  7.6 us
    pallas_call x1, Pallas kernels, payoff_sums(): pl.pallas_call(pricing_kernel, grid=(count // sets,), in_specs=[pl.BlockS...  5.55 us
    pallas_call x1, Pallas kernels, scaled(): pl.pallas_call(scaling_kernel, in_specs=[vmem], out_specs=[vmem] * 6, out...  3.08 us
  transfers between devices with their start and end apart: 10, of which 9 were waited for; matrix products, arithmetic and copies ran while one was open for 2% of the time, Pallas kernels for 0%

profile of v2, /device:TPU:0, one launch (start us, length us, event | category | flops | bytes accessed | tf_op | source)
XLA Modules:
  0.0 137.9 jit_solution(17758073502907896472)
XLA Ops:
  0.6 0.0 copy-start
  0.6 0.0 copy-start.1
  0.7 0.9 copy-done.1
  1.6 0.7 copy-done.4
  2.2 0.7 copy-done.7
  2.9 5.5 %pricing.1 = f32[256,88]{1,0:T(8,128)S(1)} custom-call(f32[8,11]{1,0:T(8,128)S(1)} %copy-done.7, f32[4,256]{1,0:T(4,128)S(1)} %bitcast.86, bf16[2,64,128]{2,1,0:T(8,128)(2,1)S(1)} %copy-done.1), custom_call_target="tpu_custom_call" | custom-call | tf_op jit(solution)/shard_map/pricing/pallas_call | solution.py:114
  8.5 0.5 collective-permute-start
  9.0 0.1 reshape.84
  9.7 0.7 reshape.88.w_out_ref
  10.4 0.1 reshape.85
  10.5 0.0 collective-permute-done
  10.6 0.7 broadcast_in_dim.2
  11.3 8.0 %all-to-all-start = ((f32[16,32,88]{2,1,0:T(8,128)}), f32[16,32,88]{2,1,0:T(8,128)S(1)}, u32[]{:S(2)}, u32[]{:S(2)}) async-start(f32[16,32,88]{2,1,0:T(8,128)} %bitcast.3), calls=%async_computation | async-start | bytes 524288 | tf_op jit(solution)/shard_map/all_to_all | solution.py:385
  19.3 0.7 broadcast_multiply_fusion.1
  20.0 0.8 pad_add_fusion.feat_ref
  20.8 9.0 %all-to-all-done = f32[16,32,88]{2,1,0:T(8,128)S(1)} async-done(((f32[16,32,88]{2,1,0:T(8,128)}), f32[16,32,88]{2,1,0:T(8,128)S(1)}, u32[]{:S(2)}, u32[]{:S(2)}) %all-to-all-start) | async-done | bytes 180256 | tf_op jit(solution)/shard_map/all_to_all | solution.py:385
  29.8 0.0 copy-done
  29.8 0.0 copy-done.2
  29.8 0.0 copy-done.3
  29.8 0.0 copy-done.5
  29.8 0.0 copy-done.6
  29.8 30.1 %network.1 = f32[8,264,128]{2,1,0:T(8,128)S(1)} custom-call(s32[1]{0:T(128)} %bitcast.6.place_ref, s32[2,2816]{1,0:T(2,128)S(1)} %copy-done.2, f32[16,128]{1,0:T(8,128)S(1)} %pad_add_fusion.feat_ref, f32[32,88]{1,0:T(8,128)S(1)} %get-tuple-element.29.sums_ref, bf16[6,1024]{1,0:T(8,128)(2,1)S(1)} %copy-done.3, f32[1,1024]{1,0:T(1,128)S(1)} %bitcast.88, ...), custom_call_target="tpu_custom_call" | custom-call | tf_op jit(solution)/shard_map/network/pallas_call | solution.py:269
  59.9 1.2 collective-permute-start.1
  61.1 11.7 %collective-permute-done.1 = f32[4,264,128]{2,1,0:T(8,128)S(1)} collective-permute-done((f32[4,264,128]{2,1,0:T(8,128)S(1)}, f32[4,264,128]{2,1,0:T(8,128)S(1)}, u32[]{:S(2)}, u32[]{:S(2)}) %collective-permute-start.1) | collective-permute-done | bytes 540704 | tf_op jit(solution)/shard_map/ppermute | solution.py:359
  72.8 0.1 bitcast_add_fusion
  72.9 0.8 collective-permute-start.2
  73.7 5.7 %collective-permute-done.2 = f32[2,264,128]{2,1,0:T(8,128)S(1)} collective-permute-done((f32[2,264,128]{2,1,0:T(8,128)S(1)}, f32[2,264,128]{2,1,0:T(8,128)S(1)}, u32[]{:S(2)}, u32[]{:S(2)}) %collective-permute-start.2) | collective-permute-done | bytes 270368 | tf_op jit(solution)/shard_map/ppermute | solution.py:359
  79.5 1.3 collective-permute-start.3
  80.8 3.8 %collective-permute-done.3 = f32[1,264,128]{2,1,0:T(8,128)S(1)} collective-permute-done((f32[1,264,128]{2,1,0:T(8,128)S(1)}, f32[1,264,128]{2,1,0:T(8,128)S(1)}, u32[]{:S(2)}, u32[]{:S(2)}) %collective-permute-start.3) | collective-permute-done | bytes 135200 | tf_op jit(solution)/shard_map/ppermute | solution.py:359
  84.6 2.3 %collective-permute-start.4 = (f32[1,264,128]{2,1,0:T(8,128)S(1)}, f32[1,264,128]{2,1,0:T(8,128)S(1)}, u32[]{:S(2)}, u32[]{:S(2)}) collective-permute-start(f32[1,264,128]{2,1,0:T(8,128)S(1)} %dynamic-slice_add_fusion), channel_id=1, source_target_pairs={{0,16},{1,17},{2,18},{3,19},{4,20},{5,21},{6,22},{7,23},{8,24},{9,... | collective-permute-start | bytes 405512 | tf_op jit(solution)/shard_map/ppermute | solution.py:359
  86.9 5.2 %collective-permute-done.4 = f32[1,264,128]{2,1,0:T(8,128)S(1)} collective-permute-done((f32[1,264,128]{2,1,0:T(8,128)S(1)}, f32[1,264,128]{2,1,0:T(8,128)S(1)}, u32[]{:S(2)}, u32[]{:S(2)}) %collective-permute-start.4) | collective-permute-done | bytes 135200 | tf_op jit(solution)/shard_map/ppermute | solution.py:359
  92.2 0.1 collective-permute-start.5
  92.3 6.4 %collective-permute-done.5 = f32[2,264,128]{2,1,0:T(8,128)S(1)} collective-permute-done((f32[2,264,128]{2,1,0:T(8,128)S(1)}, f32[2,264,128]{2,1,0:T(8,128)S(1)}, u32[]{:S(2)}, u32[]{:S(2)}) %collective-permute-start.5) | collective-permute-done | bytes 270368 | tf_op jit(solution)/shard_map/ppermute | solution.py:359
  98.7 0.1 select_bitcast_fusion.7
  98.8 0.3 collective-permute-start.6
  99.1 9.2 %collective-permute-done.6 = f32[4,264,128]{2,1,0:T(8,128)S(1)} collective-permute-done((f32[4,264,128]{2,1,0:T(8,128)S(1)}, f32[4,264,128]{2,1,0:T(8,128)S(1)}, u32[]{:S(2)}, u32[]{:S(2)}) %collective-permute-start.6) | collective-permute-done | bytes 540704 | tf_op jit(solution)/shard_map/ppermute | solution.py:359
  108.2 0.1 select_bitcast_fusion.5
  108.3 0.1 pad_maximum_fusion.2
  108.4 1.1 collective-permute-start.7
  109.5 18.4 %collective-permute-done.7 = f32[8,264,128]{2,1,0:T(8,128)S(1)} collective-permute-done((f32[8,264,128]{2,1,0:T(8,128)S(1)}, f32[8,264,128]{2,1,0:T(8,128)S(1)}, u32[]{:S(2)}, u32[]{:S(2)}) %collective-permute-start.7) | collective-permute-done | bytes 1081376 | tf_op jit(solution)/shard_map/ppermute | solution.py:359
  127.9 0.1 select_bitcast_fusion.3
  128.1 0.1 pad_maximum_fusion.1
  128.2 0.1 collective-permute-start.8
  128.3 0.6 dynamic-slice_bitcast_fusion.2
  128.9 3.8 %collective-permute-done.8 = f32[16,264,128]{2,1,0:T(8,128)} collective-permute-done((f32[16,264,128]{2,1,0:T(8,128)S(1)}, f32[16,264,128]{2,1,0:T(8,128)}, u32[]{:S(2)}, u32[]{:S(2)}) %collective-permute-start.8) | collective-permute-done | bytes 2162720 | tf_op jit(solution)/shard_map/ppermute | solution.py:359
  132.7 1.9 %select_bitcast_fusion.1 = (f32[1,16,264,128]{3,2,0,1:T(8,128)S(1)}, f32[1,16,264,128]{3,2,0,1:T(8,128)S(1)}) fusion(f32[16,264,128]{2,1,0:T(8,128)} %collective-permute-done.8, pred[]{:T(512)S(6)} %eq.26, f32[2,8,264,128]{3,2,0,1:T(8,128)S(1)} %pad_maximum_fusion.1), kind=kLoop, calls=%fused_computation.3 | loop fusion | flops 1081344 | bytes 8650753 | tf_op jit(solution)/shard_map/stack | solution.py:407
  134.6 0.3 pad_maximum_fusion
  134.8 3.1 %scaling.1 = (f32[6,1024]{1,0:T(8,128)}, f32[1,1024]{1,0:T(1,128)}, f32[1024,1024]{1,0:T(8,128)}, f32[1,1024]{1,0:T(1,128)}, f32[1,1024]{1,0:T(1,128)}, /*index=5*/f32[1,1]{1,0:T(1,128)}) custom-call(f32[2,8,2,264,128]{4,3,2,1,0:T(8,128)S(1)} %bitcast.83), custom_call_target="tpu_custom_call" | custom-call | tf_op jit(solution)/shard_map/scaling/pallas_call | solution.py:347
  (19 shorter events, 0.3 us)
Async XLA Ops:
  0.6 29.1 %copy-start = (bf16[1024,1024]{1,0:T(8,128)(2,1)S(1)}, bf16[1024,1024]{1,0:T(8,128)(2,1)}, u32[]{:S(2)}) copy-start(bf16[1024,1024]{1,0:T(8,128)(2,1)} %w_mid_ref.1) | copy-start | bytes 6291460
  0.6 0.9 copy-start.1
  1.6 0.7 copy-start.4
  2.2 0.7 copy-start.7
  2.9 26.9 %copy-start.2 = (s32[2,2816]{1,0:T(2,128)S(1)}, s32[2,2816]{1,0:T(2,128)}, u32[]{:S(2)}) copy-start(s32[2,2816]{1,0:T(2,128)} %constant.179.clone.maps_ref) | copy-start | bytes 67588
  2.9 26.9 %copy-start.3 = (bf16[6,1024]{1,0:T(8,128)(2,1)S(1)}, bf16[6,1024]{1,0:T(8,128)(2,1)}, u32[]{:S(2)}) copy-start(bf16[6,1024]{1,0:T(8,128)(2,1)} %w_in_ref.1) | copy-start | bytes 36868
  2.9 26.9 %copy-start.5 = (f32[1024]{0:T(1024)S(1)}, f32[1024]{0:T(1024)}, u32[]{:S(2)}) copy-start(f32[1024]{0:T(1024)} %param.15) | copy-start | bytes 12292
  2.9 26.9 %copy-start.6 = (f32[1024]{0:T(1024)S(1)}, f32[1024]{0:T(1024)}, u32[]{:S(2)}) copy-start(f32[1024]{0:T(1024)} %param.17) | copy-start | bytes 12292
  8.5 2.0 %collective-permute-start = (f32[256,88]{1,0:T(8,128)S(1)}, f32[256,88]{1,0:T(8,128)S(1)}, u32[]{:S(2)}, u32[]{:S(2)}) collective-permute-start(f32[256,88]{1,0:T(8,128)S(1)} %pricing.1), channel_id=1, source_target_pairs={{0,1},{1,0},{2,3},{3,2},{4,5},{5,4},{6,7},{7,6},{8,9},{9,8},{10,11... | collective-permute-start | bytes 270344 | tf_op jit(solution)/shard_map/ppermute | solution.py:359
  11.3 18.4 %all-to-all-start = ((f32[16,32,88]{2,1,0:T(8,128)}), f32[16,32,88]{2,1,0:T(8,128)S(1)}, u32[]{:S(2)}, u32[]{:S(2)}) async-start(f32[16,32,88]{2,1,0:T(8,128)} %bitcast.3), calls=%async_computation | async-start | bytes 524288 | tf_op jit(solution)/shard_map/all_to_all | solution.py:385
  59.9 12.9 %collective-permute-start.1 = (f32[4,264,128]{2,1,0:T(8,128)S(1)}, f32[4,264,128]{2,1,0:T(8,128)S(1)}, u32[]{:S(2)}, u32[]{:S(2)}) collective-permute-start(f32[4,264,128]{2,1,0:T(8,128)S(1)} %dynamic-slice_bitcast_fusion), channel_id=1, source_target_pairs={{0,8},{1,9},{2,10},{3,11},{4,12},{5,13},{6,14},{7,15},{8,0},{9,1},... | collective-permute-start | bytes 1622024 | tf_op jit(solution)/shard_map/ppermute | solution.py:359
  72.9 6.5 %collective-permute-start.2 = (f32[2,264,128]{2,1,0:T(8,128)S(1)}, f32[2,264,128]{2,1,0:T(8,128)S(1)}, u32[]{:S(2)}, u32[]{:S(2)}) collective-permute-start(f32[2,264,128]{2,1,0:T(8,128)S(1)} %dynamic-slice_bitcast_fusion.1), channel_id=1, source_target_pairs={{0,4},{1,5},{2,6},{3,7},{4,0},{5,1},{6,2},{7,3},{8,12},{9,13},{10,... | collective-permute-start | bytes 811016 | tf_op jit(solution)/shard_map/ppermute | solution.py:359
  79.5 5.1 %collective-permute-start.3 = (f32[1,264,128]{2,1,0:T(8,128)S(1)}, f32[1,264,128]{2,1,0:T(8,128)S(1)}, u32[]{:S(2)}, u32[]{:S(2)}) collective-permute-start(f32[1,264,128]{2,1,0:T(8,128)S(1)} %constant_dynamic-slice_fusion), channel_id=1, source_target_pairs={{0,2},{1,3},{2,0},{3,1},{4,6},{5,7},{6,4},{7,5},{8,10},{9,11},{10,... | collective-permute-start | bytes 405512 | tf_op jit(solution)/shard_map/ppermute | solution.py:359
  84.6 7.5 %collective-permute-start.4 = (f32[1,264,128]{2,1,0:T(8,128)S(1)}, f32[1,264,128]{2,1,0:T(8,128)S(1)}, u32[]{:S(2)}, u32[]{:S(2)}) collective-permute-start(f32[1,264,128]{2,1,0:T(8,128)S(1)} %dynamic-slice_add_fusion), channel_id=1, source_target_pairs={{0,16},{1,17},{2,18},{3,19},{4,20},{5,21},{6,22},{7,23},{8,24},{9,... | collective-permute-start | bytes 405512 | tf_op jit(solution)/shard_map/ppermute | solution.py:359
  92.2 6.5 %collective-permute-start.5 = (f32[2,264,128]{2,1,0:T(8,128)S(1)}, f32[2,264,128]{2,1,0:T(8,128)S(1)}, u32[]{:S(2)}, u32[]{:S(2)}) collective-permute-start(f32[2,264,128]{2,1,0:T(8,128)S(1)} %maximum_bitcast_fusion), channel_id=1, source_target_pairs={{0,8},{1,9},{2,10},{3,11},{4,12},{5,13},{6,14},{7,15},{8,0},{9,1},... | collective-permute-start | bytes 811016 | tf_op jit(solution)/shard_map/ppermute | solution.py:359
  98.8 9.4 %collective-permute-start.6 = (f32[4,264,128]{2,1,0:T(8,128)S(1)}, f32[4,264,128]{2,1,0:T(8,128)S(1)}, u32[]{:S(2)}, u32[]{:S(2)}) collective-permute-start(f32[4,264,128]{2,1,0:T(8,128)S(1)} %bitcast.94), channel_id=1, source_target_pairs={{0,4},{1,5},{2,6},{3,7},{4,0},{5,1},{6,2},{7,3},{8,12},{9,13},{10,... | collective-permute-start | bytes 1622024 | tf_op jit(solution)/shard_map/ppermute | solution.py:359
  108.4 19.5 %collective-permute-start.7 = (f32[8,264,128]{2,1,0:T(8,128)S(1)}, f32[8,264,128]{2,1,0:T(8,128)S(1)}, u32[]{:S(2)}, u32[]{:S(2)}) collective-permute-start(f32[8,264,128]{2,1,0:T(8,128)S(1)} %bitcast.91), channel_id=1, source_target_pairs={{0,2},{1,3},{2,0},{3,1},{4,6},{5,7},{6,4},{7,5},{8,10},{9,11},{10,... | collective-permute-start | bytes 3244040 | tf_op jit(solution)/shard_map/ppermute | solution.py:359
  128.2 4.5 %collective-permute-start.8 = (f32[16,264,128]{2,1,0:T(8,128)S(1)}, f32[16,264,128]{2,1,0:T(8,128)}, u32[]{:S(2)}, u32[]{:S(2)}) collective-permute-start(f32[16,264,128]{2,1,0:T(8,128)S(1)} %bitcast.90), channel_id=1, source_target_pairs={{0,1},{1,0},{2,3},{3,2},{4,5},{5,4},{6,7},{7,6},{8,9},{9,8},{10,11... | collective-permute-start | bytes 6488072 | tf_op jit(solution)/shard_map/ppermute | solution.py:359

commit v3 on v2

--- a/solution.py
+++ b/solution.py
@@ -17,6 +17,8 @@
 LANES = 128
 FEATURE_ROWS = 16
 ROW_TILE = 256
+CHUNK = 256
+CHUNKS = [slice(start, start + CHUNK) for start in range(0, WIDTH, CHUNK)]
 EPSILON = 1e-06
 
 
@@ -157,17 +159,20 @@
 
 def network_kernel(
     inv_sets, place_ref, maps_ref, feat_ref, sums_ref, w_in_ref, b_in_ref, w_mid_ref, b_mid_ref,
-    w_out_ref, b_out_ref, out_ref, left_ref, win_ref, turned_ref, bias_ref, read_ref, grad_ref,
-    small_ref, slope_ref, hidden_ref,
+    w_out_ref, b_out_ref, keep_a, send_a, keep_b, send_b, left_ref, win_ref, turned_ref, bias_ref, read_ref, grad_ref,
+    small_ref, slope_ref, delta_ref, extra_ref, even_hidden, odd_hidden, even_feat, odd_feat, even_gap,
+    odd_gap, even_mixed, odd_mixed, even_curve, odd_curve,
 ):
     block = place_ref[0]
     sets = sums_ref.shape[0]
-    rows = maps_ref.shape[1]
+    tiles = maps_ref.shape[1] // ROW_TILE
     cols = WIDTH // 4
     own = pl.ds(pl.multiple_of(block * cols, cols), cols)
-    groups = out_ref.shape[0]
+    groups = 2 * keep_a.shape[0]
     piece_rows = WIDTH // groups
     bf16 = jnp.bfloat16
+    even = (even_hidden, even_feat, even_gap, even_mixed, even_curve)
+    odd = (odd_hidden, odd_feat, odd_gap, odd_mixed, odd_curve)
 
     left_ref[...] = jnp.zeros_like(left_ref)
     left_ref[0:FEATURE_ROWS, :] = feat_ref[...]
@@ -188,78 +193,102 @@
     slope_ref[...] = jnp.zeros_like(slope_ref)
     readout = jnp.broadcast_to(w_out_ref[...].astype(jnp.float32), (16, WIDTH)).astype(bf16)
 
-    def tile(t, carry):
-        here = pl.ds(pl.multiple_of(t * ROW_TILE, ROW_TILE), ROW_TILE)
-        pair, group_set = maps_ref[0:1, here], maps_ref[1:2, here]
-        code = lax.broadcasted_iota(jnp.int32, (LANES, ROW_TILE), 0)
-        hot = jnp.where((code == pair) | (code == group_set), 1.0, 0.0).astype(bf16)
-        looked = dot(left, hot)
-        feat = looked[:FEATURE_ROWS].astype(bf16)
-        target = looked[FEATURE_ROWS : FEATURE_ROWS + sets]
-        for p in (1, 2):
-            first = FEATURE_ROWS + p * sets
-            target = target + looked[first : first + sets]
-        member = lax.broadcasted_iota(jnp.int32, (sets, ROW_TILE), 0) + PAIRS
-        target = jnp.sum(jnp.where(member == group_set, target, 0.0), axis=0, keepdims=True)
-
-        half_in = dot(win_ref[...], feat)
-        hidden_in = (half_in + half_in * jnp.tanh(half_in)).astype(bf16)
-        half_mid = dot(turned_ref[...], hidden_in) + bias_ref[...]
-        wave = jnp.tanh(half_mid)
-        rise = 1.0 + wave
-        hidden_mid = (half_mid * rise).astype(bf16)
-        hidden_ref[...] = hidden_mid
-        predicted = dot(readout, hidden_mid)[0:1] + b_out_ref[0]
-        slope = (predicted - target) * inv_sets
-        slope_ref[...] += slope
-        curve = read_ref[...] * (rise * (1.0 + half_mid * (1.0 - wave)))
-        delta_mid = (slope * curve).astype(bf16)
-        backward = dot(w_mid_ref[own, :], delta_mid)
-        own_half = dot(win_ref[own, :], feat)
-        own_wave = jnp.tanh(own_half)
-        own_curve = (0.5 * (1.0 + own_wave)) * (1.0 + own_half * (1.0 - own_wave))
-        delta_in = (backward * own_curve).astype(bf16)
-        own_curve_mid = slope * own_rows(curve, block, cols)
-        own_delta = own_curve_mid.astype(bf16)
-        grad_ref[...] += dot_rows(hidden_in, own_delta)
-        pieces = [piece.astype(jnp.float32) for piece in bf16_pieces(slope)]
-        lines = jnp.concatenate(
-            [feat.astype(jnp.float32)] + pieces + [jnp.zeros((13, ROW_TILE), jnp.float32)], 0
-        ).astype(bf16)
-        small_ref[:, 0:cols] += dot_rows(lines, delta_in)
-        small_ref[:, cols : 2 * cols] += dot_rows(lines, own_delta)
-        small_ref[:, 2 * cols :] += dot_rows(lines, hidden_ref[own, :])
+    def tile(t, last, coming):
+        if coming is not None:
+            hidden, feat_tile, gap_ref, mixed, curve = coming
+            here = pl.ds(pl.multiple_of(t * ROW_TILE, ROW_TILE), ROW_TILE)
+            pair, group_set = maps_ref[0:1, here], maps_ref[1:2, here]
+            code = lax.broadcasted_iota(jnp.int32, (LANES, ROW_TILE), 0)
+            hot = jnp.where((code == pair) | (code == group_set), 1.0, 0.0).astype(bf16)
+            looked = dot(left, hot)
+            feat = looked[:FEATURE_ROWS].astype(bf16)
+            feat_tile[...] = feat
+            target = looked[FEATURE_ROWS : FEATURE_ROWS + sets]
+            for p in (1, 2):
+                first = FEATURE_ROWS + p * sets
+                target = target + looked[first : first + sets]
+            member = lax.broadcasted_iota(jnp.int32, (sets, ROW_TILE), 0) + PAIRS
+            target = jnp.sum(jnp.where(member == group_set, target, 0.0), axis=0, keepdims=True)
+        if last is not None:
+            old_hidden, old_feat, old_gap, old_mixed, old_curve = last
+            slope = old_gap[...] * inv_sets
+            slope_ref[...] += slope
+            pieces = [piece.astype(jnp.float32) for piece in bf16_pieces(slope)]
+            lines = jnp.concatenate(
+                [old_feat[...].astype(jnp.float32)]
+                + pieces
+                + [jnp.zeros((13, ROW_TILE), jnp.float32)],
+                0,
+            ).astype(bf16)
+            for c in CHUNKS:
+                delta_ref[c, :] = (slope * old_curve[c, :]).astype(bf16)
+            own_half = dot(win_ref[own, :], old_feat[...])
+            own_delta = delta_ref[own, :]
+        if coming is not None:
+            for c in CHUNKS:
+                half_in = dot(win_ref[c, :], feat)
+                hidden[c, :] = (half_in + half_in * jnp.tanh(half_in)).astype(bf16)
+        if last is not None:
+            backward = dot(w_mid_ref[own, :], delta_ref[...])
+            own_wave = jnp.tanh(own_half)
+            own_curve = (0.5 * (1.0 + own_wave)) * (1.0 + own_half * (1.0 - own_wave))
+        for c in CHUNKS:
+            if coming is not None:
+                half_mid = dot(turned_ref[c, :], hidden[...]) + bias_ref[c, :]
+            if last is not None:
+                grad_ref[c, :] += dot_rows(old_hidden[c, :], own_delta)
+            if coming is not None:
+                wave = jnp.tanh(half_mid)
+                turn = half_mid * wave
+                mixed[c, :] = (half_mid + turn).astype(bf16)
+                curve[c, :] = (1.0 + wave) * (1.0 + half_mid - turn) * read_ref[c, :]
+        if last is not None:
+            delta_in = (backward * own_curve).astype(bf16)
+            small_ref[0:cols, :] += dot_rows(delta_in, lines)
+            small_ref[cols : 2 * cols, :] += dot_rows(own_delta, lines)
+            small_ref[2 * cols :, :] += dot_rows(old_mixed[own, :], lines)
+        if coming is not None:
+            predicted = dot(readout, mixed[...])[0:1] + b_out_ref[0]
+            gap_ref[...] = predicted - target
+
+    tile(0, None, even)
+
+    def two_tiles(u, carry):
+        tile(2 * u + 1, even, odd)
+        tile(2 * u + 2, odd, even)
         return carry
 
-    lax.fori_loop(0, rows // ROW_TILE, tile, 0)
-
-    extra = [small_ref[0:7, 0:cols], small_ref[6:7, cols : 2 * cols]]
-    extra.append(jnp.sum(small_ref[16:19, 2 * cols :], axis=0, keepdims=True))
+    lax.fori_loop(0, (tiles - 1) // 2, two_tiles, 0)
+    if tiles % 2 == 0:
+        tile(tiles - 1, even, odd)
+        tile(tiles, odd, None)
+    else:
+        tile(tiles, even, None)
+
+    lines = small_ref[...].T
+    extra = [lines[0:7, 0:cols], lines[6:7, cols : 2 * cols]]
+    extra.append(jnp.sum(lines[16:19, 2 * cols :], axis=0, keepdims=True))
     total = jnp.sum(slope_ref[...], axis=1, keepdims=True)
     extra.append(jnp.broadcast_to(total, (1, cols)))
     extra.append(jnp.zeros((6, cols), jnp.float32))
     extra = jnp.concatenate(extra, 0)
-    for j in range(groups):
-        for h in range(2):
-            lanes = slice(h * LANES, (h + 1) * LANES)
-            out_ref[j, h * piece_rows : (h + 1) * piece_rows, :] = grad_ref[
-                j * piece_rows : (j + 1) * piece_rows, lanes
-            ]
-        if j < 4:
-            lanes = slice((j % 2) * LANES, (j % 2 + 1) * LANES)
-            out_ref[j, 2 * piece_rows :, :] = extra[8 * (j // 2) : 8 * (j // 2) + 8, lanes]
-        else:
-            out_ref[j, 2 * piece_rows :, :] = jnp.zeros((8, LANES), jnp.float32)
-
-
-def own_rows(value, block, cols):
-    part = value[0:cols]
-    for b in range(1, 4):
-        part = jnp.where(block == b, value[b * cols : (b + 1) * cols], part)
-    return part
-
-
-def block_gradients(rows, sums, w_in, b_in, w_mid, b_mid, w_out, b_out, inv_sets, block, groups):
+    extra_ref[...] = jnp.zeros_like(extra_ref)
+    for j in range(4):
+        lanes = slice((j % 2) * LANES, (j % 2 + 1) * LANES)
+        extra_ref[j] = extra[8 * (j // 2) : 8 * (j // 2) + 8, lanes]
+    low, top = place_ref[1], place_ref[2]
+    for i in range(groups // 2):
+        for a_ref, b_ref, flip in ((keep_a, keep_b, 0), (send_a, send_b, 1)):
+            j = 2 * i + (low ^ flip)
+            piece = pl.ds(pl.multiple_of(j * piece_rows, piece_rows), piece_rows)
+            a_ref[i, 0:piece_rows, :] = grad_ref[piece, 0:LANES]
+            a_ref[i, piece_rows:, :] = extra_ref[j]
+            j = i + (top ^ flip) * (groups // 2)
+            piece = pl.ds(pl.multiple_of(j * piece_rows, piece_rows), piece_rows)
+            b_ref[i] = grad_ref[piece, LANES:]
+
+
+def block_gradients(rows, sums, w_in, b_in, w_mid, b_mid, w_out, b_out, inv_sets, place, groups):
     sets = rows.shape[1]
     cols = WIDTH // 4
     scale = jnp.array([[4.0], [1.0], [1.0], [20.0]], jnp.float32)
@@ -269,8 +298,11 @@
     return pl.pallas_call(
         functools.partial(network_kernel, inv_sets),
         in_specs=[smem] + [vmem] * 8 + [smem],
-        out_specs=vmem,
-        out_shape=jax.ShapeDtypeStruct((groups, 2 * (WIDTH // groups) + 8, LANES), jnp.float32),
+        out_specs=[vmem] * 4,
+        out_shape=[
+            jax.ShapeDtypeStruct((groups // 2, WIDTH // groups + more, LANES), jnp.float32)
+            for more in (8, 8, 0, 0)
+        ],
         scratch_shapes=[
             pltpu.VMEM((FEATURE_ROWS + 3 * sets, LANES), jnp.float32),
             pltpu.VMEM((WIDTH, FEATURE_ROWS), jnp.bfloat16),
@@ -278,30 +310,61 @@
             pltpu.VMEM((WIDTH, ROW_TILE), jnp.float32),
             pltpu.VMEM((WIDTH, ROW_TILE), jnp.float32),
             pltpu.VMEM((WIDTH, cols), jnp.float32),
-            pltpu.VMEM((32, 3 * cols), jnp.float32),
+            pltpu.VMEM((3 * cols, 32), jnp.float32),
             pltpu.VMEM((1, ROW_TILE), jnp.float32),
             pltpu.VMEM((WIDTH, ROW_TILE), jnp.bfloat16),
+            pltpu.VMEM((max(groups, 4), 8, LANES), jnp.float32),
+        ]
+        + [
+            pltpu.VMEM(shape, kind)
+            for shape, kind in (
+                ((WIDTH, ROW_TILE), jnp.bfloat16),
+                ((FEATURE_ROWS, ROW_TILE), jnp.bfloat16),
+                ((1, ROW_TILE), jnp.float32),
+                ((WIDTH, ROW_TILE), jnp.bfloat16),
+                ((WIDTH, ROW_TILE), jnp.float32),
+            )
+            for _ in range(2)
         ],
         compiler_params=pltpu.CompilerParams(vmem_limit_bytes=48 * 1024 * 1024),
         name="network",
     )(
-        block.reshape(1), jnp.asarray(row_maps(sets)), feat + feature_base(sets), sums, w_in,
+        place, jnp.asarray(row_maps(sets)), feat + feature_base(sets), sums, w_in,
         b_in.reshape(1, -1), w_mid, b_mid.reshape(1, -1), w_out.reshape(1, -1), b_out,
     )
 
 
-def scaling_kernel(
-    pieces_ref, w_in_ref, b_in_ref, w_mid_ref, b_mid_ref, w_out_ref, b_out_ref, small_ref
-):
-    groups = pieces_ref.shape[1]
+def scaling_kernel(layout, groups, owner_ref, *refs):
+    blocks = refs[: len(layout)]
+    w_in_ref, b_in_ref, w_mid_ref, b_mid_ref, w_out_ref, b_out_ref, extra_ref, small_ref = refs[
+        len(layout) :
+    ]
     piece_rows = WIDTH // groups
-    for high in range(2):
-        for core in range(2):
-            for j in range(4):
-                start = (2 * high + core) * (WIDTH // 4) + (j % 2) * LANES
-                small_ref[8 * (j // 2) : 8 * (j // 2) + 8, start : start + LANES] = pieces_ref[
-                    high, j, core, 2 * piece_rows :, :
-                ]
+    cols = WIDTH // 4
+    owner = owner_ref[0]
+    parts = []
+    for ref, (masks, contents) in zip(blocks, layout):
+        for i, mask in enumerate(masks):
+            device = owner ^ mask
+            index = (device >> 1) & (groups - 1)
+            column = 2 * (device // (2 * groups)) + (device & 1)
+            start = 0
+            for content in contents:
+                if content == "extra":
+                    extra_ref[index, column] = ref[i, start : start + 8, :]
+                    start += 8
+                else:
+                    parts.append((ref, i, start, index, column, content == "right"))
+                    start += piece_rows
+
+    total = jnp.zeros((8, LANES), jnp.float32)
+    for ref, i, start, index, column, right in parts:
+        part = ref[i, start : start + piece_rows, :]
+        total = total + jnp.sum((part * part).reshape(-1, 8, LANES), axis=0)
+    for column in range(4):
+        for j in range(4):
+            first = column * cols + (j % 2) * LANES
+            small_ref[8 * (j // 2) : 8 * (j // 2) + 8, first : first + LANES] = extra_ref[j, column]
     small = small_ref[...]
     squares = jnp.sum(small * small, axis=1, keepdims=True)
     bias_out = small_ref[9:10, 0:1]
@@ -310,14 +373,6 @@
     def factor(total, entries):
         return lax.rsqrt(total / entries + EPSILON)
 
-    def add(j, total):
-        for high in range(2):
-            for core in range(2):
-                part = pieces_ref[high, j, core, 0 : 2 * piece_rows, :]
-                total = total + jnp.sum((part * part).reshape(-1, 8, LANES), axis=0)
-        return total
-
-    total = lax.fori_loop(0, groups, add, jnp.zeros((8, LANES), jnp.float32))
     total = jnp.sum(jnp.sum(total, axis=1, keepdims=True), axis=0, keepdims=True)
     scale_mid = factor(total + squares[7:8], WIDTH * WIDTH + WIDTH)
     scale_in = factor(jnp.sum(squares[0:7], axis=0, keepdims=True), 7 * WIDTH)
@@ -327,32 +382,29 @@
     b_mid_ref[...] = small[7:8] * scale_mid
     w_out_ref[...] = small[8:9] * scale_out
     b_out_ref[...] = bias_out * scale_out
-
-    def place(j, carry):
-        rows = pl.ds(pl.multiple_of(j * piece_rows, 8), piece_rows)
-        for high in range(2):
-            for core in range(2):
-                for h in range(2):
-                    start = (2 * high + core) * (WIDTH // 4) + h * LANES
-                    part = pieces_ref[high, j, core, h * piece_rows : (h + 1) * piece_rows, :]
-                    w_mid_ref[rows, start : start + LANES] = part * scale_mid
-        return carry
-
-    lax.fori_loop(0, groups, place, 0)
-
-
-def scaled(pieces):
+    for ref, i, start, index, column, right in parts:
+        rows = pl.ds(pl.multiple_of(index * piece_rows, piece_rows), piece_rows)
+        first = pl.multiple_of(column * cols + (LANES if right else 0), LANES)
+        part = ref[i, start : start + piece_rows, :]
+        w_mid_ref[rows, pl.ds(first, LANES)] = part * scale_mid
+
+
+def scaled(owner, groups, received):
     vmem = pl.BlockSpec(memory_space=pltpu.VMEM)
     shapes = [(6, WIDTH), (1, WIDTH), (WIDTH, WIDTH), (1, WIDTH), (1, WIDTH), (1, 1)]
+    layout = [(masks, contents) for _, masks, contents in received]
     return pl.pallas_call(
-        scaling_kernel,
-        in_specs=[vmem],
+        functools.partial(scaling_kernel, layout, groups),
+        in_specs=[pl.BlockSpec(memory_space=pltpu.SMEM)] + [vmem] * len(received),
         out_specs=[vmem] * 6,
         out_shape=[jax.ShapeDtypeStruct(shape, jnp.float32) for shape in shapes],
-        scratch_shapes=[pltpu.VMEM((16, WIDTH), jnp.float32)],
+        scratch_shapes=[
+            pltpu.VMEM((max(groups, 4), 4, 8, LANES), jnp.float32),
+            pltpu.VMEM((16, WIDTH), jnp.float32),
+        ],
         compiler_params=pltpu.CompilerParams(vmem_limit_bytes=32 * 1024 * 1024),
         name="scaling",
-    )(pieces)
+    )(owner.reshape(1), *[array for array, _, _ in received])
 
 
 def swap(array, bit, devices):
@@ -361,6 +413,17 @@
 
 def pick(array, index):
     return lax.dynamic_index_in_dim(array, index, 0, keepdims=False)
+
+
+def halved(part, left, bit, group, devices):
+    axis = len(left) - 1 - left.index(bit)
+    shape = part.shape[1:]
+    cube = part.reshape((2,) * len(left) + shape)
+    mine = (group >> bit) % 2
+    keep = lax.dynamic_index_in_dim(cube, mine, axis, keepdims=False)
+    send = lax.dynamic_index_in_dim(cube, 1 - mine, axis, keepdims=False)
+    send, keep = send.reshape((-1,) + shape), keep.reshape((-1,) + shape)
+    return keep + swap(send, 2 << bit, devices)
 
 
 def on_device(params, increments, w_in, b_in, w_mid, b_mid, w_out, b_out):
@@ -378,39 +441,52 @@
     turned = params.T
 
     sums = payoff_sums(turned, increments)
+    sums = sums.reshape(2, groups, 2 * set_dev, PAIRS).swapaxes(0, 1)
+    sums = sums.reshape(groups, 4 * set_dev, PAIRS)
+    lanes = [[2 * j + c + top * h for j in range(groups)] for h in range(2) for c in range(2)]
+    sums = jnp.sum(lax.all_to_all(sums, "paths", 0, 0, axis_index_groups=lanes, tiled=True), axis=0)
     sums = sums + swap(sums, 1, devices)
-    sums = sums.reshape(2, groups, 2 * set_dev, PAIRS).swapaxes(0, 1)
-    sums = jnp.broadcast_to(sums[None], (2,) + sums.shape).reshape(top, 4 * set_dev, PAIRS)
-    lanes = [[2 * chip + c for chip in range(top)] for c in range(2)]
-    parts = lax.all_to_all(sums, "paths", 0, 0, axis_index_groups=lanes, tiled=True)
-    sums = jnp.sum(parts, axis=0) / total_paths
+    sums = (sums + swap(sums, top, devices)) / total_paths
     prices = pick(sums.reshape(4, set_dev, PAIRS), block)
 
     rows = pick(turned.reshape(4, 2, groups, 2 * set_dev).transpose(2, 0, 1, 3), group)
-    held = block_gradients(
+    place = jnp.stack([block, group % 2, group // (groups // 2)])
+    keep_a, send_a, keep_b, send_b = block_gradients(
         rows.reshape(4, 4 * set_dev), sums, w_in, b_in, w_mid, b_mid, w_out, b_out,
-        1.0 / set_count, block, groups,
+        1.0 / set_count, place, groups,
     )
 
-    bit = groups // 2
-    while bit:
-        mine = (group // bit) % 2
-        halves = held.reshape((2, held.shape[0] // 2) + held.shape[1:])
-        held = pick(halves, mine) + swap(pick(halves, 1 - mine), 2 * bit, devices)
-        bit //= 2
-
-    gathered = held.reshape((1,) + held.shape[1:])
-    bit = top
-    while bit:
-        came = swap(gathered, bit, devices)
-        first = (owner // bit) % 2 == 0
-        pair = jnp.stack([jnp.where(first, gathered, came), jnp.where(first, came, gathered)])
-        if bit == top:
-            gathered = pair.reshape((-1,) + pair.shape[2:])
-        else:
-            gathered = jnp.swapaxes(pair, 0, 1).reshape((-1,) + pair.shape[2:])
-        bit //= 2
-    result = scaled(gathered.reshape((2, groups, 2) + gathered.shape[1:]))
+    bits = [bit for bit in range(groups.bit_length() - 1)]
+    part_a = keep_a + swap(send_a, 2, devices)
+    part_b = keep_b + swap(send_b, top // 2, devices)
+    left_a, left_b = bits[1:], bits[:-1]
+    while left_a:
+        part_a = halved(part_a, left_a, left_a[0], group, devices)
+        part_b = halved(part_b, left_b, left_b[0], group, devices)
+        left_a, left_b = left_a[1:], left_b[1:]
+
+    own = jnp.concatenate([part_a, part_b], axis=1)
+    far = (0, top // 2, top, top + top // 2)
+    whole = jnp.concatenate([own] + [swap(own, mask, devices) for mask in far[1:]], axis=0)
+    received = [(whole, far, ("left", "extra", "right"))]
+    split = part_a.shape[1]
+    held_a, held_b = whole[:, :split], whole[:, split:]
+    order = [2 << bit for bit in bits[:-1]]
+    masks_a = masks_b = far
+    for bit_a, bit_b in zip(order, order[1:] + order[:1]):
+        came_a, came_b = swap(held_a, bit_a, devices), swap(held_b, bit_b, devices)
+        new_a = tuple(mask ^ bit_a for mask in masks_a)
+        new_b = tuple(mask ^ bit_b for mask in masks_b)
+        received += [(came_a, new_a, ("left", "extra")), (came_b, new_b, ("right",))]
+        if bit_a != order[-1]:
+            held_a = jnp.concatenate([held_a, came_a], axis=0)
+            held_b = jnp.concatenate([held_b, came_b], axis=0)
+        masks_a, masks_b = masks_a + new_a, masks_b + new_b
+    received += [
+        (swap(array, 1, devices), tuple(mask ^ 1 for mask in masks), contents)
+        for array, masks, contents in received
+    ]
+    result = scaled(owner, groups, received)
     direction_w_in, direction_b_in, direction_w_mid, direction_b_mid, direction_w_out, direction_b_out = result
     return (
         prices,

time: 138 us -> 111 us (0.80)
  waiting for transfers between devices: 73.1 us -> 47.6 us
  Pallas kernels: 38.7 us -> 29.3 us
  starting transfers between devices: 15.5 us -> 21.5 us
  local copies, waits for them, and re-layouts: 4.58 us -> 8.76 us
  other arithmetic: 4.42 us -> 1.86 us
    ppermute x9 -> x20, waiting for transfers between devices: 64.2 us -> 42.4 us  [swap(): return lax.ppermute(array, 'paths', [(i, i ^ bit) for i in range(devices)])]
    pallas_call x1, Pallas kernels: 30.1 us -> 19.6 us  [block_gradients(): pl.pallas_call(functools.partial(network_kernel, inv_sets), in_specs=[sme...]
    ppermute x9 -> x20, starting transfers between devices: 7.6 us -> 15.3 us  [swap(): return lax.ppermute(array, 'paths', [(i, i ^ bit) for i in range(devices)])]
    unnamed x16, local copies, waits for them, and re-layouts: 2.29 us -> 6.54 us
    all_to_all x1, waiting for transfers between devices: 8.97 us -> 5.19 us  [on_device(): lax.all_to_all(sums, 'paths', 0, 0, axis_index_groups=lanes, tiled=True)]
    another operation x9 -> x1, other arithmetic: 2.72 us -> 0.08 us  [on_device(): place = jnp.stack([block, group % 2, group // (groups // 2)])]
    all_to_all x1, starting transfers between devices: 7.95 us -> 6.18 us  [on_device(): lax.all_to_all(sums, 'paths', 0, 0, axis_index_groups=lanes, tiled=True)]
  transfers between devices with their start and end apart: 10 -> 21, of which waited for: 9 -> 15; matrix products, arithmetic and copies ran while one was open for 2% -> 3% of each run, Pallas kernels for 0% -> 0%
where the time goes in v3:
time: 111 us; the launch traced here: 110 us
  waiting for transfers between devices  47.6 us (43%)
  Pallas kernels  29.3 us (26%)
  starting transfers between devices  21.5 us (19%)
  local copies, waits for them, and re-layouts  8.76 us (8%)
  other arithmetic  1.86 us (2%)
  between operations  1.48 us (1%)
    ppermute x20, waiting for transfers between devices, swap(): return lax.ppermute(array, 'paths', [(i, i ^ bit) for i in range(devices)])  42.4 us
    pallas_call x1, Pallas kernels, block_gradients(): pl.pallas_call(functools.partial(network_kernel, inv_sets), in_specs=[sme...  19.6 us
    ppermute x20, starting transfers between devices, swap(): return lax.ppermute(array, 'paths', [(i, i ^ bit) for i in range(devices)])  15.3 us
    unnamed x16, local copies, waits for them, and re-layouts  6.54 us
    all_to_all x1, starting transfers between devices, on_device(): lax.all_to_all(sums, 'paths', 0, 0, axis_index_groups=lanes, tiled=True)  6.18 us
    pallas_call x1, Pallas kernels, payoff_sums(): pl.pallas_call(pricing_kernel, grid=(count // sets,), in_specs=[pl.BlockS...  5.55 us
    all_to_all x1, waiting for transfers between devices, on_device(): lax.all_to_all(sums, 'paths', 0, 0, axis_index_groups=lanes, tiled=True)  5.19 us
    pallas_call x1, Pallas kernels, scaled(): pl.pallas_call(functools.partial(scaling_kernel, layout, groups), in_spec...  4.2 us
  transfers between devices with their start and end apart: 21, of which 15 were waited for; matrix products, arithmetic and copies ran while one was open for 3% of the time, Pallas kernels for 0%

profile of v3, /device:TPU:0, one launch (start us, length us, event | category | flops | bytes accessed | tf_op | source)
XLA Modules:
  0.0 110.4 jit_solution(6584205545642175528)
XLA Ops:
  0.6 0.7 copy-done.1
  1.4 0.7 copy-done.4
  2.1 0.7 copy-done.7
  2.8 5.5 %pricing.1 = f32[256,88]{1,0:T(8,128)S(1)} custom-call(f32[8,11]{1,0:T(8,128)S(1)} %copy-done.7, f32[4,256]{1,0:T(4,128)S(1)} %bitcast.41, bf16[2,64,128]{2,1,0:T(8,128)(2,1)S(1)} %copy-done.1), custom_call_target="tpu_custom_call" | custom-call | tf_op jit(solution)/shard_map/pricing/pallas_call | solution.py:116
  8.3 0.7 copy.24
  9.0 6.2 %all-to-all-start = ((f32[8,32,88]{2,1,0:T(8,128)}), f32[8,32,88]{2,1,0:T(8,128)S(1)}, u32[]{:S(2)}, u32[]{:S(2)}) async-start(f32[8,32,88]{2,1,0:T(8,128)} %bitcast.3), calls=%async_computation | async-start | bytes 262144 | tf_op jit(solution)/shard_map/all_to_all | solution.py:447
  15.2 0.1 reshape.70
  15.3 0.1 reshape.71
  15.3 0.7 broadcast_multiply_fusion
  16.1 5.2 %all-to-all-done = f32[8,32,88]{2,1,0:T(8,128)S(1)} async-done(((f32[8,32,88]{2,1,0:T(8,128)}), f32[8,32,88]{2,1,0:T(8,128)S(1)}, u32[]{:S(2)}, u32[]{:S(2)}) %all-to-all-start) | async-done | bytes 90144 | tf_op jit(solution)/shard_map/all_to_all | solution.py:447
  21.4 0.8 pad_add_fusion.feat_ref
  22.1 0.4 collective-permute-done
  22.5 2.6 %collective-permute-start.1 = (f32[32,88]{1,0:T(8,128)S(1)}, f32[32,88]{1,0:T(8,128)S(1)}, u32[]{:S(2)}, u32[]{:S(2)}) collective-permute-start(f32[32,88]{1,0:T(8,128)S(1)} %add.90), channel_id=1, source_target_pairs={{0,16},{1,17},{2,18},{3,19},{4,20},{5,21},{6,22},{7,23},{8,24},{9,... | collective-permute-start | bytes 33800 | tf_op jit(solution)/shard_map/ppermute | solution.py:411
  25.1 0.1 pad_add_fusion.1.place_ref
  25.9 0.7 reshape.74.w_out_ref
  26.5 0.6 collective-permute-done.1
  27.2 1.6 %copy-done = bf16[1024,1024]{1,0:T(8,128)(2,1)S(1)} copy-done((bf16[1024,1024]{1,0:T(8,128)(2,1)S(1)}, bf16[1024,1024]{1,0:T(8,128)(2,1)}, u32[]{:S(2)}) %copy-start) | copy-done | bytes 2097176
  28.8 0.7 copy-done.2
  29.5 0.7 copy-done.3
  30.2 0.7 copy-done.5
  30.9 0.7 copy-done.6
  31.6 19.6 %network.1 = (f32[4,136,128]{2,1,0:T(8,128)S(1)}, f32[4,136,128]{2,1,0:T(8,128)S(1)}, f32[4,128,128]{2,1,0:T(8,128)S(1)}, f32[4,128,128]{2,1,0:T(8,128)S(1)}) custom-call(s32[3]{0:T(128)S(1)} %pad_add_fusion.1.place_ref, s32[2,2816]{1,0:T(2,128)S(1)} %copy-done.2, f32[16,128]{1,0:T(8,128)S(1)} %pad_add_fusion.feat_ref, ...), custom_call_target="tpu_custom_call" | custom-call | tf_op jit(solution)/shard_map/network/pallas_call | solution.py:298
  51.2 0.8 collective-permute-start.5
  52.0 0.6 collective-permute-start.2
  52.5 6.2 %collective-permute-done.5 = f32[4,128,128]{2,1,0:T(8,128)S(1)} collective-permute-done((f32[4,128,128]{2,1,0:T(8,128)S(1)}, f32[4,128,128]{2,1,0:T(8,128)S(1)}, u32[]{:S(2)}, u32[]{:S(2)}) %collective-permute-start.5) | collective-permute-done | bytes 262176 | tf_op jit(solution)/shard_map/ppermute | solution.py:411
  58.8 0.4 collective-permute-start.6
  59.2 0.3 collective-permute-done.2
  59.6 0.7 collective-permute-start.3
  60.3 3.5 %collective-permute-done.6 = f32[2,128,128]{2,1,0:T(8,128)S(1)} collective-permute-done((f32[2,128,128]{2,1,0:T(8,128)S(1)}, f32[2,128,128]{2,1,0:T(8,128)S(1)}, u32[]{:S(2)}, u32[]{:S(2)}) %collective-permute-start.6) | collective-permute-done | bytes 131104 | tf_op jit(solution)/shard_map/ppermute | solution.py:411
  63.8 0.6 collective-permute-start.7
  64.5 0.9 collective-permute-done.3
  65.5 1.6 %collective-permute-start.4 = (f32[1,136,128]{2,1,0:T(8,128)S(1)}, f32[1,136,128]{2,1,0:T(8,128)S(1)}, u32[]{:S(2)}, u32[]{:S(2)}) collective-permute-start(f32[1,136,128]{2,1,0:T(8,128)S(1)} %constant_dynamic-slice_fusion.1), channel_id=1, source_target_pairs={{0,8},{1,9},{2,10},{3,11},{4,12},{5,13},{6,14},{7,15},{8,0},{9,1},... | collective-permute-start | bytes 208904 | tf_op jit(solution)/shard_map/ppermute | solution.py:411
  67.0 1.1 %collective-permute-done.7 = f32[1,128,128]{2,1,0:T(8,128)S(1)} collective-permute-done((f32[1,128,128]{2,1,0:T(8,128)S(1)}, f32[1,128,128]{2,1,0:T(8,128)S(1)}, u32[]{:S(2)}, u32[]{:S(2)}) %collective-permute-start.7) | collective-permute-done | bytes 65568 | tf_op jit(solution)/shard_map/ppermute | solution.py:411
  68.2 2.8 %collective-permute-done.4 = f32[1,136,128]{2,1,0:T(8,128)S(1)} collective-permute-done((f32[1,136,128]{2,1,0:T(8,128)S(1)}, f32[1,136,128]{2,1,0:T(8,128)S(1)}, u32[]{:S(2)}, u32[]{:S(2)}) %collective-permute-start.4) | collective-permute-done | bytes 69664 | tf_op jit(solution)/shard_map/ppermute | solution.py:411
  71.0 5.0 %collective-permute-start.10 = (f32[1,264,128]{2,1,0:T(8,128)S(1)}, f32[1,264,128]{2,1,0:T(8,128)S(1)}, u32[]{:S(2)}, u32[]{:S(2)}) collective-permute-start(f32[1,264,128]{2,1,0:T(8,128)S(1)} %pad_maximum_fusion.3), channel_id=1, source_target_pairs={{0,24},{1,25},{2,26},{3,27},{4,28},{5,29},{6,30},{7,31},{8,16},{9,... | collective-permute-start | bytes 405512 | tf_op jit(solution)/shard_map/ppermute | solution.py:411
  76.0 0.6 collective-permute-start.8
  76.7 2.3 %collective-permute-done.10 = f32[1,264,128]{2,1,0:T(8,128)S(1)} collective-permute-done((f32[1,264,128]{2,1,0:T(8,128)S(1)}, f32[1,264,128]{2,1,0:T(8,128)S(1)}, u32[]{:S(2)}, u32[]{:S(2)}) %collective-permute-start.10) | collective-permute-done | bytes 135200 | tf_op jit(solution)/shard_map/ppermute | solution.py:411
  79.0 3.0 %collective-permute-done.9 = f32[1,264,128]{2,1,0:T(8,128)S(1)} collective-permute-done((f32[1,264,128]{2,1,0:T(8,128)S(1)}, f32[1,264,128]{2,1,0:T(8,128)S(1)}, u32[]{:S(2)}, u32[]{:S(2)}) %collective-permute-start.9) | collective-permute-done | bytes 135200 | tf_op jit(solution)/shard_map/ppermute | solution.py:411
  82.0 0.4 collective-permute-done.8
  82.7 0.6 collective-permute-start.12
  83.2 9.0 %collective-permute-done.11.refs_1_ = f32[4,136,128]{2,1,0:T(8,128)S(1)} collective-permute-done((f32[4,136,128]{2,1,0:T(8,128)S(1)}, f32[4,136,128]{2,1,0:T(8,128)S(1)}, u32[]{:S(2)}, u32[]{:S(2)}) %collective-permute-start.11) | collective-permute-done | bytes 278560 | tf_op jit(solution)/shard_map/ppermute | solution.py:411
  92.4 0.5 collective-permute-start.14
  92.9 8.9 %collective-permute-done.13.refs_3_ = f32[8,136,128]{2,1,0:T(8,128)S(1)} collective-permute-done((f32[8,136,128]{2,1,0:T(8,128)S(1)}, f32[8,136,128]{2,1,0:T(8,128)S(1)}, u32[]{:S(2)}, u32[]{:S(2)}) %collective-permute-start.13) | collective-permute-done | bytes 557088 | tf_op jit(solution)/shard_map/ppermute | solution.py:411
  101.9 0.5 collective-permute-start.15
  102.4 0.5 collective-permute-start.16
  102.9 0.6 dynamic-slice_bitcast_fusion.2
  103.5 2.7 %collective-permute-done.17.refs_7_ = f32[4,128,128]{2,1,0:T(8,128)} collective-permute-done((f32[4,128,128]{2,1,0:T(8,128)S(1)}, f32[4,128,128]{2,1,0:T(8,128)}, u32[]{:S(2)}, u32[]{:S(2)}) %collective-permute-start.17) | collective-permute-done | bytes 262176 | tf_op jit(solution)/shard_map/ppermute | solution.py:411
  106.2 4.2 %scaling.1 = (f32[6,1024]{1,0:T(8,128)}, f32[1,1024]{1,0:T(1,128)}, f32[1024,1024]{1,0:T(8,128)}, f32[1,1024]{1,0:T(1,128)}, f32[1,1024]{1,0:T(1,128)}, /*index=5*/f32[1,1]{1,0:T(1,128)}) custom-call(s32[1]{0:T(128)} %bitcast.6.owner_ref, f32[4,264,128]{2,1,0:T(8,128)S(1)} %pad_maximum_fusion.1.refs_0_, f32[4,136,128]{2,1,0:T(8,128)S(1)} %collective-permute-done.11.refs_1_, ...), custom_call_target="tpu_custom_call" | custom-call | tf_op jit(solution)/shard_map/scaling/pallas_call | solution.py:396
  (41 shorter events, 0.6 us)
Async XLA Ops:
  0.6 0.8 copy-start.1
  1.4 0.7 copy-start.4
  2.1 0.7 copy-start.7
  9.0 12.3 %all-to-all-start = ((f32[8,32,88]{2,1,0:T(8,128)}), f32[8,32,88]{2,1,0:T(8,128)S(1)}, u32[]{:S(2)}, u32[]{:S(2)}) async-start(f32[8,32,88]{2,1,0:T(8,128)} %bitcast.3), calls=%async_computation | async-start | bytes 262144 | tf_op jit(solution)/shard_map/all_to_all | solution.py:447
  21.3 1.2 %collective-permute-start = (f32[32,88]{1,0:T(8,128)S(1)}, f32[32,88]{1,0:T(8,128)S(1)}, u32[]{:S(2)}, u32[]{:S(2)}) collective-permute-start(f32[32,88]{1,0:T(8,128)S(1)} %reduce_sum.9), channel_id=1, source_target_pairs={{0,1},{1,0},{2,3},{3,2},{4,5},{5,4},{6,7},{7,6},{8,9},{9,8},{10,11... | collective-permute-start | bytes 33800 | tf_op jit(solution)/shard_map/ppermute | solution.py:411
  22.5 4.6 %collective-permute-start.1 = (f32[32,88]{1,0:T(8,128)S(1)}, f32[32,88]{1,0:T(8,128)S(1)}, u32[]{:S(2)}, u32[]{:S(2)}) collective-permute-start(f32[32,88]{1,0:T(8,128)S(1)} %add.90), channel_id=1, source_target_pairs={{0,16},{1,17},{2,18},{3,19},{4,20},{5,21},{6,22},{7,23},{8,24},{9,... | collective-permute-start | bytes 33800 | tf_op jit(solution)/shard_map/ppermute | solution.py:411
  27.2 1.6 %copy-start = (bf16[1024,1024]{1,0:T(8,128)(2,1)S(1)}, bf16[1024,1024]{1,0:T(8,128)(2,1)}, u32[]{:S(2)}) copy-start(bf16[1024,1024]{1,0:T(8,128)(2,1)} %w_mid_ref.1) | copy-start | bytes 6291460
  28.8 0.7 copy-start.2
  29.5 0.7 copy-start.3
  30.2 0.7 copy-start.5
  30.9 0.7 copy-start.6
  51.2 7.5 %collective-permute-start.5 = (f32[4,128,128]{2,1,0:T(8,128)S(1)}, f32[4,128,128]{2,1,0:T(8,128)S(1)}, u32[]{:S(2)}, u32[]{:S(2)}) collective-permute-start(f32[4,128,128]{2,1,0:T(8,128)S(1)} %get-tuple-element.20), channel_id=1, source_target_pairs={{0,8},{1,9},{2,10},{3,11},{4,12},{5,13},{6,14},{7,15},{8,0},{9,1},... | collective-permute-start | bytes 786440 | tf_op jit(solution)/shard_map/ppermute | solution.py:411
  52.0 7.5 %collective-permute-start.2 = (f32[4,136,128]{2,1,0:T(8,128)S(1)}, f32[4,136,128]{2,1,0:T(8,128)S(1)}, u32[]{:S(2)}, u32[]{:S(2)}) collective-permute-start(f32[4,136,128]{2,1,0:T(8,128)S(1)} %get-tuple-element.18), channel_id=1, source_target_pairs={{0,2},{1,3},{2,0},{3,1},{4,6},{5,7},{6,4},{7,5},{8,10},{9,11},{10,... | collective-permute-start | bytes 835592 | tf_op jit(solution)/shard_map/ppermute | solution.py:411
  58.8 5.0 %collective-permute-start.6 = (f32[2,128,128]{2,1,0:T(8,128)S(1)}, f32[2,128,128]{2,1,0:T(8,128)S(1)}, u32[]{:S(2)}, u32[]{:S(2)}) collective-permute-start(f32[2,128,128]{2,1,0:T(8,128)S(1)} %dynamic-slice_bitcast_fusion.1), channel_id=1, source_target_pairs={{0,2},{1,3},{2,0},{3,1},{4,6},{5,7},{6,4},{7,5},{8,10},{9,11},{10,... | collective-permute-start | bytes 393224 | tf_op jit(solution)/shard_map/ppermute | solution.py:411
  59.6 5.8 %collective-permute-start.3 = (f32[2,136,128]{2,1,0:T(8,128)S(1)}, f32[2,136,128]{2,1,0:T(8,128)S(1)}, u32[]{:S(2)}, u32[]{:S(2)}) collective-permute-start(f32[2,136,128]{2,1,0:T(8,128)S(1)} %dynamic-slice_bitcast_fusion), channel_id=1, source_target_pairs={{0,4},{1,5},{2,6},{3,7},{4,0},{5,1},{6,2},{7,3},{8,12},{9,13},{10,... | collective-permute-start | bytes 417800 | tf_op jit(solution)/shard_map/ppermute | solution.py:411
  63.8 4.3 %collective-permute-start.7 = (f32[1,128,128]{2,1,0:T(8,128)S(1)}, f32[1,128,128]{2,1,0:T(8,128)S(1)}, u32[]{:S(2)}, u32[]{:S(2)}) collective-permute-start(f32[1,128,128]{2,1,0:T(8,128)S(1)} %constant_dynamic-slice_fusion), channel_id=1, source_target_pairs={{0,4},{1,5},{2,6},{3,7},{4,0},{5,1},{6,2},{7,3},{8,12},{9,13},{10,... | collective-permute-start | bytes 196616 | tf_op jit(solution)/shard_map/ppermute | solution.py:411
  65.5 5.5 %collective-permute-start.4 = (f32[1,136,128]{2,1,0:T(8,128)S(1)}, f32[1,136,128]{2,1,0:T(8,128)S(1)}, u32[]{:S(2)}, u32[]{:S(2)}) collective-permute-start(f32[1,136,128]{2,1,0:T(8,128)S(1)} %constant_dynamic-slice_fusion.1), channel_id=1, source_target_pairs={{0,8},{1,9},{2,10},{3,11},{4,12},{5,13},{6,14},{7,15},{8,0},{9,1},... | collective-permute-start | bytes 208904 | tf_op jit(solution)/shard_map/ppermute | solution.py:411
  71.0 8.0 %collective-permute-start.10 = (f32[1,264,128]{2,1,0:T(8,128)S(1)}, f32[1,264,128]{2,1,0:T(8,128)S(1)}, u32[]{:S(2)}, u32[]{:S(2)}) collective-permute-start(f32[1,264,128]{2,1,0:T(8,128)S(1)} %pad_maximum_fusion.3), channel_id=1, source_target_pairs={{0,24},{1,25},{2,26},{3,27},{4,28},{5,29},{6,30},{7,31},{8,16},{9,... | collective-permute-start | bytes 405512 | tf_op jit(solution)/shard_map/ppermute | solution.py:411
  76.0 6.0 %collective-permute-start.9 = (f32[1,264,128]{2,1,0:T(8,128)S(1)}, f32[1,264,128]{2,1,0:T(8,128)S(1)}, u32[]{:S(2)}, u32[]{:S(2)}) collective-permute-start(f32[1,264,128]{2,1,0:T(8,128)S(1)} %pad_maximum_fusion.3), channel_id=1, source_target_pairs={{0,16},{1,17},{2,18},{3,19},{4,20},{5,21},{6,22},{7,23},{8,24},{9,... | collective-permute-start | bytes 405512 | tf_op jit(solution)/shard_map/ppermute | solution.py:411
  76.0 6.5 %collective-permute-start.8 = (f32[1,264,128]{2,1,0:T(8,128)S(1)}, f32[1,264,128]{2,1,0:T(8,128)S(1)}, u32[]{:S(2)}, u32[]{:S(2)}) collective-permute-start(f32[1,264,128]{2,1,0:T(8,128)S(1)} %pad_maximum_fusion.3), channel_id=1, source_target_pairs={{0,8},{1,9},{2,10},{3,11},{4,12},{5,13},{6,14},{7,15},{8,0},{9,1},... | collective-permute-start | bytes 405512 | tf_op jit(solution)/shard_map/ppermute | solution.py:411
  82.6 9.7 %collective-permute-start.11 = (f32[4,136,128]{2,1,0:T(8,128)S(1)}, f32[4,136,128]{2,1,0:T(8,128)S(1)}, u32[]{:S(2)}, u32[]{:S(2)}) collective-permute-start(f32[4,136,128]{2,1,0:T(8,128)S(1)} %slice.8), channel_id=1, source_target_pairs={{0,2},{1,3},{2,0},{3,1},{4,6},{5,7},{6,4},{7,5},{8,10},{9,11},{10,... | collective-permute-start | bytes 835592 | tf_op jit(solution)/shard_map/ppermute | solution.py:411
  82.7 9.7 %collective-permute-start.12 = (f32[4,128,128]{2,1,0:T(8,128)S(1)}, f32[4,128,128]{2,1,0:T(8,128)S(1)}, u32[]{:S(2)}, u32[]{:S(2)}) collective-permute-start(f32[4,128,128]{2,1,0:T(8,128)S(1)} %slice.9), channel_id=1, source_target_pairs={{0,4},{1,5},{2,6},{3,7},{4,0},{5,1},{6,2},{7,3},{8,12},{9,13},{10,... | collective-permute-start | bytes 786440 | tf_op jit(solution)/shard_map/ppermute | solution.py:411
  92.3 9.6 %collective-permute-start.13 = (f32[8,136,128]{2,1,0:T(8,128)S(1)}, f32[8,136,128]{2,1,0:T(8,128)S(1)}, u32[]{:S(2)}, u32[]{:S(2)}) collective-permute-start(f32[8,136,128]{2,1,0:T(8,128)S(1)} %pad_maximum_fusion), channel_id=1, source_target_pairs={{0,4},{1,5},{2,6},{3,7},{4,0},{5,1},{6,2},{7,3},{8,12},{9,13},{10,... | collective-permute-start | bytes 1671176 | tf_op jit(solution)/shard_map/ppermute | solution.py:411
  92.4 10.0 %collective-permute-start.14 = (f32[8,128,128]{2,1,0:T(8,128)S(1)}, f32[8,128,128]{2,1,0:T(8,128)S(1)}, u32[]{:S(2)}, u32[]{:S(2)}) collective-permute-start(f32[8,128,128]{2,1,0:T(8,128)S(1)} %pad_maximum_fusion.2), channel_id=1, source_target_pairs={{0,2},{1,3},{2,0},{3,1},{4,6},{5,7},{6,4},{7,5},{8,10},{9,11},{10,... | collective-permute-start | bytes 1572872 | tf_op jit(solution)/shard_map/ppermute | solution.py:411
  101.9 4.4 %collective-permute-start.18 = (f32[8,136,128]{2,1,0:T(8,128)S(1)}, f32[8,136,128]{2,1,0:T(8,128)S(1)}, u32[]{:S(2)}, u32[]{:S(2)}) collective-permute-start(f32[8,136,128]{2,1,0:T(8,128)S(1)} %collective-permute-done.13.refs_3_), channel_id=1, source_target_pairs={{0,1},{1,0},{2,3},{3,2},{4,5},{5,4},{6,7},{7,6},{8,9},{9,8},{10,11... | collective-permute-start | bytes 1671176 | tf_op jit(solution)/shard_map/ppermute | solution.py:411
  101.9 4.3 %collective-permute-start.15 = (f32[4,264,128]{2,1,0:T(8,128)S(1)}, f32[4,264,128]{2,1,0:T(8,128)S(1)}, u32[]{:S(2)}, u32[]{:S(2)}) collective-permute-start(f32[4,264,128]{2,1,0:T(8,128)S(1)} %pad_maximum_fusion.1.refs_0_), channel_id=1, source_target_pairs={{0,1},{1,0},{2,3},{3,2},{4,5},{5,4},{6,7},{7,6},{8,9},{9,8},{10,11... | collective-permute-start | bytes 1622024 | tf_op jit(solution)/shard_map/ppermute | solution.py:411
  102.4 3.8 %collective-permute-start.19 = (f32[8,128,128]{2,1,0:T(8,128)S(1)}, f32[8,128,128]{2,1,0:T(8,128)}, u32[]{:S(2)}, u32[]{:S(2)}) collective-permute-start(f32[8,128,128]{2,1,0:T(8,128)S(1)} %collective-permute-done.14.refs_4_), channel_id=1, source_target_pairs={{0,1},{1,0},{2,3},{3,2},{4,5},{5,4},{6,7},{7,6},{8,9},{9,8},{10,11... | collective-permute-start | bytes 1572872 | tf_op jit(solution)/shard_map/ppermute | solution.py:411
  102.4 3.8 %collective-permute-start.16 = (f32[4,136,128]{2,1,0:T(8,128)S(1)}, f32[4,136,128]{2,1,0:T(8,128)S(1)}, u32[]{:S(2)}, u32[]{:S(2)}) collective-permute-start(f32[4,136,128]{2,1,0:T(8,128)S(1)} %collective-permute-done.11.refs_1_), channel_id=1, source_target_pairs={{0,1},{1,0},{2,3},{3,2},{4,5},{5,4},{6,7},{7,6},{8,9},{9,8},{10,11... | collective-permute-start | bytes 835592 | tf_op jit(solution)/shard_map/ppermute | solution.py:411
  102.9 3.3 %collective-permute-start.17 = (f32[4,128,128]{2,1,0:T(8,128)S(1)}, f32[4,128,128]{2,1,0:T(8,128)}, u32[]{:S(2)}, u32[]{:S(2)}) collective-permute-start(f32[4,128,128]{2,1,0:T(8,128)S(1)} %collective-permute-done.12.refs_2_), channel_id=1, source_target_pairs={{0,1},{1,0},{2,3},{3,2},{4,5},{5,4},{6,7},{7,6},{8,9},{9,8},{10,11... | collective-permute-start | bytes 786440 | tf_op jit(solution)/shard_map/ppermute | solution.py:411

commit v4 on v3

--- a/solution.py
+++ b/solution.py
@@ -17,6 +17,8 @@
 LANES = 128
 FEATURE_ROWS = 16
 ROW_TILE = 256
+FORWARD_VMEM = 24 * 1024 * 1024
+BACKWARD_VMEM = 24 * 1024 * 1024
 CHUNK = 256
 CHUNKS = [slice(start, start + CHUNK) for start in range(0, WIDTH, CHUNK)]
 EPSILON = 1e-06
@@ -25,7 +27,6 @@
 TENORS = (np.arange(MATS, dtype=np.float32) + np.float32(1.0)) / np.float32(MATS)
 OFFSETS = np.arange(STRIKES, dtype=np.float32) - np.float32((STRIKES - 1) / 2.0)
 LOG_STRIKE = np.float32(0.05) * OFFSETS[None, :] * np.sqrt(TENORS)[:, None]
-STRIKE = np.exp(LOG_STRIKE).astype(np.float32)
 SET_BLOCK = 256
 LOG2E = 1.4426950408889634
 
@@ -38,7 +39,7 @@
     return high, mid, low
 
 
-def pricing_kernel(strike_ref, params_ref, inc_ref, out_ref, lags_ref, noise_ref, comp_ref, pay_ref):
+def pricing_kernel(params_ref, inc_ref, out_ref, lags_ref, noise_ref, comp_ref, pay_ref):
     sets = params_ref.shape[1]
     paths = inc_ref.shape[2]
     hurst = params_ref[0:1, :]
@@ -98,9 +99,11 @@
             total = total + root_variance * (shock - root_variance)
         lags_ref[...] = pltpu.roll(lags_ref[...], LANES - 8, 1)
         spot = jnp.exp2(total * growth)
+        tenor = jnp.full((8, sets), 1.0, jnp.float32) * ((m + 1).astype(jnp.float32) / MATS)
+        spread = jnp.sqrt(tenor)
         for j in range(STRIKES):
-            strike = strike_ref[m, j]
-            gains = jnp.maximum(spot, strike).reshape(paths // 8, 8, sets).sum(axis=0)
+            strike = jnp.exp((0.05 * (j - (STRIKES - 1) / 2.0)) * spread)
+            gains = jnp.maximum(spot.reshape(paths // 8, 8, sets), strike[None]).sum(axis=0)
             gains = gains - strike * (paths // 8)
             pay_ref[pl.ds(m * STRIKES + j, 1), :] = jnp.sum(gains, axis=0, keepdims=True)
         return total
@@ -117,7 +120,6 @@
         pricing_kernel,
         grid=(count // sets,),
         in_specs=[
-            pl.BlockSpec(memory_space=pltpu.SMEM),
             pl.BlockSpec((4, sets), lambda b: (0, b)),
             pl.BlockSpec((2, STEPS, paths), lambda b: (0, 0, 0)),
         ],
@@ -131,20 +133,11 @@
         ],
         compiler_params=pltpu.CompilerParams(vmem_limit_bytes=32 * 1024 * 1024),
         name="pricing",
-    )(jnp.asarray(STRIKE), params, increments)
-
-
-def row_maps(sets):
-    row = np.arange(sets * PAIRS, dtype=np.int32)
-    return np.stack([row % PAIRS, PAIRS + row // PAIRS])
-
-
-def feature_base(sets):
-    base = np.zeros((FEATURE_ROWS, LANES), np.float32)
-    base[4, :PAIRS] = (np.float32(4.0) * LOG_STRIKE).reshape(PAIRS)
-    base[5, :PAIRS] = np.repeat(TENORS, STRIKES)
-    base[6:9, PAIRS : PAIRS + sets] = 1.0
-    return base
+    )(in_hbm(params), in_hbm(increments))
+
+
+def in_hbm(array):
+    return pltpu.with_memory_space_constraint(array, pltpu.HBM)
 
 
 def dot(left, right):
@@ -157,117 +150,245 @@
     )
 
 
-def network_kernel(
-    inv_sets, place_ref, maps_ref, feat_ref, sums_ref, w_in_ref, b_in_ref, w_mid_ref, b_mid_ref,
-    w_out_ref, b_out_ref, keep_a, send_a, keep_b, send_b, left_ref, win_ref, turned_ref, bias_ref, read_ref, grad_ref,
-    small_ref, slope_ref, delta_ref, extra_ref, even_hidden, odd_hidden, even_feat, odd_feat, even_gap,
-    odd_gap, even_mixed, odd_mixed, even_curve, odd_curve,
+def one_hot(t, sets):
+    row = t * ROW_TILE + lax.broadcasted_iota(jnp.int32, (1, ROW_TILE), 1)
+    group_set = ((row.astype(jnp.float32) + 0.5) * (1.0 / PAIRS)).astype(jnp.int32)
+    pair = row - PAIRS * group_set
+    code = lax.broadcasted_iota(jnp.int32, (LANES, ROW_TILE), 0)
+    hot = jnp.where((code == pair) | (code == group_set + PAIRS), 1.0, 0.0)
+    return hot.astype(jnp.bfloat16), group_set
+
+
+def feature_table(params_ref, group, sets):
+    set_count = params_ref.shape[1]
+    lane = lax.broadcasted_iota(jnp.int32, (1, LANES), 1)
+    maturity = ((lane.astype(jnp.float32) + 0.5) * (1.0 / STRIKES)).astype(jnp.int32)
+    offset = (lane - STRIKES * maturity).astype(jnp.float32) - (STRIKES - 1) / 2.0
+    spread = jnp.zeros((1, LANES), jnp.float32)
+    for m in range(MATS):
+        spread = jnp.where(maturity == m, float(np.sqrt(TENORS)[m]), spread)
+    strikes = jnp.where(lane < PAIRS, 4.0 * (0.05 * offset * spread), 0.0)
+    tenors = jnp.where(lane < PAIRS, (maturity.astype(jnp.float32) + 1.0) / MATS, 0.0)
+    ones = jnp.where((lane >= PAIRS) & (lane < PAIRS + sets), 1.0, 0.0)
+    wide = jnp.concatenate([params_ref[...], jnp.zeros((4, set_count), jnp.float32)], 0)
+    half = sets // 2
+    own = jnp.zeros((8, LANES), jnp.float32)
+    for high in range(2):
+        first = PAIRS + high * half
+        start = high * (set_count // 2) + group * half
+        moved = pltpu.roll(wide, lax.rem(first + set_count - start, set_count), 1)[:, :LANES]
+        own = jnp.where((lane >= first) & (lane < first + half), moved, own)
+    scale = [own[0:1] * 4.0, own[1:2], own[2:3], own[3:4] * 20.0]
+    pad = jnp.zeros((FEATURE_ROWS - 9, LANES), jnp.float32)
+    return jnp.concatenate(scale + [strikes, tenors, ones, ones, ones, pad], 0)
+
+
+def prepare_kernel(
+    w_in_hbm, b_in_hbm, w_mid_hbm, win_ref, turned_ref, w_in_ref, b_in_ref, w_mid_ref, sems
 ):
-    block = place_ref[0]
-    sets = sums_ref.shape[0]
-    tiles = maps_ref.shape[1] // ROW_TILE
-    cols = WIDTH // 4
-    own = pl.ds(pl.multiple_of(block * cols, cols), cols)
-    groups = 2 * keep_a.shape[0]
-    piece_rows = WIDTH // groups
-    bf16 = jnp.bfloat16
-    even = (even_hidden, even_feat, even_gap, even_mixed, even_curve)
-    odd = (odd_hidden, odd_feat, odd_gap, odd_mixed, odd_curve)
-
-    left_ref[...] = jnp.zeros_like(left_ref)
-    left_ref[0:FEATURE_ROWS, :] = feat_ref[...]
-    for p, piece in enumerate(bf16_pieces(sums_ref[...])):
-        first = FEATURE_ROWS + p * sets
-        left_ref[first : first + sets, :PAIRS] = piece.astype(jnp.float32)
-    left = left_ref[...].astype(bf16)
-
+    copies = [
+        pltpu.make_async_copy(source, target, sems.at[i])
+        for i, (source, target) in enumerate(
+            ((w_in_hbm, w_in_ref), (b_in_hbm, b_in_ref), (w_mid_hbm, w_mid_ref))
+        )
+    ]
+    for copy in copies:
+        copy.start()
+    for copy in copies:
+        copy.wait()
     weights_in = w_in_ref[...].astype(jnp.float32)
     bias_in = [piece.astype(jnp.float32) for piece in bf16_pieces(b_in_ref[...])]
     pad = jnp.zeros((FEATURE_ROWS - weights_in.shape[0] - 3, WIDTH), jnp.float32)
-    win_ref[...] = (0.5 * jnp.concatenate([weights_in] + bias_in + [pad], 0)).T.astype(bf16)
-    turned_ref[...] = (0.5 * w_mid_ref[...].astype(jnp.float32)).T.astype(bf16)
+    win = (0.5 * jnp.concatenate([weights_in] + bias_in + [pad], 0)).T
+    win_ref[...] = win.astype(jnp.bfloat16)
+    turned_ref[...] = (0.5 * w_mid_ref[...].astype(jnp.float32)).T.astype(jnp.bfloat16)
+
+
+def prepare(w_in, b_in, w_mid):
+    vmem = pl.BlockSpec(memory_space=pltpu.VMEM)
+    hbm = pl.BlockSpec(memory_space=pltpu.HBM)
+    return pl.pallas_call(
+        prepare_kernel,
+        in_specs=[hbm] * 3,
+        out_specs=[vmem] * 2,
+        out_shape=[
+            jax.ShapeDtypeStruct((WIDTH, FEATURE_ROWS), jnp.bfloat16),
+            jax.ShapeDtypeStruct((WIDTH, WIDTH), jnp.bfloat16),
+        ],
+        scratch_shapes=[
+            pltpu.VMEM(w_in.shape, jnp.bfloat16),
+            pltpu.VMEM((1, WIDTH), jnp.float32),
+            pltpu.VMEM((WIDTH, WIDTH), jnp.bfloat16),
+            pltpu.SemaphoreType.DMA((3,)),
+        ],
+        compiler_params=pltpu.CompilerParams(vmem_limit_bytes=16 * 1024 * 1024),
+        name="prepare",
+    )(in_hbm(w_in), in_hbm(b_in.reshape(1, -1)), in_hbm(w_mid))
+
+
+def forward_kernel(
+    sets, owner_ref, params_ref, b_mid_ref, w_out_ref, win_ref, turned_ref,
+    hidden_out, curve_out, own_curve_out, mixed_out, feat_out, pred_out, bias_ref, read_ref,
+    even_hidden, odd_hidden, even_mixed, odd_mixed,
+):
+    bf16 = jnp.bfloat16
+    tiles = hidden_out.shape[1] // ROW_TILE
+    cols = WIDTH // 4
+    owner = owner_ref[0]
+    devices = params_ref.shape[1] * 4 // sets
+    block = 2 * (owner // (devices // 2)) + owner % 2
+    group = (owner // 2) % (devices // 4)
+    own = pl.ds(pl.multiple_of(block * cols, cols), cols)
+    table = feature_table(params_ref, group, sets).astype(bf16)
+    read_ref[...] = jnp.broadcast_to((0.5 * w_out_ref[...].astype(jnp.float32)).T, read_ref.shape)
+    readout = jnp.broadcast_to(w_out_ref[...].astype(jnp.float32), (16, WIDTH)).astype(bf16)
     bias_ref[...] = jnp.broadcast_to((0.5 * b_mid_ref[...]).T, bias_ref.shape)
-    read_ref[...] = jnp.broadcast_to((0.5 * w_out_ref[...].astype(jnp.float32)).T, read_ref.shape)
-    grad_ref[...] = jnp.zeros_like(grad_ref)
-    small_ref[...] = jnp.zeros_like(small_ref)
-    slope_ref[...] = jnp.zeros_like(slope_ref)
-    readout = jnp.broadcast_to(w_out_ref[...].astype(jnp.float32), (16, WIDTH)).astype(bf16)
-
-    def tile(t, last, coming):
-        if coming is not None:
-            hidden, feat_tile, gap_ref, mixed, curve = coming
-            here = pl.ds(pl.multiple_of(t * ROW_TILE, ROW_TILE), ROW_TILE)
-            pair, group_set = maps_ref[0:1, here], maps_ref[1:2, here]
-            code = lax.broadcasted_iota(jnp.int32, (LANES, ROW_TILE), 0)
-            hot = jnp.where((code == pair) | (code == group_set), 1.0, 0.0).astype(bf16)
-            looked = dot(left, hot)
-            feat = looked[:FEATURE_ROWS].astype(bf16)
-            feat_tile[...] = feat
-            target = looked[FEATURE_ROWS : FEATURE_ROWS + sets]
-            for p in (1, 2):
-                first = FEATURE_ROWS + p * sets
-                target = target + looked[first : first + sets]
-            member = lax.broadcasted_iota(jnp.int32, (sets, ROW_TILE), 0) + PAIRS
-            target = jnp.sum(jnp.where(member == group_set, target, 0.0), axis=0, keepdims=True)
-        if last is not None:
-            old_hidden, old_feat, old_gap, old_mixed, old_curve = last
-            slope = old_gap[...] * inv_sets
-            slope_ref[...] += slope
-            pieces = [piece.astype(jnp.float32) for piece in bf16_pieces(slope)]
-            lines = jnp.concatenate(
-                [old_feat[...].astype(jnp.float32)]
-                + pieces
-                + [jnp.zeros((13, ROW_TILE), jnp.float32)],
-                0,
-            ).astype(bf16)
-            for c in CHUNKS:
-                delta_ref[c, :] = (slope * old_curve[c, :]).astype(bf16)
-            own_half = dot(win_ref[own, :], old_feat[...])
-            own_delta = delta_ref[own, :]
-        if coming is not None:
-            for c in CHUNKS:
+
+    def span(t):
+        return pl.ds(pl.multiple_of(t * ROW_TILE, ROW_TILE), ROW_TILE)
+
+    def step(t, new, old, first=True, second=True, third=True):
+        new_hidden, new_mixed = new
+        old_hidden, old_mixed = old
+        if third:
+            pred_out[0:1, span(t - 2)] = dot(readout, new_mixed[...])[0:1]
+            mixed_out[:, span(t - 2)] = new_mixed[own, :]
+        if first:
+            hot, _ = one_hot(t, sets)
+            feat = dot(table, hot).astype(bf16)
+            feat_out[:, span(t)] = feat
+        for c in CHUNKS:
+            if second:
+                half_mid = dot(turned_ref[c, :], old_hidden[...]) + bias_ref[c, :]
+            if first:
                 half_in = dot(win_ref[c, :], feat)
-                hidden[c, :] = (half_in + half_in * jnp.tanh(half_in)).astype(bf16)
-        if last is not None:
-            backward = dot(w_mid_ref[own, :], delta_ref[...])
-            own_wave = jnp.tanh(own_half)
-            own_curve = (0.5 * (1.0 + own_wave)) * (1.0 + own_half * (1.0 - own_wave))
-        for c in CHUNKS:
-            if coming is not None:
-                half_mid = dot(turned_ref[c, :], hidden[...]) + bias_ref[c, :]
-            if last is not None:
-                grad_ref[c, :] += dot_rows(old_hidden[c, :], own_delta)
-            if coming is not None:
+            if second:
                 wave = jnp.tanh(half_mid)
                 turn = half_mid * wave
-                mixed[c, :] = (half_mid + turn).astype(bf16)
-                curve[c, :] = (1.0 + wave) * (1.0 + half_mid - turn) * read_ref[c, :]
-        if last is not None:
-            delta_in = (backward * own_curve).astype(bf16)
-            small_ref[0:cols, :] += dot_rows(delta_in, lines)
-            small_ref[cols : 2 * cols, :] += dot_rows(own_delta, lines)
-            small_ref[2 * cols :, :] += dot_rows(old_mixed[own, :], lines)
-        if coming is not None:
-            predicted = dot(readout, mixed[...])[0:1] + b_out_ref[0]
-            gap_ref[...] = predicted - target
-
-    tile(0, None, even)
-
-    def two_tiles(u, carry):
-        tile(2 * u + 1, even, odd)
-        tile(2 * u + 2, odd, even)
+                old_mixed[c, :] = (half_mid + turn).astype(bf16)
+                curve_out[c, span(t - 1)] = (1.0 + wave) * (1.0 + half_mid - turn) * read_ref[c, :]
+            if first:
+                value = (half_in + half_in * jnp.tanh(half_in)).astype(bf16)
+                new_hidden[c, :] = value
+                hidden_out[c, span(t)] = value
+        if first:
+            own_half = dot(win_ref[own, :], feat)
+            own_wave = jnp.tanh(own_half)
+            own_curve_out[:, span(t)] = (0.5 * (1.0 + own_wave)) * (
+                1.0 + own_half * (1.0 - own_wave)
+            )
+
+    even, odd = (even_hidden, even_mixed), (odd_hidden, odd_mixed)
+    step(0, even, odd, second=False, third=False)
+    step(1, odd, even, third=False)
+
+    def two_steps(u, carry):
+        step(2 * u + 2, even, odd)
+        step(2 * u + 3, odd, even)
         return carry
 
-    lax.fori_loop(0, (tiles - 1) // 2, two_tiles, 0)
-    if tiles % 2 == 0:
-        tile(tiles - 1, even, odd)
-        tile(tiles, odd, None)
-    else:
-        tile(tiles, even, None)
-
-    lines = small_ref[...].T
-    extra = [lines[0:7, 0:cols], lines[6:7, cols : 2 * cols]]
-    extra.append(jnp.sum(lines[16:19, 2 * cols :], axis=0, keepdims=True))
+    lax.fori_loop(0, (tiles - 2) // 2, two_steps, 0)
+    buffers = [even, odd]
+    for t in range(2 + (tiles - 2) // 2 * 2, tiles + 2):
+        step(t, buffers[t % 2], buffers[1 - t % 2], first=t < tiles, second=t <= tiles)
+
+
+def forward(owner, params, b_mid, w_out, win, turned, sets):
+    rows = sets * PAIRS
+    cols = WIDTH // 4
+    vmem = pl.BlockSpec(memory_space=pltpu.VMEM)
+    smem = pl.BlockSpec(memory_space=pltpu.SMEM)
+    outs = [
+        ((WIDTH, rows), jnp.bfloat16),
+        ((WIDTH, rows), jnp.float32),
+        ((cols, rows), jnp.float32),
+        ((cols, rows), jnp.bfloat16),
+        ((FEATURE_ROWS, rows), jnp.bfloat16),
+        ((1, rows), jnp.float32),
+    ]
+    return pl.pallas_call(
+        functools.partial(forward_kernel, sets),
+        in_specs=[smem] + [vmem] * 5,
+        out_specs=[vmem] * len(outs),
+        out_shape=[pltpu.VMEM(shape, kind) for shape, kind in outs[:-1]]
+        + [jax.ShapeDtypeStruct(*outs[-1])],
+        scratch_shapes=[
+            pltpu.VMEM((WIDTH, ROW_TILE), jnp.float32),
+            pltpu.VMEM((WIDTH, ROW_TILE), jnp.float32),
+        ]
+        + [pltpu.VMEM((WIDTH, ROW_TILE), jnp.bfloat16)] * 4,
+        compiler_params=pltpu.CompilerParams(vmem_limit_bytes=FORWARD_VMEM),
+        cost_estimate=pl.CostEstimate(
+            flops=2 * rows * WIDTH * (WIDTH + 32), bytes_accessed=4 << 20, transcendentals=0
+        ),
+        name="forward",
+    )(
+        owner.reshape(1), in_hbm(params), in_hbm(b_mid.reshape(1, -1)), w_out.reshape(1, -1), win,
+        turned,
+    )
+
+
+def backward_kernel(
+    inv_sets, owner_ref, sums_ref, near_ref, far_ref, both_ref, hidden_ref, curve_ref, own_curve_ref, mixed_ref, feat_ref,
+    pred_ref, w_mid_hbm, b_out_ref, keep_a, send_a, keep_b, send_b,
+    left_ref, back_ref, slope_ref, delta_ref, delta_in_ref, own_delta_ref, lines_ref, extra_ref,
+    grad_ref, sem,
+):
+    bf16 = jnp.bfloat16
+    sets = sums_ref.shape[0]
+    rows = hidden_ref.shape[1]
+    groups = 2 * keep_a.shape[0]
+    piece_rows = WIDTH // groups
+    cols = WIDTH // 4
+    owner = owner_ref[0]
+    block = 2 * (owner // (2 * groups)) + owner % 2
+    own = pl.ds(pl.multiple_of(block * cols, cols), cols)
+    fetch = pltpu.make_async_copy(w_mid_hbm.at[own, :], back_ref, sem)
+    fetch.start()
+
+    left_ref[...] = jnp.zeros_like(left_ref)
+    sums = (sums_ref[...] + near_ref[...]) + (far_ref[...] + both_ref[...])
+    for p, piece in enumerate(bf16_pieces(sums)):
+        left_ref[p * sets : (p + 1) * sets, :PAIRS] = piece.astype(jnp.float32)
+    left = left_ref[...].astype(bf16)
+    lines_ref[...] = jnp.zeros_like(lines_ref)
+    lines_ref[0:FEATURE_ROWS, :] = feat_ref[...]
+
+    def slopes(t, carry):
+        here = pl.ds(pl.multiple_of(t * ROW_TILE, ROW_TILE), ROW_TILE)
+        hot, group_set = one_hot(t, sets)
+        looked = dot(left, hot)
+        target = looked[:sets] + looked[sets : 2 * sets] + looked[2 * sets :]
+        member = lax.broadcasted_iota(jnp.int32, (sets, ROW_TILE), 0)
+        target = jnp.sum(jnp.where(member == group_set, target, 0.0), axis=0, keepdims=True)
+        slope = (pred_ref[0:1, here] + b_out_ref[0] - target) * inv_sets
+        slope_ref[0:1, here] = slope
+        pieces = [piece.astype(jnp.float32) for piece in bf16_pieces(slope)]
+        pieces = jnp.concatenate(pieces + [jnp.zeros((13, ROW_TILE), jnp.float32)], 0)
+        lines_ref[FEATURE_ROWS:, here] = pieces.astype(bf16)
+        return carry
+
+    lax.fori_loop(0, rows // ROW_TILE, slopes, 0)
+    fetch.wait()
+
+    def tile(t, carry):
+        here = pl.ds(pl.multiple_of(t * ROW_TILE, ROW_TILE), ROW_TILE)
+        slope = slope_ref[0:1, here]
+        for c in CHUNKS:
+            delta_ref[c, :] = (slope * curve_ref[c, here]).astype(bf16)
+        backward = dot(back_ref[...], delta_ref[...])
+        delta_in_ref[:, here] = (backward * own_curve_ref[:, here]).astype(bf16)
+        own_delta_ref[:, here] = delta_ref[own, :]
+        return carry
+
+    lax.fori_loop(0, rows // ROW_TILE, tile, 0)
+
+    for c in CHUNKS:
+        grad_ref[c, :] = dot_rows(hidden_ref[c, :], own_delta_ref[...])
+    lines = lines_ref[...]
+    extra = [dot_rows(delta_in_ref[...], lines).T[0:7]]
+    extra.append(dot_rows(own_delta_ref[...], lines).T[6:7])
+    extra.append(jnp.sum(dot_rows(mixed_ref[...], lines).T[16:19], axis=0, keepdims=True))
     total = jnp.sum(slope_ref[...], axis=1, keepdims=True)
     extra.append(jnp.broadcast_to(total, (1, cols)))
     extra.append(jnp.zeros((6, cols), jnp.float32))
@@ -276,7 +397,8 @@
     for j in range(4):
         lanes = slice((j % 2) * LANES, (j % 2 + 1) * LANES)
         extra_ref[j] = extra[8 * (j // 2) : 8 * (j // 2) + 8, lanes]
-    low, top = place_ref[1], place_ref[2]
+    group = (owner // 2) % groups
+    low, top = group % 2, group // (groups // 2)
     for i in range(groups // 2):
         for a_ref, b_ref, flip in ((keep_a, keep_b, 0), (send_a, send_b, 1)):
             j = 2 * i + (low ^ flip)
@@ -288,50 +410,36 @@
             b_ref[i] = grad_ref[piece, LANES:]
 
 
-def block_gradients(rows, sums, w_in, b_in, w_mid, b_mid, w_out, b_out, inv_sets, place, groups):
-    sets = rows.shape[1]
+def backward(owner, sums, saved, w_mid, b_out, inv_sets, groups):
+    sets = sums[0].shape[0]
+    rows = sets * PAIRS
     cols = WIDTH // 4
-    scale = jnp.array([[4.0], [1.0], [1.0], [20.0]], jnp.float32)
-    feat = jnp.pad(rows * scale, ((0, FEATURE_ROWS - 4), (PAIRS, LANES - PAIRS - sets)))
     vmem = pl.BlockSpec(memory_space=pltpu.VMEM)
     smem = pl.BlockSpec(memory_space=pltpu.SMEM)
+    hbm = pl.BlockSpec(memory_space=pltpu.HBM)
     return pl.pallas_call(
-        functools.partial(network_kernel, inv_sets),
-        in_specs=[smem] + [vmem] * 8 + [smem],
+        functools.partial(backward_kernel, inv_sets),
+        in_specs=[smem] + [vmem] * 10 + [hbm, smem],
         out_specs=[vmem] * 4,
         out_shape=[
             jax.ShapeDtypeStruct((groups // 2, WIDTH // groups + more, LANES), jnp.float32)
             for more in (8, 8, 0, 0)
         ],
         scratch_shapes=[
-            pltpu.VMEM((FEATURE_ROWS + 3 * sets, LANES), jnp.float32),
-            pltpu.VMEM((WIDTH, FEATURE_ROWS), jnp.bfloat16),
-            pltpu.VMEM((WIDTH, WIDTH), jnp.bfloat16),
-            pltpu.VMEM((WIDTH, ROW_TILE), jnp.float32),
-            pltpu.VMEM((WIDTH, ROW_TILE), jnp.float32),
+            pltpu.VMEM((3 * sets, LANES), jnp.float32),
+            pltpu.VMEM((cols, WIDTH), jnp.bfloat16),
+            pltpu.VMEM((1, rows), jnp.float32),
+            pltpu.VMEM((WIDTH, ROW_TILE), jnp.bfloat16),
+            pltpu.VMEM((cols, rows), jnp.bfloat16),
+            pltpu.VMEM((cols, rows), jnp.bfloat16),
+            pltpu.VMEM((2 * FEATURE_ROWS, rows), jnp.bfloat16),
+            pltpu.VMEM((max(groups, 4), 8, LANES), jnp.float32),
             pltpu.VMEM((WIDTH, cols), jnp.float32),
-            pltpu.VMEM((3 * cols, 32), jnp.float32),
-            pltpu.VMEM((1, ROW_TILE), jnp.float32),
-            pltpu.VMEM((WIDTH, ROW_TILE), jnp.bfloat16),
-            pltpu.VMEM((max(groups, 4), 8, LANES), jnp.float32),
-        ]
-        + [
-            pltpu.VMEM(shape, kind)
-            for shape, kind in (
-                ((WIDTH, ROW_TILE), jnp.bfloat16),
-                ((FEATURE_ROWS, ROW_TILE), jnp.bfloat16),
-                ((1, ROW_TILE), jnp.float32),
-                ((WIDTH, ROW_TILE), jnp.bfloat16),
-                ((WIDTH, ROW_TILE), jnp.float32),
-            )
-            for _ in range(2)
+            pltpu.SemaphoreType.DMA,
         ],
-        compiler_params=pltpu.CompilerParams(vmem_limit_bytes=48 * 1024 * 1024),
-        name="network",
-    )(
-        place, jnp.asarray(row_maps(sets)), feat + feature_base(sets), sums, w_in,
-        b_in.reshape(1, -1), w_mid, b_mid.reshape(1, -1), w_out.reshape(1, -1), b_out,
-    )
+        compiler_params=pltpu.CompilerParams(vmem_limit_bytes=BACKWARD_VMEM),
+        name="backward",
+    )(owner.reshape(1), *sums, *saved, in_hbm(w_mid), b_out)
 
 
 def scaling_kernel(layout, groups, owner_ref, *refs):
@@ -441,19 +549,19 @@
     turned = params.T
 
     sums = payoff_sums(turned, increments)
+    win, weights = prepare(w_in, b_in, w_mid)
     sums = sums.reshape(2, groups, 2 * set_dev, PAIRS).swapaxes(0, 1)
     sums = sums.reshape(groups, 4 * set_dev, PAIRS)
     lanes = [[2 * j + c + top * h for j in range(groups)] for h in range(2) for c in range(2)]
-    sums = jnp.sum(lax.all_to_all(sums, "paths", 0, 0, axis_index_groups=lanes, tiled=True), axis=0)
-    sums = sums + swap(sums, 1, devices)
-    sums = (sums + swap(sums, top, devices)) / total_paths
-    prices = pick(sums.reshape(4, set_dev, PAIRS), block)
-
-    rows = pick(turned.reshape(4, 2, groups, 2 * set_dev).transpose(2, 0, 1, 3), group)
-    place = jnp.stack([block, group % 2, group // (groups // 2)])
-    keep_a, send_a, keep_b, send_b = block_gradients(
-        rows.reshape(4, 4 * set_dev), sums, w_in, b_in, w_mid, b_mid, w_out, b_out,
-        1.0 / set_count, place, groups,
+    parts = lax.all_to_all(sums, "paths", 0, 0, axis_index_groups=lanes, tiled=True)
+    parts, win = lax.optimization_barrier((parts, win))
+    sums = jnp.sum(parts, axis=0) / total_paths
+    sums = [sums] + [swap(sums, mask, devices) for mask in (1, top, top + 1)]
+    prices = sum(pick(part.reshape(4, set_dev, PAIRS), block) for part in sums)
+
+    saved = forward(owner, turned, b_mid, w_out, win, weights, 4 * set_dev)
+    keep_a, send_a, keep_b, send_b = backward(
+        owner, sums, saved, w_mid, b_out, 1.0 / set_count, groups
     )
 
     bits = [bit for bit in range(groups.bit_length() - 1)]

time: 111 us -> 104 us (0.937)
  local copies, waits for them, and re-layouts: 8.76 us -> 1.47 us
  waiting for transfers between devices: 47.6 us -> 40.9 us
  Pallas kernels: 29.3 us -> 33.5 us
  starting transfers between devices: 21.5 us -> 24.2 us
    unnamed x16 -> x4, local copies, waits for them, and re-layouts: 6.54 us -> 0.01 us
    pallas_call x1 -> x3, Pallas kernels: 19.6 us -> 23.6 us  [the longest x1 12.3 us: forward(): pl.pallas_call(functools.partial(forward_kernel, sets), in_specs=[smem] +...]
    ppermute x20 -> x21, waiting for transfers between devices: 42.4 us -> 38.6 us  [swap(): return lax.ppermute(array, 'paths', [(i, i ^ bit) for i in range(devices)])]
    all_to_all x1, waiting for transfers between devices: 5.19 us -> 2.31 us  [on_device(): lax.all_to_all(sums, 'paths', 0, 0, axis_index_groups=lanes, tiled=True)]
    ppermute x20 -> x21, starting transfers between devices: 15.3 us -> 18 us  [swap(): return lax.ppermute(array, 'paths', [(i, i ^ bit) for i in range(devices)])]
  transfers between devices with their start and end apart: 21 -> 22, of which waited for: 15 -> 12; matrix products, arithmetic and copies ran while one was open for 3% -> 2% of each run, Pallas kernels for 0% -> 14%
where the time goes in v4:
time: 104 us
  waiting for transfers between devices  40.9 us (39%)
  Pallas kernels  33.5 us (32%)
  starting transfers between devices  24.2 us (23%)
  other arithmetic  2.17 us (2%)
  between operations  1.48 us (1%)
  local copies, waits for them, and re-layouts  1.47 us (1%)
    ppermute x21, waiting for transfers between devices, swap(): return lax.ppermute(array, 'paths', [(i, i ^ bit) for i in range(devices)])  38.6 us
    ppermute x21, starting transfers between devices, swap(): return lax.ppermute(array, 'paths', [(i, i ^ bit) for i in range(devices)])  18 us
    pallas_call x1, Pallas kernels, forward(): pl.pallas_call(functools.partial(forward_kernel, sets), in_specs=[smem] +...  12.3 us
    pallas_call x1, Pallas kernels, backward(): pl.pallas_call(functools.partial(backward_kernel, inv_sets), in_specs=[sm...  8.81 us
    all_to_all x1, starting transfers between devices, on_device(): lax.all_to_all(sums, 'paths', 0, 0, axis_index_groups=lanes, tiled=True)  6.18 us
    pallas_call x1, Pallas kernels, payoff_sums(): pl.pallas_call(pricing_kernel, grid=(count // sets,), in_specs=[pl.BlockS...  5.69 us
    pallas_call x1, Pallas kernels, scaled(): pl.pallas_call(functools.partial(scaling_kernel, layout, groups), in_spec...  4.2 us
    pallas_call x1, Pallas kernels, prepare(): pl.pallas_call(prepare_kernel, in_specs=[hbm] * 3, out_specs=[vmem] * 2,...  2.44 us
  transfers between devices with their start and end apart: 22, of which 12 were waited for; matrix products, arithmetic and copies ran while one was open for 2% of the time, Pallas kernels for 14%

profile of v4, /device:TPU:0, one launch (start us, length us, event | category | flops | bytes accessed | tf_op | source)
XLA Modules:
  0.0 103.7 jit_solution(16392455943458115922)
XLA Ops:
  0.6 5.7 %pricing.1 = f32[256,88]{1,0:T(8,128)S(1)} custom-call(f32[4,256]{1,0:T(4,128)} %bitcast.46, bf16[2,64,128]{2,1,0:T(8,128)(2,1)} %inc_ref.1), custom_call_target="tpu_custom_call" | custom-call | tf_op jit(solution)/shard_map/pricing/pallas_call | solution.py:119
  6.3 0.7 copy.19
  7.0 6.2 %all-to-all-start = ((f32[8,32,88]{2,1,0:T(8,128)}), f32[8,32,88]{2,1,0:T(8,128)S(1)}, u32[]{:S(2)}, u32[]{:S(2)}) async-start(f32[8,32,88]{2,1,0:T(8,128)} %bitcast.3), calls=%async_computation | async-start | bytes 262144 | tf_op jit(solution)/shard_map/all_to_all | solution.py:556
  13.2 0.7 reshape.80.w_out_ref
  14.5 2.4 %prepare.1 = (bf16[1024,16]{1,0:T(8,128)(2,1)S(1)}, bf16[1024,1024]{1,0:T(8,128)(2,1)S(1)}) custom-call(bf16[6,1024]{1,0:T(8,128)(2,1)} %w_in_hbm.1, f32[1,1024]{1,0:T(1,128)} %bitcast.45, bf16[1024,1024]{1,0:T(8,128)(2,1)} %w_mid_hbm.3), custom_call_target="tpu_custom_call" | custom-call | tf_op jit(solution)/shard_map/prepare/pallas_call | solution.py:210
  17.0 2.3 %all-to-all-done = f32[8,32,88]{2,1,0:T(8,128)S(1)} async-done(((f32[8,32,88]{2,1,0:T(8,128)}), f32[8,32,88]{2,1,0:T(8,128)S(1)}, u32[]{:S(2)}, u32[]{:S(2)}) %all-to-all-start) | async-done | bytes 90144 | tf_op jit(solution)/shard_map/all_to_all | solution.py:556
  19.3 0.6 fusion
  19.9 0.6 collective-permute-start.2
  20.5 2.0 %collective-permute-start.1 = (f32[32,88]{1,0:T(8,128)S(1)}, f32[32,88]{1,0:T(8,128)S(1)}, u32[]{:S(2)}, u32[]{:S(2)}) collective-permute-start(f32[32,88]{1,0:T(8,128)S(1)} %get-tuple-element.48.sums_ref), channel_id=1, source_target_pairs={{0,16},{1,17},{2,18},{3,19},{4,20},{5,21},{6,22},{7,23},{8,24},{9,... | collective-permute-start | bytes 33800 | tf_op jit(solution)/shard_map/ppermute | solution.py:519
  22.5 0.2 collective-permute-start
  22.7 12.3 %forward.1 = (bf16[1024,2816]{1,0:T(8,128)(2,1)S(1)}, f32[1024,2816]{1,0:T(8,128)S(1)}, f32[256,2816]{1,0:T(8,128)S(1)}, bf16[256,2816]{1,0:T(8,128)(2,1)S(1)}, ...) custom-call(s32[1]{0:T(128)} %bitcast.10.owner_ref, f32[4,256]{1,0:T(4,128)} %bitcast.47, f32[1,1024]{1,0:T(1,128)} %bitcast.48, ...), custom_call_target="tpu_custom_call" | custom-call | flops 6090129408 | bytes 4194304 | tf_op jit(solution)/shard_map/forward/pallas_call | solution.py:309
  35.0 0.0 collective-permute-done.2.both_ref
  35.0 0.0 collective-permute-done.1.far_ref
  35.0 0.0 copy-start
  35.0 0.0 collective-permute-done.near_ref
  35.0 8.8 %backward.1 = (f32[4,136,128]{2,1,0:T(8,128)S(1)}, f32[4,136,128]{2,1,0:T(8,128)S(1)}, f32[4,128,128]{2,1,0:T(8,128)S(1)}, f32[4,128,128]{2,1,0:T(8,128)S(1)}) custom-call(s32[1]{0:T(128)} %bitcast.10.owner_ref, f32[32,88]{1,0:T(8,128)S(1)} %get-tuple-element.48.sums_ref, f32[32,88]{1,0:T(8,128)S(1)} %collective-permute-done.near_ref, ...), custom_call_target="tpu_custom_call" | custom-call | tf_op jit(solution)/shard_map/backward/pallas_call | solution.py:420
  43.9 0.8 collective-permute-start.6
  44.7 0.6 collective-permute-start.3
  45.3 7.2 %collective-permute-done.6 = f32[4,128,128]{2,1,0:T(8,128)S(1)} collective-permute-done((f32[4,128,128]{2,1,0:T(8,128)S(1)}, f32[4,128,128]{2,1,0:T(8,128)S(1)}, u32[]{:S(2)}, u32[]{:S(2)}) %collective-permute-start.6) | collective-permute-done | bytes 262176 | tf_op jit(solution)/shard_map/ppermute | solution.py:519
  52.6 0.5 collective-permute-start.7
  53.0 0.3 collective-permute-done.3
  53.4 0.7 collective-permute-start.4
  54.1 3.5 %collective-permute-done.7 = f32[2,128,128]{2,1,0:T(8,128)S(1)} collective-permute-done((f32[2,128,128]{2,1,0:T(8,128)S(1)}, f32[2,128,128]{2,1,0:T(8,128)S(1)}, u32[]{:S(2)}, u32[]{:S(2)}) %collective-permute-start.7) | collective-permute-done | bytes 131104 | tf_op jit(solution)/shard_map/ppermute | solution.py:519
  57.6 0.6 collective-permute-start.8
  58.3 0.2 collective-permute-done.4
  58.5 1.7 %collective-permute-start.5 = (f32[1,136,128]{2,1,0:T(8,128)S(1)}, f32[1,136,128]{2,1,0:T(8,128)S(1)}, u32[]{:S(2)}, u32[]{:S(2)}) collective-permute-start(f32[1,136,128]{2,1,0:T(8,128)S(1)} %constant_dynamic-slice_fusion), channel_id=1, source_target_pairs={{0,8},{1,9},{2,10},{3,11},{4,12},{5,13},{6,14},{7,15},{8,0},{9,1},... | collective-permute-start | bytes 208904 | tf_op jit(solution)/shard_map/ppermute | solution.py:519
  60.2 1.7 %collective-permute-done.8 = f32[1,128,128]{2,1,0:T(8,128)S(1)} collective-permute-done((f32[1,128,128]{2,1,0:T(8,128)S(1)}, f32[1,128,128]{2,1,0:T(8,128)S(1)}, u32[]{:S(2)}, u32[]{:S(2)}) %collective-permute-start.8) | collective-permute-done | bytes 65568 | tf_op jit(solution)/shard_map/ppermute | solution.py:519
  62.0 0.9 collective-permute-done.5
  63.0 3.7 %collective-permute-start.11 = (f32[1,264,128]{2,1,0:T(8,128)S(1)}, f32[1,264,128]{2,1,0:T(8,128)S(1)}, u32[]{:S(2)}, u32[]{:S(2)}) collective-permute-start(f32[1,264,128]{2,1,0:T(8,128)S(1)} %pad_maximum_fusion.3), channel_id=1, source_target_pairs={{0,24},{1,25},{2,26},{3,27},{4,28},{5,29},{6,30},{7,31},{8,16},{9,... | collective-permute-start | bytes 405512 | tf_op jit(solution)/shard_map/ppermute | solution.py:519
  66.7 0.0 collective-permute-start.10
  66.7 0.7 collective-permute-start.9
  67.4 3.3 %collective-permute-done.11 = f32[1,264,128]{2,1,0:T(8,128)S(1)} collective-permute-done((f32[1,264,128]{2,1,0:T(8,128)S(1)}, f32[1,264,128]{2,1,0:T(8,128)S(1)}, u32[]{:S(2)}, u32[]{:S(2)}) %collective-permute-start.11) | collective-permute-done | bytes 135200 | tf_op jit(solution)/shard_map/ppermute | solution.py:519
  70.7 4.4 %collective-permute-done.10 = f32[1,264,128]{2,1,0:T(8,128)S(1)} collective-permute-done((f32[1,264,128]{2,1,0:T(8,128)S(1)}, f32[1,264,128]{2,1,0:T(8,128)S(1)}, u32[]{:S(2)}, u32[]{:S(2)}) %collective-permute-start.10) | collective-permute-done | bytes 135200 | tf_op jit(solution)/shard_map/ppermute | solution.py:519
  75.2 1.5 %collective-permute-start.12 = (f32[4,136,128]{2,1,0:T(8,128)S(1)}, f32[4,136,128]{2,1,0:T(8,128)S(1)}, u32[]{:S(2)}, u32[]{:S(2)}) collective-permute-start(f32[4,136,128]{2,1,0:T(8,128)S(1)} %slice.8), channel_id=1, source_target_pairs={{0,2},{1,3},{2,0},{3,1},{4,6},{5,7},{6,4},{7,5},{8,10},{9,11},{10,... | collective-permute-start | bytes 835592 | tf_op jit(solution)/shard_map/ppermute | solution.py:519
  76.7 0.7 collective-permute-start.13
  77.4 5.2 %collective-permute-done.12.refs_1_ = f32[4,136,128]{2,1,0:T(8,128)S(1)} collective-permute-done((f32[4,136,128]{2,1,0:T(8,128)S(1)}, f32[4,136,128]{2,1,0:T(8,128)S(1)}, u32[]{:S(2)}, u32[]{:S(2)}) %collective-permute-start.12) | collective-permute-done | bytes 278560 | tf_op jit(solution)/shard_map/ppermute | solution.py:519
  82.7 0.5 collective-permute-start.14
  83.2 2.3 %collective-permute-start.15 = (f32[8,128,128]{2,1,0:T(8,128)S(1)}, f32[8,128,128]{2,1,0:T(8,128)S(1)}, u32[]{:S(2)}, u32[]{:S(2)}) collective-permute-start(f32[8,128,128]{2,1,0:T(8,128)S(1)} %pad_maximum_fusion.2), channel_id=1, source_target_pairs={{0,2},{1,3},{2,0},{3,1},{4,6},{5,7},{6,4},{7,5},{8,10},{9,11},{10,... | collective-permute-start | bytes 1572872 | tf_op jit(solution)/shard_map/ppermute | solution.py:519
  85.5 9.6 %collective-permute-done.14.refs_3_ = f32[8,136,128]{2,1,0:T(8,128)S(1)} collective-permute-done((f32[8,136,128]{2,1,0:T(8,128)S(1)}, f32[8,136,128]{2,1,0:T(8,128)S(1)}, u32[]{:S(2)}, u32[]{:S(2)}) %collective-permute-start.14) | collective-permute-done | bytes 557088 | tf_op jit(solution)/shard_map/ppermute | solution.py:519
  95.1 0.5 collective-permute-start.16
  95.6 0.0 collective-permute-done.15.refs_4_
  95.6 0.0 collective-permute-start.20
  95.6 0.5 collective-permute-start.17
  96.1 0.0 collective-permute-start.18
  96.1 1.3 %add_bitcast_fusion = f32[8,88]{1,0:T(8,128)} fusion(f32[4,8,88]{2,1,0:T(8,128)S(1)} %bitcast.38, s32[]{:T(128)S(6)} %select_n.65, f32[4,8,88]{2,1,0:T(8,128)} %bitcast.39, f32[4,8,88]{2,1,0:T(8,128)} %bitcast.40, f32[4,8,88]{2,1,0:T(8,128)} %get-tuple-element.47), kind=kLoop, calls=%fused_computation.11 | loop fusion | flops 2112 | bytes 14084 | tf_op jit(solution)/shard_map/add | solution.py:560
  97.4 2.0 %collective-permute-done.18.refs_7_ = f32[4,128,128]{2,1,0:T(8,128)} collective-permute-done((f32[4,128,128]{2,1,0:T(8,128)S(1)}, f32[4,128,128]{2,1,0:T(8,128)}, u32[]{:S(2)}, u32[]{:S(2)}) %collective-permute-start.18) | collective-permute-done | bytes 262176 | tf_op jit(solution)/shard_map/ppermute | solution.py:519
  99.5 0.0 collective-permute-done.19.refs_8_
  99.5 4.2 %scaling.1 = (f32[6,1024]{1,0:T(8,128)}, f32[1,1024]{1,0:T(1,128)}, f32[1024,1024]{1,0:T(8,128)}, f32[1,1024]{1,0:T(1,128)}, f32[1,1024]{1,0:T(1,128)}, /*index=5*/f32[1,1]{1,0:T(1,128)}) custom-call(s32[1]{0:T(128)} %bitcast.10.owner_ref, f32[4,264,128]{2,1,0:T(8,128)S(1)} %pad_maximum_fusion.1.refs_0_, f32[4,136,128]{2,1,0:T(8,128)S(1)} %collective-permute-done.12.refs_1_, ...), custom_call_target="tpu_custom_call" | custom-call | tf_op jit(solution)/shard_map/scaling/pallas_call | solution.py:504
  (26 shorter events, 0.4 us)
Async XLA Ops:
  7.0 12.3 %all-to-all-start = ((f32[8,32,88]{2,1,0:T(8,128)}), f32[8,32,88]{2,1,0:T(8,128)S(1)}, u32[]{:S(2)}, u32[]{:S(2)}) async-start(f32[8,32,88]{2,1,0:T(8,128)} %bitcast.3), calls=%async_computation | async-start | bytes 262144 | tf_op jit(solution)/shard_map/all_to_all | solution.py:556
  19.9 15.1 %collective-permute-start.2 = (f32[32,88]{1,0:T(8,128)S(1)}, f32[32,88]{1,0:T(8,128)S(1)}, u32[]{:S(2)}, u32[]{:S(2)}) collective-permute-start(f32[32,88]{1,0:T(8,128)S(1)} %get-tuple-element.48.sums_ref), channel_id=1, source_target_pairs={{0,17},{1,16},{2,19},{3,18},{4,21},{5,20},{6,23},{7,22},{8,25},{9,... | collective-permute-start | bytes 33800 | tf_op jit(solution)/shard_map/ppermute | solution.py:519
  20.5 14.5 %collective-permute-start.1 = (f32[32,88]{1,0:T(8,128)S(1)}, f32[32,88]{1,0:T(8,128)S(1)}, u32[]{:S(2)}, u32[]{:S(2)}) collective-permute-start(f32[32,88]{1,0:T(8,128)S(1)} %get-tuple-element.48.sums_ref), channel_id=1, source_target_pairs={{0,16},{1,17},{2,18},{3,19},{4,20},{5,21},{6,22},{7,23},{8,24},{9,... | collective-permute-start | bytes 33800 | tf_op jit(solution)/shard_map/ppermute | solution.py:519
  22.5 12.5 %collective-permute-start = (f32[32,88]{1,0:T(8,128)S(1)}, f32[32,88]{1,0:T(8,128)S(1)}, u32[]{:S(2)}, u32[]{:S(2)}) collective-permute-start(f32[32,88]{1,0:T(8,128)S(1)} %get-tuple-element.48.sums_ref), channel_id=1, source_target_pairs={{0,1},{1,0},{2,3},{3,2},{4,5},{5,4},{6,7},{7,6},{8,9},{9,8},{10,11... | collective-permute-start | bytes 33800 | tf_op jit(solution)/shard_map/ppermute | solution.py:519
  35.0 8.9 %copy-start = (f32[32,88]{1,0:T(8,128)}, f32[32,88]{1,0:T(8,128)S(1)}, u32[]{:S(2)}) copy-start(f32[32,88]{1,0:T(8,128)S(1)} %collective-permute-done.1.far_ref) | copy-start | bytes 33796
  35.0 8.8 %copy-start.1 = (f32[32,88]{1,0:T(8,128)}, f32[32,88]{1,0:T(8,128)S(1)}, u32[]{:S(2)}) copy-start(f32[32,88]{1,0:T(8,128)S(1)} %collective-permute-done.near_ref) | copy-start | bytes 33796
  43.9 8.6 %collective-permute-start.6 = (f32[4,128,128]{2,1,0:T(8,128)S(1)}, f32[4,128,128]{2,1,0:T(8,128)S(1)}, u32[]{:S(2)}, u32[]{:S(2)}) collective-permute-start(f32[4,128,128]{2,1,0:T(8,128)S(1)} %get-tuple-element.40), channel_id=1, source_target_pairs={{0,8},{1,9},{2,10},{3,11},{4,12},{5,13},{6,14},{7,15},{8,0},{9,1},... | collective-permute-start | bytes 786440 | tf_op jit(solution)/shard_map/ppermute | solution.py:519
  44.7 8.6 %collective-permute-start.3 = (f32[4,136,128]{2,1,0:T(8,128)S(1)}, f32[4,136,128]{2,1,0:T(8,128)S(1)}, u32[]{:S(2)}, u32[]{:S(2)}) collective-permute-start(f32[4,136,128]{2,1,0:T(8,128)S(1)} %get-tuple-element.38), channel_id=1, source_target_pairs={{0,2},{1,3},{2,0},{3,1},{4,6},{5,7},{6,4},{7,5},{8,10},{9,11},{10,... | collective-permute-start | bytes 835592 | tf_op jit(solution)/shard_map/ppermute | solution.py:519
  52.6 5.0 %collective-permute-start.7 = (f32[2,128,128]{2,1,0:T(8,128)S(1)}, f32[2,128,128]{2,1,0:T(8,128)S(1)}, u32[]{:S(2)}, u32[]{:S(2)}) collective-permute-start(f32[2,128,128]{2,1,0:T(8,128)S(1)} %dynamic-slice_bitcast_fusion.1), channel_id=1, source_target_pairs={{0,2},{1,3},{2,0},{3,1},{4,6},{5,7},{6,4},{7,5},{8,10},{9,11},{10,... | collective-permute-start | bytes 393224 | tf_op jit(solution)/shard_map/ppermute | solution.py:519
  53.4 5.1 %collective-permute-start.4 = (f32[2,136,128]{2,1,0:T(8,128)S(1)}, f32[2,136,128]{2,1,0:T(8,128)S(1)}, u32[]{:S(2)}, u32[]{:S(2)}) collective-permute-start(f32[2,136,128]{2,1,0:T(8,128)S(1)} %dynamic-slice_bitcast_fusion), channel_id=1, source_target_pairs={{0,4},{1,5},{2,6},{3,7},{4,0},{5,1},{6,2},{7,3},{8,12},{9,13},{10,... | collective-permute-start | bytes 417800 | tf_op jit(solution)/shard_map/ppermute | solution.py:519
  57.6 4.3 %collective-permute-start.8 = (f32[1,128,128]{2,1,0:T(8,128)S(1)}, f32[1,128,128]{2,1,0:T(8,128)S(1)}, u32[]{:S(2)}, u32[]{:S(2)}) collective-permute-start(f32[1,128,128]{2,1,0:T(8,128)S(1)} %constant_dynamic-slice_fusion.1), channel_id=1, source_target_pairs={{0,4},{1,5},{2,6},{3,7},{4,0},{5,1},{6,2},{7,3},{8,12},{9,13},{10,... | collective-permute-start | bytes 196616 | tf_op jit(solution)/shard_map/ppermute | solution.py:519
  58.5 4.4 %collective-permute-start.5 = (f32[1,136,128]{2,1,0:T(8,128)S(1)}, f32[1,136,128]{2,1,0:T(8,128)S(1)}, u32[]{:S(2)}, u32[]{:S(2)}) collective-permute-start(f32[1,136,128]{2,1,0:T(8,128)S(1)} %constant_dynamic-slice_fusion), channel_id=1, source_target_pairs={{0,8},{1,9},{2,10},{3,11},{4,12},{5,13},{6,14},{7,15},{8,0},{9,1},... | collective-permute-start | bytes 208904 | tf_op jit(solution)/shard_map/ppermute | solution.py:519
  63.0 7.8 %collective-permute-start.11 = (f32[1,264,128]{2,1,0:T(8,128)S(1)}, f32[1,264,128]{2,1,0:T(8,128)S(1)}, u32[]{:S(2)}, u32[]{:S(2)}) collective-permute-start(f32[1,264,128]{2,1,0:T(8,128)S(1)} %pad_maximum_fusion.3), channel_id=1, source_target_pairs={{0,24},{1,25},{2,26},{3,27},{4,28},{5,29},{6,30},{7,31},{8,16},{9,... | collective-permute-start | bytes 405512 | tf_op jit(solution)/shard_map/ppermute | solution.py:519
  66.7 8.5 %collective-permute-start.10 = (f32[1,264,128]{2,1,0:T(8,128)S(1)}, f32[1,264,128]{2,1,0:T(8,128)S(1)}, u32[]{:S(2)}, u32[]{:S(2)}) collective-permute-start(f32[1,264,128]{2,1,0:T(8,128)S(1)} %pad_maximum_fusion.3), channel_id=1, source_target_pairs={{0,16},{1,17},{2,18},{3,19},{4,20},{5,21},{6,22},{7,23},{8,24},{9,... | collective-permute-start | bytes 405512 | tf_op jit(solution)/shard_map/ppermute | solution.py:519
  66.7 8.5 %collective-permute-start.9 = (f32[1,264,128]{2,1,0:T(8,128)S(1)}, f32[1,264,128]{2,1,0:T(8,128)S(1)}, u32[]{:S(2)}, u32[]{:S(2)}) collective-permute-start(f32[1,264,128]{2,1,0:T(8,128)S(1)} %pad_maximum_fusion.3), channel_id=1, source_target_pairs={{0,8},{1,9},{2,10},{3,11},{4,12},{5,13},{6,14},{7,15},{8,0},{9,1},... | collective-permute-start | bytes 405512 | tf_op jit(solution)/shard_map/ppermute | solution.py:519
  75.2 7.4 %collective-permute-start.12 = (f32[4,136,128]{2,1,0:T(8,128)S(1)}, f32[4,136,128]{2,1,0:T(8,128)S(1)}, u32[]{:S(2)}, u32[]{:S(2)}) collective-permute-start(f32[4,136,128]{2,1,0:T(8,128)S(1)} %slice.8), channel_id=1, source_target_pairs={{0,2},{1,3},{2,0},{3,1},{4,6},{5,7},{6,4},{7,5},{8,10},{9,11},{10,... | collective-permute-start | bytes 835592 | tf_op jit(solution)/shard_map/ppermute | solution.py:519
  76.7 6.5 %collective-permute-start.13 = (f32[4,128,128]{2,1,0:T(8,128)S(1)}, f32[4,128,128]{2,1,0:T(8,128)S(1)}, u32[]{:S(2)}, u32[]{:S(2)}) collective-permute-start(f32[4,128,128]{2,1,0:T(8,128)S(1)} %slice.9), channel_id=1, source_target_pairs={{0,4},{1,5},{2,6},{3,7},{4,0},{5,1},{6,2},{7,3},{8,12},{9,13},{10,... | collective-permute-start | bytes 786440 | tf_op jit(solution)/shard_map/ppermute | solution.py:519
  82.7 12.4 %collective-permute-start.14 = (f32[8,136,128]{2,1,0:T(8,128)S(1)}, f32[8,136,128]{2,1,0:T(8,128)S(1)}, u32[]{:S(2)}, u32[]{:S(2)}) collective-permute-start(f32[8,136,128]{2,1,0:T(8,128)S(1)} %pad_maximum_fusion), channel_id=1, source_target_pairs={{0,4},{1,5},{2,6},{3,7},{4,0},{5,1},{6,2},{7,3},{8,12},{9,13},{10,... | collective-permute-start | bytes 1671176 | tf_op jit(solution)/shard_map/ppermute | solution.py:519
  83.2 12.4 %collective-permute-start.15 = (f32[8,128,128]{2,1,0:T(8,128)S(1)}, f32[8,128,128]{2,1,0:T(8,128)S(1)}, u32[]{:S(2)}, u32[]{:S(2)}) collective-permute-start(f32[8,128,128]{2,1,0:T(8,128)S(1)} %pad_maximum_fusion.2), channel_id=1, source_target_pairs={{0,2},{1,3},{2,0},{3,1},{4,6},{5,7},{6,4},{7,5},{8,10},{9,11},{10,... | collective-permute-start | bytes 1572872 | tf_op jit(solution)/shard_map/ppermute | solution.py:519
  95.1 4.4 %collective-permute-start.19 = (f32[8,136,128]{2,1,0:T(8,128)S(1)}, f32[8,136,128]{2,1,0:T(8,128)S(1)}, u32[]{:S(2)}, u32[]{:S(2)}) collective-permute-start(f32[8,136,128]{2,1,0:T(8,128)S(1)} %collective-permute-done.14.refs_3_), channel_id=1, source_target_pairs={{0,1},{1,0},{2,3},{3,2},{4,5},{5,4},{6,7},{7,6},{8,9},{9,8},{10,11... | collective-permute-start | bytes 1671176 | tf_op jit(solution)/shard_map/ppermute | solution.py:519
  95.1 4.3 %collective-permute-start.16 = (f32[4,264,128]{2,1,0:T(8,128)S(1)}, f32[4,264,128]{2,1,0:T(8,128)S(1)}, u32[]{:S(2)}, u32[]{:S(2)}) collective-permute-start(f32[4,264,128]{2,1,0:T(8,128)S(1)} %pad_maximum_fusion.1.refs_0_), channel_id=1, source_target_pairs={{0,1},{1,0},{2,3},{3,2},{4,5},{5,4},{6,7},{7,6},{8,9},{9,8},{10,11... | collective-permute-start | bytes 1622024 | tf_op jit(solution)/shard_map/ppermute | solution.py:519
  95.6 3.8 %collective-permute-start.20 = (f32[8,128,128]{2,1,0:T(8,128)S(1)}, f32[8,128,128]{2,1,0:T(8,128)}, u32[]{:S(2)}, u32[]{:S(2)}) collective-permute-start(f32[8,128,128]{2,1,0:T(8,128)S(1)} %collective-permute-done.15.refs_4_), channel_id=1, source_target_pairs={{0,1},{1,0},{2,3},{3,2},{4,5},{5,4},{6,7},{7,6},{8,9},{9,8},{10,11... | collective-permute-start | bytes 1572872 | tf_op jit(solution)/shard_map/ppermute | solution.py:519
  95.6 3.8 %collective-permute-start.17 = (f32[4,136,128]{2,1,0:T(8,128)S(1)}, f32[4,136,128]{2,1,0:T(8,128)S(1)}, u32[]{:S(2)}, u32[]{:S(2)}) collective-permute-start(f32[4,136,128]{2,1,0:T(8,128)S(1)} %collective-permute-done.12.refs_1_), channel_id=1, source_target_pairs={{0,1},{1,0},{2,3},{3,2},{4,5},{5,4},{6,7},{7,6},{8,9},{9,8},{10,11... | collective-permute-start | bytes 835592 | tf_op jit(solution)/shard_map/ppermute | solution.py:519
  96.1 3.3 %collective-permute-start.18 = (f32[4,128,128]{2,1,0:T(8,128)S(1)}, f32[4,128,128]{2,1,0:T(8,128)}, u32[]{:S(2)}, u32[]{:S(2)}) collective-permute-start(f32[4,128,128]{2,1,0:T(8,128)S(1)} %collective-permute-done.13.refs_2_), channel_id=1, source_target_pairs={{0,1},{1,0},{2,3},{3,2},{4,5},{5,4},{6,7},{7,6},{8,9},{9,8},{10,11... | collective-permute-start | bytes 786440 | tf_op jit(solution)/shard_map/ppermute | solution.py:519

commit v5 on v4

--- a/solution.py
+++ b/solution.py
@@ -109,22 +109,35 @@
         return total
 
     lax.fori_loop(0, MATS, maturity, jnp.zeros((paths, sets), jnp.float32))
-    out_ref[...] = pay_ref[...].T[:, :PAIRS]
-
-
-def payoff_sums(params, increments):
+    paid = pay_ref[...].T[:, :PAIRS]
+    blocks, halves, half = out_ref.shape[:3]
+    for h in range(halves):
+        rows = paid[h * blocks * half : (h + 1) * blocks * half]
+        out_ref[:, h] = rows.reshape(blocks, half, PAIRS)
+
+
+def payoff_sums(params, increments, groups):
     count = params.shape[1]
     paths = increments.shape[2]
     sets = math.gcd(count, SET_BLOCK)
+    steps = count // sets
+    half = count // groups // 2
+    halves = 2 if steps == 1 else 1
+    blocks = sets // half // halves
     return pl.pallas_call(
         pricing_kernel,
-        grid=(count // sets,),
+        grid=(steps,),
         in_specs=[
             pl.BlockSpec((4, sets), lambda b: (0, b)),
             pl.BlockSpec((2, STEPS, paths), lambda b: (0, 0, 0)),
         ],
-        out_specs=pl.BlockSpec((sets, PAIRS), lambda b: (b, 0)),
-        out_shape=jax.ShapeDtypeStruct((count, PAIRS), jnp.float32),
+        out_specs=pl.BlockSpec(
+            (blocks, halves, half, PAIRS),
+            (lambda b: (0, 0, 0, 0))
+            if steps == 1
+            else (lambda b: (b % (steps // 2), b // (steps // 2), 0, 0)),
+        ),
+        out_shape=jax.ShapeDtypeStruct((groups, 2, half, PAIRS), jnp.float32),
         scratch_shapes=[
             pltpu.VMEM((paths, LANES), jnp.float32),
             pltpu.VMEM((MATS, paths, LANES), jnp.bfloat16),
@@ -184,7 +197,8 @@
 
 
 def prepare_kernel(
-    w_in_hbm, b_in_hbm, w_mid_hbm, win_ref, turned_ref, w_in_ref, b_in_ref, w_mid_ref, sems
+    sets, owner_ref, params_ref, w_in_hbm, b_in_hbm, w_mid_hbm, win_ref, turned_ref, feat_ref,
+    w_in_ref, b_in_ref, w_mid_ref, sems,
 ):
     copies = [
         pltpu.make_async_copy(source, target, sems.at[i])
@@ -194,6 +208,13 @@
     ]
     for copy in copies:
         copy.start()
+    devices = params_ref.shape[1] * 4 // sets
+    group = (owner_ref[0] // 2) % (devices // 4)
+    table = feature_table(params_ref, group, sets).astype(jnp.bfloat16)
+    for t in range(feat_ref.shape[1] // ROW_TILE):
+        hot, _ = one_hot(t, sets)
+        feat = dot(table, hot).astype(jnp.bfloat16)
+        feat_ref[:, t * ROW_TILE : (t + 1) * ROW_TILE] = feat
     for copy in copies:
         copy.wait()
     weights_in = w_in_ref[...].astype(jnp.float32)
@@ -204,16 +225,18 @@
     turned_ref[...] = (0.5 * w_mid_ref[...].astype(jnp.float32)).T.astype(jnp.bfloat16)
 
 
-def prepare(w_in, b_in, w_mid):
+def prepare(owner, params, w_in, b_in, w_mid, sets):
+    smem = pl.BlockSpec(memory_space=pltpu.SMEM)
     vmem = pl.BlockSpec(memory_space=pltpu.VMEM)
     hbm = pl.BlockSpec(memory_space=pltpu.HBM)
     return pl.pallas_call(
-        prepare_kernel,
-        in_specs=[hbm] * 3,
-        out_specs=[vmem] * 2,
+        functools.partial(prepare_kernel, sets),
+        in_specs=[smem, vmem] + [hbm] * 3,
+        out_specs=[vmem] * 3,
         out_shape=[
             jax.ShapeDtypeStruct((WIDTH, FEATURE_ROWS), jnp.bfloat16),
             jax.ShapeDtypeStruct((WIDTH, WIDTH), jnp.bfloat16),
+            jax.ShapeDtypeStruct((FEATURE_ROWS, sets * PAIRS), jnp.bfloat16),
         ],
         scratch_shapes=[
             pltpu.VMEM(w_in.shape, jnp.bfloat16),
@@ -223,23 +246,22 @@
         ],
         compiler_params=pltpu.CompilerParams(vmem_limit_bytes=16 * 1024 * 1024),
         name="prepare",
-    )(in_hbm(w_in), in_hbm(b_in.reshape(1, -1)), in_hbm(w_mid))
+    )(
+        owner.reshape(1), in_hbm(params), in_hbm(w_in), in_hbm(b_in.reshape(1, -1)), in_hbm(w_mid)
+    )
 
 
 def forward_kernel(
-    sets, owner_ref, params_ref, b_mid_ref, w_out_ref, win_ref, turned_ref,
-    hidden_out, curve_out, own_curve_out, mixed_out, feat_out, pred_out, bias_ref, read_ref,
+    owner_ref, b_mid_ref, w_out_ref, win_ref, turned_ref, feat_ref,
+    hidden_out, curve_out, mixed_out, pred_out, bias_ref, read_ref,
     even_hidden, odd_hidden, even_mixed, odd_mixed,
 ):
     bf16 = jnp.bfloat16
     tiles = hidden_out.shape[1] // ROW_TILE
     cols = WIDTH // 4
     owner = owner_ref[0]
-    devices = params_ref.shape[1] * 4 // sets
-    block = 2 * (owner // (devices // 2)) + owner % 2
-    group = (owner // 2) % (devices // 4)
+    block = 2 * (owner // owner_ref[1]) + owner % 2
     own = pl.ds(pl.multiple_of(block * cols, cols), cols)
-    table = feature_table(params_ref, group, sets).astype(bf16)
     read_ref[...] = jnp.broadcast_to((0.5 * w_out_ref[...].astype(jnp.float32)).T, read_ref.shape)
     readout = jnp.broadcast_to(w_out_ref[...].astype(jnp.float32), (16, WIDTH)).astype(bf16)
     bias_ref[...] = jnp.broadcast_to((0.5 * b_mid_ref[...]).T, bias_ref.shape)
@@ -250,19 +272,25 @@
     def step(t, new, old, first=True, second=True, third=True):
         new_hidden, new_mixed = new
         old_hidden, old_mixed = old
+        if first:
+            feat = feat_ref[:, span(t)]
+
+        def products(c):
+            return (
+                dot(turned_ref[c, :], old_hidden[...]) if second else None,
+                dot(win_ref[c, :], feat) if first else None,
+            )
+
+        ahead = products(CHUNKS[0])
         if third:
-            pred_out[0:1, span(t - 2)] = dot(readout, new_mixed[...])[0:1]
+            predicted = dot(readout, new_mixed[...])
             mixed_out[:, span(t - 2)] = new_mixed[own, :]
-        if first:
-            hot, _ = one_hot(t, sets)
-            feat = dot(table, hot).astype(bf16)
-            feat_out[:, span(t)] = feat
-        for c in CHUNKS:
+        for n, c in enumerate(CHUNKS):
+            half_mid, half_in = ahead
+            if n + 1 < len(CHUNKS):
+                ahead = products(CHUNKS[n + 1])
             if second:
-                half_mid = dot(turned_ref[c, :], old_hidden[...]) + bias_ref[c, :]
-            if first:
-                half_in = dot(win_ref[c, :], feat)
-            if second:
+                half_mid = half_mid + bias_ref[c, :]
                 wave = jnp.tanh(half_mid)
                 turn = half_mid * wave
                 old_mixed[c, :] = (half_mid + turn).astype(bf16)
@@ -271,12 +299,8 @@
                 value = (half_in + half_in * jnp.tanh(half_in)).astype(bf16)
                 new_hidden[c, :] = value
                 hidden_out[c, span(t)] = value
-        if first:
-            own_half = dot(win_ref[own, :], feat)
-            own_wave = jnp.tanh(own_half)
-            own_curve_out[:, span(t)] = (0.5 * (1.0 + own_wave)) * (
-                1.0 + own_half * (1.0 - own_wave)
-            )
+        if third:
+            pred_out[0:1, span(t - 2)] = predicted[0:1]
 
     even, odd = (even_hidden, even_mixed), (odd_hidden, odd_mixed)
     step(0, even, odd, second=False, third=False)
@@ -293,21 +317,19 @@
         step(t, buffers[t % 2], buffers[1 - t % 2], first=t < tiles, second=t <= tiles)
 
 
-def forward(owner, params, b_mid, w_out, win, turned, sets):
-    rows = sets * PAIRS
+def forward(place, b_mid, w_out, win, turned, feat):
+    rows = feat.shape[1]
     cols = WIDTH // 4
     vmem = pl.BlockSpec(memory_space=pltpu.VMEM)
     smem = pl.BlockSpec(memory_space=pltpu.SMEM)
     outs = [
         ((WIDTH, rows), jnp.bfloat16),
         ((WIDTH, rows), jnp.float32),
-        ((cols, rows), jnp.float32),
         ((cols, rows), jnp.bfloat16),
-        ((FEATURE_ROWS, rows), jnp.bfloat16),
         ((1, rows), jnp.float32),
     ]
     return pl.pallas_call(
-        functools.partial(forward_kernel, sets),
+        forward_kernel,
         in_specs=[smem] + [vmem] * 5,
         out_specs=[vmem] * len(outs),
         out_shape=[pltpu.VMEM(shape, kind) for shape, kind in outs[:-1]]
@@ -322,17 +344,14 @@
             flops=2 * rows * WIDTH * (WIDTH + 32), bytes_accessed=4 << 20, transcendentals=0
         ),
         name="forward",
-    )(
-        owner.reshape(1), in_hbm(params), in_hbm(b_mid.reshape(1, -1)), w_out.reshape(1, -1), win,
-        turned,
-    )
+    )(place, in_hbm(b_mid.reshape(1, -1)), w_out.reshape(1, -1), win, turned, feat)
 
 
 def backward_kernel(
-    inv_sets, owner_ref, sums_ref, near_ref, far_ref, both_ref, hidden_ref, curve_ref, own_curve_ref, mixed_ref, feat_ref,
-    pred_ref, w_mid_hbm, b_out_ref, keep_a, send_a, keep_b, send_b,
-    left_ref, back_ref, slope_ref, delta_ref, delta_in_ref, own_delta_ref, lines_ref, extra_ref,
-    grad_ref, sem,
+    inv_sets, owner_ref, sums_ref, near_ref, far_ref, both_ref, hidden_ref, curve_ref, mixed_ref, pred_ref, win_ref,
+    feat_ref, w_mid_hbm, b_out_ref, keep_a, send_a, keep_b, send_b,
+    left_ref, back_ref, slope_ref, even_delta, odd_delta, delta_in_ref, own_delta_ref, bias_ref,
+    read_ref, extra_ref, grad_ref, sem,
 ):
     bf16 = jnp.bfloat16
     sets = sums_ref.shape[0]
@@ -351,44 +370,39 @@
     for p, piece in enumerate(bf16_pieces(sums)):
         left_ref[p * sets : (p + 1) * sets, :PAIRS] = piece.astype(jnp.float32)
     left = left_ref[...].astype(bf16)
-    lines_ref[...] = jnp.zeros_like(lines_ref)
-    lines_ref[0:FEATURE_ROWS, :] = feat_ref[...]
-
-    def slopes(t, carry):
-        here = pl.ds(pl.multiple_of(t * ROW_TILE, ROW_TILE), ROW_TILE)
+    tiles = [slice(first, first + ROW_TILE) for first in range(0, rows, ROW_TILE)]
+    for t, here in enumerate(tiles):
         hot, group_set = one_hot(t, sets)
         looked = dot(left, hot)
         target = looked[:sets] + looked[sets : 2 * sets] + looked[2 * sets :]
         member = lax.broadcasted_iota(jnp.int32, (sets, ROW_TILE), 0)
         target = jnp.sum(jnp.where(member == group_set, target, 0.0), axis=0, keepdims=True)
-        slope = (pred_ref[0:1, here] + b_out_ref[0] - target) * inv_sets
-        slope_ref[0:1, here] = slope
-        pieces = [piece.astype(jnp.float32) for piece in bf16_pieces(slope)]
-        pieces = jnp.concatenate(pieces + [jnp.zeros((13, ROW_TILE), jnp.float32)], 0)
-        lines_ref[FEATURE_ROWS:, here] = pieces.astype(bf16)
-        return carry
-
-    lax.fori_loop(0, rows // ROW_TILE, slopes, 0)
+        slope_ref[0:1, here] = (pred_ref[0:1, here] + b_out_ref[0] - target) * inv_sets
     fetch.wait()
-
-    def tile(t, carry):
-        here = pl.ds(pl.multiple_of(t * ROW_TILE, ROW_TILE), ROW_TILE)
+    for t, here in enumerate(tiles):
+        delta_ref = (even_delta, odd_delta)[t % 2]
         slope = slope_ref[0:1, here]
         for c in CHUNKS:
             delta_ref[c, :] = (slope * curve_ref[c, here]).astype(bf16)
         backward = dot(back_ref[...], delta_ref[...])
-        delta_in_ref[:, here] = (backward * own_curve_ref[:, here]).astype(bf16)
-        own_delta_ref[:, here] = delta_ref[own, :]
-        return carry
-
-    lax.fori_loop(0, rows // ROW_TILE, tile, 0)
+        own_delta = (slope * curve_ref[own, here]).astype(bf16)
+        own_delta_ref[:, here] = own_delta
+        bias = own_delta.astype(jnp.float32)
+        read = mixed_ref[:, here].astype(jnp.float32) * slope
+        bias = bias[:, :LANES] + bias[:, LANES:]
+        read = read[:, :LANES] + read[:, LANES:]
+        bias_ref[...] = bias if t == 0 else bias_ref[...] + bias
+        read_ref[...] = read if t == 0 else read_ref[...] + read
+        half = dot(win_ref[own, :], feat_ref[:, here])
+        wave = jnp.tanh(half)
+        curve = (0.5 * (1.0 + wave)) * (1.0 + half * (1.0 - wave))
+        delta_in_ref[:, here] = (backward * curve).astype(bf16)
 
     for c in CHUNKS:
         grad_ref[c, :] = dot_rows(hidden_ref[c, :], own_delta_ref[...])
-    lines = lines_ref[...]
-    extra = [dot_rows(delta_in_ref[...], lines).T[0:7]]
-    extra.append(dot_rows(own_delta_ref[...], lines).T[6:7])
-    extra.append(jnp.sum(dot_rows(mixed_ref[...], lines).T[16:19], axis=0, keepdims=True))
+    extra = [dot_rows(delta_in_ref[...], feat_ref[...]).T[0:7]]
+    extra.append(jnp.sum(bias_ref[...].T, axis=0, keepdims=True))
+    extra.append(jnp.sum(read_ref[...].T, axis=0, keepdims=True))
     total = jnp.sum(slope_ref[...], axis=1, keepdims=True)
     extra.append(jnp.broadcast_to(total, (1, cols)))
     extra.append(jnp.zeros((6, cols), jnp.float32))
@@ -410,7 +424,7 @@
             b_ref[i] = grad_ref[piece, LANES:]
 
 
-def backward(owner, sums, saved, w_mid, b_out, inv_sets, groups):
+def backward(owner, sums, saved, win, feat, w_mid, b_out, inv_sets, groups):
     sets = sums[0].shape[0]
     rows = sets * PAIRS
     cols = WIDTH // 4
@@ -430,16 +444,18 @@
             pltpu.VMEM((cols, WIDTH), jnp.bfloat16),
             pltpu.VMEM((1, rows), jnp.float32),
             pltpu.VMEM((WIDTH, ROW_TILE), jnp.bfloat16),
+            pltpu.VMEM((WIDTH, ROW_TILE), jnp.bfloat16),
             pltpu.VMEM((cols, rows), jnp.bfloat16),
             pltpu.VMEM((cols, rows), jnp.bfloat16),
-            pltpu.VMEM((2 * FEATURE_ROWS, rows), jnp.bfloat16),
+            pltpu.VMEM((cols, LANES), jnp.float32),
+            pltpu.VMEM((cols, LANES), jnp.float32),
             pltpu.VMEM((max(groups, 4), 8, LANES), jnp.float32),
             pltpu.VMEM((WIDTH, cols), jnp.float32),
             pltpu.SemaphoreType.DMA,
         ],
         compiler_params=pltpu.CompilerParams(vmem_limit_bytes=BACKWARD_VMEM),
         name="backward",
-    )(owner.reshape(1), *sums, *saved, in_hbm(w_mid), b_out)
+    )(owner.reshape(1), *sums, *saved, win, feat, in_hbm(w_mid), b_out)
 
 
 def scaling_kernel(layout, groups, owner_ref, *refs):
@@ -548,10 +564,8 @@
     block = 2 * high + core
     turned = params.T
 
-    sums = payoff_sums(turned, increments)
-    win, weights = prepare(w_in, b_in, w_mid)
-    sums = sums.reshape(2, groups, 2 * set_dev, PAIRS).swapaxes(0, 1)
-    sums = sums.reshape(groups, 4 * set_dev, PAIRS)
+    sums = payoff_sums(turned, increments, groups).reshape(groups, 4 * set_dev, PAIRS)
+    win, weights, feat = prepare(owner, turned, w_in, b_in, w_mid, 4 * set_dev)
     lanes = [[2 * j + c + top * h for j in range(groups)] for h in range(2) for c in range(2)]
     parts = lax.all_to_all(sums, "paths", 0, 0, axis_index_groups=lanes, tiled=True)
     parts, win = lax.optimization_barrier((parts, win))
@@ -559,9 +573,10 @@
     sums = [sums] + [swap(sums, mask, devices) for mask in (1, top, top + 1)]
     prices = sum(pick(part.reshape(4, set_dev, PAIRS), block) for part in sums)
 
-    saved = forward(owner, turned, b_mid, w_out, win, weights, 4 * set_dev)
+    place = jnp.stack([owner, jnp.int32(top)])
+    saved = forward(place, b_mid, w_out, win, weights, feat)
     keep_a, send_a, keep_b, send_b = backward(
-        owner, sums, saved, w_mid, b_out, 1.0 / set_count, groups
+        owner, sums, saved, win, feat, w_mid, b_out, 1.0 / set_count, groups
     )
 
     bits = [bit for bit in range(groups.bit_length() - 1)]

time: 104 us -> 101 us (0.971)
  waiting for transfers between devices: 40.9 us -> 38.9 us
  Pallas kernels: 33.5 us -> 31.8 us
  starting transfers between devices: 24.2 us -> 25.6 us
    pallas_call x1, Pallas kernels: 8.81 us -> 5.77 us  [backward(): pl.pallas_call(functools.partial(backward_kernel, inv_sets), in_specs=[sm...]
    ppermute x21, starting transfers between devices: 18 us -> 19.4 us  [swap(): return lax.ppermute(array, 'paths', [(i, i ^ bit) for i in range(devices)])]
    pallas_call x3, Pallas kernels: 20.4 us -> 21.8 us  [the longest x1 12.3 us: forward(): pl.pallas_call(forward_kernel, in_specs=[smem] + [vmem] * 5, out_specs=[v...]
    ppermute x21, waiting for transfers between devices: 38.6 us -> 37.4 us  [swap(): return lax.ppermute(array, 'paths', [(i, i ^ bit) for i in range(devices)])]
  transfers between devices with their start and end apart: 22 -> 22, of which waited for: 12 -> 12; matrix products, arithmetic and copies ran while one was open for 2% -> 2% of each run, Pallas kernels for 14% -> 15%
where the time goes in v5:
time: 101 us
  waiting for transfers between devices  38.9 us (39%)
  Pallas kernels  31.8 us (31%)
  starting transfers between devices  25.6 us (25%)
  other arithmetic  2.26 us (2%)
  between operations  1.47 us (1%)
    ppermute x21, waiting for transfers between devices, swap(): return lax.ppermute(array, 'paths', [(i, i ^ bit) for i in range(devices)])  37.4 us
    ppermute x21, starting transfers between devices, swap(): return lax.ppermute(array, 'paths', [(i, i ^ bit) for i in range(devices)])  19.4 us
    pallas_call x1, Pallas kernels, forward(): pl.pallas_call(forward_kernel, in_specs=[smem] + [vmem] * 5, out_specs=[v...  12.3 us
    pallas_call x1, Pallas kernels, payoff_sums(): pl.pallas_call(pricing_kernel, grid=(steps,), in_specs=[pl.BlockSpec((4,...  6.36 us
    all_to_all x1, starting transfers between devices, on_device(): lax.all_to_all(sums, 'paths', 0, 0, axis_index_groups=lanes, tiled=True)  6.18 us
    pallas_call x1, Pallas kernels, backward(): pl.pallas_call(functools.partial(backward_kernel, inv_sets), in_specs=[sm...  5.77 us
    pallas_call x1, Pallas kernels, scaled(): pl.pallas_call(functools.partial(scaling_kernel, layout, groups), in_spec...  4.2 us
    pallas_call x1, Pallas kernels, prepare(): pl.pallas_call(functools.partial(prepare_kernel, sets), in_specs=[smem, v...  3.15 us
  transfers between devices with their start and end apart: 22, of which 12 were waited for; matrix products, arithmetic and copies ran while one was open for 2% of the time, Pallas kernels for 15%

profile of v5, /device:TPU:0, one launch (start us, length us, event | category | flops | bytes accessed | tf_op | source)
XLA Modules:
  0.0 100.9 jit_solution(5157588935692114973)
XLA Ops:
  0.6 6.4 %pricing.1 = f32[8,2,16,88]{3,2,1,0:T(8,128)} custom-call(f32[4,256]{1,0:T(4,128)} %bitcast.41, bf16[2,64,128]{2,1,0:T(8,128)(2,1)} %inc_ref.1), custom_call_target="tpu_custom_call" | custom-call | tf_op jit(solution)/shard_map/pricing/pallas_call | solution.py:127
  7.0 6.2 %all-to-all-start = ((f32[8,32,88]{2,1,0:T(8,128)}), f32[8,32,88]{2,1,0:T(8,128)S(1)}, u32[]{:S(2)}, u32[]{:S(2)}) async-start(f32[8,32,88]{2,1,0:T(8,128)} %bitcast.1), calls=%async_computation | async-start | bytes 262144 | tf_op jit(solution)/shard_map/all_to_all | solution.py:570
  13.2 0.7 reshape.76.w_out_ref
  14.5 3.1 %prepare.1 = (bf16[1024,16]{1,0:T(8,128)(2,1)S(1)}, bf16[1024,1024]{1,0:T(8,128)(2,1)S(1)}, bf16[16,2816]{1,0:T(8,128)(2,1)S(1)}) custom-call(s32[1]{0:T(128)} %bitcast.2.owner_ref, f32[4,256]{1,0:T(4,128)} %bitcast.42, bf16[6,1024]{1,0:T(8,128)(2,1)} %w_in_hbm.1, f32[1,1024]{1,0:T(1,128)} %bitcast.43, bf16[1024,1024]{1,0:T(8,128)(2,1)} %w_mid_hbm.3), custom_call_target="tpu_custom_call" | custom-call | tf_op jit(solution)/shard_map/prepare/pallas_call | solution.py:232
  17.7 0.1 pad_add_fusion.owner_ref
  17.7 1.5 %all-to-all-done = f32[8,32,88]{2,1,0:T(8,128)S(1)} async-done(((f32[8,32,88]{2,1,0:T(8,128)}), f32[8,32,88]{2,1,0:T(8,128)S(1)}, u32[]{:S(2)}, u32[]{:S(2)}) %all-to-all-start) | async-done | bytes 90144 | tf_op jit(solution)/shard_map/all_to_all | solution.py:570
  19.3 0.6 fusion
  19.9 0.6 collective-permute-start.2
  20.5 2.0 %collective-permute-start.1 = (f32[32,88]{1,0:T(8,128)S(1)}, f32[32,88]{1,0:T(8,128)S(1)}, u32[]{:S(2)}, u32[]{:S(2)}) collective-permute-start(f32[32,88]{1,0:T(8,128)S(1)} %get-tuple-element.46.sums_ref), channel_id=1, source_target_pairs={{0,16},{1,17},{2,18},{3,19},{4,20},{5,21},{6,22},{7,23},{8,24},{9,... | collective-permute-start | bytes 33800 | tf_op jit(solution)/shard_map/ppermute | solution.py:535
  22.5 0.2 collective-permute-start
  22.7 12.3 %forward.1 = (bf16[1024,2816]{1,0:T(8,128)(2,1)S(1)}, f32[1024,2816]{1,0:T(8,128)S(1)}, bf16[256,2816]{1,0:T(8,128)(2,1)S(1)}, f32[1,2816]{1,0:T(1,128)S(1)}) custom-call(s32[2]{0:T(128)S(1)} %pad_add_fusion.owner_ref, f32[1,1024]{1,0:T(1,128)} %bitcast.44, bf16[1,1024]{1,0:T(2,128)(2,1)S(1)} %reshape.76.w_out_ref, ...), custom_call_target="tpu_custom_call" | custom-call | flops 6090129408 | bytes 4194304 | tf_op jit(solution)/shard_map/forward/pallas_call | solution.py:331
  35.0 0.0 copy-start
  35.0 0.0 collective-permute-done.near_ref
  35.0 5.8 %backward.1 = (f32[4,136,128]{2,1,0:T(8,128)S(1)}, f32[4,136,128]{2,1,0:T(8,128)S(1)}, f32[4,128,128]{2,1,0:T(8,128)S(1)}, f32[4,128,128]{2,1,0:T(8,128)S(1)}) custom-call(s32[1]{0:T(128)} %bitcast.2.owner_ref, f32[32,88]{1,0:T(8,128)S(1)} %get-tuple-element.46.sums_ref, f32[32,88]{1,0:T(8,128)S(1)} %collective-permute-done.near_ref, ...), custom_call_target="tpu_custom_call" | custom-call | tf_op jit(solution)/shard_map/backward/pallas_call | solution.py:434
  40.8 0.8 collective-permute-start.6
  41.6 1.2 %collective-permute-start.3 = (f32[4,136,128]{2,1,0:T(8,128)S(1)}, f32[4,136,128]{2,1,0:T(8,128)S(1)}, u32[]{:S(2)}, u32[]{:S(2)}) collective-permute-start(f32[4,136,128]{2,1,0:T(8,128)S(1)} %get-tuple-element.36), channel_id=1, source_target_pairs={{0,2},{1,3},{2,0},{3,1},{4,6},{5,7},{6,4},{7,5},{8,10},{9,11},{10,... | collective-permute-start | bytes 835592 | tf_op jit(solution)/shard_map/ppermute | solution.py:535
  42.9 6.6 %collective-permute-done.6 = f32[4,128,128]{2,1,0:T(8,128)S(1)} collective-permute-done((f32[4,128,128]{2,1,0:T(8,128)S(1)}, f32[4,128,128]{2,1,0:T(8,128)S(1)}, u32[]{:S(2)}, u32[]{:S(2)}) %collective-permute-start.6) | collective-permute-done | bytes 262176 | tf_op jit(solution)/shard_map/ppermute | solution.py:535
  49.5 0.6 collective-permute-start.7
  50.1 0.2 collective-permute-done.3
  50.3 1.4 %collective-permute-start.4 = (f32[2,136,128]{2,1,0:T(8,128)S(1)}, f32[2,136,128]{2,1,0:T(8,128)S(1)}, u32[]{:S(2)}, u32[]{:S(2)}) collective-permute-start(f32[2,136,128]{2,1,0:T(8,128)S(1)} %dynamic-slice_bitcast_fusion), channel_id=1, source_target_pairs={{0,4},{1,5},{2,6},{3,7},{4,0},{5,1},{6,2},{7,3},{8,12},{9,13},{10,... | collective-permute-start | bytes 417800 | tf_op jit(solution)/shard_map/ppermute | solution.py:535
  51.7 2.9 %collective-permute-done.7 = f32[2,128,128]{2,1,0:T(8,128)S(1)} collective-permute-done((f32[2,128,128]{2,1,0:T(8,128)S(1)}, f32[2,128,128]{2,1,0:T(8,128)S(1)}, u32[]{:S(2)}, u32[]{:S(2)}) %collective-permute-start.7) | collective-permute-done | bytes 131104 | tf_op jit(solution)/shard_map/ppermute | solution.py:535
  54.6 0.6 collective-permute-start.8
  55.2 0.2 collective-permute-done.4
  55.5 1.7 %collective-permute-start.5 = (f32[1,136,128]{2,1,0:T(8,128)S(1)}, f32[1,136,128]{2,1,0:T(8,128)S(1)}, u32[]{:S(2)}, u32[]{:S(2)}) collective-permute-start(f32[1,136,128]{2,1,0:T(8,128)S(1)} %constant_dynamic-slice_fusion), channel_id=1, source_target_pairs={{0,8},{1,9},{2,10},{3,11},{4,12},{5,13},{6,14},{7,15},{8,0},{9,1},... | collective-permute-start | bytes 208904 | tf_op jit(solution)/shard_map/ppermute | solution.py:535
  57.2 1.7 %collective-permute-done.8 = f32[1,128,128]{2,1,0:T(8,128)S(1)} collective-permute-done((f32[1,128,128]{2,1,0:T(8,128)S(1)}, f32[1,128,128]{2,1,0:T(8,128)S(1)}, u32[]{:S(2)}, u32[]{:S(2)}) %collective-permute-start.8) | collective-permute-done | bytes 65568 | tf_op jit(solution)/shard_map/ppermute | solution.py:535
  59.0 0.9 collective-permute-done.5
  59.9 3.7 %collective-permute-start.11 = (f32[1,264,128]{2,1,0:T(8,128)S(1)}, f32[1,264,128]{2,1,0:T(8,128)S(1)}, u32[]{:S(2)}, u32[]{:S(2)}) collective-permute-start(f32[1,264,128]{2,1,0:T(8,128)S(1)} %pad_maximum_fusion.3), channel_id=1, source_target_pairs={{0,24},{1,25},{2,26},{3,27},{4,28},{5,29},{6,30},{7,31},{8,16},{9,... | collective-permute-start | bytes 405512 | tf_op jit(solution)/shard_map/ppermute | solution.py:535
  63.6 0.0 collective-permute-start.10
  63.6 0.7 collective-permute-start.9
  64.4 3.3 %collective-permute-done.11 = f32[1,264,128]{2,1,0:T(8,128)S(1)} collective-permute-done((f32[1,264,128]{2,1,0:T(8,128)S(1)}, f32[1,264,128]{2,1,0:T(8,128)S(1)}, u32[]{:S(2)}, u32[]{:S(2)}) %collective-permute-start.11) | collective-permute-done | bytes 135200 | tf_op jit(solution)/shard_map/ppermute | solution.py:535
  67.6 4.5 %collective-permute-done.10 = f32[1,264,128]{2,1,0:T(8,128)S(1)} collective-permute-done((f32[1,264,128]{2,1,0:T(8,128)S(1)}, f32[1,264,128]{2,1,0:T(8,128)S(1)}, u32[]{:S(2)}, u32[]{:S(2)}) %collective-permute-start.10) | collective-permute-done | bytes 135200 | tf_op jit(solution)/shard_map/ppermute | solution.py:535
  72.2 1.6 %collective-permute-start.12 = (f32[4,136,128]{2,1,0:T(8,128)S(1)}, f32[4,136,128]{2,1,0:T(8,128)S(1)}, u32[]{:S(2)}, u32[]{:S(2)}) collective-permute-start(f32[4,136,128]{2,1,0:T(8,128)S(1)} %slice.8), channel_id=1, source_target_pairs={{0,2},{1,3},{2,0},{3,1},{4,6},{5,7},{6,4},{7,5},{8,10},{9,11},{10,... | collective-permute-start | bytes 835592 | tf_op jit(solution)/shard_map/ppermute | solution.py:535
  73.9 1.2 %collective-permute-start.13 = (f32[4,128,128]{2,1,0:T(8,128)S(1)}, f32[4,128,128]{2,1,0:T(8,128)S(1)}, u32[]{:S(2)}, u32[]{:S(2)}) collective-permute-start(f32[4,128,128]{2,1,0:T(8,128)S(1)} %slice.9), channel_id=1, source_target_pairs={{0,4},{1,5},{2,6},{3,7},{4,0},{5,1},{6,2},{7,3},{8,12},{9,13},{10,... | collective-permute-start | bytes 786440 | tf_op jit(solution)/shard_map/ppermute | solution.py:535
  75.1 4.6 %collective-permute-done.12.refs_1_ = f32[4,136,128]{2,1,0:T(8,128)S(1)} collective-permute-done((f32[4,136,128]{2,1,0:T(8,128)S(1)}, f32[4,136,128]{2,1,0:T(8,128)S(1)}, u32[]{:S(2)}, u32[]{:S(2)}) %collective-permute-start.12) | collective-permute-done | bytes 278560 | tf_op jit(solution)/shard_map/ppermute | solution.py:535
  79.8 1.0 collective-permute-start.14
  80.8 1.1 %collective-permute-start.15 = (f32[8,128,128]{2,1,0:T(8,128)S(1)}, f32[8,128,128]{2,1,0:T(8,128)S(1)}, u32[]{:S(2)}, u32[]{:S(2)}) collective-permute-start(f32[8,128,128]{2,1,0:T(8,128)S(1)} %pad_maximum_fusion.2), channel_id=1, source_target_pairs={{0,2},{1,3},{2,0},{3,1},{4,6},{5,7},{6,4},{7,5},{8,10},{9,11},{10,... | collective-permute-start | bytes 1572872 | tf_op jit(solution)/shard_map/ppermute | solution.py:535
  81.9 10.4 %collective-permute-done.14.refs_3_ = f32[8,136,128]{2,1,0:T(8,128)S(1)} collective-permute-done((f32[8,136,128]{2,1,0:T(8,128)S(1)}, f32[8,136,128]{2,1,0:T(8,128)S(1)}, u32[]{:S(2)}, u32[]{:S(2)}) %collective-permute-start.14) | collective-permute-done | bytes 557088 | tf_op jit(solution)/shard_map/ppermute | solution.py:535
  92.3 0.5 collective-permute-start.16
  92.8 0.0 collective-permute-done.15.refs_4_
  92.8 0.0 collective-permute-start.20
  92.8 0.5 collective-permute-start.17
  93.3 0.0 collective-permute-start.18
  93.3 1.3 %add_bitcast_fusion = f32[8,88]{1,0:T(8,128)} fusion(f32[4,8,88]{2,1,0:T(8,128)S(1)} %bitcast.34, s32[]{:T(128)S(6)} %select_n.65, f32[4,8,88]{2,1,0:T(8,128)} %bitcast.35, f32[4,8,88]{2,1,0:T(8,128)} %bitcast.36, f32[4,8,88]{2,1,0:T(8,128)} %get-tuple-element.45), kind=kLoop, calls=%fused_computation.11 | loop fusion | flops 2112 | bytes 14084 | tf_op jit(solution)/shard_map/add | solution.py:574
  94.6 2.0 %collective-permute-done.18.refs_7_ = f32[4,128,128]{2,1,0:T(8,128)} collective-permute-done((f32[4,128,128]{2,1,0:T(8,128)S(1)}, f32[4,128,128]{2,1,0:T(8,128)}, u32[]{:S(2)}, u32[]{:S(2)}) %collective-permute-start.18) | collective-permute-done | bytes 262176 | tf_op jit(solution)/shard_map/ppermute | solution.py:535
  96.7 0.0 collective-permute-done.17.refs_6_
  96.7 0.0 collective-permute-done.20.refs_9_
  96.7 0.0 collective-permute-done.19.refs_8_
  96.7 4.2 %scaling.1 = (f32[6,1024]{1,0:T(8,128)}, f32[1,1024]{1,0:T(1,128)}, f32[1024,1024]{1,0:T(8,128)}, f32[1,1024]{1,0:T(1,128)}, f32[1,1024]{1,0:T(1,128)}, /*index=5*/f32[1,1]{1,0:T(1,128)}) custom-call(s32[1]{0:T(128)} %bitcast.2.owner_ref, f32[4,264,128]{2,1,0:T(8,128)S(1)} %pad_maximum_fusion.1.refs_0_, f32[4,136,128]{2,1,0:T(8,128)S(1)} %collective-permute-done.12.refs_1_, ...), custom_call_target="tpu_custom_call" | custom-call | tf_op jit(solution)/shard_map/scaling/pallas_call | solution.py:520
  (26 shorter events, 0.4 us)
Async XLA Ops:
  7.0 12.3 %all-to-all-start = ((f32[8,32,88]{2,1,0:T(8,128)}), f32[8,32,88]{2,1,0:T(8,128)S(1)}, u32[]{:S(2)}, u32[]{:S(2)}) async-start(f32[8,32,88]{2,1,0:T(8,128)} %bitcast.1), calls=%async_computation | async-start | bytes 262144 | tf_op jit(solution)/shard_map/all_to_all | solution.py:570
  19.9 15.1 %collective-permute-start.2 = (f32[32,88]{1,0:T(8,128)S(1)}, f32[32,88]{1,0:T(8,128)S(1)}, u32[]{:S(2)}, u32[]{:S(2)}) collective-permute-start(f32[32,88]{1,0:T(8,128)S(1)} %get-tuple-element.46.sums_ref), channel_id=1, source_target_pairs={{0,17},{1,16},{2,19},{3,18},{4,21},{5,20},{6,23},{7,22},{8,25},{9,... | collective-permute-start | bytes 33800 | tf_op jit(solution)/shard_map/ppermute | solution.py:535
  20.5 14.5 %collective-permute-start.1 = (f32[32,88]{1,0:T(8,128)S(1)}, f32[32,88]{1,0:T(8,128)S(1)}, u32[]{:S(2)}, u32[]{:S(2)}) collective-permute-start(f32[32,88]{1,0:T(8,128)S(1)} %get-tuple-element.46.sums_ref), channel_id=1, source_target_pairs={{0,16},{1,17},{2,18},{3,19},{4,20},{5,21},{6,22},{7,23},{8,24},{9,... | collective-permute-start | bytes 33800 | tf_op jit(solution)/shard_map/ppermute | solution.py:535
  22.5 12.5 %collective-permute-start = (f32[32,88]{1,0:T(8,128)S(1)}, f32[32,88]{1,0:T(8,128)S(1)}, u32[]{:S(2)}, u32[]{:S(2)}) collective-permute-start(f32[32,88]{1,0:T(8,128)S(1)} %get-tuple-element.46.sums_ref), channel_id=1, source_target_pairs={{0,1},{1,0},{2,3},{3,2},{4,5},{5,4},{6,7},{7,6},{8,9},{9,8},{10,11... | collective-permute-start | bytes 33800 | tf_op jit(solution)/shard_map/ppermute | solution.py:535
  35.0 5.8 %copy-start = (f32[32,88]{1,0:T(8,128)}, f32[32,88]{1,0:T(8,128)S(1)}, u32[]{:S(2)}) copy-start(f32[32,88]{1,0:T(8,128)S(1)} %collective-permute-done.1.far_ref) | copy-start | bytes 33796
  35.0 5.8 %copy-start.1 = (f32[32,88]{1,0:T(8,128)}, f32[32,88]{1,0:T(8,128)S(1)}, u32[]{:S(2)}) copy-start(f32[32,88]{1,0:T(8,128)S(1)} %collective-permute-done.near_ref) | copy-start | bytes 33796
  40.8 8.6 %collective-permute-start.6 = (f32[4,128,128]{2,1,0:T(8,128)S(1)}, f32[4,128,128]{2,1,0:T(8,128)S(1)}, u32[]{:S(2)}, u32[]{:S(2)}) collective-permute-start(f32[4,128,128]{2,1,0:T(8,128)S(1)} %get-tuple-element.38), channel_id=1, source_target_pairs={{0,8},{1,9},{2,10},{3,11},{4,12},{5,13},{6,14},{7,15},{8,0},{9,1},... | collective-permute-start | bytes 786440 | tf_op jit(solution)/shard_map/ppermute | solution.py:535
  41.6 8.6 %collective-permute-start.3 = (f32[4,136,128]{2,1,0:T(8,128)S(1)}, f32[4,136,128]{2,1,0:T(8,128)S(1)}, u32[]{:S(2)}, u32[]{:S(2)}) collective-permute-start(f32[4,136,128]{2,1,0:T(8,128)S(1)} %get-tuple-element.36), channel_id=1, source_target_pairs={{0,2},{1,3},{2,0},{3,1},{4,6},{5,7},{6,4},{7,5},{8,10},{9,11},{10,... | collective-permute-start | bytes 835592 | tf_op jit(solution)/shard_map/ppermute | solution.py:535
  49.5 5.0 %collective-permute-start.7 = (f32[2,128,128]{2,1,0:T(8,128)S(1)}, f32[2,128,128]{2,1,0:T(8,128)S(1)}, u32[]{:S(2)}, u32[]{:S(2)}) collective-permute-start(f32[2,128,128]{2,1,0:T(8,128)S(1)} %dynamic-slice_bitcast_fusion.1), channel_id=1, source_target_pairs={{0,2},{1,3},{2,0},{3,1},{4,6},{5,7},{6,4},{7,5},{8,10},{9,11},{10,... | collective-permute-start | bytes 393224 | tf_op jit(solution)/shard_map/ppermute | solution.py:535
  50.3 5.1 %collective-permute-start.4 = (f32[2,136,128]{2,1,0:T(8,128)S(1)}, f32[2,136,128]{2,1,0:T(8,128)S(1)}, u32[]{:S(2)}, u32[]{:S(2)}) collective-permute-start(f32[2,136,128]{2,1,0:T(8,128)S(1)} %dynamic-slice_bitcast_fusion), channel_id=1, source_target_pairs={{0,4},{1,5},{2,6},{3,7},{4,0},{5,1},{6,2},{7,3},{8,12},{9,13},{10,... | collective-permute-start | bytes 417800 | tf_op jit(solution)/shard_map/ppermute | solution.py:535
  54.6 4.3 %collective-permute-start.8 = (f32[1,128,128]{2,1,0:T(8,128)S(1)}, f32[1,128,128]{2,1,0:T(8,128)S(1)}, u32[]{:S(2)}, u32[]{:S(2)}) collective-permute-start(f32[1,128,128]{2,1,0:T(8,128)S(1)} %constant_dynamic-slice_fusion.1), channel_id=1, source_target_pairs={{0,4},{1,5},{2,6},{3,7},{4,0},{5,1},{6,2},{7,3},{8,12},{9,13},{10,... | collective-permute-start | bytes 196616 | tf_op jit(solution)/shard_map/ppermute | solution.py:535
  55.5 4.4 %collective-permute-start.5 = (f32[1,136,128]{2,1,0:T(8,128)S(1)}, f32[1,136,128]{2,1,0:T(8,128)S(1)}, u32[]{:S(2)}, u32[]{:S(2)}) collective-permute-start(f32[1,136,128]{2,1,0:T(8,128)S(1)} %constant_dynamic-slice_fusion), channel_id=1, source_target_pairs={{0,8},{1,9},{2,10},{3,11},{4,12},{5,13},{6,14},{7,15},{8,0},{9,1},... | collective-permute-start | bytes 208904 | tf_op jit(solution)/shard_map/ppermute | solution.py:535
  59.9 7.7 %collective-permute-start.11 = (f32[1,264,128]{2,1,0:T(8,128)S(1)}, f32[1,264,128]{2,1,0:T(8,128)S(1)}, u32[]{:S(2)}, u32[]{:S(2)}) collective-permute-start(f32[1,264,128]{2,1,0:T(8,128)S(1)} %pad_maximum_fusion.3), channel_id=1, source_target_pairs={{0,24},{1,25},{2,26},{3,27},{4,28},{5,29},{6,30},{7,31},{8,16},{9,... | collective-permute-start | bytes 405512 | tf_op jit(solution)/shard_map/ppermute | solution.py:535
  63.6 8.5 %collective-permute-start.10 = (f32[1,264,128]{2,1,0:T(8,128)S(1)}, f32[1,264,128]{2,1,0:T(8,128)S(1)}, u32[]{:S(2)}, u32[]{:S(2)}) collective-permute-start(f32[1,264,128]{2,1,0:T(8,128)S(1)} %pad_maximum_fusion.3), channel_id=1, source_target_pairs={{0,16},{1,17},{2,18},{3,19},{4,20},{5,21},{6,22},{7,23},{8,24},{9,... | collective-permute-start | bytes 405512 | tf_op jit(solution)/shard_map/ppermute | solution.py:535
  63.6 8.5 %collective-permute-start.9 = (f32[1,264,128]{2,1,0:T(8,128)S(1)}, f32[1,264,128]{2,1,0:T(8,128)S(1)}, u32[]{:S(2)}, u32[]{:S(2)}) collective-permute-start(f32[1,264,128]{2,1,0:T(8,128)S(1)} %pad_maximum_fusion.3), channel_id=1, source_target_pairs={{0,8},{1,9},{2,10},{3,11},{4,12},{5,13},{6,14},{7,15},{8,0},{9,1},... | collective-permute-start | bytes 405512 | tf_op jit(solution)/shard_map/ppermute | solution.py:535
  72.2 7.5 %collective-permute-start.12 = (f32[4,136,128]{2,1,0:T(8,128)S(1)}, f32[4,136,128]{2,1,0:T(8,128)S(1)}, u32[]{:S(2)}, u32[]{:S(2)}) collective-permute-start(f32[4,136,128]{2,1,0:T(8,128)S(1)} %slice.8), channel_id=1, source_target_pairs={{0,2},{1,3},{2,0},{3,1},{4,6},{5,7},{6,4},{7,5},{8,10},{9,11},{10,... | collective-permute-start | bytes 835592 | tf_op jit(solution)/shard_map/ppermute | solution.py:535
  73.9 6.9 %collective-permute-start.13 = (f32[4,128,128]{2,1,0:T(8,128)S(1)}, f32[4,128,128]{2,1,0:T(8,128)S(1)}, u32[]{:S(2)}, u32[]{:S(2)}) collective-permute-start(f32[4,128,128]{2,1,0:T(8,128)S(1)} %slice.9), channel_id=1, source_target_pairs={{0,4},{1,5},{2,6},{3,7},{4,0},{5,1},{6,2},{7,3},{8,12},{9,13},{10,... | collective-permute-start | bytes 786440 | tf_op jit(solution)/shard_map/ppermute | solution.py:535
  79.8 12.5 %collective-permute-start.14 = (f32[8,136,128]{2,1,0:T(8,128)S(1)}, f32[8,136,128]{2,1,0:T(8,128)S(1)}, u32[]{:S(2)}, u32[]{:S(2)}) collective-permute-start(f32[8,136,128]{2,1,0:T(8,128)S(1)} %pad_maximum_fusion), channel_id=1, source_target_pairs={{0,4},{1,5},{2,6},{3,7},{4,0},{5,1},{6,2},{7,3},{8,12},{9,13},{10,... | collective-permute-start | bytes 1671176 | tf_op jit(solution)/shard_map/ppermute | solution.py:535
  80.8 12.0 %collective-permute-start.15 = (f32[8,128,128]{2,1,0:T(8,128)S(1)}, f32[8,128,128]{2,1,0:T(8,128)S(1)}, u32[]{:S(2)}, u32[]{:S(2)}) collective-permute-start(f32[8,128,128]{2,1,0:T(8,128)S(1)} %pad_maximum_fusion.2), channel_id=1, source_target_pairs={{0,2},{1,3},{2,0},{3,1},{4,6},{5,7},{6,4},{7,5},{8,10},{9,11},{10,... | collective-permute-start | bytes 1572872 | tf_op jit(solution)/shard_map/ppermute | solution.py:535
  92.3 4.4 %collective-permute-start.19 = (f32[8,136,128]{2,1,0:T(8,128)S(1)}, f32[8,136,128]{2,1,0:T(8,128)S(1)}, u32[]{:S(2)}, u32[]{:S(2)}) collective-permute-start(f32[8,136,128]{2,1,0:T(8,128)S(1)} %collective-permute-done.14.refs_3_), channel_id=1, source_target_pairs={{0,1},{1,0},{2,3},{3,2},{4,5},{5,4},{6,7},{7,6},{8,9},{9,8},{10,11... | collective-permute-start | bytes 1671176 | tf_op jit(solution)/shard_map/ppermute | solution.py:535
  92.3 4.3 %collective-permute-start.16 = (f32[4,264,128]{2,1,0:T(8,128)S(1)}, f32[4,264,128]{2,1,0:T(8,128)S(1)}, u32[]{:S(2)}, u32[]{:S(2)}) collective-permute-start(f32[4,264,128]{2,1,0:T(8,128)S(1)} %pad_maximum_fusion.1.refs_0_), channel_id=1, source_target_pairs={{0,1},{1,0},{2,3},{3,2},{4,5},{5,4},{6,7},{7,6},{8,9},{9,8},{10,11... | collective-permute-start | bytes 1622024 | tf_op jit(solution)/shard_map/ppermute | solution.py:535
  92.8 3.8 %collective-permute-start.20 = (f32[8,128,128]{2,1,0:T(8,128)S(1)}, f32[8,128,128]{2,1,0:T(8,128)}, u32[]{:S(2)}, u32[]{:S(2)}) collective-permute-start(f32[8,128,128]{2,1,0:T(8,128)S(1)} %collective-permute-done.15.refs_4_), channel_id=1, source_target_pairs={{0,1},{1,0},{2,3},{3,2},{4,5},{5,4},{6,7},{7,6},{8,9},{9,8},{10,11... | collective-permute-start | bytes 1572872 | tf_op jit(solution)/shard_map/ppermute | solution.py:535
  92.8 3.8 %collective-permute-start.17 = (f32[4,136,128]{2,1,0:T(8,128)S(1)}, f32[4,136,128]{2,1,0:T(8,128)S(1)}, u32[]{:S(2)}, u32[]{:S(2)}) collective-permute-start(f32[4,136,128]{2,1,0:T(8,128)S(1)} %collective-permute-done.12.refs_1_), channel_id=1, source_target_pairs={{0,1},{1,0},{2,3},{3,2},{4,5},{5,4},{6,7},{7,6},{8,9},{9,8},{10,11... | collective-permute-start | bytes 835592 | tf_op jit(solution)/shard_map/ppermute | solution.py:535
  93.3 3.3 %collective-permute-start.18 = (f32[4,128,128]{2,1,0:T(8,128)S(1)}, f32[4,128,128]{2,1,0:T(8,128)}, u32[]{:S(2)}, u32[]{:S(2)}) collective-permute-start(f32[4,128,128]{2,1,0:T(8,128)S(1)} %collective-permute-done.13.refs_2_), channel_id=1, source_target_pairs={{0,1},{1,0},{2,3},{3,2},{4,5},{5,4},{6,7},{7,6},{8,9},{9,8},{10,11... | collective-permute-start | bytes 786440 | tf_op jit(solution)/shard_map/ppermute | solution.py:535

commit v6 on v5

--- a/solution.py
+++ b/solution.py
@@ -349,7 +349,7 @@
 
 def backward_kernel(
     inv_sets, owner_ref, sums_ref, near_ref, far_ref, both_ref, hidden_ref, curve_ref, mixed_ref, pred_ref, win_ref,
-    feat_ref, w_mid_hbm, b_out_ref, keep_a, send_a, keep_b, send_b,
+    feat_ref, w_mid_hbm, b_out_ref, keep_a, send_a, keep_b, send_b, prices_ref,
     left_ref, back_ref, slope_ref, even_delta, odd_delta, delta_in_ref, own_delta_ref, bias_ref,
     read_ref, extra_ref, grad_ref, sem,
 ):
@@ -367,6 +367,11 @@
 
     left_ref[...] = jnp.zeros_like(left_ref)
     sums = (sums_ref[...] + near_ref[...]) + (far_ref[...] + both_ref[...])
+    set_dev = sets // 4
+    prices = sums[:set_dev]
+    for b in range(1, 4):
+        prices = jnp.where(block == b, sums[b * set_dev : (b + 1) * set_dev], prices)
+    prices_ref[...] = prices
     for p, piece in enumerate(bf16_pieces(sums)):
         left_ref[p * sets : (p + 1) * sets, :PAIRS] = piece.astype(jnp.float32)
     left = left_ref[...].astype(bf16)
@@ -434,11 +439,12 @@
     return pl.pallas_call(
         functools.partial(backward_kernel, inv_sets),
         in_specs=[smem] + [vmem] * 10 + [hbm, smem],
-        out_specs=[vmem] * 4,
+        out_specs=[vmem] * 5,
         out_shape=[
             jax.ShapeDtypeStruct((groups // 2, WIDTH // groups + more, LANES), jnp.float32)
             for more in (8, 8, 0, 0)
-        ],
+        ]
+        + [jax.ShapeDtypeStruct((sets // 4, PAIRS), jnp.float32)],
         scratch_shapes=[
             pltpu.VMEM((3 * sets, LANES), jnp.float32),
             pltpu.VMEM((cols, WIDTH), jnp.bfloat16),
@@ -571,11 +577,10 @@
     parts, win = lax.optimization_barrier((parts, win))
     sums = jnp.sum(parts, axis=0) / total_paths
     sums = [sums] + [swap(sums, mask, devices) for mask in (1, top, top + 1)]
-    prices = sum(pick(part.reshape(4, set_dev, PAIRS), block) for part in sums)
 
     place = jnp.stack([owner, jnp.int32(top)])
     saved = forward(place, b_mid, w_out, win, weights, feat)
-    keep_a, send_a, keep_b, send_b = backward(
+    keep_a, send_a, keep_b, send_b, prices = backward(
         owner, sums, saved, win, feat, w_mid, b_out, 1.0 / set_count, groups
     )
 
@@ -600,14 +605,18 @@
         came_a, came_b = swap(held_a, bit_a, devices), swap(held_b, bit_b, devices)
         new_a = tuple(mask ^ bit_a for mask in masks_a)
         new_b = tuple(mask ^ bit_b for mask in masks_b)
+        if bit_a == order[-1]:
+            near = [swap(array, 1, devices) for array, _, _ in received]
+            came_a, came_b, *near = lax.optimization_barrier((came_a, came_b, *near))
         received += [(came_a, new_a, ("left", "extra")), (came_b, new_b, ("right",))]
         if bit_a != order[-1]:
             held_a = jnp.concatenate([held_a, came_a], axis=0)
             held_b = jnp.concatenate([held_b, came_b], axis=0)
         masks_a, masks_b = masks_a + new_a, masks_b + new_b
+    near += [swap(array, 1, devices) for array, _, _ in received[len(near) :]]
     received += [
-        (swap(array, 1, devices), tuple(mask ^ 1 for mask in masks), contents)
-        for array, masks, contents in received
+        (array, tuple(mask ^ 1 for mask in masks), contents)
+        for array, (_, masks, contents) in zip(near, received)
     ]
     result = scaled(owner, groups, received)
     direction_w_in, direction_b_in, direction_w_mid, direction_b_mid, direction_w_out, direction_b_out = result

time: 101 us -> 98.8 us (0.978)
  other arithmetic: 2.26 us -> 0.34 us
    add x1 -> x0, other arithmetic: 1.3 us -> none  [on_device(): sum((pick(part.reshape(4, set_dev, PAIRS), block) for part in sums))]
    pallas_call x1, Pallas kernels: 4.2 us -> 3.07 us  [scaled(): pl.pallas_call(functools.partial(scaling_kernel, layout, groups), in_spec...]
  transfers between devices with their start and end apart: 22 -> 22, of which waited for: 12 -> 14; matrix products, arithmetic and copies ran while one was open for 2% -> 1% of each run, Pallas kernels for 15% -> 16%
where the time goes in v6:
time: 98.8 us; the launch traced here: 98.4 us
  waiting for transfers between devices  38.2 us (39%)
  Pallas kernels  31.5 us (32%)
  starting transfers between devices  26.2 us (27%)
  between operations  1.44 us (1%)
    ppermute x21, waiting for transfers between devices, swap(): return lax.ppermute(array, 'paths', [(i, i ^ bit) for i in range(devices)])  36.6 us
    ppermute x21, starting transfers between devices, swap(): return lax.ppermute(array, 'paths', [(i, i ^ bit) for i in range(devices)])  20 us
    pallas_call x1, Pallas kernels, forward(): pl.pallas_call(forward_kernel, in_specs=[smem] + [vmem] * 5, out_specs=[v...  12.3 us
    pallas_call x1, Pallas kernels, backward(): pl.pallas_call(functools.partial(backward_kernel, inv_sets), in_specs=[sm...  6.58 us
    pallas_call x1, Pallas kernels, payoff_sums(): pl.pallas_call(pricing_kernel, grid=(steps,), in_specs=[pl.BlockSpec((4,...  6.36 us
    all_to_all x1, starting transfers between devices, on_device(): lax.all_to_all(sums, 'paths', 0, 0, axis_index_groups=lanes, tiled=True)  6.18 us
    pallas_call x1, Pallas kernels, prepare(): pl.pallas_call(functools.partial(prepare_kernel, sets), in_specs=[smem, v...  3.15 us
    pallas_call x1, Pallas kernels, scaled(): pl.pallas_call(functools.partial(scaling_kernel, layout, groups), in_spec...  3.07 us
  transfers between devices with their start and end apart: 22, of which 14 were waited for; matrix products, arithmetic and copies ran while one was open for 1% of the time, Pallas kernels for 16%

profile of v6, /device:TPU:0, one launch (start us, length us, event | category | flops | bytes accessed | tf_op | source)
XLA Modules:
  0.0 98.4 jit_solution(16889430769143197242)
XLA Ops:
  0.6 6.4 %pricing.1 = f32[8,2,16,88]{3,2,1,0:T(8,128)} custom-call(f32[4,256]{1,0:T(4,128)} %bitcast.31, bf16[2,64,128]{2,1,0:T(8,128)(2,1)} %inc_ref.1), custom_call_target="tpu_custom_call" | custom-call | tf_op jit(solution)/shard_map/pricing/pallas_call | solution.py:127
  7.0 6.2 %all-to-all-start = ((f32[8,32,88]{2,1,0:T(8,128)}), f32[8,32,88]{2,1,0:T(8,128)S(1)}, u32[]{:S(2)}, u32[]{:S(2)}) async-start(f32[8,32,88]{2,1,0:T(8,128)} %bitcast.2), calls=%async_computation | async-start | bytes 262144 | tf_op jit(solution)/shard_map/all_to_all | solution.py:576
  13.2 0.7 reshape.57.w_out_ref
  14.5 3.1 %prepare.1 = (bf16[1024,16]{1,0:T(8,128)(2,1)S(1)}, bf16[1024,1024]{1,0:T(8,128)(2,1)S(1)}, bf16[16,2816]{1,0:T(8,128)(2,1)S(1)}) custom-call(s32[1]{0:T(128)} %bitcast.owner_ref, f32[4,256]{1,0:T(4,128)} %bitcast.32, bf16[6,1024]{1,0:T(8,128)(2,1)} %w_in_hbm.1, f32[1,1024]{1,0:T(1,128)} %bitcast.33, bf16[1024,1024]{1,0:T(8,128)(2,1)} %w_mid_hbm.3), custom_call_target="tpu_custom_call" | custom-call | tf_op jit(solution)/shard_map/prepare/pallas_call | solution.py:232
  17.7 0.1 pad_add_fusion.owner_ref
  17.7 1.5 %all-to-all-done = f32[8,32,88]{2,1,0:T(8,128)S(1)} async-done(((f32[8,32,88]{2,1,0:T(8,128)}), f32[8,32,88]{2,1,0:T(8,128)S(1)}, u32[]{:S(2)}, u32[]{:S(2)}) %all-to-all-start) | async-done | bytes 90144 | tf_op jit(solution)/shard_map/all_to_all | solution.py:576
  19.3 0.1 collective-permute-start
  19.4 2.7 %collective-permute-start.1 = (f32[32,88]{1,0:T(8,128)S(1)}, f32[32,88]{1,0:T(8,128)S(1)}, u32[]{:S(2)}, u32[]{:S(2)}) collective-permute-start(f32[32,88]{1,0:T(8,128)S(1)} %broadcast_multiply_fusion.sums_ref), channel_id=1, source_target_pairs={{0,16},{1,17},{2,18},{3,19},{4,20},{5,21},{6,22},{7,23},{8,24},{9,... | collective-permute-start | bytes 33800 | tf_op jit(solution)/shard_map/ppermute | solution.py:541
  22.0 0.1 collective-permute-start.2
  22.1 12.3 %forward.1 = (bf16[1024,2816]{1,0:T(8,128)(2,1)S(1)}, f32[1024,2816]{1,0:T(8,128)S(1)}, bf16[256,2816]{1,0:T(8,128)(2,1)S(1)}, f32[1,2816]{1,0:T(1,128)S(1)}) custom-call(s32[2]{0:T(128)S(1)} %pad_add_fusion.owner_ref, f32[1,1024]{1,0:T(1,128)} %bitcast.34, bf16[1,1024]{1,0:T(2,128)(2,1)S(1)} %reshape.57.w_out_ref, ...), custom_call_target="tpu_custom_call" | custom-call | flops 6090129408 | bytes 4194304 | tf_op jit(solution)/shard_map/forward/pallas_call | solution.py:331
  34.5 0.0 collective-permute-done.near_ref
  34.5 0.0 collective-permute-done.1.far_ref
  34.5 0.0 collective-permute-done.2.both_ref
  34.5 6.6 %backward.1 = (f32[4,136,128]{2,1,0:T(8,128)S(1)}, f32[4,136,128]{2,1,0:T(8,128)S(1)}, f32[4,128,128]{2,1,0:T(8,128)S(1)}, f32[4,128,128]{2,1,0:T(8,128)S(1)}, f32[8,88]{1,0:T(8,128)}) custom-call(s32[1]{0:T(128)} %bitcast.owner_ref, f32[32,88]{1,0:T(8,128)S(1)} %broadcast_multiply_fusion.sums_ref, f32[32,88]{1,0:T(8,128)S(1)} %collective-permute-done.near_ref, ...), custom_call_target="tpu_custom_call" | custom-call | tf_op jit(solution)/shard_map/backward/pallas_call | solution.py:439
  41.1 0.8 collective-permute-start.6
  41.9 1.2 %collective-permute-start.3 = (f32[4,136,128]{2,1,0:T(8,128)S(1)}, f32[4,136,128]{2,1,0:T(8,128)S(1)}, u32[]{:S(2)}, u32[]{:S(2)}) collective-permute-start(f32[4,136,128]{2,1,0:T(8,128)S(1)} %get-tuple-element.43), channel_id=1, source_target_pairs={{0,2},{1,3},{2,0},{3,1},{4,6},{5,7},{6,4},{7,5},{8,10},{9,11},{10,... | collective-permute-start | bytes 835592 | tf_op jit(solution)/shard_map/ppermute | solution.py:541
  43.1 6.6 %collective-permute-done.6 = f32[4,128,128]{2,1,0:T(8,128)S(1)} collective-permute-done((f32[4,128,128]{2,1,0:T(8,128)S(1)}, f32[4,128,128]{2,1,0:T(8,128)S(1)}, u32[]{:S(2)}, u32[]{:S(2)}) %collective-permute-start.6) | collective-permute-done | bytes 262176 | tf_op jit(solution)/shard_map/ppermute | solution.py:541
  49.8 0.6 collective-permute-start.7
  50.3 0.2 collective-permute-done.3
  50.6 1.4 %collective-permute-start.4 = (f32[2,136,128]{2,1,0:T(8,128)S(1)}, f32[2,136,128]{2,1,0:T(8,128)S(1)}, u32[]{:S(2)}, u32[]{:S(2)}) collective-permute-start(f32[2,136,128]{2,1,0:T(8,128)S(1)} %dynamic-slice_bitcast_fusion), channel_id=1, source_target_pairs={{0,4},{1,5},{2,6},{3,7},{4,0},{5,1},{6,2},{7,3},{8,12},{9,13},{10,... | collective-permute-start | bytes 417800 | tf_op jit(solution)/shard_map/ppermute | solution.py:541
  51.9 2.9 %collective-permute-done.7 = f32[2,128,128]{2,1,0:T(8,128)S(1)} collective-permute-done((f32[2,128,128]{2,1,0:T(8,128)S(1)}, f32[2,128,128]{2,1,0:T(8,128)S(1)}, u32[]{:S(2)}, u32[]{:S(2)}) %collective-permute-start.7) | collective-permute-done | bytes 131104 | tf_op jit(solution)/shard_map/ppermute | solution.py:541
  54.8 0.6 collective-permute-start.8
  55.5 0.2 collective-permute-done.4
  55.7 1.7 %collective-permute-start.5 = (f32[1,136,128]{2,1,0:T(8,128)S(1)}, f32[1,136,128]{2,1,0:T(8,128)S(1)}, u32[]{:S(2)}, u32[]{:S(2)}) collective-permute-start(f32[1,136,128]{2,1,0:T(8,128)S(1)} %constant_dynamic-slice_fusion.1), channel_id=1, source_target_pairs={{0,8},{1,9},{2,10},{3,11},{4,12},{5,13},{6,14},{7,15},{8,0},{9,1},... | collective-permute-start | bytes 208904 | tf_op jit(solution)/shard_map/ppermute | solution.py:541
  57.4 1.7 %collective-permute-done.8 = f32[1,128,128]{2,1,0:T(8,128)S(1)} collective-permute-done((f32[1,128,128]{2,1,0:T(8,128)S(1)}, f32[1,128,128]{2,1,0:T(8,128)S(1)}, u32[]{:S(2)}, u32[]{:S(2)}) %collective-permute-start.8) | collective-permute-done | bytes 65568 | tf_op jit(solution)/shard_map/ppermute | solution.py:541
  59.2 0.9 collective-permute-done.5
  60.1 3.7 %collective-permute-start.11 = (f32[1,264,128]{2,1,0:T(8,128)S(1)}, f32[1,264,128]{2,1,0:T(8,128)S(1)}, u32[]{:S(2)}, u32[]{:S(2)}) collective-permute-start(f32[1,264,128]{2,1,0:T(8,128)S(1)} %pad_maximum_fusion.3), channel_id=1, source_target_pairs={{0,24},{1,25},{2,26},{3,27},{4,28},{5,29},{6,30},{7,31},{8,16},{9,... | collective-permute-start | bytes 405512 | tf_op jit(solution)/shard_map/ppermute | solution.py:541
  63.8 0.0 collective-permute-start.10
  63.8 0.7 collective-permute-start.9
  64.6 3.5 %collective-permute-done.11 = f32[1,264,128]{2,1,0:T(8,128)S(1)} collective-permute-done((f32[1,264,128]{2,1,0:T(8,128)S(1)}, f32[1,264,128]{2,1,0:T(8,128)S(1)}, u32[]{:S(2)}, u32[]{:S(2)}) %collective-permute-start.11) | collective-permute-done | bytes 135200 | tf_op jit(solution)/shard_map/ppermute | solution.py:541
  68.1 4.4 %collective-permute-done.10 = f32[1,264,128]{2,1,0:T(8,128)S(1)} collective-permute-done((f32[1,264,128]{2,1,0:T(8,128)S(1)}, f32[1,264,128]{2,1,0:T(8,128)S(1)}, u32[]{:S(2)}, u32[]{:S(2)}) %collective-permute-start.10) | collective-permute-done | bytes 135200 | tf_op jit(solution)/shard_map/ppermute | solution.py:541
  72.5 0.0 collective-permute-done.9
  72.5 1.7 %collective-permute-start.12 = (f32[4,136,128]{2,1,0:T(8,128)S(1)}, f32[4,136,128]{2,1,0:T(8,128)S(1)}, u32[]{:S(2)}, u32[]{:S(2)}) collective-permute-start(f32[4,136,128]{2,1,0:T(8,128)S(1)} %slice.8), channel_id=1, source_target_pairs={{0,2},{1,3},{2,0},{3,1},{4,6},{5,7},{6,4},{7,5},{8,10},{9,11},{10,... | collective-permute-start | bytes 835592 | tf_op jit(solution)/shard_map/ppermute | solution.py:541
  74.2 1.3 %collective-permute-start.13 = (f32[4,128,128]{2,1,0:T(8,128)S(1)}, f32[4,128,128]{2,1,0:T(8,128)S(1)}, u32[]{:S(2)}, u32[]{:S(2)}) collective-permute-start(f32[4,128,128]{2,1,0:T(8,128)S(1)} %slice.9), channel_id=1, source_target_pairs={{0,4},{1,5},{2,6},{3,7},{4,0},{5,1},{6,2},{7,3},{8,12},{9,13},{10,... | collective-permute-start | bytes 786440 | tf_op jit(solution)/shard_map/ppermute | solution.py:541
  75.6 0.0 collective-permute-start.16
  75.6 4.3 %collective-permute-done.12.refs_1_ = f32[4,136,128]{2,1,0:T(8,128)S(1)} collective-permute-done((f32[4,136,128]{2,1,0:T(8,128)S(1)}, f32[4,136,128]{2,1,0:T(8,128)S(1)}, u32[]{:S(2)}, u32[]{:S(2)}) %collective-permute-start.12) | collective-permute-done | bytes 278560 | tf_op jit(solution)/shard_map/ppermute | solution.py:541
  79.9 1.1 %collective-permute-start.14 = (f32[8,136,128]{2,1,0:T(8,128)S(1)}, f32[8,136,128]{2,1,0:T(8,128)S(1)}, u32[]{:S(2)}, u32[]{:S(2)}) collective-permute-start(f32[8,136,128]{2,1,0:T(8,128)S(1)} %pad_maximum_fusion), channel_id=1, source_target_pairs={{0,4},{1,5},{2,6},{3,7},{4,0},{5,1},{6,2},{7,3},{8,12},{9,13},{10,... | collective-permute-start | bytes 1671176 | tf_op jit(solution)/shard_map/ppermute | solution.py:541
  81.1 0.0 collective-permute-done.13.refs_2_
  81.1 1.3 %collective-permute-start.15 = (f32[8,128,128]{2,1,0:T(8,128)S(1)}, f32[8,128,128]{2,1,0:T(8,128)S(1)}, u32[]{:S(2)}, u32[]{:S(2)}) collective-permute-start(f32[8,128,128]{2,1,0:T(8,128)S(1)} %pad_maximum_fusion.2), channel_id=1, source_target_pairs={{0,2},{1,3},{2,0},{3,1},{4,6},{5,7},{6,4},{7,5},{8,10},{9,11},{10,... | collective-permute-start | bytes 1572872 | tf_op jit(solution)/shard_map/ppermute | solution.py:541
  82.4 0.0 collective-permute-start.17
  82.4 0.5 collective-permute-start.18
  82.9 1.4 %collective-permute-done.18.refs_7_ = f32[4,128,128]{2,1,0:T(8,128)S(1)} collective-permute-done((f32[4,128,128]{2,1,0:T(8,128)S(1)}, f32[4,128,128]{2,1,0:T(8,128)S(1)}, u32[]{:S(2)}, u32[]{:S(2)}) %collective-permute-start.18) | collective-permute-done | bytes 262176 | tf_op jit(solution)/shard_map/ppermute | solution.py:541
  84.3 0.0 collective-permute-done.16.refs_5_
  84.3 7.7 %collective-permute-done.15.refs_4_ = f32[8,128,128]{2,1,0:T(8,128)S(1)} collective-permute-done((f32[8,128,128]{2,1,0:T(8,128)S(1)}, f32[8,128,128]{2,1,0:T(8,128)S(1)}, u32[]{:S(2)}, u32[]{:S(2)}) %collective-permute-start.15) | collective-permute-done | bytes 524320 | tf_op jit(solution)/shard_map/ppermute | solution.py:541
  92.0 0.6 collective-permute-done.14.refs_3_
  92.6 0.5 collective-permute-start.20
  93.1 2.2 %collective-permute-done.20.refs_9_ = f32[8,128,128]{2,1,0:T(8,128)S(1)} collective-permute-done((f32[8,128,128]{2,1,0:T(8,128)S(1)}, f32[8,128,128]{2,1,0:T(8,128)S(1)}, u32[]{:S(2)}, u32[]{:S(2)}) %collective-permute-start.20) | collective-permute-done | bytes 524320 | tf_op jit(solution)/shard_map/ppermute | solution.py:541
  95.3 3.1 %scaling.1 = (f32[6,1024]{1,0:T(8,128)}, f32[1,1024]{1,0:T(1,128)}, f32[1024,1024]{1,0:T(8,128)}, f32[1,1024]{1,0:T(1,128)}, f32[1,1024]{1,0:T(1,128)}, /*index=5*/f32[1,1]{1,0:T(1,128)}) custom-call(s32[1]{0:T(128)} %bitcast.owner_ref, f32[4,264,128]{2,1,0:T(8,128)S(1)} %pad_maximum_fusion.1.refs_0_, f32[4,136,128]{2,1,0:T(8,128)S(1)} %collective-permute-done.12.refs_1_, ...), custom_call_target="tpu_custom_call" | custom-call | tf_op jit(solution)/shard_map/scaling/pallas_call | solution.py:526
  (21 shorter events, 0.4 us)
Async XLA Ops:
  7.0 12.3 %all-to-all-start = ((f32[8,32,88]{2,1,0:T(8,128)}), f32[8,32,88]{2,1,0:T(8,128)S(1)}, u32[]{:S(2)}, u32[]{:S(2)}) async-start(f32[8,32,88]{2,1,0:T(8,128)} %bitcast.2), calls=%async_computation | async-start | bytes 262144 | tf_op jit(solution)/shard_map/all_to_all | solution.py:576
  19.3 15.2 %collective-permute-start = (f32[32,88]{1,0:T(8,128)S(1)}, f32[32,88]{1,0:T(8,128)S(1)}, u32[]{:S(2)}, u32[]{:S(2)}) collective-permute-start(f32[32,88]{1,0:T(8,128)S(1)} %broadcast_multiply_fusion.sums_ref), channel_id=1, source_target_pairs={{0,1},{1,0},{2,3},{3,2},{4,5},{5,4},{6,7},{7,6},{8,9},{9,8},{10,11... | collective-permute-start | bytes 33800 | tf_op jit(solution)/shard_map/ppermute | solution.py:541
  19.4 15.1 %collective-permute-start.1 = (f32[32,88]{1,0:T(8,128)S(1)}, f32[32,88]{1,0:T(8,128)S(1)}, u32[]{:S(2)}, u32[]{:S(2)}) collective-permute-start(f32[32,88]{1,0:T(8,128)S(1)} %broadcast_multiply_fusion.sums_ref), channel_id=1, source_target_pairs={{0,16},{1,17},{2,18},{3,19},{4,20},{5,21},{6,22},{7,23},{8,24},{9,... | collective-permute-start | bytes 33800 | tf_op jit(solution)/shard_map/ppermute | solution.py:541
  22.0 12.4 %collective-permute-start.2 = (f32[32,88]{1,0:T(8,128)S(1)}, f32[32,88]{1,0:T(8,128)S(1)}, u32[]{:S(2)}, u32[]{:S(2)}) collective-permute-start(f32[32,88]{1,0:T(8,128)S(1)} %broadcast_multiply_fusion.sums_ref), channel_id=1, source_target_pairs={{0,17},{1,16},{2,19},{3,18},{4,21},{5,20},{6,23},{7,22},{8,25},{9,... | collective-permute-start | bytes 33800 | tf_op jit(solution)/shard_map/ppermute | solution.py:541
  41.1 8.6 %collective-permute-start.6 = (f32[4,128,128]{2,1,0:T(8,128)S(1)}, f32[4,128,128]{2,1,0:T(8,128)S(1)}, u32[]{:S(2)}, u32[]{:S(2)}) collective-permute-start(f32[4,128,128]{2,1,0:T(8,128)S(1)} %get-tuple-element.45), channel_id=1, source_target_pairs={{0,8},{1,9},{2,10},{3,11},{4,12},{5,13},{6,14},{7,15},{8,0},{9,1},... | collective-permute-start | bytes 786440 | tf_op jit(solution)/shard_map/ppermute | solution.py:541
  41.9 8.6 %collective-permute-start.3 = (f32[4,136,128]{2,1,0:T(8,128)S(1)}, f32[4,136,128]{2,1,0:T(8,128)S(1)}, u32[]{:S(2)}, u32[]{:S(2)}) collective-permute-start(f32[4,136,128]{2,1,0:T(8,128)S(1)} %get-tuple-element.43), channel_id=1, source_target_pairs={{0,2},{1,3},{2,0},{3,1},{4,6},{5,7},{6,4},{7,5},{8,10},{9,11},{10,... | collective-permute-start | bytes 835592 | tf_op jit(solution)/shard_map/ppermute | solution.py:541
  49.8 5.0 %collective-permute-start.7 = (f32[2,128,128]{2,1,0:T(8,128)S(1)}, f32[2,128,128]{2,1,0:T(8,128)S(1)}, u32[]{:S(2)}, u32[]{:S(2)}) collective-permute-start(f32[2,128,128]{2,1,0:T(8,128)S(1)} %dynamic-slice_bitcast_fusion.1), channel_id=1, source_target_pairs={{0,2},{1,3},{2,0},{3,1},{4,6},{5,7},{6,4},{7,5},{8,10},{9,11},{10,... | collective-permute-start | bytes 393224 | tf_op jit(solution)/shard_map/ppermute | solution.py:541
  50.6 5.1 %collective-permute-start.4 = (f32[2,136,128]{2,1,0:T(8,128)S(1)}, f32[2,136,128]{2,1,0:T(8,128)S(1)}, u32[]{:S(2)}, u32[]{:S(2)}) collective-permute-start(f32[2,136,128]{2,1,0:T(8,128)S(1)} %dynamic-slice_bitcast_fusion), channel_id=1, source_target_pairs={{0,4},{1,5},{2,6},{3,7},{4,0},{5,1},{6,2},{7,3},{8,12},{9,13},{10,... | collective-permute-start | bytes 417800 | tf_op jit(solution)/shard_map/ppermute | solution.py:541
  54.8 4.3 %collective-permute-start.8 = (f32[1,128,128]{2,1,0:T(8,128)S(1)}, f32[1,128,128]{2,1,0:T(8,128)S(1)}, u32[]{:S(2)}, u32[]{:S(2)}) collective-permute-start(f32[1,128,128]{2,1,0:T(8,128)S(1)} %constant_dynamic-slice_fusion), channel_id=1, source_target_pairs={{0,4},{1,5},{2,6},{3,7},{4,0},{5,1},{6,2},{7,3},{8,12},{9,13},{10,... | collective-permute-start | bytes 196616 | tf_op jit(solution)/shard_map/ppermute | solution.py:541
  55.7 4.4 %collective-permute-start.5 = (f32[1,136,128]{2,1,0:T(8,128)S(1)}, f32[1,136,128]{2,1,0:T(8,128)S(1)}, u32[]{:S(2)}, u32[]{:S(2)}) collective-permute-start(f32[1,136,128]{2,1,0:T(8,128)S(1)} %constant_dynamic-slice_fusion.1), channel_id=1, source_target_pairs={{0,8},{1,9},{2,10},{3,11},{4,12},{5,13},{6,14},{7,15},{8,0},{9,1},... | collective-permute-start | bytes 208904 | tf_op jit(solution)/shard_map/ppermute | solution.py:541
  60.1 8.0 %collective-permute-start.11 = (f32[1,264,128]{2,1,0:T(8,128)S(1)}, f32[1,264,128]{2,1,0:T(8,128)S(1)}, u32[]{:S(2)}, u32[]{:S(2)}) collective-permute-start(f32[1,264,128]{2,1,0:T(8,128)S(1)} %pad_maximum_fusion.3), channel_id=1, source_target_pairs={{0,24},{1,25},{2,26},{3,27},{4,28},{5,29},{6,30},{7,31},{8,16},{9,... | collective-permute-start | bytes 405512 | tf_op jit(solution)/shard_map/ppermute | solution.py:541
  63.8 8.6 %collective-permute-start.10 = (f32[1,264,128]{2,1,0:T(8,128)S(1)}, f32[1,264,128]{2,1,0:T(8,128)S(1)}, u32[]{:S(2)}, u32[]{:S(2)}) collective-permute-start(f32[1,264,128]{2,1,0:T(8,128)S(1)} %pad_maximum_fusion.3), channel_id=1, source_target_pairs={{0,16},{1,17},{2,18},{3,19},{4,20},{5,21},{6,22},{7,23},{8,24},{9,... | collective-permute-start | bytes 405512 | tf_op jit(solution)/shard_map/ppermute | solution.py:541
  63.8 8.6 %collective-permute-start.9 = (f32[1,264,128]{2,1,0:T(8,128)S(1)}, f32[1,264,128]{2,1,0:T(8,128)S(1)}, u32[]{:S(2)}, u32[]{:S(2)}) collective-permute-start(f32[1,264,128]{2,1,0:T(8,128)S(1)} %pad_maximum_fusion.3), channel_id=1, source_target_pairs={{0,8},{1,9},{2,10},{3,11},{4,12},{5,13},{6,14},{7,15},{8,0},{9,1},... | collective-permute-start | bytes 405512 | tf_op jit(solution)/shard_map/ppermute | solution.py:541
  72.5 7.4 %collective-permute-start.12 = (f32[4,136,128]{2,1,0:T(8,128)S(1)}, f32[4,136,128]{2,1,0:T(8,128)S(1)}, u32[]{:S(2)}, u32[]{:S(2)}) collective-permute-start(f32[4,136,128]{2,1,0:T(8,128)S(1)} %slice.8), channel_id=1, source_target_pairs={{0,2},{1,3},{2,0},{3,1},{4,6},{5,7},{6,4},{7,5},{8,10},{9,11},{10,... | collective-permute-start | bytes 835592 | tf_op jit(solution)/shard_map/ppermute | solution.py:541
  74.2 6.8 %collective-permute-start.13 = (f32[4,128,128]{2,1,0:T(8,128)S(1)}, f32[4,128,128]{2,1,0:T(8,128)S(1)}, u32[]{:S(2)}, u32[]{:S(2)}) collective-permute-start(f32[4,128,128]{2,1,0:T(8,128)S(1)} %slice.9), channel_id=1, source_target_pairs={{0,4},{1,5},{2,6},{3,7},{4,0},{5,1},{6,2},{7,3},{8,12},{9,13},{10,... | collective-permute-start | bytes 786440 | tf_op jit(solution)/shard_map/ppermute | solution.py:541
  75.6 8.8 %collective-permute-start.16 = (f32[4,264,128]{2,1,0:T(8,128)S(1)}, f32[4,264,128]{2,1,0:T(8,128)S(1)}, u32[]{:S(2)}, u32[]{:S(2)}) collective-permute-start(f32[4,264,128]{2,1,0:T(8,128)S(1)} %pad_maximum_fusion.1.refs_0_), channel_id=1, source_target_pairs={{0,1},{1,0},{2,3},{3,2},{4,5},{5,4},{6,7},{7,6},{8,9},{9,8},{10,11... | collective-permute-start | bytes 1622024 | tf_op jit(solution)/shard_map/ppermute | solution.py:541
  79.9 12.6 %collective-permute-start.14 = (f32[8,136,128]{2,1,0:T(8,128)S(1)}, f32[8,136,128]{2,1,0:T(8,128)S(1)}, u32[]{:S(2)}, u32[]{:S(2)}) collective-permute-start(f32[8,136,128]{2,1,0:T(8,128)S(1)} %pad_maximum_fusion), channel_id=1, source_target_pairs={{0,4},{1,5},{2,6},{3,7},{4,0},{5,1},{6,2},{7,3},{8,12},{9,13},{10,... | collective-permute-start | bytes 1671176 | tf_op jit(solution)/shard_map/ppermute | solution.py:541
  81.1 10.9 %collective-permute-start.15 = (f32[8,128,128]{2,1,0:T(8,128)S(1)}, f32[8,128,128]{2,1,0:T(8,128)S(1)}, u32[]{:S(2)}, u32[]{:S(2)}) collective-permute-start(f32[8,128,128]{2,1,0:T(8,128)S(1)} %pad_maximum_fusion.2), channel_id=1, source_target_pairs={{0,2},{1,3},{2,0},{3,1},{4,6},{5,7},{6,4},{7,5},{8,10},{9,11},{10,... | collective-permute-start | bytes 1572872 | tf_op jit(solution)/shard_map/ppermute | solution.py:541
  82.4 1.9 %collective-permute-start.17 = (f32[4,136,128]{2,1,0:T(8,128)S(1)}, f32[4,136,128]{2,1,0:T(8,128)S(1)}, u32[]{:S(2)}, u32[]{:S(2)}) collective-permute-start(f32[4,136,128]{2,1,0:T(8,128)S(1)} %collective-permute-done.12.refs_1_), channel_id=1, source_target_pairs={{0,1},{1,0},{2,3},{3,2},{4,5},{5,4},{6,7},{7,6},{8,9},{9,8},{10,11... | collective-permute-start | bytes 835592 | tf_op jit(solution)/shard_map/ppermute | solution.py:541
  82.4 1.9 %collective-permute-start.18 = (f32[4,128,128]{2,1,0:T(8,128)S(1)}, f32[4,128,128]{2,1,0:T(8,128)S(1)}, u32[]{:S(2)}, u32[]{:S(2)}) collective-permute-start(f32[4,128,128]{2,1,0:T(8,128)S(1)} %collective-permute-done.13.refs_2_), channel_id=1, source_target_pairs={{0,1},{1,0},{2,3},{3,2},{4,5},{5,4},{6,7},{7,6},{8,9},{9,8},{10,11... | collective-permute-start | bytes 786440 | tf_op jit(solution)/shard_map/ppermute | solution.py:541
  92.6 2.7 %collective-permute-start.19 = (f32[8,136,128]{2,1,0:T(8,128)S(1)}, f32[8,136,128]{2,1,0:T(8,128)S(1)}, u32[]{:S(2)}, u32[]{:S(2)}) collective-permute-start(f32[8,136,128]{2,1,0:T(8,128)S(1)} %collective-permute-done.14.refs_3_), channel_id=1, source_target_pairs={{0,1},{1,0},{2,3},{3,2},{4,5},{5,4},{6,7},{7,6},{8,9},{9,8},{10,11... | collective-permute-start | bytes 1671176 | tf_op jit(solution)/shard_map/ppermute | solution.py:541
  92.6 2.7 %collective-permute-start.20 = (f32[8,128,128]{2,1,0:T(8,128)S(1)}, f32[8,128,128]{2,1,0:T(8,128)S(1)}, u32[]{:S(2)}, u32[]{:S(2)}) collective-permute-start(f32[8,128,128]{2,1,0:T(8,128)S(1)} %collective-permute-done.15.refs_4_), channel_id=1, source_target_pairs={{0,1},{1,0},{2,3},{3,2},{4,5},{5,4},{6,7},{7,6},{8,9},{9,8},{10,11... | collective-permute-start | bytes 1572872 | tf_op jit(solution)/shard_map/ppermute | solution.py:541

commit v7 on v6

--- a/solution.py
+++ b/solution.py
@@ -349,14 +349,14 @@
 
 def backward_kernel(
     inv_sets, owner_ref, sums_ref, near_ref, far_ref, both_ref, hidden_ref, curve_ref, mixed_ref, pred_ref, win_ref,
-    feat_ref, w_mid_hbm, b_out_ref, keep_a, send_a, keep_b, send_b, prices_ref,
+    feat_ref, w_mid_hbm, b_out_ref, keep_x, send_x, keep_y, send_y, keep_z, send_z, prices_ref,
     left_ref, back_ref, slope_ref, even_delta, odd_delta, delta_in_ref, own_delta_ref, bias_ref,
-    read_ref, extra_ref, grad_ref, sem,
+    read_ref, pieces_ref, sem,
 ):
     bf16 = jnp.bfloat16
     sets = sums_ref.shape[0]
     rows = hidden_ref.shape[1]
-    groups = 2 * keep_a.shape[0]
+    groups = pieces_ref.shape[0]
     piece_rows = WIDTH // groups
     cols = WIDTH // 4
     owner = owner_ref[0]
@@ -404,7 +404,12 @@
         delta_in_ref[:, here] = (backward * curve).astype(bf16)
 
     for c in CHUNKS:
-        grad_ref[c, :] = dot_rows(hidden_ref[c, :], own_delta_ref[...])
+        total = dot_rows(hidden_ref[c, :], own_delta_ref[...])
+        for first in range(0, CHUNK, piece_rows):
+            j = (c.start + first) // piece_rows
+            part = total[first : first + piece_rows]
+            pieces_ref[j, 0:piece_rows, :] = part[:, :LANES]
+            pieces_ref[j, piece_rows + 8 :, :] = part[:, LANES:]
     extra = [dot_rows(delta_in_ref[...], feat_ref[...]).T[0:7]]
     extra.append(jnp.sum(bias_ref[...].T, axis=0, keepdims=True))
     extra.append(jnp.sum(read_ref[...].T, axis=0, keepdims=True))
@@ -412,25 +417,29 @@
     extra.append(jnp.broadcast_to(total, (1, cols)))
     extra.append(jnp.zeros((6, cols), jnp.float32))
     extra = jnp.concatenate(extra, 0)
-    extra_ref[...] = jnp.zeros_like(extra_ref)
-    for j in range(4):
+    for j in range(groups):
         lanes = slice((j % 2) * LANES, (j % 2 + 1) * LANES)
-        extra_ref[j] = extra[8 * (j // 2) : 8 * (j // 2) + 8, lanes]
+        part = extra[8 * (j // 2) : 8 * (j // 2) + 8, lanes] if j < 4 else jnp.zeros((8, LANES))
+        pieces_ref[j, piece_rows : piece_rows + 8, :] = part
     group = (owner // 2) % groups
-    low, top = group % 2, group // (groups // 2)
-    for i in range(groups // 2):
-        for a_ref, b_ref, flip in ((keep_a, keep_b, 0), (send_a, send_b, 1)):
-            j = 2 * i + (low ^ flip)
-            piece = pl.ds(pl.multiple_of(j * piece_rows, piece_rows), piece_rows)
-            a_ref[i, 0:piece_rows, :] = grad_ref[piece, 0:LANES]
-            a_ref[i, piece_rows:, :] = extra_ref[j]
-            j = i + (top ^ flip) * (groups // 2)
-            piece = pl.ds(pl.multiple_of(j * piece_rows, piece_rows), piece_rows)
-            b_ref[i] = grad_ref[piece, LANES:]
+    cuts = part_cuts(groups)
+    for bit, (keep, send) in enumerate(((keep_x, send_x), (keep_y, send_y), (keep_z, send_z))):
+        mine = (group // 2**bit) % 2
+        for i in range(groups // 2):
+            base = (i >> bit << (bit + 1)) + (i & (2**bit - 1))
+            keep[i] = pieces_ref[base + mine * 2**bit, cuts[bit] : cuts[bit + 1], :]
+            send[i] = pieces_ref[base + (1 - mine) * 2**bit, cuts[bit] : cuts[bit + 1], :]
+
+
+def part_cuts(groups):
+    rows = 2 * (WIDTH // groups) + 8
+    third = rows // 24 * 8
+    return (0, third, 2 * third, rows)
 
 
 def backward(owner, sums, saved, win, feat, w_mid, b_out, inv_sets, groups):
     sets = sums[0].shape[0]
+    cuts = part_cuts(groups)
     rows = sets * PAIRS
     cols = WIDTH // 4
     vmem = pl.BlockSpec(memory_space=pltpu.VMEM)
@@ -439,10 +448,11 @@
     return pl.pallas_call(
         functools.partial(backward_kernel, inv_sets),
         in_specs=[smem] + [vmem] * 10 + [hbm, smem],
-        out_specs=[vmem] * 5,
+        out_specs=[vmem] * 7,
         out_shape=[
-            jax.ShapeDtypeStruct((groups // 2, WIDTH // groups + more, LANES), jnp.float32)
-            for more in (8, 8, 0, 0)
+            jax.ShapeDtypeStruct((groups // 2, stop - start, LANES), jnp.float32)
+            for start, stop in zip(cuts, cuts[1:])
+            for _ in range(2)
         ]
         + [jax.ShapeDtypeStruct((sets // 4, PAIRS), jnp.float32)],
         scratch_shapes=[
@@ -455,8 +465,7 @@
             pltpu.VMEM((cols, rows), jnp.bfloat16),
             pltpu.VMEM((cols, LANES), jnp.float32),
             pltpu.VMEM((cols, LANES), jnp.float32),
-            pltpu.VMEM((max(groups, 4), 8, LANES), jnp.float32),
-            pltpu.VMEM((WIDTH, cols), jnp.float32),
+            pltpu.VMEM((groups, 2 * (WIDTH // groups) + 8, LANES), jnp.float32),
             pltpu.SemaphoreType.DMA,
         ],
         compiler_params=pltpu.CompilerParams(vmem_limit_bytes=BACKWARD_VMEM),
@@ -580,24 +589,27 @@
 
     place = jnp.stack([owner, jnp.int32(top)])
     saved = forward(place, b_mid, w_out, win, weights, feat)
-    keep_a, send_a, keep_b, send_b, prices = backward(
+    *parts, prices = backward(
         owner, sums, saved, win, feat, w_mid, b_out, 1.0 / set_count, groups
     )
 
     bits = [bit for bit in range(groups.bit_length() - 1)]
-    part_a = keep_a + swap(send_a, 2, devices)
-    part_b = keep_b + swap(send_b, top // 2, devices)
-    left_a, left_b = bits[1:], bits[:-1]
-    while left_a:
-        part_a = halved(part_a, left_a, left_a[0], group, devices)
-        part_b = halved(part_b, left_b, left_b[0], group, devices)
-        left_a, left_b = left_a[1:], left_b[1:]
-
-    own = jnp.concatenate([part_a, part_b], axis=1)
+    orders = [bits[first:] + bits[:first] for first in range(3)]
+    parts = [
+        parts[2 * n] + swap(parts[2 * n + 1], 2 << order[0], devices)
+        for n, order in enumerate(orders)
+    ]
+    for step in range(1, len(bits)):
+        parts = [
+            halved(part, sorted(order[step:]), order[step], group, devices)
+            for part, order in zip(parts, orders)
+        ]
+
+    own = jnp.concatenate(parts, axis=1)
     far = (0, top // 2, top, top + top // 2)
     whole = jnp.concatenate([own] + [swap(own, mask, devices) for mask in far[1:]], axis=0)
     received = [(whole, far, ("left", "extra", "right"))]
-    split = part_a.shape[1]
+    split = WIDTH // groups + 8
     held_a, held_b = whole[:, :split], whole[:, split:]
     order = [2 << bit for bit in bits[:-1]]
     masks_a = masks_b = far

time: 98.8 us -> 97.1 us (0.983)
  waiting for transfers between devices: 38.2 us -> 32.8 us
  starting transfers between devices: 26.2 us -> 29.6 us
    ppermute x21 -> x24, waiting for transfers between devices: 36.6 us -> 31.2 us  [swap(): return lax.ppermute(array, 'paths', [(i, i ^ bit) for i in range(devices)])]
    ppermute x21 -> x24, starting transfers between devices: 20 us -> 23.4 us  [swap(): return lax.ppermute(array, 'paths', [(i, i ^ bit) for i in range(devices)])]
  transfers between devices with their start and end apart: 22 -> 25, of which waited for: 14 -> 13; matrix products, arithmetic and copies ran while one was open for 1% -> 1% of each run, Pallas kernels for 16% -> 16%
where the time goes in v7:
time: 97.1 us; the launch traced here: 96.6 us
  waiting for transfers between devices  32.8 us (34%)
  Pallas kernels  31.6 us (33%)
  starting transfers between devices  29.6 us (30%)
  between operations  1.47 us (2%)
    ppermute x24, waiting for transfers between devices, swap(): return lax.ppermute(array, 'paths', [(i, i ^ bit) for i in range(devices)])  31.2 us
    ppermute x24, starting transfers between devices, swap(): return lax.ppermute(array, 'paths', [(i, i ^ bit) for i in range(devices)])  23.4 us
    pallas_call x1, Pallas kernels, forward(): pl.pallas_call(forward_kernel, in_specs=[smem] + [vmem] * 5, out_specs=[v...  12.3 us
    pallas_call x1, Pallas kernels, backward(): pl.pallas_call(functools.partial(backward_kernel, inv_sets), in_specs=[sm...  6.75 us
    pallas_call x1, Pallas kernels, payoff_sums(): pl.pallas_call(pricing_kernel, grid=(steps,), in_specs=[pl.BlockSpec((4,...  6.36 us
    all_to_all x1, starting transfers between devices, on_device(): lax.all_to_all(sums, 'paths', 0, 0, axis_index_groups=lanes, tiled=True)  6.18 us
    pallas_call x1, Pallas kernels, prepare(): pl.pallas_call(functools.partial(prepare_kernel, sets), in_specs=[smem, v...  3.15 us
    pallas_call x1, Pallas kernels, scaled(): pl.pallas_call(functools.partial(scaling_kernel, layout, groups), in_spec...  3.07 us
  transfers between devices with their start and end apart: 25, of which 13 were waited for; matrix products, arithmetic and copies ran while one was open for 1% of the time, Pallas kernels for 16%

profile of v7, /device:TPU:0, one launch (start us, length us, event | category | flops | bytes accessed | tf_op | source)
XLA Modules:
  0.0 96.6 jit_solution(15326798185717757132)
XLA Ops:
  0.6 6.4 %pricing.1 = f32[8,2,16,88]{3,2,1,0:T(8,128)} custom-call(f32[4,256]{1,0:T(4,128)} %bitcast.38, bf16[2,64,128]{2,1,0:T(8,128)(2,1)} %inc_ref.1), custom_call_target="tpu_custom_call" | custom-call | tf_op jit(solution)/shard_map/pricing/pallas_call | solution.py:127
  7.0 6.2 %all-to-all-start = ((f32[8,32,88]{2,1,0:T(8,128)}), f32[8,32,88]{2,1,0:T(8,128)S(1)}, u32[]{:S(2)}, u32[]{:S(2)}) async-start(f32[8,32,88]{2,1,0:T(8,128)} %bitcast.2), calls=%async_computation | async-start | bytes 262144 | tf_op jit(solution)/shard_map/all_to_all | solution.py:585
  13.2 0.7 reshape.62.w_out_ref
  14.5 3.1 %prepare.1 = (bf16[1024,16]{1,0:T(8,128)(2,1)S(1)}, bf16[1024,1024]{1,0:T(8,128)(2,1)S(1)}, bf16[16,2816]{1,0:T(8,128)(2,1)S(1)}) custom-call(s32[1]{0:T(128)} %bitcast.owner_ref, f32[4,256]{1,0:T(4,128)} %bitcast.39, bf16[6,1024]{1,0:T(8,128)(2,1)} %w_in_hbm.1, f32[1,1024]{1,0:T(1,128)} %bitcast.40, bf16[1024,1024]{1,0:T(8,128)(2,1)} %w_mid_hbm.3), custom_call_target="tpu_custom_call" | custom-call | tf_op jit(solution)/shard_map/prepare/pallas_call | solution.py:232
  17.7 0.1 pad_add_fusion.owner_ref
  17.7 1.5 %all-to-all-done = f32[8,32,88]{2,1,0:T(8,128)S(1)} async-done(((f32[8,32,88]{2,1,0:T(8,128)}), f32[8,32,88]{2,1,0:T(8,128)S(1)}, u32[]{:S(2)}, u32[]{:S(2)}) %all-to-all-start) | async-done | bytes 90144 | tf_op jit(solution)/shard_map/all_to_all | solution.py:585
  19.3 0.1 collective-permute-start
  19.4 2.7 %collective-permute-start.1 = (f32[32,88]{1,0:T(8,128)S(1)}, f32[32,88]{1,0:T(8,128)S(1)}, u32[]{:S(2)}, u32[]{:S(2)}) collective-permute-start(f32[32,88]{1,0:T(8,128)S(1)} %broadcast_multiply_fusion.sums_ref), channel_id=1, source_target_pairs={{0,16},{1,17},{2,18},{3,19},{4,20},{5,21},{6,22},{7,23},{8,24},{9,... | collective-permute-start | bytes 33800 | tf_op jit(solution)/shard_map/ppermute | solution.py:550
  22.0 0.1 collective-permute-start.2
  22.1 12.3 %forward.1 = (bf16[1024,2816]{1,0:T(8,128)(2,1)S(1)}, f32[1024,2816]{1,0:T(8,128)S(1)}, bf16[256,2816]{1,0:T(8,128)(2,1)S(1)}, f32[1,2816]{1,0:T(1,128)S(1)}) custom-call(s32[2]{0:T(128)S(1)} %pad_add_fusion.owner_ref, f32[1,1024]{1,0:T(1,128)} %bitcast.41, bf16[1,1024]{1,0:T(2,128)(2,1)S(1)} %reshape.62.w_out_ref, ...), custom_call_target="tpu_custom_call" | custom-call | flops 6090129408 | bytes 4194304 | tf_op jit(solution)/shard_map/forward/pallas_call | solution.py:331
  34.5 0.0 collective-permute-done.near_ref
  34.5 0.0 collective-permute-done.1.far_ref
  34.5 6.7 %backward.1 = (f32[4,88,128]{2,1,0:T(8,128)S(1)}, f32[4,88,128]{2,1,0:T(8,128)S(1)}, f32[4,88,128]{2,1,0:T(8,128)S(1)}, f32[4,88,128]{2,1,0:T(8,128)S(1)}, f32[4...) custom-call(s32[1]{0:T(128)} %bitcast.owner_ref, f32[32,88]{1,0:T(8,128)S(1)} %broadcast_multiply_fusion.sums_ref, ...), custom_call_target="tpu_custom_call" | custom-call | tf_op jit(solution)/shard_map/backward/pallas_call | solution.py:448
  41.2 0.8 collective-permute-start.9
  42.0 1.2 %collective-permute-start.6 = (f32[4,88,128]{2,1,0:T(8,128)S(1)}, f32[4,88,128]{2,1,0:T(8,128)S(1)}, u32[]{:S(2)}, u32[]{:S(2)}) collective-permute-start(f32[4,88,128]{2,1,0:T(8,128)S(1)} %get-tuple-element.47), channel_id=1, source_target_pairs={{0,4},{1,5},{2,6},{3,7},{4,0},{5,1},{6,2},{7,3},{8,12},{9,13},{10,... | collective-permute-start | bytes 540680 | tf_op jit(solution)/shard_map/ppermute | solution.py:550
  43.3 1.5 %collective-permute-start.3 = (f32[4,88,128]{2,1,0:T(8,128)S(1)}, f32[4,88,128]{2,1,0:T(8,128)S(1)}, u32[]{:S(2)}, u32[]{:S(2)}) collective-permute-start(f32[4,88,128]{2,1,0:T(8,128)S(1)} %get-tuple-element.45), channel_id=1, source_target_pairs={{0,2},{1,3},{2,0},{3,1},{4,6},{5,7},{6,4},{7,5},{8,10},{9,11},{10,... | collective-permute-start | bytes 540680 | tf_op jit(solution)/shard_map/ppermute | solution.py:550
  44.7 3.4 %collective-permute-done.9 = f32[4,88,128]{2,1,0:T(8,128)S(1)} collective-permute-done((f32[4,88,128]{2,1,0:T(8,128)S(1)}, f32[4,88,128]{2,1,0:T(8,128)S(1)}, u32[]{:S(2)}, u32[]{:S(2)}) %collective-permute-start.9) | collective-permute-done | bytes 180256 | tf_op jit(solution)/shard_map/ppermute | solution.py:550
  48.2 0.6 collective-permute-start.10
  48.7 0.0 collective-permute-done.6
  48.8 1.5 %collective-permute-start.7 = (f32[2,88,128]{2,1,0:T(8,128)S(1)}, f32[2,88,128]{2,1,0:T(8,128)S(1)}, u32[]{:S(2)}, u32[]{:S(2)}) collective-permute-start(f32[2,88,128]{2,1,0:T(8,128)S(1)} %dynamic-slice_bitcast_fusion.1), channel_id=1, source_target_pairs={{0,8},{1,9},{2,10},{3,11},{4,12},{5,13},{6,14},{7,15},{8,0},{9,1},... | collective-permute-start | bytes 270344 | tf_op jit(solution)/shard_map/ppermute | solution.py:550
  50.3 0.0 collective-permute-done.3
  50.4 1.5 %collective-permute-start.4 = (f32[2,88,128]{2,1,0:T(8,128)S(1)}, f32[2,88,128]{2,1,0:T(8,128)S(1)}, u32[]{:S(2)}, u32[]{:S(2)}) collective-permute-start(f32[2,88,128]{2,1,0:T(8,128)S(1)} %dynamic-slice_bitcast_fusion.2), channel_id=1, source_target_pairs={{0,4},{1,5},{2,6},{3,7},{4,0},{5,1},{6,2},{7,3},{8,12},{9,13},{10,... | collective-permute-start | bytes 270344 | tf_op jit(solution)/shard_map/ppermute | solution.py:550
  51.9 0.9 collective-permute-done.10
  52.8 0.6 collective-permute-start.11
  53.4 0.0 collective-permute-done.7
  53.4 1.5 %collective-permute-start.8 = (f32[1,88,128]{2,1,0:T(8,128)S(1)}, f32[1,88,128]{2,1,0:T(8,128)S(1)}, u32[]{:S(2)}, u32[]{:S(2)}) collective-permute-start(f32[1,88,128]{2,1,0:T(8,128)S(1)} %constant_dynamic-slice_fusion.1), channel_id=1, source_target_pairs={{0,2},{1,3},{2,0},{3,1},{4,6},{5,7},{6,4},{7,5},{8,10},{9,11},{10,... | collective-permute-start | bytes 135176 | tf_op jit(solution)/shard_map/ppermute | solution.py:550
  55.0 0.3 collective-permute-done.4
  55.3 1.2 %collective-permute-start.5 = (f32[1,88,128]{2,1,0:T(8,128)S(1)}, f32[1,88,128]{2,1,0:T(8,128)S(1)}, u32[]{:S(2)}, u32[]{:S(2)}) collective-permute-start(f32[1,88,128]{2,1,0:T(8,128)S(1)} %constant_dynamic-slice_fusion.2), channel_id=1, source_target_pairs={{0,8},{1,9},{2,10},{3,11},{4,12},{5,13},{6,14},{7,15},{8,0},{9,1},... | collective-permute-start | bytes 135176 | tf_op jit(solution)/shard_map/ppermute | solution.py:550
  56.5 0.4 collective-permute-done.11
  56.9 0.6 collective-permute-done.8
  57.6 1.9 %collective-permute-done.5 = f32[1,88,128]{2,1,0:T(8,128)S(1)} collective-permute-done((f32[1,88,128]{2,1,0:T(8,128)S(1)}, f32[1,88,128]{2,1,0:T(8,128)S(1)}, u32[]{:S(2)}, u32[]{:S(2)}) %collective-permute-start.5) | collective-permute-done | bytes 45088 | tf_op jit(solution)/shard_map/ppermute | solution.py:550
  59.5 3.2 %collective-permute-start.14 = (f32[1,264,128]{2,1,0:T(8,128)S(1)}, f32[1,264,128]{2,1,0:T(8,128)S(1)}, u32[]{:S(2)}, u32[]{:S(2)}) collective-permute-start(f32[1,264,128]{2,1,0:T(8,128)S(1)} %pad_maximum_fusion.3), channel_id=1, source_target_pairs={{0,24},{1,25},{2,26},{3,27},{4,28},{5,29},{6,30},{7,31},{8,16},{9,... | collective-permute-start | bytes 405512 | tf_op jit(solution)/shard_map/ppermute | solution.py:550
  62.7 1.3 %collective-permute-start.12 = (f32[1,264,128]{2,1,0:T(8,128)S(1)}, f32[1,264,128]{2,1,0:T(8,128)S(1)}, u32[]{:S(2)}, u32[]{:S(2)}) collective-permute-start(f32[1,264,128]{2,1,0:T(8,128)S(1)} %pad_maximum_fusion.3), channel_id=1, source_target_pairs={{0,8},{1,9},{2,10},{3,11},{4,12},{5,13},{6,14},{7,15},{8,0},{9,1},... | collective-permute-start | bytes 405512 | tf_op jit(solution)/shard_map/ppermute | solution.py:550
  63.9 3.1 %collective-permute-done.14 = f32[1,264,128]{2,1,0:T(8,128)S(1)} collective-permute-done((f32[1,264,128]{2,1,0:T(8,128)S(1)}, f32[1,264,128]{2,1,0:T(8,128)S(1)}, u32[]{:S(2)}, u32[]{:S(2)}) %collective-permute-start.14) | collective-permute-done | bytes 135200 | tf_op jit(solution)/shard_map/ppermute | solution.py:550
  67.0 4.2 %collective-permute-done.13 = f32[1,264,128]{2,1,0:T(8,128)S(1)} collective-permute-done((f32[1,264,128]{2,1,0:T(8,128)S(1)}, f32[1,264,128]{2,1,0:T(8,128)S(1)}, u32[]{:S(2)}, u32[]{:S(2)}) %collective-permute-start.13) | collective-permute-done | bytes 135200 | tf_op jit(solution)/shard_map/ppermute | solution.py:550
  71.2 0.0 collective-permute-done.12
  71.3 0.7 collective-permute-start.15
  72.0 1.4 %collective-permute-start.16 = (f32[4,128,128]{2,1,0:T(8,128)S(1)}, f32[4,128,128]{2,1,0:T(8,128)S(1)}, u32[]{:S(2)}, u32[]{:S(2)}) collective-permute-start(f32[4,128,128]{2,1,0:T(8,128)S(1)} %slice.9), channel_id=1, source_target_pairs={{0,4},{1,5},{2,6},{3,7},{4,0},{5,1},{6,2},{7,3},{8,12},{9,13},{10,... | collective-permute-start | bytes 786440 | tf_op jit(solution)/shard_map/ppermute | solution.py:550
  73.5 0.0 collective-permute-start.19
  73.5 4.8 %collective-permute-done.15.refs_1_ = f32[4,136,128]{2,1,0:T(8,128)S(1)} collective-permute-done((f32[4,136,128]{2,1,0:T(8,128)S(1)}, f32[4,136,128]{2,1,0:T(8,128)S(1)}, u32[]{:S(2)}, u32[]{:S(2)}) %collective-permute-start.15) | collective-permute-done | bytes 278560 | tf_op jit(solution)/shard_map/ppermute | solution.py:550
  78.3 1.5 %collective-permute-start.17 = (f32[8,136,128]{2,1,0:T(8,128)S(1)}, f32[8,136,128]{2,1,0:T(8,128)S(1)}, u32[]{:S(2)}, u32[]{:S(2)}) collective-permute-start(f32[8,136,128]{2,1,0:T(8,128)S(1)} %pad_maximum_fusion), channel_id=1, source_target_pairs={{0,4},{1,5},{2,6},{3,7},{4,0},{5,1},{6,2},{7,3},{8,12},{9,13},{10,... | collective-permute-start | bytes 1671176 | tf_op jit(solution)/shard_map/ppermute | solution.py:550
  79.8 1.0 %collective-permute-start.18 = (f32[8,128,128]{2,1,0:T(8,128)S(1)}, f32[8,128,128]{2,1,0:T(8,128)S(1)}, u32[]{:S(2)}, u32[]{:S(2)}) collective-permute-start(f32[8,128,128]{2,1,0:T(8,128)S(1)} %pad_maximum_fusion.2), channel_id=1, source_target_pairs={{0,2},{1,3},{2,0},{3,1},{4,6},{5,7},{6,4},{7,5},{8,10},{9,11},{10,... | collective-permute-start | bytes 1572872 | tf_op jit(solution)/shard_map/ppermute | solution.py:550
  80.9 0.5 collective-permute-start.21
  81.4 1.4 %collective-permute-done.21.refs_7_ = f32[4,128,128]{2,1,0:T(8,128)S(1)} collective-permute-done((f32[4,128,128]{2,1,0:T(8,128)S(1)}, f32[4,128,128]{2,1,0:T(8,128)S(1)}, u32[]{:S(2)}, u32[]{:S(2)}) %collective-permute-start.21) | collective-permute-done | bytes 262176 | tf_op jit(solution)/shard_map/ppermute | solution.py:550
  82.8 8.0 %collective-permute-done.18.refs_4_ = f32[8,128,128]{2,1,0:T(8,128)S(1)} collective-permute-done((f32[8,128,128]{2,1,0:T(8,128)S(1)}, f32[8,128,128]{2,1,0:T(8,128)S(1)}, u32[]{:S(2)}, u32[]{:S(2)}) %collective-permute-start.18) | collective-permute-done | bytes 524320 | tf_op jit(solution)/shard_map/ppermute | solution.py:550
  90.9 0.5 collective-permute-start.23
  91.4 2.2 %collective-permute-done.23.refs_9_ = f32[8,128,128]{2,1,0:T(8,128)S(1)} collective-permute-done((f32[8,128,128]{2,1,0:T(8,128)S(1)}, f32[8,128,128]{2,1,0:T(8,128)S(1)}, u32[]{:S(2)}, u32[]{:S(2)}) %collective-permute-start.23) | collective-permute-done | bytes 524320 | tf_op jit(solution)/shard_map/ppermute | solution.py:550
  93.6 3.1 %scaling.1 = (f32[6,1024]{1,0:T(8,128)}, f32[1,1024]{1,0:T(1,128)}, f32[1024,1024]{1,0:T(8,128)}, f32[1,1024]{1,0:T(1,128)}, f32[1,1024]{1,0:T(1,128)}, /*index=5*/f32[1,1]{1,0:T(1,128)}) custom-call(s32[1]{0:T(128)} %bitcast.owner_ref, f32[4,264,128]{2,1,0:T(8,128)S(1)} %pad_maximum_fusion.1.refs_0_, f32[4,136,128]{2,1,0:T(8,128)S(1)} %collective-permute-done.15.refs_1_, ...), custom_call_target="tpu_custom_call" | custom-call | tf_op jit(solution)/shard_map/scaling/pallas_call | solution.py:535
  (32 shorter events, 0.4 us)
Async XLA Ops:
  7.0 12.3 %all-to-all-start = ((f32[8,32,88]{2,1,0:T(8,128)}), f32[8,32,88]{2,1,0:T(8,128)S(1)}, u32[]{:S(2)}, u32[]{:S(2)}) async-start(f32[8,32,88]{2,1,0:T(8,128)} %bitcast.2), calls=%async_computation | async-start | bytes 262144 | tf_op jit(solution)/shard_map/all_to_all | solution.py:585
  19.3 15.2 %collective-permute-start = (f32[32,88]{1,0:T(8,128)S(1)}, f32[32,88]{1,0:T(8,128)S(1)}, u32[]{:S(2)}, u32[]{:S(2)}) collective-permute-start(f32[32,88]{1,0:T(8,128)S(1)} %broadcast_multiply_fusion.sums_ref), channel_id=1, source_target_pairs={{0,1},{1,0},{2,3},{3,2},{4,5},{5,4},{6,7},{7,6},{8,9},{9,8},{10,11... | collective-permute-start | bytes 33800 | tf_op jit(solution)/shard_map/ppermute | solution.py:550
  19.4 15.1 %collective-permute-start.1 = (f32[32,88]{1,0:T(8,128)S(1)}, f32[32,88]{1,0:T(8,128)S(1)}, u32[]{:S(2)}, u32[]{:S(2)}) collective-permute-start(f32[32,88]{1,0:T(8,128)S(1)} %broadcast_multiply_fusion.sums_ref), channel_id=1, source_target_pairs={{0,16},{1,17},{2,18},{3,19},{4,20},{5,21},{6,22},{7,23},{8,24},{9,... | collective-permute-start | bytes 33800 | tf_op jit(solution)/shard_map/ppermute | solution.py:550
  22.0 12.4 %collective-permute-start.2 = (f32[32,88]{1,0:T(8,128)S(1)}, f32[32,88]{1,0:T(8,128)S(1)}, u32[]{:S(2)}, u32[]{:S(2)}) collective-permute-start(f32[32,88]{1,0:T(8,128)S(1)} %broadcast_multiply_fusion.sums_ref), channel_id=1, source_target_pairs={{0,17},{1,16},{2,19},{3,18},{4,21},{5,20},{6,23},{7,22},{8,25},{9,... | collective-permute-start | bytes 33800 | tf_op jit(solution)/shard_map/ppermute | solution.py:550
  41.2 6.9 %collective-permute-start.9 = (f32[4,88,128]{2,1,0:T(8,128)S(1)}, f32[4,88,128]{2,1,0:T(8,128)S(1)}, u32[]{:S(2)}, u32[]{:S(2)}) collective-permute-start(f32[4,88,128]{2,1,0:T(8,128)S(1)} %get-tuple-element.49), channel_id=1, source_target_pairs={{0,8},{1,9},{2,10},{3,11},{4,12},{5,13},{6,14},{7,15},{8,0},{9,1},... | collective-permute-start | bytes 540680 | tf_op jit(solution)/shard_map/ppermute | solution.py:550
  42.0 6.7 %collective-permute-start.6 = (f32[4,88,128]{2,1,0:T(8,128)S(1)}, f32[4,88,128]{2,1,0:T(8,128)S(1)}, u32[]{:S(2)}, u32[]{:S(2)}) collective-permute-start(f32[4,88,128]{2,1,0:T(8,128)S(1)} %get-tuple-element.47), channel_id=1, source_target_pairs={{0,4},{1,5},{2,6},{3,7},{4,0},{5,1},{6,2},{7,3},{8,12},{9,13},{10,... | collective-permute-start | bytes 540680 | tf_op jit(solution)/shard_map/ppermute | solution.py:550
  43.3 7.0 %collective-permute-start.3 = (f32[4,88,128]{2,1,0:T(8,128)S(1)}, f32[4,88,128]{2,1,0:T(8,128)S(1)}, u32[]{:S(2)}, u32[]{:S(2)}) collective-permute-start(f32[4,88,128]{2,1,0:T(8,128)S(1)} %get-tuple-element.45), channel_id=1, source_target_pairs={{0,2},{1,3},{2,0},{3,1},{4,6},{5,7},{6,4},{7,5},{8,10},{9,11},{10,... | collective-permute-start | bytes 540680 | tf_op jit(solution)/shard_map/ppermute | solution.py:550
  48.2 4.6 %collective-permute-start.10 = (f32[2,88,128]{2,1,0:T(8,128)S(1)}, f32[2,88,128]{2,1,0:T(8,128)S(1)}, u32[]{:S(2)}, u32[]{:S(2)}) collective-permute-start(f32[2,88,128]{2,1,0:T(8,128)S(1)} %dynamic-slice_bitcast_fusion), channel_id=1, source_target_pairs={{0,2},{1,3},{2,0},{3,1},{4,6},{5,7},{6,4},{7,5},{8,10},{9,11},{10,... | collective-permute-start | bytes 270344 | tf_op jit(solution)/shard_map/ppermute | solution.py:550
  48.8 4.6 %collective-permute-start.7 = (f32[2,88,128]{2,1,0:T(8,128)S(1)}, f32[2,88,128]{2,1,0:T(8,128)S(1)}, u32[]{:S(2)}, u32[]{:S(2)}) collective-permute-start(f32[2,88,128]{2,1,0:T(8,128)S(1)} %dynamic-slice_bitcast_fusion.1), channel_id=1, source_target_pairs={{0,8},{1,9},{2,10},{3,11},{4,12},{5,13},{6,14},{7,15},{8,0},{9,1},... | collective-permute-start | bytes 270344 | tf_op jit(solution)/shard_map/ppermute | solution.py:550
  50.4 4.9 %collective-permute-start.4 = (f32[2,88,128]{2,1,0:T(8,128)S(1)}, f32[2,88,128]{2,1,0:T(8,128)S(1)}, u32[]{:S(2)}, u32[]{:S(2)}) collective-permute-start(f32[2,88,128]{2,1,0:T(8,128)S(1)} %dynamic-slice_bitcast_fusion.2), channel_id=1, source_target_pairs={{0,4},{1,5},{2,6},{3,7},{4,0},{5,1},{6,2},{7,3},{8,12},{9,13},{10,... | collective-permute-start | bytes 270344 | tf_op jit(solution)/shard_map/ppermute | solution.py:550
  52.8 4.1 %collective-permute-start.11 = (f32[1,88,128]{2,1,0:T(8,128)S(1)}, f32[1,88,128]{2,1,0:T(8,128)S(1)}, u32[]{:S(2)}, u32[]{:S(2)}) collective-permute-start(f32[1,88,128]{2,1,0:T(8,128)S(1)} %constant_dynamic-slice_fusion), channel_id=1, source_target_pairs={{0,4},{1,5},{2,6},{3,7},{4,0},{5,1},{6,2},{7,3},{8,12},{9,13},{10,... | collective-permute-start | bytes 135176 | tf_op jit(solution)/shard_map/ppermute | solution.py:550
  53.4 4.1 %collective-permute-start.8 = (f32[1,88,128]{2,1,0:T(8,128)S(1)}, f32[1,88,128]{2,1,0:T(8,128)S(1)}, u32[]{:S(2)}, u32[]{:S(2)}) collective-permute-start(f32[1,88,128]{2,1,0:T(8,128)S(1)} %constant_dynamic-slice_fusion.1), channel_id=1, source_target_pairs={{0,2},{1,3},{2,0},{3,1},{4,6},{5,7},{6,4},{7,5},{8,10},{9,11},{10,... | collective-permute-start | bytes 135176 | tf_op jit(solution)/shard_map/ppermute | solution.py:550
  55.3 4.1 %collective-permute-start.5 = (f32[1,88,128]{2,1,0:T(8,128)S(1)}, f32[1,88,128]{2,1,0:T(8,128)S(1)}, u32[]{:S(2)}, u32[]{:S(2)}) collective-permute-start(f32[1,88,128]{2,1,0:T(8,128)S(1)} %constant_dynamic-slice_fusion.2), channel_id=1, source_target_pairs={{0,8},{1,9},{2,10},{3,11},{4,12},{5,13},{6,14},{7,15},{8,0},{9,1},... | collective-permute-start | bytes 135176 | tf_op jit(solution)/shard_map/ppermute | solution.py:550
  59.5 7.5 %collective-permute-start.14 = (f32[1,264,128]{2,1,0:T(8,128)S(1)}, f32[1,264,128]{2,1,0:T(8,128)S(1)}, u32[]{:S(2)}, u32[]{:S(2)}) collective-permute-start(f32[1,264,128]{2,1,0:T(8,128)S(1)} %pad_maximum_fusion.3), channel_id=1, source_target_pairs={{0,24},{1,25},{2,26},{3,27},{4,28},{5,29},{6,30},{7,31},{8,16},{9,... | collective-permute-start | bytes 405512 | tf_op jit(solution)/shard_map/ppermute | solution.py:550
  62.7 8.6 %collective-permute-start.13 = (f32[1,264,128]{2,1,0:T(8,128)S(1)}, f32[1,264,128]{2,1,0:T(8,128)S(1)}, u32[]{:S(2)}, u32[]{:S(2)}) collective-permute-start(f32[1,264,128]{2,1,0:T(8,128)S(1)} %pad_maximum_fusion.3), channel_id=1, source_target_pairs={{0,16},{1,17},{2,18},{3,19},{4,20},{5,21},{6,22},{7,23},{8,24},{9,... | collective-permute-start | bytes 405512 | tf_op jit(solution)/shard_map/ppermute | solution.py:550
  62.7 8.6 %collective-permute-start.12 = (f32[1,264,128]{2,1,0:T(8,128)S(1)}, f32[1,264,128]{2,1,0:T(8,128)S(1)}, u32[]{:S(2)}, u32[]{:S(2)}) collective-permute-start(f32[1,264,128]{2,1,0:T(8,128)S(1)} %pad_maximum_fusion.3), channel_id=1, source_target_pairs={{0,8},{1,9},{2,10},{3,11},{4,12},{5,13},{6,14},{7,15},{8,0},{9,1},... | collective-permute-start | bytes 405512 | tf_op jit(solution)/shard_map/ppermute | solution.py:550
  71.3 7.0 %collective-permute-start.15 = (f32[4,136,128]{2,1,0:T(8,128)S(1)}, f32[4,136,128]{2,1,0:T(8,128)S(1)}, u32[]{:S(2)}, u32[]{:S(2)}) collective-permute-start(f32[4,136,128]{2,1,0:T(8,128)S(1)} %slice.8), channel_id=1, source_target_pairs={{0,2},{1,3},{2,0},{3,1},{4,6},{5,7},{6,4},{7,5},{8,10},{9,11},{10,... | collective-permute-start | bytes 835592 | tf_op jit(solution)/shard_map/ppermute | solution.py:550
  72.0 7.8 %collective-permute-start.16 = (f32[4,128,128]{2,1,0:T(8,128)S(1)}, f32[4,128,128]{2,1,0:T(8,128)S(1)}, u32[]{:S(2)}, u32[]{:S(2)}) collective-permute-start(f32[4,128,128]{2,1,0:T(8,128)S(1)} %slice.9), channel_id=1, source_target_pairs={{0,4},{1,5},{2,6},{3,7},{4,0},{5,1},{6,2},{7,3},{8,12},{9,13},{10,... | collective-permute-start | bytes 786440 | tf_op jit(solution)/shard_map/ppermute | solution.py:550
  73.5 9.3 %collective-permute-start.19 = (f32[4,264,128]{2,1,0:T(8,128)S(1)}, f32[4,264,128]{2,1,0:T(8,128)S(1)}, u32[]{:S(2)}, u32[]{:S(2)}) collective-permute-start(f32[4,264,128]{2,1,0:T(8,128)S(1)} %pad_maximum_fusion.1.refs_0_), channel_id=1, source_target_pairs={{0,1},{1,0},{2,3},{3,2},{4,5},{5,4},{6,7},{7,6},{8,9},{9,8},{10,11... | collective-permute-start | bytes 1622024 | tf_op jit(solution)/shard_map/ppermute | solution.py:550
  78.3 12.5 %collective-permute-start.17 = (f32[8,136,128]{2,1,0:T(8,128)S(1)}, f32[8,136,128]{2,1,0:T(8,128)S(1)}, u32[]{:S(2)}, u32[]{:S(2)}) collective-permute-start(f32[8,136,128]{2,1,0:T(8,128)S(1)} %pad_maximum_fusion), channel_id=1, source_target_pairs={{0,4},{1,5},{2,6},{3,7},{4,0},{5,1},{6,2},{7,3},{8,12},{9,13},{10,... | collective-permute-start | bytes 1671176 | tf_op jit(solution)/shard_map/ppermute | solution.py:550
  79.8 11.0 %collective-permute-start.18 = (f32[8,128,128]{2,1,0:T(8,128)S(1)}, f32[8,128,128]{2,1,0:T(8,128)S(1)}, u32[]{:S(2)}, u32[]{:S(2)}) collective-permute-start(f32[8,128,128]{2,1,0:T(8,128)S(1)} %pad_maximum_fusion.2), channel_id=1, source_target_pairs={{0,2},{1,3},{2,0},{3,1},{4,6},{5,7},{6,4},{7,5},{8,10},{9,11},{10,... | collective-permute-start | bytes 1572872 | tf_op jit(solution)/shard_map/ppermute | solution.py:550
  80.9 1.9 %collective-permute-start.20 = (f32[4,136,128]{2,1,0:T(8,128)S(1)}, f32[4,136,128]{2,1,0:T(8,128)S(1)}, u32[]{:S(2)}, u32[]{:S(2)}) collective-permute-start(f32[4,136,128]{2,1,0:T(8,128)S(1)} %collective-permute-done.15.refs_1_), channel_id=1, source_target_pairs={{0,1},{1,0},{2,3},{3,2},{4,5},{5,4},{6,7},{7,6},{8,9},{9,8},{10,11... | collective-permute-start | bytes 835592 | tf_op jit(solution)/shard_map/ppermute | solution.py:550
  80.9 1.9 %collective-permute-start.21 = (f32[4,128,128]{2,1,0:T(8,128)S(1)}, f32[4,128,128]{2,1,0:T(8,128)S(1)}, u32[]{:S(2)}, u32[]{:S(2)}) collective-permute-start(f32[4,128,128]{2,1,0:T(8,128)S(1)} %collective-permute-done.16.refs_2_), channel_id=1, source_target_pairs={{0,1},{1,0},{2,3},{3,2},{4,5},{5,4},{6,7},{7,6},{8,9},{9,8},{10,11... | collective-permute-start | bytes 786440 | tf_op jit(solution)/shard_map/ppermute | solution.py:550
  90.8 2.7 %collective-permute-start.22 = (f32[8,136,128]{2,1,0:T(8,128)S(1)}, f32[8,136,128]{2,1,0:T(8,128)S(1)}, u32[]{:S(2)}, u32[]{:S(2)}) collective-permute-start(f32[8,136,128]{2,1,0:T(8,128)S(1)} %collective-permute-done.17.refs_3_), channel_id=1, source_target_pairs={{0,1},{1,0},{2,3},{3,2},{4,5},{5,4},{6,7},{7,6},{8,9},{9,8},{10,11... | collective-permute-start | bytes 1671176 | tf_op jit(solution)/shard_map/ppermute | solution.py:550
  90.9 2.7 %collective-permute-start.23 = (f32[8,128,128]{2,1,0:T(8,128)S(1)}, f32[8,128,128]{2,1,0:T(8,128)S(1)}, u32[]{:S(2)}, u32[]{:S(2)}) collective-permute-start(f32[8,128,128]{2,1,0:T(8,128)S(1)} %collective-permute-done.18.refs_4_), channel_id=1, source_target_pairs={{0,1},{1,0},{2,3},{3,2},{4,5},{5,4},{6,7},{7,6},{8,9},{9,8},{10,11... | collective-permute-start | bytes 1572872 | tf_op jit(solution)/shard_map/ppermute | solution.py:550

commit v8 on v7

--- a/solution.py
+++ b/solution.py
@@ -19,7 +19,7 @@
 ROW_TILE = 256
 FORWARD_VMEM = 24 * 1024 * 1024
 BACKWARD_VMEM = 24 * 1024 * 1024
-CHUNK = 256
+CHUNK = 512
 CHUNKS = [slice(start, start + CHUNK) for start in range(0, WIDTH, CHUNK)]
 EPSILON = 1e-06
 
@@ -266,6 +266,9 @@
     readout = jnp.broadcast_to(w_out_ref[...].astype(jnp.float32), (16, WIDTH)).astype(bf16)
     bias_ref[...] = jnp.broadcast_to((0.5 * b_mid_ref[...]).T, bias_ref.shape)
 
+    def wide(column):
+        return jnp.concatenate([column] * (ROW_TILE // LANES), axis=1)
+
     def span(t):
         return pl.ds(pl.multiple_of(t * ROW_TILE, ROW_TILE), ROW_TILE)
 
@@ -290,11 +293,11 @@
             if n + 1 < len(CHUNKS):
                 ahead = products(CHUNKS[n + 1])
             if second:
-                half_mid = half_mid + bias_ref[c, :]
+                half_mid = half_mid + wide(bias_ref[c, :])
                 wave = jnp.tanh(half_mid)
                 turn = half_mid * wave
                 old_mixed[c, :] = (half_mid + turn).astype(bf16)
-                curve_out[c, span(t - 1)] = (1.0 + wave) * (1.0 + half_mid - turn) * read_ref[c, :]
+                curve_out[c, span(t - 1)] = (1.0 + wave) * (1.0 + half_mid - turn) * wide(read_ref[c, :])
             if first:
                 value = (half_in + half_in * jnp.tanh(half_in)).astype(bf16)
                 new_hidden[c, :] = value
@@ -335,8 +338,8 @@
         out_shape=[pltpu.VMEM(shape, kind) for shape, kind in outs[:-1]]
         + [jax.ShapeDtypeStruct(*outs[-1])],
         scratch_shapes=[
-            pltpu.VMEM((WIDTH, ROW_TILE), jnp.float32),
-            pltpu.VMEM((WIDTH, ROW_TILE), jnp.float32),
+            pltpu.VMEM((WIDTH, LANES), jnp.float32),
+            pltpu.VMEM((WIDTH, LANES), jnp.float32),
         ]
         + [pltpu.VMEM((WIDTH, ROW_TILE), jnp.bfloat16)] * 4,
         compiler_params=pltpu.CompilerParams(vmem_limit_bytes=FORWARD_VMEM),
@@ -606,7 +609,7 @@
         ]
 
     own = jnp.concatenate(parts, axis=1)
-    far = (0, top // 2, top, top + top // 2)
+    far = (0, top + top // 2, top, top // 2)
     whole = jnp.concatenate([own] + [swap(own, mask, devices) for mask in far[1:]], axis=0)
     received = [(whole, far, ("left", "extra", "right"))]
     split = WIDTH // groups + 8

time: 97.1 us -> 96.1 us (0.990)
  waiting for transfers between devices: 32.8 us -> 31.7 us
    ppermute x24, waiting for transfers between devices: 31.2 us -> 30.2 us  [swap(): return lax.ppermute(array, 'paths', [(i, i ^ bit) for i in range(devices)])]
  transfers between devices with their start and end apart: 25 -> 25, of which waited for: 13 -> 14; matrix products, arithmetic and copies ran while one was open for 1% -> 1% of each run, Pallas kernels for 16% -> 16%
where the time goes in v8:
time: 96.1 us; the launch traced here: 95.6 us
  waiting for transfers between devices  31.7 us (33%)
  Pallas kernels  31.3 us (33%)
  starting transfers between devices  30 us (31%)
  between operations  1.47 us (2%)
    ppermute x24, waiting for transfers between devices, swap(): return lax.ppermute(array, 'paths', [(i, i ^ bit) for i in range(devices)])  30.2 us
    ppermute x24, starting transfers between devices, swap(): return lax.ppermute(array, 'paths', [(i, i ^ bit) for i in range(devices)])  23.8 us
    pallas_call x1, Pallas kernels, forward(): pl.pallas_call(forward_kernel, in_specs=[smem] + [vmem] * 5, out_specs=[v...  12.1 us
    pallas_call x1, Pallas kernels, backward(): pl.pallas_call(functools.partial(backward_kernel, inv_sets), in_specs=[sm...  6.65 us
    pallas_call x1, Pallas kernels, payoff_sums(): pl.pallas_call(pricing_kernel, grid=(steps,), in_specs=[pl.BlockSpec((4,...  6.36 us
    all_to_all x1, starting transfers between devices, on_device(): lax.all_to_all(sums, 'paths', 0, 0, axis_index_groups=lanes, tiled=True)  6.18 us
    pallas_call x1, Pallas kernels, prepare(): pl.pallas_call(functools.partial(prepare_kernel, sets), in_specs=[smem, v...  3.15 us
    pallas_call x1, Pallas kernels, scaled(): pl.pallas_call(functools.partial(scaling_kernel, layout, groups), in_spec...  3.06 us
  transfers between devices with their start and end apart: 25, of which 14 were waited for; matrix products, arithmetic and copies ran while one was open for 1% of the time, Pallas kernels for 16%

profile of v8, /device:TPU:0, one launch (start us, length us, event | category | flops | bytes accessed | tf_op | source)
XLA Modules:
  0.0 95.6 jit_solution(17453695409236289127)
XLA Ops:
  0.6 6.4 %pricing.1 = f32[8,2,16,88]{3,2,1,0:T(8,128)} custom-call(f32[4,256]{1,0:T(4,128)} %bitcast.38, bf16[2,64,128]{2,1,0:T(8,128)(2,1)} %inc_ref.1), custom_call_target="tpu_custom_call" | custom-call | tf_op jit(solution)/shard_map/pricing/pallas_call | solution.py:127
  7.0 6.2 %all-to-all-start = ((f32[8,32,88]{2,1,0:T(8,128)}), f32[8,32,88]{2,1,0:T(8,128)S(1)}, u32[]{:S(2)}, u32[]{:S(2)}) async-start(f32[8,32,88]{2,1,0:T(8,128)} %bitcast.2), calls=%async_computation | async-start | bytes 262144 | tf_op jit(solution)/shard_map/all_to_all | solution.py:588
  13.2 0.7 reshape.62.w_out_ref
  14.5 3.1 %prepare.1 = (bf16[1024,16]{1,0:T(8,128)(2,1)S(1)}, bf16[1024,1024]{1,0:T(8,128)(2,1)S(1)}, bf16[16,2816]{1,0:T(8,128)(2,1)S(1)}) custom-call(s32[1]{0:T(128)} %bitcast.owner_ref, f32[4,256]{1,0:T(4,128)} %bitcast.39, bf16[6,1024]{1,0:T(8,128)(2,1)} %w_in_hbm.1, f32[1,1024]{1,0:T(1,128)} %bitcast.40, bf16[1024,1024]{1,0:T(8,128)(2,1)} %w_mid_hbm.3), custom_call_target="tpu_custom_call" | custom-call | tf_op jit(solution)/shard_map/prepare/pallas_call | solution.py:232
  17.7 0.1 pad_add_fusion.owner_ref
  17.7 1.5 %all-to-all-done = f32[8,32,88]{2,1,0:T(8,128)S(1)} async-done(((f32[8,32,88]{2,1,0:T(8,128)}), f32[8,32,88]{2,1,0:T(8,128)S(1)}, u32[]{:S(2)}, u32[]{:S(2)}) %all-to-all-start) | async-done | bytes 90144 | tf_op jit(solution)/shard_map/all_to_all | solution.py:588
  19.3 0.1 collective-permute-start
  19.4 2.7 %collective-permute-start.1 = (f32[32,88]{1,0:T(8,128)S(1)}, f32[32,88]{1,0:T(8,128)S(1)}, u32[]{:S(2)}, u32[]{:S(2)}) collective-permute-start(f32[32,88]{1,0:T(8,128)S(1)} %broadcast_multiply_fusion.sums_ref), channel_id=1, source_target_pairs={{0,16},{1,17},{2,18},{3,19},{4,20},{5,21},{6,22},{7,23},{8,24},{9,... | collective-permute-start | bytes 33800 | tf_op jit(solution)/shard_map/ppermute | solution.py:553
  22.0 0.1 collective-permute-start.2
  22.1 12.1 %forward.1 = (bf16[1024,2816]{1,0:T(8,128)(2,1)S(1)}, f32[1024,2816]{1,0:T(8,128)S(1)}, bf16[256,2816]{1,0:T(8,128)(2,1)S(1)}, f32[1,2816]{1,0:T(1,128)S(1)}) custom-call(s32[2]{0:T(128)S(1)} %pad_add_fusion.owner_ref, f32[1,1024]{1,0:T(1,128)} %bitcast.41, bf16[1,1024]{1,0:T(2,128)(2,1)S(1)} %reshape.62.w_out_ref, ...), custom_call_target="tpu_custom_call" | custom-call | flops 6090129408 | bytes 4194304 | tf_op jit(solution)/shard_map/forward/pallas_call | solution.py:334
  34.3 0.0 collective-permute-done.1.far_ref
  34.3 0.0 collective-permute-done.2.both_ref
  34.3 6.7 %backward.1 = (f32[4,88,128]{2,1,0:T(8,128)S(1)}, f32[4,88,128]{2,1,0:T(8,128)S(1)}, f32[4,88,128]{2,1,0:T(8,128)S(1)}, f32[4,88,128]{2,1,0:T(8,128)S(1)}, f32[4...) custom-call(s32[1]{0:T(128)} %bitcast.owner_ref, f32[32,88]{1,0:T(8,128)S(1)} %broadcast_multiply_fusion.sums_ref, ...), custom_call_target="tpu_custom_call" | custom-call | tf_op jit(solution)/shard_map/backward/pallas_call | solution.py:451
  40.9 0.8 collective-permute-start.9
  41.8 1.2 %collective-permute-start.6 = (f32[4,88,128]{2,1,0:T(8,128)S(1)}, f32[4,88,128]{2,1,0:T(8,128)S(1)}, u32[]{:S(2)}, u32[]{:S(2)}) collective-permute-start(f32[4,88,128]{2,1,0:T(8,128)S(1)} %get-tuple-element.47), channel_id=1, source_target_pairs={{0,4},{1,5},{2,6},{3,7},{4,0},{5,1},{6,2},{7,3},{8,12},{9,13},{10,... | collective-permute-start | bytes 540680 | tf_op jit(solution)/shard_map/ppermute | solution.py:553
  43.0 1.5 %collective-permute-start.3 = (f32[4,88,128]{2,1,0:T(8,128)S(1)}, f32[4,88,128]{2,1,0:T(8,128)S(1)}, u32[]{:S(2)}, u32[]{:S(2)}) collective-permute-start(f32[4,88,128]{2,1,0:T(8,128)S(1)} %get-tuple-element.45), channel_id=1, source_target_pairs={{0,2},{1,3},{2,0},{3,1},{4,6},{5,7},{6,4},{7,5},{8,10},{9,11},{10,... | collective-permute-start | bytes 540680 | tf_op jit(solution)/shard_map/ppermute | solution.py:553
  44.4 3.4 %collective-permute-done.9 = f32[4,88,128]{2,1,0:T(8,128)S(1)} collective-permute-done((f32[4,88,128]{2,1,0:T(8,128)S(1)}, f32[4,88,128]{2,1,0:T(8,128)S(1)}, u32[]{:S(2)}, u32[]{:S(2)}) %collective-permute-start.9) | collective-permute-done | bytes 180256 | tf_op jit(solution)/shard_map/ppermute | solution.py:553
  47.9 0.6 collective-permute-start.10
  48.4 0.0 collective-permute-done.6
  48.5 1.5 %collective-permute-start.7 = (f32[2,88,128]{2,1,0:T(8,128)S(1)}, f32[2,88,128]{2,1,0:T(8,128)S(1)}, u32[]{:S(2)}, u32[]{:S(2)}) collective-permute-start(f32[2,88,128]{2,1,0:T(8,128)S(1)} %dynamic-slice_bitcast_fusion.1), channel_id=1, source_target_pairs={{0,8},{1,9},{2,10},{3,11},{4,12},{5,13},{6,14},{7,15},{8,0},{9,1},... | collective-permute-start | bytes 270344 | tf_op jit(solution)/shard_map/ppermute | solution.py:553
  50.0 0.0 collective-permute-done.3
  50.1 1.5 %collective-permute-start.4 = (f32[2,88,128]{2,1,0:T(8,128)S(1)}, f32[2,88,128]{2,1,0:T(8,128)S(1)}, u32[]{:S(2)}, u32[]{:S(2)}) collective-permute-start(f32[2,88,128]{2,1,0:T(8,128)S(1)} %dynamic-slice_bitcast_fusion.2), channel_id=1, source_target_pairs={{0,4},{1,5},{2,6},{3,7},{4,0},{5,1},{6,2},{7,3},{8,12},{9,13},{10,... | collective-permute-start | bytes 270344 | tf_op jit(solution)/shard_map/ppermute | solution.py:553
  51.6 0.9 collective-permute-done.10
  52.5 0.6 collective-permute-start.11
  53.1 0.0 collective-permute-done.7
  53.2 1.6 %collective-permute-start.8 = (f32[1,88,128]{2,1,0:T(8,128)S(1)}, f32[1,88,128]{2,1,0:T(8,128)S(1)}, u32[]{:S(2)}, u32[]{:S(2)}) collective-permute-start(f32[1,88,128]{2,1,0:T(8,128)S(1)} %constant_dynamic-slice_fusion.1), channel_id=1, source_target_pairs={{0,2},{1,3},{2,0},{3,1},{4,6},{5,7},{6,4},{7,5},{8,10},{9,11},{10,... | collective-permute-start | bytes 135176 | tf_op jit(solution)/shard_map/ppermute | solution.py:553
  54.7 0.3 collective-permute-done.4
  55.0 1.2 %collective-permute-start.5 = (f32[1,88,128]{2,1,0:T(8,128)S(1)}, f32[1,88,128]{2,1,0:T(8,128)S(1)}, u32[]{:S(2)}, u32[]{:S(2)}) collective-permute-start(f32[1,88,128]{2,1,0:T(8,128)S(1)} %constant_dynamic-slice_fusion.2), channel_id=1, source_target_pairs={{0,8},{1,9},{2,10},{3,11},{4,12},{5,13},{6,14},{7,15},{8,0},{9,1},... | collective-permute-start | bytes 135176 | tf_op jit(solution)/shard_map/ppermute | solution.py:553
  56.2 0.4 collective-permute-done.11
  56.6 0.6 collective-permute-done.8
  57.3 2.4 %collective-permute-done.5 = f32[1,88,128]{2,1,0:T(8,128)S(1)} collective-permute-done((f32[1,88,128]{2,1,0:T(8,128)S(1)}, f32[1,88,128]{2,1,0:T(8,128)S(1)}, u32[]{:S(2)}, u32[]{:S(2)}) %collective-permute-start.5) | collective-permute-done | bytes 45088 | tf_op jit(solution)/shard_map/ppermute | solution.py:553
  59.7 1.0 %collective-permute-start.14 = (f32[1,264,128]{2,1,0:T(8,128)S(1)}, f32[1,264,128]{2,1,0:T(8,128)S(1)}, u32[]{:S(2)}, u32[]{:S(2)}) collective-permute-start(f32[1,264,128]{2,1,0:T(8,128)S(1)} %pad_maximum_fusion.3), channel_id=1, source_target_pairs={{0,8},{1,9},{2,10},{3,11},{4,12},{5,13},{6,14},{7,15},{8,0},{9,1},... | collective-permute-start | bytes 405512 | tf_op jit(solution)/shard_map/ppermute | solution.py:553
  60.7 2.6 %collective-permute-start.13 = (f32[1,264,128]{2,1,0:T(8,128)S(1)}, f32[1,264,128]{2,1,0:T(8,128)S(1)}, u32[]{:S(2)}, u32[]{:S(2)}) collective-permute-start(f32[1,264,128]{2,1,0:T(8,128)S(1)} %pad_maximum_fusion.3), channel_id=1, source_target_pairs={{0,16},{1,17},{2,18},{3,19},{4,20},{5,21},{6,22},{7,23},{8,24},{9,... | collective-permute-start | bytes 405512 | tf_op jit(solution)/shard_map/ppermute | solution.py:553
  63.3 0.9 collective-permute-start.12
  64.1 2.7 %collective-permute-done.14 = f32[1,264,128]{2,1,0:T(8,128)S(1)} collective-permute-done((f32[1,264,128]{2,1,0:T(8,128)S(1)}, f32[1,264,128]{2,1,0:T(8,128)S(1)}, u32[]{:S(2)}, u32[]{:S(2)}) %collective-permute-start.14) | collective-permute-done | bytes 135200 | tf_op jit(solution)/shard_map/ppermute | solution.py:553
  66.8 3.9 %collective-permute-done.13 = f32[1,264,128]{2,1,0:T(8,128)S(1)} collective-permute-done((f32[1,264,128]{2,1,0:T(8,128)S(1)}, f32[1,264,128]{2,1,0:T(8,128)S(1)}, u32[]{:S(2)}, u32[]{:S(2)}) %collective-permute-start.13) | collective-permute-done | bytes 135200 | tf_op jit(solution)/shard_map/ppermute | solution.py:553
  70.8 0.7 collective-permute-start.15
  71.5 1.4 %collective-permute-start.16 = (f32[4,128,128]{2,1,0:T(8,128)S(1)}, f32[4,128,128]{2,1,0:T(8,128)S(1)}, u32[]{:S(2)}, u32[]{:S(2)}) collective-permute-start(f32[4,128,128]{2,1,0:T(8,128)S(1)} %slice.9), channel_id=1, source_target_pairs={{0,4},{1,5},{2,6},{3,7},{4,0},{5,1},{6,2},{7,3},{8,12},{9,13},{10,... | collective-permute-start | bytes 786440 | tf_op jit(solution)/shard_map/ppermute | solution.py:553
  72.9 5.2 %collective-permute-done.15.refs_1_ = f32[4,136,128]{2,1,0:T(8,128)S(1)} collective-permute-done((f32[4,136,128]{2,1,0:T(8,128)S(1)}, f32[4,136,128]{2,1,0:T(8,128)S(1)}, u32[]{:S(2)}, u32[]{:S(2)}) %collective-permute-start.15) | collective-permute-done | bytes 278560 | tf_op jit(solution)/shard_map/ppermute | solution.py:553
  78.1 1.6 %collective-permute-start.17 = (f32[8,136,128]{2,1,0:T(8,128)S(1)}, f32[8,136,128]{2,1,0:T(8,128)S(1)}, u32[]{:S(2)}, u32[]{:S(2)}) collective-permute-start(f32[8,136,128]{2,1,0:T(8,128)S(1)} %pad_maximum_fusion), channel_id=1, source_target_pairs={{0,4},{1,5},{2,6},{3,7},{4,0},{5,1},{6,2},{7,3},{8,12},{9,13},{10,... | collective-permute-start | bytes 1671176 | tf_op jit(solution)/shard_map/ppermute | solution.py:553
  79.8 1.4 %collective-permute-start.18 = (f32[8,128,128]{2,1,0:T(8,128)S(1)}, f32[8,128,128]{2,1,0:T(8,128)S(1)}, u32[]{:S(2)}, u32[]{:S(2)}) collective-permute-start(f32[8,128,128]{2,1,0:T(8,128)S(1)} %pad_maximum_fusion.2), channel_id=1, source_target_pairs={{0,2},{1,3},{2,0},{3,1},{4,6},{5,7},{6,4},{7,5},{8,10},{9,11},{10,... | collective-permute-start | bytes 1572872 | tf_op jit(solution)/shard_map/ppermute | solution.py:553
  81.1 0.5 collective-permute-start.21
  81.6 1.4 %collective-permute-done.21.refs_7_ = f32[4,128,128]{2,1,0:T(8,128)S(1)} collective-permute-done((f32[4,128,128]{2,1,0:T(8,128)S(1)}, f32[4,128,128]{2,1,0:T(8,128)S(1)}, u32[]{:S(2)}, u32[]{:S(2)}) %collective-permute-start.21) | collective-permute-done | bytes 262176 | tf_op jit(solution)/shard_map/ppermute | solution.py:553
  83.1 5.9 %collective-permute-done.18.refs_4_ = f32[8,128,128]{2,1,0:T(8,128)S(1)} collective-permute-done((f32[8,128,128]{2,1,0:T(8,128)S(1)}, f32[8,128,128]{2,1,0:T(8,128)S(1)}, u32[]{:S(2)}, u32[]{:S(2)}) %collective-permute-start.18) | collective-permute-done | bytes 524320 | tf_op jit(solution)/shard_map/ppermute | solution.py:553
  89.0 0.9 collective-permute-done.17.refs_3_
  89.9 0.5 collective-permute-start.23
  90.4 2.2 %collective-permute-done.23.refs_9_ = f32[8,128,128]{2,1,0:T(8,128)S(1)} collective-permute-done((f32[8,128,128]{2,1,0:T(8,128)S(1)}, f32[8,128,128]{2,1,0:T(8,128)S(1)}, u32[]{:S(2)}, u32[]{:S(2)}) %collective-permute-start.23) | collective-permute-done | bytes 524320 | tf_op jit(solution)/shard_map/ppermute | solution.py:553
  92.6 3.1 %scaling.1 = (f32[6,1024]{1,0:T(8,128)}, f32[1,1024]{1,0:T(1,128)}, f32[1024,1024]{1,0:T(8,128)}, f32[1,1024]{1,0:T(1,128)}, f32[1,1024]{1,0:T(1,128)}, /*index=5*/f32[1,1]{1,0:T(1,128)}) custom-call(s32[1]{0:T(128)} %bitcast.owner_ref, f32[4,264,128]{2,1,0:T(8,128)S(1)} %pad_maximum_fusion.1.refs_0_, f32[4,136,128]{2,1,0:T(8,128)S(1)} %collective-permute-done.15.refs_1_, ...), custom_call_target="tpu_custom_call" | custom-call | tf_op jit(solution)/shard_map/scaling/pallas_call | solution.py:538
  (32 shorter events, 0.4 us)
Async XLA Ops:
  7.0 12.3 %all-to-all-start = ((f32[8,32,88]{2,1,0:T(8,128)}), f32[8,32,88]{2,1,0:T(8,128)S(1)}, u32[]{:S(2)}, u32[]{:S(2)}) async-start(f32[8,32,88]{2,1,0:T(8,128)} %bitcast.2), calls=%async_computation | async-start | bytes 262144 | tf_op jit(solution)/shard_map/all_to_all | solution.py:588
  19.3 15.0 %collective-permute-start = (f32[32,88]{1,0:T(8,128)S(1)}, f32[32,88]{1,0:T(8,128)S(1)}, u32[]{:S(2)}, u32[]{:S(2)}) collective-permute-start(f32[32,88]{1,0:T(8,128)S(1)} %broadcast_multiply_fusion.sums_ref), channel_id=1, source_target_pairs={{0,1},{1,0},{2,3},{3,2},{4,5},{5,4},{6,7},{7,6},{8,9},{9,8},{10,11... | collective-permute-start | bytes 33800 | tf_op jit(solution)/shard_map/ppermute | solution.py:553
  19.4 14.9 %collective-permute-start.1 = (f32[32,88]{1,0:T(8,128)S(1)}, f32[32,88]{1,0:T(8,128)S(1)}, u32[]{:S(2)}, u32[]{:S(2)}) collective-permute-start(f32[32,88]{1,0:T(8,128)S(1)} %broadcast_multiply_fusion.sums_ref), channel_id=1, source_target_pairs={{0,16},{1,17},{2,18},{3,19},{4,20},{5,21},{6,22},{7,23},{8,24},{9,... | collective-permute-start | bytes 33800 | tf_op jit(solution)/shard_map/ppermute | solution.py:553
  22.0 12.2 %collective-permute-start.2 = (f32[32,88]{1,0:T(8,128)S(1)}, f32[32,88]{1,0:T(8,128)S(1)}, u32[]{:S(2)}, u32[]{:S(2)}) collective-permute-start(f32[32,88]{1,0:T(8,128)S(1)} %broadcast_multiply_fusion.sums_ref), channel_id=1, source_target_pairs={{0,17},{1,16},{2,19},{3,18},{4,21},{5,20},{6,23},{7,22},{8,25},{9,... | collective-permute-start | bytes 33800 | tf_op jit(solution)/shard_map/ppermute | solution.py:553
  40.9 6.9 %collective-permute-start.9 = (f32[4,88,128]{2,1,0:T(8,128)S(1)}, f32[4,88,128]{2,1,0:T(8,128)S(1)}, u32[]{:S(2)}, u32[]{:S(2)}) collective-permute-start(f32[4,88,128]{2,1,0:T(8,128)S(1)} %get-tuple-element.49), channel_id=1, source_target_pairs={{0,8},{1,9},{2,10},{3,11},{4,12},{5,13},{6,14},{7,15},{8,0},{9,1},... | collective-permute-start | bytes 540680 | tf_op jit(solution)/shard_map/ppermute | solution.py:553
  41.8 6.7 %collective-permute-start.6 = (f32[4,88,128]{2,1,0:T(8,128)S(1)}, f32[4,88,128]{2,1,0:T(8,128)S(1)}, u32[]{:S(2)}, u32[]{:S(2)}) collective-permute-start(f32[4,88,128]{2,1,0:T(8,128)S(1)} %get-tuple-element.47), channel_id=1, source_target_pairs={{0,4},{1,5},{2,6},{3,7},{4,0},{5,1},{6,2},{7,3},{8,12},{9,13},{10,... | collective-permute-start | bytes 540680 | tf_op jit(solution)/shard_map/ppermute | solution.py:553
  43.0 7.0 %collective-permute-start.3 = (f32[4,88,128]{2,1,0:T(8,128)S(1)}, f32[4,88,128]{2,1,0:T(8,128)S(1)}, u32[]{:S(2)}, u32[]{:S(2)}) collective-permute-start(f32[4,88,128]{2,1,0:T(8,128)S(1)} %get-tuple-element.45), channel_id=1, source_target_pairs={{0,2},{1,3},{2,0},{3,1},{4,6},{5,7},{6,4},{7,5},{8,10},{9,11},{10,... | collective-permute-start | bytes 540680 | tf_op jit(solution)/shard_map/ppermute | solution.py:553
  47.9 4.6 %collective-permute-start.10 = (f32[2,88,128]{2,1,0:T(8,128)S(1)}, f32[2,88,128]{2,1,0:T(8,128)S(1)}, u32[]{:S(2)}, u32[]{:S(2)}) collective-permute-start(f32[2,88,128]{2,1,0:T(8,128)S(1)} %dynamic-slice_bitcast_fusion), channel_id=1, source_target_pairs={{0,2},{1,3},{2,0},{3,1},{4,6},{5,7},{6,4},{7,5},{8,10},{9,11},{10,... | collective-permute-start | bytes 270344 | tf_op jit(solution)/shard_map/ppermute | solution.py:553
  48.5 4.6 %collective-permute-start.7 = (f32[2,88,128]{2,1,0:T(8,128)S(1)}, f32[2,88,128]{2,1,0:T(8,128)S(1)}, u32[]{:S(2)}, u32[]{:S(2)}) collective-permute-start(f32[2,88,128]{2,1,0:T(8,128)S(1)} %dynamic-slice_bitcast_fusion.1), channel_id=1, source_target_pairs={{0,8},{1,9},{2,10},{3,11},{4,12},{5,13},{6,14},{7,15},{8,0},{9,1},... | collective-permute-start | bytes 270344 | tf_op jit(solution)/shard_map/ppermute | solution.py:553
  50.1 4.9 %collective-permute-start.4 = (f32[2,88,128]{2,1,0:T(8,128)S(1)}, f32[2,88,128]{2,1,0:T(8,128)S(1)}, u32[]{:S(2)}, u32[]{:S(2)}) collective-permute-start(f32[2,88,128]{2,1,0:T(8,128)S(1)} %dynamic-slice_bitcast_fusion.2), channel_id=1, source_target_pairs={{0,4},{1,5},{2,6},{3,7},{4,0},{5,1},{6,2},{7,3},{8,12},{9,13},{10,... | collective-permute-start | bytes 270344 | tf_op jit(solution)/shard_map/ppermute | solution.py:553
  52.5 4.1 %collective-permute-start.11 = (f32[1,88,128]{2,1,0:T(8,128)S(1)}, f32[1,88,128]{2,1,0:T(8,128)S(1)}, u32[]{:S(2)}, u32[]{:S(2)}) collective-permute-start(f32[1,88,128]{2,1,0:T(8,128)S(1)} %constant_dynamic-slice_fusion), channel_id=1, source_target_pairs={{0,4},{1,5},{2,6},{3,7},{4,0},{5,1},{6,2},{7,3},{8,12},{9,13},{10,... | collective-permute-start | bytes 135176 | tf_op jit(solution)/shard_map/ppermute | solution.py:553
  53.2 4.1 %collective-permute-start.8 = (f32[1,88,128]{2,1,0:T(8,128)S(1)}, f32[1,88,128]{2,1,0:T(8,128)S(1)}, u32[]{:S(2)}, u32[]{:S(2)}) collective-permute-start(f32[1,88,128]{2,1,0:T(8,128)S(1)} %constant_dynamic-slice_fusion.1), channel_id=1, source_target_pairs={{0,2},{1,3},{2,0},{3,1},{4,6},{5,7},{6,4},{7,5},{8,10},{9,11},{10,... | collective-permute-start | bytes 135176 | tf_op jit(solution)/shard_map/ppermute | solution.py:553
  55.0 4.6 %collective-permute-start.5 = (f32[1,88,128]{2,1,0:T(8,128)S(1)}, f32[1,88,128]{2,1,0:T(8,128)S(1)}, u32[]{:S(2)}, u32[]{:S(2)}) collective-permute-start(f32[1,88,128]{2,1,0:T(8,128)S(1)} %constant_dynamic-slice_fusion.2), channel_id=1, source_target_pairs={{0,8},{1,9},{2,10},{3,11},{4,12},{5,13},{6,14},{7,15},{8,0},{9,1},... | collective-permute-start | bytes 135176 | tf_op jit(solution)/shard_map/ppermute | solution.py:553
  59.7 7.1 %collective-permute-start.14 = (f32[1,264,128]{2,1,0:T(8,128)S(1)}, f32[1,264,128]{2,1,0:T(8,128)S(1)}, u32[]{:S(2)}, u32[]{:S(2)}) collective-permute-start(f32[1,264,128]{2,1,0:T(8,128)S(1)} %pad_maximum_fusion.3), channel_id=1, source_target_pairs={{0,8},{1,9},{2,10},{3,11},{4,12},{5,13},{6,14},{7,15},{8,0},{9,1},... | collective-permute-start | bytes 405512 | tf_op jit(solution)/shard_map/ppermute | solution.py:553
  60.7 10.0 %collective-permute-start.13 = (f32[1,264,128]{2,1,0:T(8,128)S(1)}, f32[1,264,128]{2,1,0:T(8,128)S(1)}, u32[]{:S(2)}, u32[]{:S(2)}) collective-permute-start(f32[1,264,128]{2,1,0:T(8,128)S(1)} %pad_maximum_fusion.3), channel_id=1, source_target_pairs={{0,16},{1,17},{2,18},{3,19},{4,20},{5,21},{6,22},{7,23},{8,24},{9,... | collective-permute-start | bytes 405512 | tf_op jit(solution)/shard_map/ppermute | solution.py:553
  63.3 7.4 %collective-permute-start.12 = (f32[1,264,128]{2,1,0:T(8,128)S(1)}, f32[1,264,128]{2,1,0:T(8,128)S(1)}, u32[]{:S(2)}, u32[]{:S(2)}) collective-permute-start(f32[1,264,128]{2,1,0:T(8,128)S(1)} %pad_maximum_fusion.3), channel_id=1, source_target_pairs={{0,24},{1,25},{2,26},{3,27},{4,28},{5,29},{6,30},{7,31},{8,16},{9,... | collective-permute-start | bytes 405512 | tf_op jit(solution)/shard_map/ppermute | solution.py:553
  70.8 7.3 %collective-permute-start.15 = (f32[4,136,128]{2,1,0:T(8,128)S(1)}, f32[4,136,128]{2,1,0:T(8,128)S(1)}, u32[]{:S(2)}, u32[]{:S(2)}) collective-permute-start(f32[4,136,128]{2,1,0:T(8,128)S(1)} %slice.8), channel_id=1, source_target_pairs={{0,2},{1,3},{2,0},{3,1},{4,6},{5,7},{6,4},{7,5},{8,10},{9,11},{10,... | collective-permute-start | bytes 835592 | tf_op jit(solution)/shard_map/ppermute | solution.py:553
  71.5 8.2 %collective-permute-start.16 = (f32[4,128,128]{2,1,0:T(8,128)S(1)}, f32[4,128,128]{2,1,0:T(8,128)S(1)}, u32[]{:S(2)}, u32[]{:S(2)}) collective-permute-start(f32[4,128,128]{2,1,0:T(8,128)S(1)} %slice.9), channel_id=1, source_target_pairs={{0,4},{1,5},{2,6},{3,7},{4,0},{5,1},{6,2},{7,3},{8,12},{9,13},{10,... | collective-permute-start | bytes 786440 | tf_op jit(solution)/shard_map/ppermute | solution.py:553
  72.9 10.1 %collective-permute-start.19 = (f32[4,264,128]{2,1,0:T(8,128)S(1)}, f32[4,264,128]{2,1,0:T(8,128)S(1)}, u32[]{:S(2)}, u32[]{:S(2)}) collective-permute-start(f32[4,264,128]{2,1,0:T(8,128)S(1)} %pad_maximum_fusion.1.refs_0_), channel_id=1, source_target_pairs={{0,1},{1,0},{2,3},{3,2},{4,5},{5,4},{6,7},{7,6},{8,9},{9,8},{10,11... | collective-permute-start | bytes 1622024 | tf_op jit(solution)/shard_map/ppermute | solution.py:553
  78.1 11.7 %collective-permute-start.17 = (f32[8,136,128]{2,1,0:T(8,128)S(1)}, f32[8,136,128]{2,1,0:T(8,128)S(1)}, u32[]{:S(2)}, u32[]{:S(2)}) collective-permute-start(f32[8,136,128]{2,1,0:T(8,128)S(1)} %pad_maximum_fusion), channel_id=1, source_target_pairs={{0,4},{1,5},{2,6},{3,7},{4,0},{5,1},{6,2},{7,3},{8,12},{9,13},{10,... | collective-permute-start | bytes 1671176 | tf_op jit(solution)/shard_map/ppermute | solution.py:553
  79.8 9.2 %collective-permute-start.18 = (f32[8,128,128]{2,1,0:T(8,128)S(1)}, f32[8,128,128]{2,1,0:T(8,128)S(1)}, u32[]{:S(2)}, u32[]{:S(2)}) collective-permute-start(f32[8,128,128]{2,1,0:T(8,128)S(1)} %pad_maximum_fusion.2), channel_id=1, source_target_pairs={{0,2},{1,3},{2,0},{3,1},{4,6},{5,7},{6,4},{7,5},{8,10},{9,11},{10,... | collective-permute-start | bytes 1572872 | tf_op jit(solution)/shard_map/ppermute | solution.py:553
  81.1 1.9 %collective-permute-start.20 = (f32[4,136,128]{2,1,0:T(8,128)S(1)}, f32[4,136,128]{2,1,0:T(8,128)S(1)}, u32[]{:S(2)}, u32[]{:S(2)}) collective-permute-start(f32[4,136,128]{2,1,0:T(8,128)S(1)} %collective-permute-done.15.refs_1_), channel_id=1, source_target_pairs={{0,1},{1,0},{2,3},{3,2},{4,5},{5,4},{6,7},{7,6},{8,9},{9,8},{10,11... | collective-permute-start | bytes 835592 | tf_op jit(solution)/shard_map/ppermute | solution.py:553
  81.1 1.9 %collective-permute-start.21 = (f32[4,128,128]{2,1,0:T(8,128)S(1)}, f32[4,128,128]{2,1,0:T(8,128)S(1)}, u32[]{:S(2)}, u32[]{:S(2)}) collective-permute-start(f32[4,128,128]{2,1,0:T(8,128)S(1)} %collective-permute-done.16.refs_2_), channel_id=1, source_target_pairs={{0,1},{1,0},{2,3},{3,2},{4,5},{5,4},{6,7},{7,6},{8,9},{9,8},{10,11... | collective-permute-start | bytes 786440 | tf_op jit(solution)/shard_map/ppermute | solution.py:553
  89.9 2.7 %collective-permute-start.22 = (f32[8,136,128]{2,1,0:T(8,128)S(1)}, f32[8,136,128]{2,1,0:T(8,128)S(1)}, u32[]{:S(2)}, u32[]{:S(2)}) collective-permute-start(f32[8,136,128]{2,1,0:T(8,128)S(1)} %collective-permute-done.17.refs_3_), channel_id=1, source_target_pairs={{0,1},{1,0},{2,3},{3,2},{4,5},{5,4},{6,7},{7,6},{8,9},{9,8},{10,11... | collective-permute-start | bytes 1671176 | tf_op jit(solution)/shard_map/ppermute | solution.py:553
  89.9 2.7 %collective-permute-start.23 = (f32[8,128,128]{2,1,0:T(8,128)S(1)}, f32[8,128,128]{2,1,0:T(8,128)S(1)}, u32[]{:S(2)}, u32[]{:S(2)}) collective-permute-start(f32[8,128,128]{2,1,0:T(8,128)S(1)} %collective-permute-done.18.refs_4_), channel_id=1, source_target_pairs={{0,1},{1,0},{2,3},{3,2},{4,5},{5,4},{6,7},{7,6},{8,9},{9,8},{10,11... | collective-permute-start | bytes 1572872 | tf_op jit(solution)/shard_map/ppermute | solution.py:553

commit v9 on v8

--- a/solution.py
+++ b/solution.py
@@ -86,17 +86,21 @@
     lane = lax.broadcasted_iota(jnp.int32, (paths, LANES), 1)
 
     def maturity(m, total):
-        noise = noise_ref[m]
-        for k in range(8):
-            i = 8 * m + k
-            window = lags_ref[...] if k == 0 else pltpu.roll(lags_ref[...], LANES - k, 1)
-            drive = jnp.dot(
-                window.astype(jnp.bfloat16), weights, preferred_element_type=jnp.float32
-            )
-            picked = jnp.where(lane % 8 == k, noise.astype(jnp.float32), 0.0).astype(jnp.bfloat16)
-            shock = jnp.dot(picked, noise_weights, preferred_element_type=jnp.float32)
-            root_variance = jnp.exp2(drive * half_scale - comp_ref[pl.ds(i, 1), :])
-            total = total + root_variance * (shock - root_variance)
+        noise = noise_ref[m].astype(jnp.float32)
+        lags = lags_ref[...]
+        for first in range(0, 8, 4):
+            steps = range(first, first + 4)
+            windows = [lags if k == 0 else pltpu.roll(lags, LANES - k, 1) for k in steps]
+            windows = jnp.concatenate(windows, 0).astype(jnp.bfloat16)
+            drives = jnp.dot(windows, weights, preferred_element_type=jnp.float32)
+            picked = [jnp.where(lane % 8 == k, noise, 0.0) for k in steps]
+            picked = jnp.concatenate(picked, 0).astype(jnp.bfloat16)
+            shocks = jnp.dot(picked, noise_weights, preferred_element_type=jnp.float32)
+            for n, k in enumerate(steps):
+                here = slice(n * paths, (n + 1) * paths)
+                lift = drives[here] * half_scale - comp_ref[pl.ds(8 * m + k, 1), :]
+                root_variance = jnp.exp2(lift)
+                total = total + root_variance * (shocks[here] - root_variance)
         lags_ref[...] = pltpu.roll(lags_ref[...], LANES - 8, 1)
         spot = jnp.exp2(total * growth)
         tenor = jnp.full((8, sets), 1.0, jnp.float32) * ((m + 1).astype(jnp.float32) / MATS)
@@ -197,7 +201,7 @@
 
 
 def prepare_kernel(
-    sets, owner_ref, params_ref, w_in_hbm, b_in_hbm, w_mid_hbm, win_ref, turned_ref, feat_ref,
+    sets, owner_ref, params_ref, w_in_hbm, b_in_hbm, w_mid_hbm, b_mid_ref, win_ref, turned_ref, feat_ref, bias_ref,
     w_in_ref, b_in_ref, w_mid_ref, sems,
 ):
     copies = [
@@ -215,6 +219,7 @@
         hot, _ = one_hot(t, sets)
         feat = dot(table, hot).astype(jnp.bfloat16)
         feat_ref[:, t * ROW_TILE : (t + 1) * ROW_TILE] = feat
+    bias_ref[...] = jnp.broadcast_to((0.5 * b_mid_ref[...]).T, bias_ref.shape)
     for copy in copies:
         copy.wait()
     weights_in = w_in_ref[...].astype(jnp.float32)
@@ -225,18 +230,19 @@
     turned_ref[...] = (0.5 * w_mid_ref[...].astype(jnp.float32)).T.astype(jnp.bfloat16)
 
 
-def prepare(owner, params, w_in, b_in, w_mid, sets):
+def prepare(owner, params, w_in, b_in, w_mid, b_mid, sets):
     smem = pl.BlockSpec(memory_space=pltpu.SMEM)
     vmem = pl.BlockSpec(memory_space=pltpu.VMEM)
     hbm = pl.BlockSpec(memory_space=pltpu.HBM)
     return pl.pallas_call(
         functools.partial(prepare_kernel, sets),
-        in_specs=[smem, vmem] + [hbm] * 3,
-        out_specs=[vmem] * 3,
+        in_specs=[smem, vmem] + [hbm] * 3 + [vmem],
+        out_specs=[vmem] * 4,
         out_shape=[
             jax.ShapeDtypeStruct((WIDTH, FEATURE_ROWS), jnp.bfloat16),
             jax.ShapeDtypeStruct((WIDTH, WIDTH), jnp.bfloat16),
             jax.ShapeDtypeStruct((FEATURE_ROWS, sets * PAIRS), jnp.bfloat16),
+            jax.ShapeDtypeStruct((WIDTH, LANES), jnp.float32),
         ],
         scratch_shapes=[
             pltpu.VMEM(w_in.shape, jnp.bfloat16),
@@ -247,13 +253,14 @@
         compiler_params=pltpu.CompilerParams(vmem_limit_bytes=16 * 1024 * 1024),
         name="prepare",
     )(
-        owner.reshape(1), in_hbm(params), in_hbm(w_in), in_hbm(b_in.reshape(1, -1)), in_hbm(w_mid)
+        owner.reshape(1), in_hbm(params), in_hbm(w_in), in_hbm(b_in.reshape(1, -1)), in_hbm(w_mid),
+        in_hbm(b_mid.reshape(1, -1)),
     )
 
 
 def forward_kernel(
-    owner_ref, b_mid_ref, w_out_ref, win_ref, turned_ref, feat_ref,
-    hidden_out, curve_out, mixed_out, pred_out, bias_ref, read_ref,
+    owner_ref, bias_ref, w_out_ref, win_ref, turned_ref, feat_ref,
+    hidden_out, curve_out, mixed_out, pred_out, read_ref,
     even_hidden, odd_hidden, even_mixed, odd_mixed,
 ):
     bf16 = jnp.bfloat16
@@ -264,7 +271,6 @@
     own = pl.ds(pl.multiple_of(block * cols, cols), cols)
     read_ref[...] = jnp.broadcast_to((0.5 * w_out_ref[...].astype(jnp.float32)).T, read_ref.shape)
     readout = jnp.broadcast_to(w_out_ref[...].astype(jnp.float32), (16, WIDTH)).astype(bf16)
-    bias_ref[...] = jnp.broadcast_to((0.5 * b_mid_ref[...]).T, bias_ref.shape)
 
     def wide(column):
         return jnp.concatenate([column] * (ROW_TILE // LANES), axis=1)
@@ -320,7 +326,7 @@
         step(t, buffers[t % 2], buffers[1 - t % 2], first=t < tiles, second=t <= tiles)
 
 
-def forward(place, b_mid, w_out, win, turned, feat):
+def forward(place, bias, w_out, win, turned, feat):
     rows = feat.shape[1]
     cols = WIDTH // 4
     vmem = pl.BlockSpec(memory_space=pltpu.VMEM)
@@ -339,7 +345,6 @@
         + [jax.ShapeDtypeStruct(*outs[-1])],
         scratch_shapes=[
             pltpu.VMEM((WIDTH, LANES), jnp.float32),
-            pltpu.VMEM((WIDTH, LANES), jnp.float32),
         ]
         + [pltpu.VMEM((WIDTH, ROW_TILE), jnp.bfloat16)] * 4,
         compiler_params=pltpu.CompilerParams(vmem_limit_bytes=FORWARD_VMEM),
@@ -347,7 +352,7 @@
             flops=2 * rows * WIDTH * (WIDTH + 32), bytes_accessed=4 << 20, transcendentals=0
         ),
         name="forward",
-    )(place, in_hbm(b_mid.reshape(1, -1)), w_out.reshape(1, -1), win, turned, feat)
+    )(place, bias, w_out.reshape(1, -1), win, turned, feat)
 
 
 def backward_kernel(
@@ -583,7 +588,7 @@
     turned = params.T
 
     sums = payoff_sums(turned, increments, groups).reshape(groups, 4 * set_dev, PAIRS)
-    win, weights, feat = prepare(owner, turned, w_in, b_in, w_mid, 4 * set_dev)
+    win, weights, feat, bias = prepare(owner, turned, w_in, b_in, w_mid, b_mid, 4 * set_dev)
     lanes = [[2 * j + c + top * h for j in range(groups)] for h in range(2) for c in range(2)]
     parts = lax.all_to_all(sums, "paths", 0, 0, axis_index_groups=lanes, tiled=True)
     parts, win = lax.optimization_barrier((parts, win))
@@ -591,7 +596,7 @@
     sums = [sums] + [swap(sums, mask, devices) for mask in (1, top, top + 1)]
 
     place = jnp.stack([owner, jnp.int32(top)])
-    saved = forward(place, b_mid, w_out, win, weights, feat)
+    saved = forward(place, bias, w_out, win, weights, feat)
     *parts, prices = backward(
         owner, sums, saved, win, feat, w_mid, b_out, 1.0 / set_count, groups
     )

time: 96.1 us -> 95.9 us (level)
  no operation moved by 1% of the time
where the time goes in v9:
time: 95.9 us; the launch traced here: 95.4 us
  waiting for transfers between devices  31.5 us (33%)
  Pallas kernels  31.2 us (33%)
  starting transfers between devices  30.2 us (31%)
  between operations  1.47 us (2%)
    ppermute x24, waiting for transfers between devices, swap(): return lax.ppermute(array, 'paths', [(i, i ^ bit) for i in range(devices)])  30 us
    ppermute x24, starting transfers between devices, swap(): return lax.ppermute(array, 'paths', [(i, i ^ bit) for i in range(devices)])  24 us
    pallas_call x1, Pallas kernels, forward(): pl.pallas_call(forward_kernel, in_specs=[smem] + [vmem] * 5, out_specs=[v...  12 us
    pallas_call x1, Pallas kernels, backward(): pl.pallas_call(functools.partial(backward_kernel, inv_sets), in_specs=[sm...  6.66 us
    pallas_call x1, Pallas kernels, payoff_sums(): pl.pallas_call(pricing_kernel, grid=(steps,), in_specs=[pl.BlockSpec((4,...  6.27 us
    all_to_all x1, starting transfers between devices, on_device(): lax.all_to_all(sums, 'paths', 0, 0, axis_index_groups=lanes, tiled=True)  6.18 us
    pallas_call x1, Pallas kernels, prepare(): pl.pallas_call(functools.partial(prepare_kernel, sets), in_specs=[smem, v...  3.18 us
    pallas_call x1, Pallas kernels, scaled(): pl.pallas_call(functools.partial(scaling_kernel, layout, groups), in_spec...  3.06 us
  transfers between devices with their start and end apart: 25, of which 14 were waited for; matrix products, arithmetic and copies ran while one was open for 1% of the time, Pallas kernels for 16%

profile of v9, /device:TPU:0, one launch (start us, length us, event | category | flops | bytes accessed | tf_op | source)
XLA Modules:
  0.0 95.4 jit_solution(17412123811510609462)
XLA Ops:
  0.6 6.3 %pricing.1 = f32[8,2,16,88]{3,2,1,0:T(8,128)} custom-call(f32[4,256]{1,0:T(4,128)} %bitcast.38, bf16[2,64,128]{2,1,0:T(8,128)(2,1)} %inc_ref.1), custom_call_target="tpu_custom_call" | custom-call | tf_op jit(solution)/shard_map/pricing/pallas_call | solution.py:131
  6.9 6.2 %all-to-all-start = ((f32[8,32,88]{2,1,0:T(8,128)}), f32[8,32,88]{2,1,0:T(8,128)S(1)}, u32[]{:S(2)}, u32[]{:S(2)}) async-start(f32[8,32,88]{2,1,0:T(8,128)} %bitcast.2), calls=%async_computation | async-start | bytes 262144 | tf_op jit(solution)/shard_map/all_to_all | solution.py:593
  13.1 0.7 reshape.62.w_out_ref
  14.4 3.2 %prepare.1 = (bf16[1024,16]{1,0:T(8,128)(2,1)S(1)}, bf16[1024,1024]{1,0:T(8,128)(2,1)S(1)}, bf16[16,2816]{1,0:T(8,128)(2,1)S(1)}, f32[1024,128]{1,0:T(8,128)S(1)}) custom-call(s32[1]{0:T(128)} %bitcast.owner_ref, f32[4,256]{1,0:T(4,128)} %bitcast.39, bf16[6,1024]{1,0:T(8,128)(2,1)} %w_in_hbm.1, f32[1,1024]{1,0:T(1,128)} %bitcast.40, ...), custom_call_target="tpu_custom_call" | custom-call | tf_op jit(solution)/shard_map/prepare/pallas_call | solution.py:237
  17.6 0.1 pad_add_fusion.owner_ref
  17.7 1.5 %all-to-all-done = f32[8,32,88]{2,1,0:T(8,128)S(1)} async-done(((f32[8,32,88]{2,1,0:T(8,128)}), f32[8,32,88]{2,1,0:T(8,128)S(1)}, u32[]{:S(2)}, u32[]{:S(2)}) %all-to-all-start) | async-done | bytes 90144 | tf_op jit(solution)/shard_map/all_to_all | solution.py:593
  19.2 0.1 collective-permute-start
  19.3 2.7 %collective-permute-start.1 = (f32[32,88]{1,0:T(8,128)S(1)}, f32[32,88]{1,0:T(8,128)S(1)}, u32[]{:S(2)}, u32[]{:S(2)}) collective-permute-start(f32[32,88]{1,0:T(8,128)S(1)} %broadcast_multiply_fusion.sums_ref), channel_id=1, source_target_pairs={{0,16},{1,17},{2,18},{3,19},{4,20},{5,21},{6,22},{7,23},{8,24},{9,... | collective-permute-start | bytes 33800 | tf_op jit(solution)/shard_map/ppermute | solution.py:558
  21.9 0.1 collective-permute-start.2
  22.1 12.0 %forward.1 = (bf16[1024,2816]{1,0:T(8,128)(2,1)S(1)}, f32[1024,2816]{1,0:T(8,128)S(1)}, bf16[256,2816]{1,0:T(8,128)(2,1)S(1)}, f32[1,2816]{1,0:T(1,128)S(1)}) custom-call(s32[2]{0:T(128)S(1)} %pad_add_fusion.owner_ref, f32[1024,128]{1,0:T(8,128)S(1)} %get-tuple-element.37.bias_ref, bf16[1,1024]{1,0:T(2,128)(2,1)S(1)} %reshape.62.w_out_ref, ...), custom_call_target="tpu_custom_call" | custom-call | flops 6090129408 | bytes 4194304 | tf_op jit(solution)/shard_map/forward/pallas_call | solution.py:340
  34.1 0.0 collective-permute-done.near_ref
  34.1 0.0 collective-permute-done.1.far_ref
  34.1 6.7 %backward.1 = (f32[4,88,128]{2,1,0:T(8,128)S(1)}, f32[4,88,128]{2,1,0:T(8,128)S(1)}, f32[4,88,128]{2,1,0:T(8,128)S(1)}, f32[4,88,128]{2,1,0:T(8,128)S(1)}, f32[4...) custom-call(s32[1]{0:T(128)} %bitcast.owner_ref, f32[32,88]{1,0:T(8,128)S(1)} %broadcast_multiply_fusion.sums_ref, ...), custom_call_target="tpu_custom_call" | custom-call | tf_op jit(solution)/shard_map/backward/pallas_call | solution.py:456
  40.8 0.8 collective-permute-start.9
  41.6 1.3 %collective-permute-start.6 = (f32[4,88,128]{2,1,0:T(8,128)S(1)}, f32[4,88,128]{2,1,0:T(8,128)S(1)}, u32[]{:S(2)}, u32[]{:S(2)}) collective-permute-start(f32[4,88,128]{2,1,0:T(8,128)S(1)} %get-tuple-element.49), channel_id=1, source_target_pairs={{0,4},{1,5},{2,6},{3,7},{4,0},{5,1},{6,2},{7,3},{8,12},{9,13},{10,... | collective-permute-start | bytes 540680 | tf_op jit(solution)/shard_map/ppermute | solution.py:558
  42.8 1.5 %collective-permute-start.3 = (f32[4,88,128]{2,1,0:T(8,128)S(1)}, f32[4,88,128]{2,1,0:T(8,128)S(1)}, u32[]{:S(2)}, u32[]{:S(2)}) collective-permute-start(f32[4,88,128]{2,1,0:T(8,128)S(1)} %get-tuple-element.47), channel_id=1, source_target_pairs={{0,2},{1,3},{2,0},{3,1},{4,6},{5,7},{6,4},{7,5},{8,10},{9,11},{10,... | collective-permute-start | bytes 540680 | tf_op jit(solution)/shard_map/ppermute | solution.py:558
  44.3 3.3 %collective-permute-done.9 = f32[4,88,128]{2,1,0:T(8,128)S(1)} collective-permute-done((f32[4,88,128]{2,1,0:T(8,128)S(1)}, f32[4,88,128]{2,1,0:T(8,128)S(1)}, u32[]{:S(2)}, u32[]{:S(2)}) %collective-permute-start.9) | collective-permute-done | bytes 180256 | tf_op jit(solution)/shard_map/ppermute | solution.py:558
  47.7 0.6 collective-permute-start.10
  48.3 1.5 %collective-permute-start.7 = (f32[2,88,128]{2,1,0:T(8,128)S(1)}, f32[2,88,128]{2,1,0:T(8,128)S(1)}, u32[]{:S(2)}, u32[]{:S(2)}) collective-permute-start(f32[2,88,128]{2,1,0:T(8,128)S(1)} %dynamic-slice_bitcast_fusion.1), channel_id=1, source_target_pairs={{0,8},{1,9},{2,10},{3,11},{4,12},{5,13},{6,14},{7,15},{8,0},{9,1},... | collective-permute-start | bytes 270344 | tf_op jit(solution)/shard_map/ppermute | solution.py:558
  49.9 1.5 %collective-permute-start.4 = (f32[2,88,128]{2,1,0:T(8,128)S(1)}, f32[2,88,128]{2,1,0:T(8,128)S(1)}, u32[]{:S(2)}, u32[]{:S(2)}) collective-permute-start(f32[2,88,128]{2,1,0:T(8,128)S(1)} %dynamic-slice_bitcast_fusion.2), channel_id=1, source_target_pairs={{0,4},{1,5},{2,6},{3,7},{4,0},{5,1},{6,2},{7,3},{8,12},{9,13},{10,... | collective-permute-start | bytes 270344 | tf_op jit(solution)/shard_map/ppermute | solution.py:558
  51.4 0.8 collective-permute-done.10
  52.3 0.6 collective-permute-start.11
  52.9 0.0 collective-permute-done.7
  53.0 1.5 %collective-permute-start.8 = (f32[1,88,128]{2,1,0:T(8,128)S(1)}, f32[1,88,128]{2,1,0:T(8,128)S(1)}, u32[]{:S(2)}, u32[]{:S(2)}) collective-permute-start(f32[1,88,128]{2,1,0:T(8,128)S(1)} %constant_dynamic-slice_fusion.1), channel_id=1, source_target_pairs={{0,2},{1,3},{2,0},{3,1},{4,6},{5,7},{6,4},{7,5},{8,10},{9,11},{10,... | collective-permute-start | bytes 135176 | tf_op jit(solution)/shard_map/ppermute | solution.py:558
  54.5 0.3 collective-permute-done.4
  54.8 1.2 %collective-permute-start.5 = (f32[1,88,128]{2,1,0:T(8,128)S(1)}, f32[1,88,128]{2,1,0:T(8,128)S(1)}, u32[]{:S(2)}, u32[]{:S(2)}) collective-permute-start(f32[1,88,128]{2,1,0:T(8,128)S(1)} %constant_dynamic-slice_fusion.2), channel_id=1, source_target_pairs={{0,8},{1,9},{2,10},{3,11},{4,12},{5,13},{6,14},{7,15},{8,0},{9,1},... | collective-permute-start | bytes 135176 | tf_op jit(solution)/shard_map/ppermute | solution.py:558
  56.0 0.4 collective-permute-done.11
  56.4 0.7 collective-permute-done.8
  57.1 2.3 %collective-permute-done.5 = f32[1,88,128]{2,1,0:T(8,128)S(1)} collective-permute-done((f32[1,88,128]{2,1,0:T(8,128)S(1)}, f32[1,88,128]{2,1,0:T(8,128)S(1)}, u32[]{:S(2)}, u32[]{:S(2)}) %collective-permute-start.5) | collective-permute-done | bytes 45088 | tf_op jit(solution)/shard_map/ppermute | solution.py:558
  59.5 1.1 %collective-permute-start.14 = (f32[1,264,128]{2,1,0:T(8,128)S(1)}, f32[1,264,128]{2,1,0:T(8,128)S(1)}, u32[]{:S(2)}, u32[]{:S(2)}) collective-permute-start(f32[1,264,128]{2,1,0:T(8,128)S(1)} %pad_maximum_fusion.3), channel_id=1, source_target_pairs={{0,8},{1,9},{2,10},{3,11},{4,12},{5,13},{6,14},{7,15},{8,0},{9,1},... | collective-permute-start | bytes 405512 | tf_op jit(solution)/shard_map/ppermute | solution.py:558
  60.5 2.6 %collective-permute-start.13 = (f32[1,264,128]{2,1,0:T(8,128)S(1)}, f32[1,264,128]{2,1,0:T(8,128)S(1)}, u32[]{:S(2)}, u32[]{:S(2)}) collective-permute-start(f32[1,264,128]{2,1,0:T(8,128)S(1)} %pad_maximum_fusion.3), channel_id=1, source_target_pairs={{0,16},{1,17},{2,18},{3,19},{4,20},{5,21},{6,22},{7,23},{8,24},{9,... | collective-permute-start | bytes 405512 | tf_op jit(solution)/shard_map/ppermute | solution.py:558
  63.1 0.8 collective-permute-start.12
  63.9 2.7 %collective-permute-done.14 = f32[1,264,128]{2,1,0:T(8,128)S(1)} collective-permute-done((f32[1,264,128]{2,1,0:T(8,128)S(1)}, f32[1,264,128]{2,1,0:T(8,128)S(1)}, u32[]{:S(2)}, u32[]{:S(2)}) %collective-permute-start.14) | collective-permute-done | bytes 135200 | tf_op jit(solution)/shard_map/ppermute | solution.py:558
  66.6 4.0 %collective-permute-done.13 = f32[1,264,128]{2,1,0:T(8,128)S(1)} collective-permute-done((f32[1,264,128]{2,1,0:T(8,128)S(1)}, f32[1,264,128]{2,1,0:T(8,128)S(1)}, u32[]{:S(2)}, u32[]{:S(2)}) %collective-permute-start.13) | collective-permute-done | bytes 135200 | tf_op jit(solution)/shard_map/ppermute | solution.py:558
  70.5 0.0 collective-permute-done.12
  70.6 0.7 collective-permute-start.15
  71.3 1.5 %collective-permute-start.16 = (f32[4,128,128]{2,1,0:T(8,128)S(1)}, f32[4,128,128]{2,1,0:T(8,128)S(1)}, u32[]{:S(2)}, u32[]{:S(2)}) collective-permute-start(f32[4,128,128]{2,1,0:T(8,128)S(1)} %slice.9), channel_id=1, source_target_pairs={{0,4},{1,5},{2,6},{3,7},{4,0},{5,1},{6,2},{7,3},{8,12},{9,13},{10,... | collective-permute-start | bytes 786440 | tf_op jit(solution)/shard_map/ppermute | solution.py:558
  72.8 0.0 collective-permute-start.19
  72.8 5.1 %collective-permute-done.15.refs_1_ = f32[4,136,128]{2,1,0:T(8,128)S(1)} collective-permute-done((f32[4,136,128]{2,1,0:T(8,128)S(1)}, f32[4,136,128]{2,1,0:T(8,128)S(1)}, u32[]{:S(2)}, u32[]{:S(2)}) %collective-permute-start.15) | collective-permute-done | bytes 278560 | tf_op jit(solution)/shard_map/ppermute | solution.py:558
  78.0 1.5 %collective-permute-start.17 = (f32[8,136,128]{2,1,0:T(8,128)S(1)}, f32[8,136,128]{2,1,0:T(8,128)S(1)}, u32[]{:S(2)}, u32[]{:S(2)}) collective-permute-start(f32[8,136,128]{2,1,0:T(8,128)S(1)} %pad_maximum_fusion), channel_id=1, source_target_pairs={{0,4},{1,5},{2,6},{3,7},{4,0},{5,1},{6,2},{7,3},{8,12},{9,13},{10,... | collective-permute-start | bytes 1671176 | tf_op jit(solution)/shard_map/ppermute | solution.py:558
  79.5 1.4 %collective-permute-start.18 = (f32[8,128,128]{2,1,0:T(8,128)S(1)}, f32[8,128,128]{2,1,0:T(8,128)S(1)}, u32[]{:S(2)}, u32[]{:S(2)}) collective-permute-start(f32[8,128,128]{2,1,0:T(8,128)S(1)} %pad_maximum_fusion.2), channel_id=1, source_target_pairs={{0,2},{1,3},{2,0},{3,1},{4,6},{5,7},{6,4},{7,5},{8,10},{9,11},{10,... | collective-permute-start | bytes 1572872 | tf_op jit(solution)/shard_map/ppermute | solution.py:558
  80.9 0.5 collective-permute-start.21
  81.5 1.4 %collective-permute-done.21.refs_7_ = f32[4,128,128]{2,1,0:T(8,128)S(1)} collective-permute-done((f32[4,128,128]{2,1,0:T(8,128)S(1)}, f32[4,128,128]{2,1,0:T(8,128)S(1)}, u32[]{:S(2)}, u32[]{:S(2)}) %collective-permute-start.21) | collective-permute-done | bytes 262176 | tf_op jit(solution)/shard_map/ppermute | solution.py:558
  82.9 5.9 %collective-permute-done.18.refs_4_ = f32[8,128,128]{2,1,0:T(8,128)S(1)} collective-permute-done((f32[8,128,128]{2,1,0:T(8,128)S(1)}, f32[8,128,128]{2,1,0:T(8,128)S(1)}, u32[]{:S(2)}, u32[]{:S(2)}) %collective-permute-start.18) | collective-permute-done | bytes 524320 | tf_op jit(solution)/shard_map/ppermute | solution.py:558
  88.8 0.9 collective-permute-done.17.refs_3_
  89.7 0.5 collective-permute-start.23
  90.2 2.2 %collective-permute-done.23.refs_9_ = f32[8,128,128]{2,1,0:T(8,128)S(1)} collective-permute-done((f32[8,128,128]{2,1,0:T(8,128)S(1)}, f32[8,128,128]{2,1,0:T(8,128)S(1)}, u32[]{:S(2)}, u32[]{:S(2)}) %collective-permute-start.23) | collective-permute-done | bytes 524320 | tf_op jit(solution)/shard_map/ppermute | solution.py:558
  92.4 3.1 %scaling.1 = (f32[6,1024]{1,0:T(8,128)}, f32[1,1024]{1,0:T(1,128)}, f32[1024,1024]{1,0:T(8,128)}, f32[1,1024]{1,0:T(1,128)}, f32[1,1024]{1,0:T(1,128)}, /*index=5*/f32[1,1]{1,0:T(1,128)}) custom-call(s32[1]{0:T(128)} %bitcast.owner_ref, f32[4,264,128]{2,1,0:T(8,128)S(1)} %pad_maximum_fusion.1.refs_0_, f32[4,136,128]{2,1,0:T(8,128)S(1)} %collective-permute-done.15.refs_1_, ...), custom_call_target="tpu_custom_call" | custom-call | tf_op jit(solution)/shard_map/scaling/pallas_call | solution.py:543
  (32 shorter events, 0.4 us)
Async XLA Ops:
  6.9 12.3 %all-to-all-start = ((f32[8,32,88]{2,1,0:T(8,128)}), f32[8,32,88]{2,1,0:T(8,128)S(1)}, u32[]{:S(2)}, u32[]{:S(2)}) async-start(f32[8,32,88]{2,1,0:T(8,128)} %bitcast.2), calls=%async_computation | async-start | bytes 262144 | tf_op jit(solution)/shard_map/all_to_all | solution.py:593
  19.2 14.9 %collective-permute-start = (f32[32,88]{1,0:T(8,128)S(1)}, f32[32,88]{1,0:T(8,128)S(1)}, u32[]{:S(2)}, u32[]{:S(2)}) collective-permute-start(f32[32,88]{1,0:T(8,128)S(1)} %broadcast_multiply_fusion.sums_ref), channel_id=1, source_target_pairs={{0,1},{1,0},{2,3},{3,2},{4,5},{5,4},{6,7},{7,6},{8,9},{9,8},{10,11... | collective-permute-start | bytes 33800 | tf_op jit(solution)/shard_map/ppermute | solution.py:558
  19.3 14.8 %collective-permute-start.1 = (f32[32,88]{1,0:T(8,128)S(1)}, f32[32,88]{1,0:T(8,128)S(1)}, u32[]{:S(2)}, u32[]{:S(2)}) collective-permute-start(f32[32,88]{1,0:T(8,128)S(1)} %broadcast_multiply_fusion.sums_ref), channel_id=1, source_target_pairs={{0,16},{1,17},{2,18},{3,19},{4,20},{5,21},{6,22},{7,23},{8,24},{9,... | collective-permute-start | bytes 33800 | tf_op jit(solution)/shard_map/ppermute | solution.py:558
  21.9 12.1 %collective-permute-start.2 = (f32[32,88]{1,0:T(8,128)S(1)}, f32[32,88]{1,0:T(8,128)S(1)}, u32[]{:S(2)}, u32[]{:S(2)}) collective-permute-start(f32[32,88]{1,0:T(8,128)S(1)} %broadcast_multiply_fusion.sums_ref), channel_id=1, source_target_pairs={{0,17},{1,16},{2,19},{3,18},{4,21},{5,20},{6,23},{7,22},{8,25},{9,... | collective-permute-start | bytes 33800 | tf_op jit(solution)/shard_map/ppermute | solution.py:558
  40.8 6.9 %collective-permute-start.9 = (f32[4,88,128]{2,1,0:T(8,128)S(1)}, f32[4,88,128]{2,1,0:T(8,128)S(1)}, u32[]{:S(2)}, u32[]{:S(2)}) collective-permute-start(f32[4,88,128]{2,1,0:T(8,128)S(1)} %get-tuple-element.51), channel_id=1, source_target_pairs={{0,8},{1,9},{2,10},{3,11},{4,12},{5,13},{6,14},{7,15},{8,0},{9,1},... | collective-permute-start | bytes 540680 | tf_op jit(solution)/shard_map/ppermute | solution.py:558
  41.6 6.7 %collective-permute-start.6 = (f32[4,88,128]{2,1,0:T(8,128)S(1)}, f32[4,88,128]{2,1,0:T(8,128)S(1)}, u32[]{:S(2)}, u32[]{:S(2)}) collective-permute-start(f32[4,88,128]{2,1,0:T(8,128)S(1)} %get-tuple-element.49), channel_id=1, source_target_pairs={{0,4},{1,5},{2,6},{3,7},{4,0},{5,1},{6,2},{7,3},{8,12},{9,13},{10,... | collective-permute-start | bytes 540680 | tf_op jit(solution)/shard_map/ppermute | solution.py:558
  42.8 7.0 %collective-permute-start.3 = (f32[4,88,128]{2,1,0:T(8,128)S(1)}, f32[4,88,128]{2,1,0:T(8,128)S(1)}, u32[]{:S(2)}, u32[]{:S(2)}) collective-permute-start(f32[4,88,128]{2,1,0:T(8,128)S(1)} %get-tuple-element.47), channel_id=1, source_target_pairs={{0,2},{1,3},{2,0},{3,1},{4,6},{5,7},{6,4},{7,5},{8,10},{9,11},{10,... | collective-permute-start | bytes 540680 | tf_op jit(solution)/shard_map/ppermute | solution.py:558
  47.7 4.6 %collective-permute-start.10 = (f32[2,88,128]{2,1,0:T(8,128)S(1)}, f32[2,88,128]{2,1,0:T(8,128)S(1)}, u32[]{:S(2)}, u32[]{:S(2)}) collective-permute-start(f32[2,88,128]{2,1,0:T(8,128)S(1)} %dynamic-slice_bitcast_fusion), channel_id=1, source_target_pairs={{0,2},{1,3},{2,0},{3,1},{4,6},{5,7},{6,4},{7,5},{8,10},{9,11},{10,... | collective-permute-start | bytes 270344 | tf_op jit(solution)/shard_map/ppermute | solution.py:558
  48.3 4.6 %collective-permute-start.7 = (f32[2,88,128]{2,1,0:T(8,128)S(1)}, f32[2,88,128]{2,1,0:T(8,128)S(1)}, u32[]{:S(2)}, u32[]{:S(2)}) collective-permute-start(f32[2,88,128]{2,1,0:T(8,128)S(1)} %dynamic-slice_bitcast_fusion.1), channel_id=1, source_target_pairs={{0,8},{1,9},{2,10},{3,11},{4,12},{5,13},{6,14},{7,15},{8,0},{9,1},... | collective-permute-start | bytes 270344 | tf_op jit(solution)/shard_map/ppermute | solution.py:558
  49.9 4.9 %collective-permute-start.4 = (f32[2,88,128]{2,1,0:T(8,128)S(1)}, f32[2,88,128]{2,1,0:T(8,128)S(1)}, u32[]{:S(2)}, u32[]{:S(2)}) collective-permute-start(f32[2,88,128]{2,1,0:T(8,128)S(1)} %dynamic-slice_bitcast_fusion.2), channel_id=1, source_target_pairs={{0,4},{1,5},{2,6},{3,7},{4,0},{5,1},{6,2},{7,3},{8,12},{9,13},{10,... | collective-permute-start | bytes 270344 | tf_op jit(solution)/shard_map/ppermute | solution.py:558
  52.3 4.1 %collective-permute-start.11 = (f32[1,88,128]{2,1,0:T(8,128)S(1)}, f32[1,88,128]{2,1,0:T(8,128)S(1)}, u32[]{:S(2)}, u32[]{:S(2)}) collective-permute-start(f32[1,88,128]{2,1,0:T(8,128)S(1)} %constant_dynamic-slice_fusion), channel_id=1, source_target_pairs={{0,4},{1,5},{2,6},{3,7},{4,0},{5,1},{6,2},{7,3},{8,12},{9,13},{10,... | collective-permute-start | bytes 135176 | tf_op jit(solution)/shard_map/ppermute | solution.py:558
  53.0 4.1 %collective-permute-start.8 = (f32[1,88,128]{2,1,0:T(8,128)S(1)}, f32[1,88,128]{2,1,0:T(8,128)S(1)}, u32[]{:S(2)}, u32[]{:S(2)}) collective-permute-start(f32[1,88,128]{2,1,0:T(8,128)S(1)} %constant_dynamic-slice_fusion.1), channel_id=1, source_target_pairs={{0,2},{1,3},{2,0},{3,1},{4,6},{5,7},{6,4},{7,5},{8,10},{9,11},{10,... | collective-permute-start | bytes 135176 | tf_op jit(solution)/shard_map/ppermute | solution.py:558
  54.8 4.6 %collective-permute-start.5 = (f32[1,88,128]{2,1,0:T(8,128)S(1)}, f32[1,88,128]{2,1,0:T(8,128)S(1)}, u32[]{:S(2)}, u32[]{:S(2)}) collective-permute-start(f32[1,88,128]{2,1,0:T(8,128)S(1)} %constant_dynamic-slice_fusion.2), channel_id=1, source_target_pairs={{0,8},{1,9},{2,10},{3,11},{4,12},{5,13},{6,14},{7,15},{8,0},{9,1},... | collective-permute-start | bytes 135176 | tf_op jit(solution)/shard_map/ppermute | solution.py:558
  59.5 7.1 %collective-permute-start.14 = (f32[1,264,128]{2,1,0:T(8,128)S(1)}, f32[1,264,128]{2,1,0:T(8,128)S(1)}, u32[]{:S(2)}, u32[]{:S(2)}) collective-permute-start(f32[1,264,128]{2,1,0:T(8,128)S(1)} %pad_maximum_fusion.3), channel_id=1, source_target_pairs={{0,8},{1,9},{2,10},{3,11},{4,12},{5,13},{6,14},{7,15},{8,0},{9,1},... | collective-permute-start | bytes 405512 | tf_op jit(solution)/shard_map/ppermute | solution.py:558
  60.5 10.0 %collective-permute-start.13 = (f32[1,264,128]{2,1,0:T(8,128)S(1)}, f32[1,264,128]{2,1,0:T(8,128)S(1)}, u32[]{:S(2)}, u32[]{:S(2)}) collective-permute-start(f32[1,264,128]{2,1,0:T(8,128)S(1)} %pad_maximum_fusion.3), channel_id=1, source_target_pairs={{0,16},{1,17},{2,18},{3,19},{4,20},{5,21},{6,22},{7,23},{8,24},{9,... | collective-permute-start | bytes 405512 | tf_op jit(solution)/shard_map/ppermute | solution.py:558
  63.1 7.4 %collective-permute-start.12 = (f32[1,264,128]{2,1,0:T(8,128)S(1)}, f32[1,264,128]{2,1,0:T(8,128)S(1)}, u32[]{:S(2)}, u32[]{:S(2)}) collective-permute-start(f32[1,264,128]{2,1,0:T(8,128)S(1)} %pad_maximum_fusion.3), channel_id=1, source_target_pairs={{0,24},{1,25},{2,26},{3,27},{4,28},{5,29},{6,30},{7,31},{8,16},{9,... | collective-permute-start | bytes 405512 | tf_op jit(solution)/shard_map/ppermute | solution.py:558
  70.6 7.3 %collective-permute-start.15 = (f32[4,136,128]{2,1,0:T(8,128)S(1)}, f32[4,136,128]{2,1,0:T(8,128)S(1)}, u32[]{:S(2)}, u32[]{:S(2)}) collective-permute-start(f32[4,136,128]{2,1,0:T(8,128)S(1)} %slice.8), channel_id=1, source_target_pairs={{0,2},{1,3},{2,0},{3,1},{4,6},{5,7},{6,4},{7,5},{8,10},{9,11},{10,... | collective-permute-start | bytes 835592 | tf_op jit(solution)/shard_map/ppermute | solution.py:558
  71.3 8.2 %collective-permute-start.16 = (f32[4,128,128]{2,1,0:T(8,128)S(1)}, f32[4,128,128]{2,1,0:T(8,128)S(1)}, u32[]{:S(2)}, u32[]{:S(2)}) collective-permute-start(f32[4,128,128]{2,1,0:T(8,128)S(1)} %slice.9), channel_id=1, source_target_pairs={{0,4},{1,5},{2,6},{3,7},{4,0},{5,1},{6,2},{7,3},{8,12},{9,13},{10,... | collective-permute-start | bytes 786440 | tf_op jit(solution)/shard_map/ppermute | solution.py:558
  72.8 10.1 %collective-permute-start.19 = (f32[4,264,128]{2,1,0:T(8,128)S(1)}, f32[4,264,128]{2,1,0:T(8,128)S(1)}, u32[]{:S(2)}, u32[]{:S(2)}) collective-permute-start(f32[4,264,128]{2,1,0:T(8,128)S(1)} %pad_maximum_fusion.1.refs_0_), channel_id=1, source_target_pairs={{0,1},{1,0},{2,3},{3,2},{4,5},{5,4},{6,7},{7,6},{8,9},{9,8},{10,11... | collective-permute-start | bytes 1622024 | tf_op jit(solution)/shard_map/ppermute | solution.py:558
  78.0 11.7 %collective-permute-start.17 = (f32[8,136,128]{2,1,0:T(8,128)S(1)}, f32[8,136,128]{2,1,0:T(8,128)S(1)}, u32[]{:S(2)}, u32[]{:S(2)}) collective-permute-start(f32[8,136,128]{2,1,0:T(8,128)S(1)} %pad_maximum_fusion), channel_id=1, source_target_pairs={{0,4},{1,5},{2,6},{3,7},{4,0},{5,1},{6,2},{7,3},{8,12},{9,13},{10,... | collective-permute-start | bytes 1671176 | tf_op jit(solution)/shard_map/ppermute | solution.py:558
  79.5 9.2 %collective-permute-start.18 = (f32[8,128,128]{2,1,0:T(8,128)S(1)}, f32[8,128,128]{2,1,0:T(8,128)S(1)}, u32[]{:S(2)}, u32[]{:S(2)}) collective-permute-start(f32[8,128,128]{2,1,0:T(8,128)S(1)} %pad_maximum_fusion.2), channel_id=1, source_target_pairs={{0,2},{1,3},{2,0},{3,1},{4,6},{5,7},{6,4},{7,5},{8,10},{9,11},{10,... | collective-permute-start | bytes 1572872 | tf_op jit(solution)/shard_map/ppermute | solution.py:558
  80.9 1.9 %collective-permute-start.20 = (f32[4,136,128]{2,1,0:T(8,128)S(1)}, f32[4,136,128]{2,1,0:T(8,128)S(1)}, u32[]{:S(2)}, u32[]{:S(2)}) collective-permute-start(f32[4,136,128]{2,1,0:T(8,128)S(1)} %collective-permute-done.15.refs_1_), channel_id=1, source_target_pairs={{0,1},{1,0},{2,3},{3,2},{4,5},{5,4},{6,7},{7,6},{8,9},{9,8},{10,11... | collective-permute-start | bytes 835592 | tf_op jit(solution)/shard_map/ppermute | solution.py:558
  80.9 1.9 %collective-permute-start.21 = (f32[4,128,128]{2,1,0:T(8,128)S(1)}, f32[4,128,128]{2,1,0:T(8,128)S(1)}, u32[]{:S(2)}, u32[]{:S(2)}) collective-permute-start(f32[4,128,128]{2,1,0:T(8,128)S(1)} %collective-permute-done.16.refs_2_), channel_id=1, source_target_pairs={{0,1},{1,0},{2,3},{3,2},{4,5},{5,4},{6,7},{7,6},{8,9},{9,8},{10,11... | collective-permute-start | bytes 786440 | tf_op jit(solution)/shard_map/ppermute | solution.py:558
  89.7 2.7 %collective-permute-start.22 = (f32[8,136,128]{2,1,0:T(8,128)S(1)}, f32[8,136,128]{2,1,0:T(8,128)S(1)}, u32[]{:S(2)}, u32[]{:S(2)}) collective-permute-start(f32[8,136,128]{2,1,0:T(8,128)S(1)} %collective-permute-done.17.refs_3_), channel_id=1, source_target_pairs={{0,1},{1,0},{2,3},{3,2},{4,5},{5,4},{6,7},{7,6},{8,9},{9,8},{10,11... | collective-permute-start | bytes 1671176 | tf_op jit(solution)/shard_map/ppermute | solution.py:558
  89.7 2.7 %collective-permute-start.23 = (f32[8,128,128]{2,1,0:T(8,128)S(1)}, f32[8,128,128]{2,1,0:T(8,128)S(1)}, u32[]{:S(2)}, u32[]{:S(2)}) collective-permute-start(f32[8,128,128]{2,1,0:T(8,128)S(1)} %collective-permute-done.18.refs_4_), channel_id=1, source_target_pairs={{0,1},{1,0},{2,3},{3,2},{4,5},{5,4},{6,7},{7,6},{8,9},{9,8},{10,11... | collective-permute-start | bytes 1572872 | tf_op jit(solution)/shard_map/ppermute | solution.py:558
